TPU v7x, 32 devices: a whole 2x2x4 slice. The times are simulated.
32 devices in a mesh: section: 2 (over core), dp: 4 (over y, x), tensor: 4 (over z).
Axes of the slice: x: 2, y: 2, z: 4, core: 2. Of those that a mesh axis runs over, the one named last changes fastest.
Arguments:
- codes: bfloat16 [8, 256, 3, 1024], P('dp', 'tensor'), may hold values from -4 to 4
- lengths: int32 [8], P('dp'), may hold values from 33 to 256, as said below
- gains: float32 [2, 2, 1024], P('section'), may hold values from 0.5 to 1.5
- w_qkv: bfloat16 [2, 1024, 3, 1024], P('section', None, None, 'tensor'), may hold values from -0.1875 to 0.1875
- w_out: bfloat16 [2, 1024, 1024], P('section', 'tensor'), may hold values from -0.5 to 0.5
- w_up: bfloat16 [2, 1024, 4096], P('section', None, 'tensor'), may hold values from -0.1875 to 0.1875
- w_down: bfloat16 [2, 4096, 1024], P('section', 'tensor'), may hold values from -0.09375 to 0.09375
- cotangent: bfloat16 [8, 256, 3, 1024], P('dp', 'tensor'), may hold values from -6 to 6
Outputs:
- output: bfloat16 [8, 256, 3, 1024], P('dp', 'tensor', None, 'section')
- code_grad: float32 [8, 256, 3, 1024], P('dp', 'tensor', None, 'section')
- gain_grad: float32 [2, 2, 1024], P('section')
- qkv_grad: float32 [2, 1024, 3, 1024], P('section', None, None, 'tensor')
- out_grad: float32 [2, 1024, 1024], P('section', 'tensor')
- up_grad: float32 [2, 1024, 4096], P('section', None, 'tensor')
- down_grad: float32 [2, 4096, 1024], P('section', 'tensor')
Inputs may be any that keep to these rules, and one draw needn't show every extreme that they name: `lengths`: each utterance's valid frames come first; in every draw some utterance has all 256 frames valid.
All inputs are finite; a program needn't handle non-finite values.
Results may differ from a plain program's by a relative error of at most 0.017.
Values may be sent and summed in bfloat16 or wider, within the bound.
No kernel may reach another device: no remote copies, remote signals or barrier semaphores. Data moves between devices by JAX's collectives and lax.ppermute only.
A program may use at most 256 MiB of HBM per device.

v0:
```python
import jax
import jax.numpy as jnp
from jax import lax
from jax.sharding import PartitionSpec as P

HEAD_DIM = 64


epsilon = 1e-06
negative = -1e30


def shifted(value, axis, steps):
    count = lax.axis_size(axis)
    initial, last = (max(0, -steps), min(count, count - steps))
    return lax.ppermute(value, axis, [(source, source + steps) for source in range(initial, last)])


def gelu_exact(values):
    return jax.nn.gelu(values, approximate=False)


def guarded(flag, compute, operand):

    def empty(inner):
        return jax.tree.map(jnp.zeros_like, compute(inner))

    return lax.cond(flag, compute, empty, operand)


def norm_forward(values, gain_vector):
    factor = lax.rsqrt(jnp.mean(values * values, axis=-1, keepdims=True) + epsilon)
    return (values * factor * gain_vector, factor)


def norm_backward(values, factor, gain_vector, upstream):
    weighted = upstream * gain_vector
    inner = jnp.mean(weighted * values, axis=-1, keepdims=True)
    grad_values = factor * weighted - values * (factor * factor * factor) * inner
    return (grad_values, jnp.sum(upstream * values * factor, axis=0))


def row_gather(values):
    return lax.all_gather(values, "tensor", axis=0, tiled=True)


def row_scatter(values):
    return lax.psum_scatter(values, "tensor", scatter_dimension=0, tiled=True)


def grad_gather(values):
    return lax.all_gather(values, "tensor", axis=0, tiled=True)


def grad_scatter(values):
    return lax.psum_scatter(values, "tensor", scatter_dimension=0, tiled=True)


def masked_scores(queries, key_rows, allowed):
    scores = jnp.einsum(
        "gqhd,gkhd->ghqk", queries, key_rows, preferred_element_type=jnp.float32
    ) * HEAD_DIM ** (-0.5)
    return jnp.where(allowed[:, None], scores, negative)


def attend(shaped, allowed):
    scores = masked_scores(shaped[:, :, 0], shaped[:, :, 1], allowed)
    row_peak = jnp.max(scores, axis=-1, keepdims=True)
    raised = jnp.exp(scores - row_peak)
    row_total = jnp.sum(raised, axis=-1, keepdims=True)
    weights_low = (raised / row_total).astype(jnp.bfloat16)
    mixed = jnp.einsum(
        "ghqk,gkhd->gqhd", weights_low, shaped[:, :, 2], preferred_element_type=jnp.float32
    )
    return (mixed.astype(jnp.bfloat16), row_peak + jnp.log(row_total))


def attend_back(shaped, allowed, summary, grad_mixed):
    queries = shaped[:, :, 0]
    key_rows = shaped[:, :, 1]
    value_rows = shaped[:, :, 2]
    exact_probs = jnp.exp(masked_scores(queries, key_rows, allowed) - summary)
    weights_low = exact_probs.astype(jnp.bfloat16)
    grad_values = jnp.einsum(
        "ghqk,gqhd->gkhd", weights_low, grad_mixed, preferred_element_type=jnp.float32
    )
    grad_probs = jnp.einsum(
        "gqhd,gkhd->ghqk", grad_mixed, value_rows, preferred_element_type=jnp.float32
    )
    center = jnp.sum(grad_probs * exact_probs, axis=-1, keepdims=True)
    grad_scores = (exact_probs * (grad_probs - center)).astype(jnp.bfloat16)
    score_scale = HEAD_DIM ** (-0.5)
    grad_queries = (
        jnp.einsum("ghqk,gkhd->gqhd", grad_scores, key_rows, preferred_element_type=jnp.float32)
        * score_scale
    )
    grad_keys = (
        jnp.einsum("ghqk,gqhd->gkhd", grad_scores, queries, preferred_element_type=jnp.float32)
        * score_scale
    )
    return jnp.stack([grad_queries, grad_keys, grad_values], axis=2).astype(jnp.bfloat16)


def attention_forward(first_rows, w_query, w_mix, allowed, span):
    packed = jnp.einsum(
        "rd,dce->rce", first_rows, w_query, preferred_element_type=jnp.float32
    ).astype(jnp.bfloat16)
    row_count = packed.shape[0]
    shaped = packed.reshape(row_count // span, span, 3, -1, HEAD_DIM)
    mixed, summary = attend(shaped, allowed)
    mixed_rows = mixed.reshape(row_count, -1)
    branch = jnp.dot(mixed_rows, w_mix, preferred_element_type=jnp.float32)
    return (branch, shaped, mixed_rows, summary)


def feed_forward(second_rows, w_lift, w_drop):
    lifted = jnp.dot(second_rows, w_lift, preferred_element_type=jnp.float32)
    active = gelu_exact(lifted).astype(jnp.bfloat16)
    branch = jnp.dot(active, w_drop, preferred_element_type=jnp.float32)
    return (lifted, active, branch)


def feed_backward(top_rows, second_rows, lifted, active, w_lift, w_drop):
    grad_drop = jnp.einsum("rf,rd->fd", active, top_rows, preferred_element_type=jnp.float32)
    grad_active = jnp.einsum("rd,fd->rf", top_rows, w_drop, preferred_element_type=jnp.float32)
    grad_lifted = jax.vjp(gelu_exact, lifted)[1](grad_active)[0].astype(jnp.bfloat16)
    grad_lift = jnp.einsum(
        "rd,rf->df", second_rows, grad_lifted, preferred_element_type=jnp.float32
    )
    partial_second = jnp.einsum(
        "rf,df->rd", grad_lifted, w_lift, preferred_element_type=jnp.float32
    )
    return (grad_drop, grad_lift, partial_second)


def attention_backward(mid_rows, mixed_rows, shaped, summary, first_rows, w_query, w_mix, allowed):
    grad_mix = jnp.einsum("re,rd->ed", mixed_rows, mid_rows, preferred_element_type=jnp.float32)
    grad_mixed = jnp.einsum(
        "rd,ed->re", mid_rows, w_mix, preferred_element_type=jnp.float32
    ).astype(jnp.bfloat16)
    grad_mixed = grad_mixed.reshape(shaped.shape[0], shaped.shape[1], shaped.shape[3], HEAD_DIM)
    grad_packed = attend_back(shaped, allowed, summary, grad_mixed).reshape(
        first_rows.shape[0], 3, -1
    )
    grad_query = jnp.einsum(
        "rd,rce->dce", first_rows, grad_packed, preferred_element_type=jnp.float32
    )
    partial_first = jnp.einsum(
        "rce,dce->rd", grad_packed, w_query, preferred_element_type=jnp.float32
    )
    return (grad_mix, grad_query, partial_first)


def frame_forward(start, allowed, flag, gain_pair, weights):
    w_query, w_mix, w_lift, w_drop = weights
    first_norm, first_factor = norm_forward(start, gain_pair[0])
    first_rows = row_gather(first_norm.astype(jnp.bfloat16))
    span = first_rows.shape[0]

    def attention_part(rows):
        return attention_forward(rows, w_query, w_mix, allowed, span)

    branch, shaped, mixed_rows, summary = guarded(flag, attention_part, first_rows)
    hidden = start + row_scatter(branch)
    second_norm, second_factor = norm_forward(hidden, gain_pair[1])
    second_rows = row_gather(second_norm.astype(jnp.bfloat16))

    def feed_part(rows):
        return feed_forward(rows, w_lift, w_drop)

    lifted, active, branch = guarded(flag, feed_part, second_rows)
    result = hidden + row_scatter(branch)
    saved_values = (
        start,
        first_factor,
        first_rows,
        shaped,
        mixed_rows,
        summary,
        hidden,
        second_factor,
        second_rows,
        lifted,
        active,
    )
    return (result, saved_values)


def frame_backward(upstream, saved_values, flag, gain_pair, weights, allowed):
    w_query, w_mix, w_lift, w_drop = weights
    (
        start,
        first_factor,
        first_rows,
        shaped,
        mixed_rows,
        summary,
        hidden,
        second_factor,
        second_rows,
        lifted,
        active,
    ) = saved_values
    top_rows = grad_gather(upstream.astype(jnp.bfloat16))

    def feed_part(operands):
        return feed_backward(operands[0], operands[1], operands[2], operands[3], w_lift, w_drop)

    grad_drop, grad_lift, partial_second = guarded(
        flag, feed_part, (top_rows, second_rows, lifted, active)
    )
    grad_second = grad_scatter(partial_second)
    through_second, gain_second = norm_backward(hidden, second_factor, gain_pair[1], grad_second)
    grad_hidden = upstream + through_second
    mid_rows = grad_gather(grad_hidden.astype(jnp.bfloat16))

    def attention_part(operands):
        return attention_backward(
            operands[0], operands[1], operands[2], operands[3], operands[4], w_query, w_mix, allowed
        )

    grad_mix, grad_query, partial_first = guarded(
        flag, attention_part, (mid_rows, mixed_rows, shaped, summary, first_rows)
    )
    grad_first = grad_scatter(partial_first)
    through_first, gain_first = norm_backward(start, first_factor, gain_pair[0], grad_first)
    return (
        grad_hidden + through_first,
        jnp.stack([gain_first, gain_second]),
        (grad_query, grad_mix, grad_lift, grad_drop),
    )


def local_forward(start, gain_pair, weights, allowed, span):
    w_query, w_mix, w_lift, w_drop = weights
    first_norm, first_factor = norm_forward(start, gain_pair[0])
    first_rows = first_norm.astype(jnp.bfloat16)
    branch, shaped, mixed_rows, summary = attention_forward(
        first_rows, w_query, w_mix, allowed, span
    )
    hidden = start + branch
    second_norm, second_factor = norm_forward(hidden, gain_pair[1])
    second_rows = second_norm.astype(jnp.bfloat16)
    lifted, active, branch = feed_forward(second_rows, w_lift, w_drop)
    result = hidden + branch
    saved_values = (
        start,
        first_factor,
        first_rows,
        shaped,
        mixed_rows,
        summary,
        hidden,
        second_factor,
        second_rows,
        lifted,
        active,
    )
    return (result, saved_values)


def local_backward(upstream, saved_values, gain_pair, weights, allowed):
    w_query, w_mix, w_lift, w_drop = weights
    (
        start,
        first_factor,
        first_rows,
        shaped,
        mixed_rows,
        summary,
        hidden,
        second_factor,
        second_rows,
        lifted,
        active,
    ) = saved_values
    top_rows = upstream.astype(jnp.bfloat16)
    grad_drop, grad_lift, grad_second = feed_backward(
        top_rows, second_rows, lifted, active, w_lift, w_drop
    )
    through_second, gain_second = norm_backward(hidden, second_factor, gain_pair[1], grad_second)
    grad_hidden = upstream + through_second
    mid_rows = grad_hidden.astype(jnp.bfloat16)
    grad_mix, grad_query, grad_first = attention_backward(
        mid_rows, mixed_rows, shaped, summary, first_rows, w_query, w_mix, allowed
    )
    through_first, gain_first = norm_backward(start, first_factor, gain_pair[0], grad_first)
    return (
        grad_hidden + through_first,
        jnp.stack([gain_first, gain_second]),
        (grad_query, grad_mix, grad_lift, grad_drop),
    )


def on_device(codes, lengths, gains, w_qkv, w_out, w_up, w_down, cotangent):
    section_index = lax.axis_index("section")
    is_first = section_index == 0
    is_second = section_index == 1
    first_flag = is_first.astype(jnp.float32)
    tensor_index = lax.axis_index("tensor")
    tensor_count = lax.axis_size("tensor")
    micro_count, frame_count, code_count, model_width = codes.shape
    total_frames = frame_count * tensor_count
    own_gains = gains[0]
    own_weights = (w_qkv[0], w_out[0], w_up[0], w_down[0])
    positions = jnp.arange(total_frames)
    causal = positions[None, :] <= positions[:, None]
    code_positions = jnp.arange(code_count)
    code_allowed = (code_positions[None, :] <= code_positions[:, None])[None]
    shard_positions = tensor_index * frame_count + jnp.arange(frame_count)
    zero_rows = jnp.zeros((frame_count, model_width), jnp.bfloat16)
    gathered = (
        lax.all_gather(w_qkv, "tensor", axis=3, tiled=True),
        lax.all_gather(w_out, "tensor", axis=1, tiled=True),
        lax.all_gather(w_up, "tensor", axis=2, tiled=True),
        lax.all_gather(w_down, "tensor", axis=1, tiled=True),
    )
    local_weights = tuple((weight[0] for weight in gathered))
    totals = (
        jnp.zeros(codes.shape, jnp.float32),
        jnp.zeros(codes.shape, jnp.float32),
        jnp.zeros((2, model_width), jnp.float32),
        tuple((jnp.zeros(weight.shape, jnp.float32) for weight in own_weights)),
        tuple((jnp.zeros(weight.shape, jnp.float32) for weight in local_weights)),
    )

    def global_allowed(batch_index):
        return (causal & (positions < lengths[batch_index])[None, :])[None]

    def global_forward(batch_index):
        start = jnp.sum(codes[batch_index].astype(jnp.float32), axis=1)
        result, saved_values = frame_forward(
            start, global_allowed(batch_index), is_first, own_gains, own_weights
        )
        return result.astype(jnp.bfloat16)

    def global_backward(batch_index, incoming, totals):
        start = jnp.sum(codes[batch_index].astype(jnp.float32), axis=1)
        allowed = global_allowed(batch_index)
        result, saved_values = frame_forward(start, allowed, is_first, own_gains, own_weights)
        grad_start, grad_gains, grad_weights = frame_backward(
            incoming.astype(jnp.float32), saved_values, is_first, own_gains, own_weights, allowed
        )
        spread_grad = jnp.broadcast_to(
            (grad_start * first_flag)[:, None, :], (frame_count, code_count, model_width)
        )
        code_totals = totals[0].at[batch_index].add(spread_grad)
        sharded = tuple((left + right for left, right in zip(totals[3], grad_weights)))
        return (code_totals, totals[1], totals[2] + grad_gains * first_flag, sharded, totals[4])

    def local_pass(batch_index, incoming, totals):
        start = incoming.astype(jnp.float32)[:, None, :] + codes[batch_index].astype(jnp.float32)
        start = start.reshape(frame_count * code_count, model_width)
        result, saved_values = local_forward(
            start, own_gains, local_weights, code_allowed, code_count
        )
        valid = (shard_positions < lengths[batch_index]).astype(jnp.float32)[:, None, None]
        final = result.reshape(frame_count, code_count, model_width) * valid
        upstream = (cotangent[batch_index].astype(jnp.float32) * valid).reshape(
            frame_count * code_count, model_width
        )
        grad_start, grad_gains, grad_weights = local_backward(
            upstream, saved_values, own_gains, local_weights, code_allowed
        )
        grad_start = grad_start.reshape(frame_count, code_count, model_width)
        outgoing = jnp.sum(grad_start, axis=1).astype(jnp.bfloat16)
        code_totals = totals[0].at[batch_index].add(grad_start)
        output_totals = totals[1].at[batch_index].set(final)
        full_sums = tuple((left + right for left, right in zip(totals[4], grad_weights)))
        return (
            outgoing,
            (code_totals, output_totals, totals[2] + grad_gains, totals[3], full_sums),
        )

    outgoing_rows = jnp.stack([global_forward(batch_index) for batch_index in range(micro_count)])
    arrived = shifted(outgoing_rows, "section", 1)
    returned = []
    for batch_index in range(micro_count):
        run_incoming = arrived[batch_index]

        def work(carried):
            return local_pass(batch_index, run_incoming, carried)

        def skip(carried):
            return (zero_rows, carried)

        outgoing, totals = lax.cond(is_second, work, skip, totals)
        returned.append(outgoing)
    returned_grads = shifted(jnp.stack(returned), "section", -1)
    for batch_index in range(micro_count):
        totals = global_backward(batch_index, returned_grads[batch_index], totals)
    full_grads = totals[4]
    spread_grads = (
        lax.psum_scatter(
            full_grads[0].astype(jnp.bfloat16), "tensor", scatter_dimension=2, tiled=True
        ).astype(jnp.float32),
        lax.psum_scatter(
            full_grads[1].astype(jnp.bfloat16), "tensor", scatter_dimension=0, tiled=True
        ).astype(jnp.float32),
        lax.psum_scatter(
            full_grads[2].astype(jnp.bfloat16), "tensor", scatter_dimension=1, tiled=True
        ).astype(jnp.float32),
        lax.psum_scatter(
            full_grads[3].astype(jnp.bfloat16), "tensor", scatter_dimension=0, tiled=True
        ).astype(jnp.float32),
    )
    sharded = tuple((left + right for left, right in zip(totals[3], spread_grads)))
    weight_total = lax.psum(sharded, "dp")
    gain_total = lax.psum(totals[2], ("dp", "tensor"))
    halves = (micro_count, frame_count, code_count, 2, model_width // 2)
    code_split, output_split = (
        lax.psum_scatter(totals[0].reshape(halves), "section", scatter_dimension=3, tiled=True),
        lax.psum_scatter(totals[1].reshape(halves), "section", scatter_dimension=3, tiled=True),
    )
    narrow = (micro_count, frame_count, code_count, model_width // 2)
    code_grad = code_split.reshape(narrow)
    output = output_split.reshape(narrow).astype(jnp.bfloat16)
    return (
        output,
        code_grad,
        gain_total[None],
        weight_total[0][None],
        weight_total[1][None],
        weight_total[2][None],
        weight_total[3][None],
    )


def solution(mesh):
    in_specs = (
        P("dp", "tensor", None, None),
        P("dp"),
        P("section", None, None),
        P("section", None, None, "tensor"),
        P("section", "tensor", None),
        P("section", None, "tensor"),
        P("section", "tensor", None),
        P("dp", "tensor", None, None),
    )
    out_specs = (
        P("dp", "tensor", None, "section"),
        P("dp", "tensor", None, "section"),
        P("section", None, None),
        P("section", None, None, "tensor"),
        P("section", "tensor", None),
        P("section", None, "tensor"),
        P("section", "tensor", None),
    )
    return jax.shard_map(
        on_device, mesh=mesh, in_specs=in_specs, out_specs=out_specs, check_vma=False
    )
```

profile of v0, /device:TPU:0, one launch (start us, length us, event | category | flops | bytes accessed | tf_op | source)
XLA Modules:
  0.0 1974.1 jit_solution(2564673735975139068)
XLA Ops:
  11.3 17.3 all_gather.46
  30.1 7.1 conditional.24
  37.8 7.6 conditional.16
  46.1 20.7 %all_gather.44 = bf16[256,1024]{1,0:T(8,128)(2,1)S(1)} all-gather(bf16[64,1024]{1,0:T(8,128)(2,1)S(1)} %get-tuple-element.883), channel_id=1, replica_groups=mesh['section'=2,'dp'=4,'tensor'=4] {'tensor'}, dimensions={0}, use_global_device_ids=true | all-gather | bytes 655360 | tf_op jit(solution)/shard_map/all_gather | solution.py:44
  66.9 7.1 conditional.20
  74.6 5.9 conditional.14
  80.7 18.6 reduce-scatter.21.cloned.1.call-done
  101.0 26.9 %reduce-scatter.27.cloned.1.call-done = f32[64,1024]{1,0:T(8,128)} async-done(((f32[256,1024]{1,0:T(8,128)}), f32[64,1024]{1,0:T(8,128)}) %reduce-scatter.27.cloned.1.call-update) | async-done | bytes 262160 | tf_op jit(solution)/shard_map/reduce_scatter | solution.py:48
  128.0 28.7 %reduce-scatter.17.cloned.1.call-done = f32[64,1024]{1,0:T(8,128)} async-done(((f32[256,1024]{1,0:T(8,128)}), f32[64,1024]{1,0:T(8,128)}) %reduce-scatter.17.cloned.1.call-update) | async-done | bytes 262160 | tf_op jit(solution)/shard_map/reduce_scatter | solution.py:48
  159.8 16.4 all_gather.45
  176.2 5.4 conditional.15
  182.7 18.6 all_gather.47
  212.2 27.7 %reduce-scatter.23.cloned.1.call-done = f32[64,1024]{1,0:T(8,128)} async-done(((f32[256,1024]{1,0:T(8,128)}), f32[64,1024]{1,0:T(8,128)}) %reduce-scatter.23.cloned.1.call-update) | async-done | bytes 262160 | tf_op jit(solution)/shard_map/reduce_scatter | solution.py:48
  243.1 43.0 %all-gather.9.cloned.1.call-done = bf16[1,1024,1024]{2,1,0:T(8,128)(2,1)} async-done(((bf16[1,256,1024]{2,1,0:T(8,128)(2,1)}), bf16[1,1024,1024]{2,1,0:T(8,128)(2,1)}) %all-gather.9.cloned.1.call-update) | async-done | bytes 2097168 | tf_op jit(solution)/shard_map/all_gather | solution.py:314
  286.0 115.2 %all-gather.7.cloned.1.call-done = bf16[1,1024,3,1024]{3,1,2,0:T(8,128)(2,1)} async-done(((bf16[1,1024,3,256]{3,1,2,0:T(8,128)(2,1)}), bf16[1,1024,3,1024]{3,1,2,0:T(8,128)(2,1)}) %all-gather.7.cloned.1.call-update) | async-done | bytes 6291472 | tf_op jit(solution)/shard_map/all_gather | solution.py:313
  401.2 149.4 %all-gather.11.cloned.1.call-done = bf16[1,1024,4096]{2,1,0:T(8,128)(2,1)} async-done(((bf16[1,1024,1024]{2,1,0:T(8,128)(2,1)}), bf16[1,1024,4096]{2,1,0:T(8,128)(2,1)}) %all-gather.11.cloned.1.call-update) | async-done | bytes 8388624 | tf_op jit(solution)/shard_map/all_gather | solution.py:315
  550.6 149.3 %all-gather.13.cloned.1.call-done = bf16[1,4096,1024]{2,1,0:T(8,128)(2,1)} async-done(((bf16[1,1024,1024]{2,1,0:T(8,128)(2,1)}), bf16[1,4096,1024]{2,1,0:T(8,128)(2,1)}) %all-gather.13.cloned.1.call-update) | async-done | bytes 8388624 | tf_op jit(solution)/shard_map/all_gather | solution.py:316
  699.9 32.5 %conditional.18 = (f32[2,64,3,1024]{3,2,1,0:T(4,128)}, f32[2,64,3,1024]{3,2,1,0:T(4,128)}, f32[2,1024]{1,0:T(2,128)}, f32[1024,3,1024]{2,0,1:T(8,128)}, f32[1024...) conditional(s32[]{:T(128)} %convert_element_type.375, ...), branch_computations={%region_22.23_spmd, %region_23.34_spmd} | conditional | flops 14577913856 | bytes 251456512 | solution.py:387
  699.9 7.9 broadcast_in_dim.113
  707.8 7.9 broadcast_in_dim.114
  715.7 6.1 broadcast_in_dim.112
  733.1 15.2 conditional.19
  750.6 14.7 all_gather.55
  769.6 234.3 %collective-permute-done.1 = bf16[2,64,1024]{2,1,0:T(8,128)(2,1)S(1)} collective-permute-done((bf16[2,64,1024]{2,1,0:T(8,128)(2,1)S(1)}, bf16[2,64,1024]{2,1,0:T(8,128)(2,1)S(1)}, u32[]{:S(2)}, u32[]{:S(2)}) %collective-permute-start.1) | collective-permute-done | bytes 262176 | tf_op jit(solution)/shard_map/ppermute | solution.py:16
  1004.6 15.0 all-gather.1
  1019.5 19.1 conditional.26
  1028.5 5.5 copy.308
  1040.3 19.0 all-gather
  1059.3 9.7 reduce-scatter.35.cloned.1.call-done
  1070.3 16.2 all_gather.52
  1089.5 19.3 conditional.22
  1109.9 25.7 %reduce-scatter.29.cloned.1.call-done = f32[64,1024]{1,0:T(8,128)} async-done(((f32[256,1024]{1,0:T(8,128)}), f32[64,1024]{1,0:T(8,128)}) %reduce-scatter.29.cloned.1.call-update) | async-done | bytes 262160 | tf_op jit(solution)/shard_map/reduce_scatter | solution.py:56
  1139.0 16.0 all_gather.57
  1155.0 15.3 conditional.27
  1170.5 18.2 all_gather.54
  1188.7 15.5 conditional.23
  1208.3 8.4 convert_element_type.394
  1216.7 9.2 convert_element_type.400
  1225.9 9.1 convert_element_type.398
  1253.9 22.0 %reduce-scatter.43.cloned.1.call-done = bf16[256,1024]{1,0:T(8,128)(2,1)} async-done(((bf16[1024,1024]{1,0:T(8,128)(2,1)}), bf16[256,1024]{1,0:T(8,128)(2,1)}) %reduce-scatter.43.cloned.1.call-update) | async-done | bytes 524304 | tf_op jit(solution)/shard_map/reduce_scatter | solution.py:397
  1278.9 109.3 %reduce-scatter.41.cloned.1.call-done = bf16[1024,3,256]{2,0,1:T(8,128)(2,1)} async-done(((bf16[1024,3,1024]{2,0,1:T(8,128)(2,1)}), bf16[1024,3,256]{2,0,1:T(8,128)(2,1)}) %reduce-scatter.41.cloned.1.call-update) | async-done | bytes 1572880 | tf_op jit(solution)/shard_map/reduce_scatter | solution.py:394
  1388.2 5.5 add_bitcast_fusion.4
  1393.7 141.9 %reduce-scatter.47.cloned.1.call-done = bf16[1024,1024]{1,0:T(8,128)(2,1)} async-done(((bf16[4096,1024]{1,0:T(8,128)(2,1)}), bf16[1024,1024]{1,0:T(8,128)(2,1)}) %reduce-scatter.47.cloned.1.call-update) | async-done | bytes 2097168 | tf_op jit(solution)/shard_map/reduce_scatter | solution.py:403
  1535.5 7.7 add_bitcast_fusion.2
  1543.2 139.9 %reduce-scatter.45.cloned.1.call-done = bf16[1024,1024]{1,0:T(8,128)(2,1)} async-done(((bf16[1024,4096]{1,0:T(8,128)(2,1)}), bf16[1024,1024]{1,0:T(8,128)(2,1)}) %reduce-scatter.45.cloned.1.call-update) | async-done | bytes 2097168 | tf_op jit(solution)/shard_map/reduce_scatter | solution.py:400
  1683.1 7.7 add_bitcast_fusion.3
  1697.9 44.0 %psum.35 = f32[1,2,1024]{2,1,0:T(2,128)} all-reduce(f32[1,2,1024]{2,1,0:T(2,128)S(1)} %fusion.314), channel_id=1, replica_groups=mesh['section'=2,'dp'=4,'tensor'=4] {'dp','tensor'}, use_global_device_ids=true, to_apply=%region_86.87 | all-reduce | flops 2048 | bytes 16384 | tf_op jit(solution)/shard_map/psum | solution.py:409
  1741.8 214.6 %all-reduce.5.cloned.1.call-done = (f32[1,1024,3,256]{3,1,2,0:T(8,128)}, f32[1,256,1024]{2,1,0:T(8,128)}, f32[1,1024,1024]{2,1,0:T(8,128)}, f32[1,1024,1024]{2,1,0:T(8,128)}) async-done(((f32[1,1024,3,256]{3,1,2,0:T(8,128)}, f32[1,256,1024]{2,1,0:T(8,128)}, f32[1,1024,1024]{2,1,0:T(8,128)}, f32[1,1024,1024]{2,1,0:T(8,128)}), (f32[1,1024,3,256]{3,1,2,0:T(8,128)}, f32[1,256,1024]{2,1,0:T(8,128)}, ...) | async-done | bytes 12582928 | tf_op jit(solution)/shard_map/psum | solution.py:408
  (312 shorter events, 204.7 us)
Async XLA Ops:
  7.2 73.5 %reduce-scatter.33.cloned.1.call-start = ((), (), s32[]{:S(2)}) async-start(), calls=%async_computation.28 | async-start | bytes 1310720 | tf_op jit(solution)/shard_map/reduce_scatter | solution.py:48
  8.7 90.6 %copy-start.17 = (f32[64,1024]{1,0:T(8,128)}, f32[64,1024]{1,0:T(8,128)S(1)}, u32[]{:S(2)}) copy-start(f32[64,1024]{1,0:T(8,128)S(1)} %get-tuple-element.795) | copy-start | bytes 786436
  8.7 147.9 %copy-start.19 = (f32[64,1024]{1,0:T(8,128)}, f32[64,1024]{1,0:T(8,128)S(1)}, u32[]{:S(2)}) copy-start(f32[64,1024]{1,0:T(8,128)S(1)} %get-tuple-element.794) | copy-start | bytes 786436
  10.7 148.3 %copy-start.76 = (f32[1,1,1024]{2,1,0:T(1,128)}, f32[1,1,1024]{2,1,0:T(1,128)S(1)}, u32[]{:S(2)}) copy-start(f32[1,1,1024]{2,1,0:T(1,128)S(1)} %get-tuple-element.876) | copy-start | bytes 12292
  37.2 62.0 %reduce-scatter.21.cloned.1.call-start = ((), (), s32[]{:S(2)}) async-start(), calls=%async_computation.18 | async-start | bytes 1310720 | tf_op jit(solution)/shard_map/reduce_scatter | solution.py:48
  45.4 82.6 %reduce-scatter.27.cloned.1.call-start = ((), (), s32[]{:S(2)}) async-start(), calls=%async_computation.25 | async-start | bytes 1310720 | tf_op jit(solution)/shard_map/reduce_scatter | solution.py:48
  74.1 82.6 %reduce-scatter.17.cloned.1.call-start = ((), (), s32[]{:S(2)}) async-start(), calls=%async_computation.16 | async-start | bytes 1310720 | tf_op jit(solution)/shard_map/reduce_scatter | solution.py:48
  80.6 95.7 %copy-start.4 = (bf16[1,1024,1024]{2,1,0:T(8,128)(2,1)S(1)}, bf16[1,1024,1024]{2,1,0:T(8,128)(2,1)}, u32[]{:S(2)}) copy-start(bf16[1,1024,1024]{2,1,0:T(8,128)(2,1)} %param.53) | copy-start | bytes 6291460
  80.6 130.6 %reduce-scatter.19.cloned.1.call-start = ((), (), s32[]{:S(2)}) async-start(), calls=%async_computation.17 | async-start | bytes 1310720 | tf_op jit(solution)/shard_map/reduce_scatter | solution.py:48
  100.5 75.8 %copy-start.36 = (f32[64,1024]{1,0:T(8,128)}, f32[64,1024]{1,0:T(8,128)S(1)}, u32[]{:S(2)}) copy-start(f32[64,1024]{1,0:T(8,128)S(1)} %get-tuple-element.815) | copy-start | bytes 786436
  101.0 75.2 %copy-start.92 = (f32[64]{0:T(128)}, f32[64]{0:T(128)S(1)}, u32[]{:S(2)}) copy-start(f32[64]{0:T(128)S(1)} %get-tuple-element.888) | copy-start | bytes 772
  182.7 57.2 %reduce-scatter.23.cloned.1.call-start = ((), (), s32[]{:S(2)}) async-start(), calls=%async_computation.19 | async-start | bytes 1310720 | tf_op jit(solution)/shard_map/reduce_scatter | solution.py:48
  207.6 78.4 %all-gather.9.cloned.1.call-start = ((), (), s32[]{:S(2)}) async-start(), calls=%async_computation.21 | async-start | bytes 2621440 | tf_op jit(solution)/shard_map/all_gather | solution.py:314
  208.4 192.8 %all-gather.7.cloned.1.call-start = ((), (), s32[]{:S(2)}) async-start(), calls=%async_computation.20 | async-start | bytes 7864320 | tf_op jit(solution)/shard_map/all_gather | solution.py:313
  209.1 490.8 %copy-start.28 = (bf16[2,64,3,1024]{3,1,2,0:T(8,128)(2,1)S(1)}, bf16[2,64,3,1024]{3,1,2,0:T(8,128)(2,1)}, u32[]{:S(2)}) copy-start(bf16[2,64,3,1024]{3,1,2,0:T(8,128)(2,1)} %param.48) | copy-start | bytes 2359300
  209.1 490.8 %copy-start.78 = (f32[1,2,1024]{2,1,0:T(2,128)S(1)}, f32[1,2,1024]{2,1,0:T(2,128)}, u32[]{:S(2)}) copy-start(f32[1,2,1024]{2,1,0:T(2,128)} %param.50) | copy-start | bytes 24580
  209.2 490.7 %copy-start.108 = (s32[2]{0:T(128)S(1)}, s32[2]{0:T(128)}, u32[]{:S(2)}) copy-start(s32[2]{0:T(128)} %param.49) | copy-start | bytes 28
  209.2 341.5 %all-gather.11.cloned.1.call-start = ((), (), s32[]{:S(2)}) async-start(), calls=%async_computation.22 | async-start | bytes 10485760 | tf_op jit(solution)/shard_map/all_gather | solution.py:315
  209.9 490.0 %all-gather.13.cloned.1.call-start = ((), (), s32[]{:S(2)}) async-start(), calls=%async_computation.23 | async-start | bytes 10485760 | tf_op jit(solution)/shard_map/all_gather | solution.py:316
  210.5 858.5 %reduce-scatter.35.cloned.1.call-start = ((), (), s32[]{:S(2)}) async-start(), calls=%async_computation.29 | async-start | bytes 1310720 | tf_op jit(solution)/shard_map/reduce_scatter | solution.py:56
  240.9 45.1 %collective-permute-start = (bf16[2,64,1024]{2,1,0:T(8,128)(2,1)S(1)}, bf16[2,64,1024]{2,1,0:T(8,128)(2,1)S(1)}, u32[]{:S(2)}, u32[]{:S(2)}) collective-permute-start(bf16[2,64,1024]{2,1,0:T(8,128)(2,1)S(1)} %pad_maximum_fusion.7), channel_id=1, source_target_pairs={{0,16},{1,17},{2,18},{3,19},{4,20},{5,21},{6,22},{7,23},{8,24},{9,... | collective-permute-start | bytes 786440 | tf_op jit(solution)/shard_map/ppermute | solution.py:16
  242.5 457.4 %copy-start.82 = (pred[3,3]{1,0:T(4,128)(4,1)}, pred[3,3]{1,0:T(4,128)(4,1)S(1)}, u32[]{:S(2)}) copy-start(pred[3,3]{1,0:T(4,128)(4,1)S(1)} %iota_compare_fusion.1) | copy-start | bytes 31
  286.0 413.9 %copy-start.66 = (bf16[2,64,1024]{2,1,0:T(8,128)(2,1)}, bf16[2,64,1024]{2,1,0:T(8,128)(2,1)S(1)}, u32[]{:S(2)}) copy-start(bf16[2,64,1024]{2,1,0:T(8,128)(2,1)S(1)} %collective-permute-done) | copy-start | bytes 786436
  749.3 254.6 %collective-permute-start.1 = (bf16[2,64,1024]{2,1,0:T(8,128)(2,1)S(1)}, bf16[2,64,1024]{2,1,0:T(8,128)(2,1)S(1)}, u32[]{:S(2)}, u32[]{:S(2)}) collective-permute-start(bf16[2,64,1024]{2,1,0:T(8,128)(2,1)S(1)} %pad_maximum_fusion.8), channel_id=1, source_target_pairs={{16,0},{17,1},{18,2},{19,3},{20,4},{21,5},{22,6},{23,7},{24,8},{25... | collective-permute-start | bytes 786440 | tf_op jit(solution)/shard_map/ppermute | solution.py:16
  1019.5 49.5 %copy-start.37 = (f32[64,1024]{1,0:T(8,128)S(1)}, f32[64,1024]{1,0:T(8,128)}, u32[]{:S(2)}) copy-start(f32[64,1024]{1,0:T(8,128)} %copy-done.36) | copy-start | bytes 786436
  1019.5 49.5 %copy-start.77 = (f32[1,1,1024]{2,1,0:T(1,128)S(1)}, f32[1,1,1024]{2,1,0:T(1,128)}, u32[]{:S(2)}) copy-start(f32[1,1,1024]{2,1,0:T(1,128)} %copy-done.76) | copy-start | bytes 12292
  1019.5 49.5 %copy-start.93 = (f32[64]{0:T(128)S(1)}, f32[64]{0:T(128)}, u32[]{:S(2)}) copy-start(f32[64]{0:T(128)} %copy-done.92) | copy-start | bytes 772
  1038.7 47.8 %copy-start.5 = (bf16[1,1024,1024]{2,1,0:T(8,128)(2,1)S(1)}, bf16[1,1024,1024]{2,1,0:T(8,128)(2,1)}, u32[]{:S(2)}) copy-start(bf16[1,1024,1024]{2,1,0:T(8,128)(2,1)} %param.53) | copy-start | bytes 6291460
  1039.7 95.8 %reduce-scatter.29.cloned.1.call-start = ((), (), s32[]{:S(2)}) async-start(), calls=%async_computation.26 | async-start | bytes 1310720 | tf_op jit(solution)/shard_map/reduce_scatter | solution.py:56
  1040.3 46.2 %copy-start.98 = (f32[64]{0:T(128)}, f32[64]{0:T(128)S(1)}, u32[]{:S(2)}) copy-start(f32[64]{0:T(128)S(1)} %get-tuple-element.892) | copy-start | bytes 772
  1089.5 46.0 %copy-start.99 = (f32[64]{0:T(128)S(1)}, f32[64]{0:T(128)}, u32[]{:S(2)}) copy-start(f32[64]{0:T(128)} %copy-done.98) | copy-start | bytes 772
  1089.5 47.2 %copy-start.114 = (f32[64]{0:T(128)S(1)}, f32[64]{0:T(128)}, u32[]{:S(2)}) copy-start(f32[64]{0:T(128)} %get-tuple-element.887) | copy-start | bytes 772
  1089.5 47.2 %copy-start.116 = (f32[64]{0:T(128)S(1)}, f32[64]{0:T(128)}, u32[]{:S(2)}) copy-start(f32[64]{0:T(128)} %get-tuple-element.891) | copy-start | bytes 772
  1108.8 46.2 %copy-start.3 = (bf16[1,256,1024]{2,1,0:T(8,128)(2,1)S(1)}, bf16[1,256,1024]{2,1,0:T(8,128)(2,1)}, u32[]{:S(2)}) copy-start(bf16[1,256,1024]{2,1,0:T(8,128)(2,1)} %param.52) | copy-start | bytes 1572868
  1108.8 46.2 %copy-start.8 = (bf16[1,1024,3,256]{3,1,2,0:T(8,128)(2,1)S(1)}, bf16[1,1024,3,256]{3,1,2,0:T(8,128)(2,1)}, u32[]{:S(2)}) copy-start(bf16[1,1024,3,256]{3,1,2,0:T(8,128)(2,1)} %param.51) | copy-start | bytes 4718596
  1108.8 46.2 %copy-start.69 = (pred[256,256]{0,1:T(8,128)(4,1)S(1)}, pred[256,256]{0,1:T(8,128)(4,1)}, u32[]{:S(2)}) copy-start(pred[256,256]{0,1:T(8,128)(4,1)} %copy-done.68) | copy-start | bytes 196612
  1108.8 46.2 %copy-start.101 = (f32[1,4,256,1]{2,1,3,0:T(4,128)S(1)}, f32[1,4,256,1]{2,1,3,0:T(4,128)}, u32[]{:S(2)}) copy-start(f32[1,4,256,1]{2,1,3,0:T(4,128)} %copy-done.100) | copy-start | bytes 12292
  1109.8 45.2 %copy-start.50 = (bf16[256,1024]{1,0:T(8,128)(2,1)S(1)}, bf16[256,1024]{1,0:T(8,128)(2,1)}, u32[]{:S(2)}) copy-start(bf16[256,1024]{1,0:T(8,128)(2,1)} %copy-done.49) | copy-start | bytes 1572868
  1109.8 130.4 %reduce-scatter.37.cloned.1.call-start = ((), (), s32[]{:S(2)}) async-start(), calls=%async_computation.30 | async-start | bytes 1310720 | tf_op jit(solution)/shard_map/reduce_scatter | solution.py:56
  1155.0 33.7 %copy-start.103 = (f32[1,4,256,1]{2,1,3,0:T(4,128)S(1)}, f32[1,4,256,1]{2,1,3,0:T(4,128)}, u32[]{:S(2)}) copy-start(f32[1,4,256,1]{2,1,3,0:T(4,128)} %copy-done.102) | copy-start | bytes 12292
  1170.4 71.0 %reduce-scatter.31.cloned.1.call-start = ((), (), s32[]{:S(2)}) async-start(), calls=%async_computation.27 | async-start | bytes 1310720 | tf_op jit(solution)/shard_map/reduce_scatter | solution.py:56
  1204.3 71.6 %reduce-scatter.43.cloned.1.call-start = ((), (), s32[]{:S(2)}) async-start(), calls=%async_computation.33 | async-start | bytes 2621440 | tf_op jit(solution)/shard_map/reduce_scatter | solution.py:397
  1208.2 179.9 %reduce-scatter.41.cloned.1.call-start = ((), (), s32[]{:S(2)}) async-start(), calls=%async_computation.32 | async-start | bytes 7864320 | tf_op jit(solution)/shard_map/reduce_scatter | solution.py:394
  1216.7 318.9 %reduce-scatter.47.cloned.1.call-start = ((), (), s32[]{:S(2)}) async-start(), calls=%async_computation.35 | async-start | bytes 10485760 | tf_op jit(solution)/shard_map/reduce_scatter | solution.py:403
  1225.9 457.2 %reduce-scatter.45.cloned.1.call-start = ((), (), s32[]{:S(2)}) async-start(), calls=%async_computation.34 | async-start | bytes 10485760 | tf_op jit(solution)/shard_map/reduce_scatter | solution.py:400
  1235.1 460.1 %reduce-scatter.25.cloned.1.call-start = ((), (), s32[]{:S(2)}) async-start(), calls=%async_computation.24 | async-start | bytes 2359296 | tf_op jit(solution)/shard_map/reduce_scatter | solution.py:413
  1240.1 501.8 %reduce-scatter.39.cloned.1.call-start = ((), (), s32[]{:S(2)}) async-start(), calls=%async_computation.31 | async-start | bytes 2359296 | tf_op jit(solution)/shard_map/reduce_scatter | solution.py:412
  1253.7 702.8 %all-reduce.5.cloned.1.call-start = ((), (), s32[]{:S(2)}) async-start(), calls=%async_computation.36 | async-start | bytes 25165824 | tf_op jit(solution)/shard_map/psum | solution.py:408
  (48 other events, 268.7 us)
Sparse Core Ops, SparseCore 0:
  37.4 33.1 reduce-scatter.32
  73.5 25.7 reduce-scatter.20
  102.1 25.7 reduce-scatter.26
  130.8 25.7 reduce-scatter.16
  182.8 28.3 reduce-scatter.18
  214.0 25.8 reduce-scatter.22
  241.4 44.5 all-gather.8
  287.6 113.5 all-gather.6
  402.8 147.8 all-gather.10
  552.0 147.8 all-gather.12
  1039.8 29.1 reduce-scatter.34
  1109.9 25.5 reduce-scatter.28
  1170.5 28.0 reduce-scatter.36
  1204.4 26.7 reduce-scatter.30
  1233.3 42.5 reduce-scatter.42
  1278.2 109.9 reduce-scatter.40
  1390.5 144.9 reduce-scatter.46
  1537.9 145.1 reduce-scatter.44
  1685.4 9.7 reduce-scatter.24
  1697.9 10.2 reduce-scatter.38
  1713.2 243.2 all-reduce.4
where the time goes:
time: 1980 us; the launch traced here: 1970 us
  waiting for transfers between devices  1460 us (74%)
  blocking collectives  216 us (11%)
  matrix products  90.8 us (5%)
  other arithmetic  84.3 us (4%)
  local copies, waits for them, and re-layouts  80.2 us (4%)
    ppermute x2, waiting for transfers between devices, shifted(): lax.ppermute(value, axis, [(source, source + steps) for source in range(i...  234 us
    psum x1, waiting for transfers between devices, on_device(): weight_total = lax.psum(sharded, 'dp')  215 us
    all_gather x1, waiting for transfers between devices, on_device(): lax.all_gather(w_up, 'tensor', axis=2, tiled=True)  149 us
    all_gather x1, waiting for transfers between devices, on_device(): lax.all_gather(w_down, 'tensor', axis=1, tiled=True)  149 us
    reduce_scatter x1, waiting for transfers between devices, on_device(): lax.psum_scatter(full_grads[3].astype(jnp.bfloat16), 'tensor', scatter_di...  142 us
    reduce_scatter x1, waiting for transfers between devices, on_device(): lax.psum_scatter(full_grads[2].astype(jnp.bfloat16), 'tensor', scatter_di...  140 us
    all_gather x1, waiting for transfers between devices, on_device(): lax.all_gather(w_qkv, 'tensor', axis=3, tiled=True)  115 us
    reduce_scatter x1, waiting for transfers between devices, on_device(): lax.psum_scatter(full_grads[0].astype(jnp.bfloat16), 'tensor', scatter_di...  109 us
  transfers between devices with their start and end apart: 23, of which 18 were waited for; matrix products, arithmetic and copies ran while one was open for 6% of the time, Pallas kernels for 0%

commit v1 on v0

v1 whole, which is shorter than its diff:
```python
import jax
import jax.numpy as jnp
from jax import lax
from jax.sharding import PartitionSpec as P

HEAD_DIM = 64
SCALE = HEAD_DIM ** (-0.5)
QUARTERS = 4
epsilon = 1e-06
negative = -1e30
f32 = jnp.float32
low16 = jnp.bfloat16


def swap(value, axis, flip):
    count = lax.axis_size(axis)
    return lax.ppermute(value, axis, [(i, i ^ flip) for i in range(count)])


def dot(a, b):
    return jnp.dot(a, b, preferred_element_type=f32)


def dot_tn(a, b):
    return lax.dot_general(a, b, (((0,), (0,)), ((), ())), preferred_element_type=f32)


def dot_nt(a, b):
    return lax.dot_general(a, b, (((1,), (1,)), ((), ())), preferred_element_type=f32)


def norm_forward(values, gain_vector):
    factor = lax.rsqrt(jnp.mean(values * values, axis=-1, keepdims=True) + epsilon)
    return (values * factor * gain_vector, factor)


def norm_backward(values, factor, gain_vector, upstream):
    weighted = upstream * gain_vector
    inner = jnp.mean(weighted * values, axis=-1, keepdims=True)
    grad_values = factor * weighted - values * (factor * factor * factor) * inner
    return (grad_values, jnp.sum(upstream * values * factor, axis=0))


def gelu_exact(values):
    return jax.nn.gelu(values, approximate=False)


def gelu_grad(values, upstream):
    return jax.vjp(gelu_exact, values)[1](upstream)[0]


def row_gather(rows):
    return jnp.concatenate([rows] + [swap(rows, "tensor", k) for k in (1, 2, 3)], axis=0)


def row_scatter(partial):
    pieces = partial.astype(low16).reshape(4, -1, partial.shape[-1])
    total = pieces[0].astype(f32)
    for k in (1, 2, 3):
        total = total + swap(pieces[k], "tensor", k).astype(f32)
    return total


def pair_sum(partial):
    mine = partial.astype(low16)
    return mine.astype(f32) + swap(mine, "section", 1).astype(f32)


def reorder(values, low, axis):
    axis = axis % values.ndim
    width = values.shape[axis] // QUARTERS
    parts = [
        lax.dynamic_slice_in_dim(values, (low ^ m) * width, width, axis) for m in range(QUARTERS)
    ]
    return jnp.concatenate(parts, axis=axis)


def half_of(values, index, axis):
    width = values.shape[axis] // 2
    return lax.dynamic_slice_in_dim(values, index * width, width, axis)


def attention_units(w_query, w_mix):
    unit_a = jnp.concatenate([w_query[:, 0], w_query[:, 1]], axis=1)
    stacked = jnp.concatenate([w_mix[:, :128], w_mix[:, 128:]], axis=0)
    unit_b = jnp.concatenate([w_query[:, 2], stacked], axis=1)
    return (unit_a, unit_b)


def gather_chunk(unit_a, unit_b):
    own = jnp.stack([unit_a, unit_b])
    far = swap(own, "tensor", 2)
    near = swap(jnp.stack([own, far]), "tensor", 1)
    parts_a = jnp.stack([near[0, 0], far[0], near[1, 0]])
    parts_b = jnp.stack([near[0, 1], far[1], near[1, 1]])
    a1 = swap(parts_a, "dp", 1)
    b2 = swap(parts_b, "dp", 2)
    a23 = swap(jnp.stack([parts_a, a1]), "dp", 2)
    b13 = swap(jnp.stack([parts_b, b2]), "dp", 1)
    table_a = [parts_a, a1, a23[0], a23[1]]
    table_b = [parts_b, b13[0], b2, b13[1]]
    return (table_a, table_b)


def sum_rest(value):
    step = QUARTERS
    while step < lax.axis_size("dp"):
        value = (value.astype(f32) + swap(value, "dp", step).astype(f32)).astype(low16)
        step *= 2
    return value


def add16(a, b):
    return (a.astype(f32) + b.astype(f32)).astype(low16)


def scatter_dp(table_a, table_b):
    a = swap(jnp.stack([table_a[1], table_a[3]]), "dp", 1)
    b = swap(jnp.stack([table_b[2], table_b[3]]), "dp", 2)
    a0, a2 = add16(table_a[0], a[0]), add16(table_a[2], a[1])
    b0, b1 = add16(table_b[0], b[0]), add16(table_b[1], b[1])
    a = swap(a2, "dp", 2)
    b = swap(b1, "dp", 1)
    return sum_rest(jnp.stack([add16(a0, a), add16(b0, b)]))


def scatter_z(units):
    arrived = swap(jnp.stack([units[:, 1], units[:, 3]]), "tensor", 1)
    own = add16(units[:, 0], arrived[0])
    far = add16(units[:, 2], arrived[1])
    return add16(own, swap(far, "tensor", 2))


def gather_dp(piece_a, piece_b):
    a1 = swap(piece_a, "dp", 1)
    b2 = swap(piece_b, "dp", 2)
    a23 = swap(jnp.stack([piece_a, a1]), "dp", 2)
    b13 = swap(jnp.stack([piece_b, b2]), "dp", 1)
    return ([piece_a, a1, a23[0], a23[1]], [piece_b, b13[0], b2, b13[1]])


def global_attention(packed, allowed):
    rows = packed.shape[0]
    shaped = packed.reshape(rows, 3, -1, HEAD_DIM)
    queries, keys, values = shaped[:, 0], shaped[:, 1], shaped[:, 2]
    scores = jnp.einsum("qhd,khd->hqk", queries, keys, preferred_element_type=f32) * SCALE
    scores = jnp.where(allowed[None], scores, negative)
    peak = jnp.max(scores, axis=-1, keepdims=True)
    raised = jnp.exp(scores - peak)
    probs = raised / jnp.sum(raised, axis=-1, keepdims=True)
    mixed = jnp.einsum(
        "hqk,khd->qhd", probs.astype(low16), values, preferred_element_type=f32
    ).astype(low16)
    return (mixed.reshape(rows, -1), probs)


def global_attention_back(packed, probs, grad_mixed):
    rows = packed.shape[0]
    shaped = packed.reshape(rows, 3, -1, HEAD_DIM)
    queries, keys, values = shaped[:, 0], shaped[:, 1], shaped[:, 2]
    grad_mixed = grad_mixed.reshape(rows, -1, HEAD_DIM)
    grad_values = jnp.einsum(
        "hqk,qhd->khd", probs.astype(low16), grad_mixed, preferred_element_type=f32
    )
    grad_probs = jnp.einsum("qhd,khd->hqk", grad_mixed, values, preferred_element_type=f32)
    center = jnp.sum(grad_probs * probs, axis=-1, keepdims=True)
    grad_scores = (probs * (grad_probs - center)).astype(low16)
    grad_queries = jnp.einsum("hqk,khd->qhd", grad_scores, keys, preferred_element_type=f32)
    grad_keys = jnp.einsum("hqk,qhd->khd", grad_scores, queries, preferred_element_type=f32)
    grads = jnp.stack([grad_queries * SCALE, grad_keys * SCALE, grad_values], axis=1)
    return grads.astype(low16).reshape(rows, -1)


def head_table(width):
    lane = jnp.arange(width)[:, None] // HEAD_DIM
    return (lane == jnp.arange(width // HEAD_DIM)[None, :]).astype(f32)


def head_sums(products):
    return lax.dot_general(
        products,
        head_table(products.shape[-1]),
        (((products.ndim - 1,), (0,)), ((), ())),
        precision=lax.Precision.HIGHEST,
        preferred_element_type=f32,
    )


def head_spread(values, width):
    return lax.dot_general(
        values,
        head_table(width).astype(low16),
        (((values.ndim - 1,), (1,)), ((), ())),
        preferred_element_type=f32,
    )


PAIRS = [(i, j) for i in range(3) for j in range(i + 1)]


def local_attention(queries, keys, values):
    width = queries.shape[-1]
    products = jnp.stack([queries[i] * keys[j] for i, j in PAIRS])
    scores = head_sums(products) * SCALE
    probs = {}
    for i in range(3):
        own = jnp.stack([scores[PAIRS.index((i, j))] for j in range(i + 1)])
        raised = jnp.exp(own - jnp.max(own, axis=0, keepdims=True))
        raised = raised / jnp.sum(raised, axis=0, keepdims=True)
        for j in range(i + 1):
            probs[(i, j)] = raised[j]
    stacked = jnp.stack([probs[pair] for pair in PAIRS])
    spread = head_spread(stacked.astype(low16), width)
    mixed = jnp.stack(
        [sum(spread[PAIRS.index((i, j))] * values[j] for j in range(i + 1)) for i in range(3)]
    )
    return (mixed.astype(low16), stacked, spread)


def local_attention_back(queries, keys, values, stacked, spread, grad_mixed):
    width = queries.shape[-1]
    products = jnp.stack([grad_mixed[i] * values[j] for i, j in PAIRS])
    grad_probs = head_sums(products)
    weighted = grad_probs * stacked
    grad_scores = []
    for p, (i, j) in enumerate(PAIRS):
        center = sum(weighted[PAIRS.index((i, t))] for t in range(i + 1))
        grad_scores.append(stacked[p] * (grad_probs[p] - center))
    wide = head_spread(jnp.stack(grad_scores).astype(low16), width)
    grad_queries = jnp.stack(
        [sum(wide[PAIRS.index((i, j))] * keys[j] for j in range(i + 1)) for i in range(3)]
    )
    grad_keys = jnp.stack(
        [sum(wide[PAIRS.index((i, j))] * queries[i] for i in range(j, 3)) for j in range(3)]
    )
    grad_values = jnp.stack(
        [sum(spread[PAIRS.index((i, j))] * grad_mixed[i] for i in range(j, 3)) for j in range(3)]
    )
    return (
        (grad_queries * SCALE).astype(low16),
        (grad_keys * SCALE).astype(low16),
        grad_values.astype(low16),
    )


def on_device(codes, lengths, gains, w_qkv, w_out, w_up, w_down, cotangent):
    sec = lax.axis_index("section")
    low = lax.axis_index("dp") % QUARTERS
    z = lax.axis_index("tensor")
    first = sec == 0
    utts, frames, code_count, width = codes.shape
    block = width // QUARTERS
    rows_local = utts * frames * code_count
    heads_width = w_out.shape[1]
    half_width = heads_width // 2
    hidden_width = w_up.shape[2]
    half_hidden = hidden_width // 2

    def choose(a, b):
        return jnp.where(first, a, b)

    code_rows = reorder(jnp.transpose(codes, (2, 0, 1, 3)), low, 3)
    cot_rows = reorder(jnp.transpose(cotangent, (2, 0, 1, 3)), low, 3)

    other_gains = swap(gains[0], "section", 1)
    gain_g = reorder(choose(gains[0], other_gains), low, 1)
    gain_l = reorder(choose(other_gains, gains[0]), low, 1)

    own_w = (w_qkv[0].reshape(width, 3 * heads_width), w_out[0], w_up[0], w_down[0])
    other_w = tuple(swap(w, "section", 1) for w in own_w)
    full_g = tuple(choose(a, b) for a, b in zip(own_w, other_w))
    full_l = tuple(choose(b, a) for a, b in zip(own_w, other_w))
    qkv_g = reorder(full_g[0], low, 0)
    out_g = reorder(full_g[1], low, 1)
    up_g = reorder(full_g[2], low, 0)
    down_g = reorder(full_g[3], low, 1)

    qkv_l = reorder(half_of(full_l[0].reshape(width, 3, heads_width), sec, 2), low, 0)
    out_l = reorder(half_of(full_l[1], sec, 0), low, 1)
    up_l = reorder(half_of(full_l[2], sec, 1), low, 0)
    down_l = reorder(half_of(full_l[3], sec, 0), low, 1)

    def units_of(m):
        span = slice(m * block, (m + 1) * block)
        attn = attention_units(qkv_l[span], out_l[:, span])
        lift = (up_l[span, : half_hidden // 2], up_l[span, half_hidden // 2 :])
        drop = (down_l[: half_hidden // 2, span], down_l[half_hidden // 2 :, span])
        return (attn, lift, drop)

    own_units = [units_of(m) for m in range(QUARTERS)]
    tables = [gather_chunk(*own_units[0][chunk]) for chunk in range(3)]

    def unit(chunk, part, k, m):
        if k == 0:
            return own_units[m][chunk][part]
        return tables[chunk][part][m][k - 1]

    def assembled(make):
        return jnp.concatenate(
            [jnp.concatenate([make(k, m) for k in range(4)], axis=1) for m in range(QUARTERS)],
            axis=0,
        )

    def assembled_t(make):
        return jnp.concatenate(
            [jnp.concatenate([make(k, m) for m in range(QUARTERS)], axis=1) for k in range(4)],
            axis=0,
        )

    def mix_block(k, m):
        stacked = unit(0, 1, k, m)[:, half_width:]
        return jnp.concatenate([stacked[:half_width], stacked[half_width:]], axis=1)

    local_q = assembled(lambda k, m: unit(0, 0, k, m)[:, :half_width])
    local_k = assembled(lambda k, m: unit(0, 0, k, m)[:, half_width:])
    local_v = assembled(lambda k, m: unit(0, 1, k, m)[:, :half_width])
    local_qkv = jnp.concatenate([local_q, local_k, local_v], axis=1)
    local_out = assembled_t(mix_block)
    local_up = assembled(
        lambda k, m: jnp.concatenate([unit(1, 0, k, m), unit(1, 1, k, m)], axis=1)
    )
    local_down = assembled_t(
        lambda k, m: jnp.concatenate([unit(2, 0, k, m), unit(2, 1, k, m)], axis=0)
    )

    own_codes = lax.dynamic_index_in_dim(code_rows, sec, 1, keepdims=False).astype(f32)
    start_g = jnp.sum(own_codes, axis=0)
    length = lax.dynamic_index_in_dim(lengths, sec, 0, keepdims=False)
    order = jnp.stack([z ^ k for k in range(4)])
    positions = (order[:, None] * frames + jnp.arange(frames)[None, :]).reshape(-1)
    allowed = (positions[None, :] <= positions[:, None]) & (positions < length)[None, :]

    n1, r1 = norm_forward(start_g, gain_g[0])
    first_g = row_gather(n1.astype(low16))
    packed_g = dot(first_g, qkv_g).astype(low16)
    mixed_g, probs_g = global_attention(packed_g, allowed)
    hidden_g = start_g + row_scatter(dot(mixed_g, out_g))
    n2, r2 = norm_forward(hidden_g, gain_g[1])
    second_g = row_gather(n2.astype(low16))
    lifted_g = dot(second_g, up_g)
    active_g = gelu_exact(lifted_g).astype(low16)
    result_g = hidden_g + row_scatter(dot(active_g, down_g))
    sent = result_g.astype(low16)

    other_sent = swap(sent, "section", 1)
    both_sent = jnp.stack([choose(sent, other_sent), choose(other_sent, sent)])
    start_l = (both_sent.astype(f32)[None] + code_rows.astype(f32)).reshape(rows_local, width)
    n1l, r1l = norm_forward(start_l, gain_l[0])
    first_l = n1l.astype(low16)
    packed_l = dot(first_l, local_qkv).astype(low16)
    split = packed_l.reshape(code_count, utts * frames, 3, 4 * half_width).astype(f32)
    q_l, k_l, v_l = split[:, :, 0], split[:, :, 1], split[:, :, 2]
    mixed_l, probs_l, spread_l = local_attention(q_l, k_l, v_l)
    mixed_l = mixed_l.reshape(rows_local, -1)
    hidden_l = start_l + pair_sum(dot(mixed_l, local_out))
    n2l, r2l = norm_forward(hidden_l, gain_l[1])
    second_l = n2l.astype(low16)
    lifted_l = dot(second_l, local_up)
    active_l = gelu_exact(lifted_l).astype(low16)

    own_frames = z * frames + jnp.arange(frames)
    valid = (own_frames[None, :] < lengths[:, None])[None, :, :, None]
    top_l = jnp.where(valid, cot_rows, jnp.zeros_like(cot_rows)).reshape(rows_local, width)
    grad_down_l = dot_tn(active_l, top_l).astype(low16)
    grad_lifted_l = gelu_grad(lifted_l, dot_nt(top_l, local_down)).astype(low16)
    grad_up_l = dot_tn(second_l, grad_lifted_l).astype(low16)
    grad_second_l = pair_sum(dot_nt(grad_lifted_l, local_up))
    through, gain2_l = norm_backward(hidden_l, r2l, gain_l[1], grad_second_l)
    grad_hidden_l = top_l.astype(f32) + through
    mid_l = grad_hidden_l.astype(low16)
    grad_out_l = dot_tn(mixed_l, mid_l).astype(low16)
    grad_mixed_l = dot_nt(mid_l, local_out).astype(low16)
    grad_mixed_l = grad_mixed_l.reshape(code_count, utts * frames, -1).astype(f32)
    grad_q, grad_k, grad_v = local_attention_back(
        q_l, k_l, v_l, probs_l, spread_l, grad_mixed_l
    )
    grad_packed_l = jnp.concatenate([grad_q, grad_k, grad_v], axis=2).reshape(rows_local, -1)
    grad_qkv_l = dot_tn(first_l, grad_packed_l).astype(low16)
    grad_first_l = pair_sum(dot_nt(grad_packed_l, local_qkv))
    through, gain1_l = norm_backward(start_l, r1l, gain_l[0], grad_first_l)
    grad_codes = (grad_hidden_l + through).reshape(code_count, utts, frames, width)

    absolute = lambda value: half_of(reorder(value, low, -1), sec, value.ndim - 1)
    other_half = lambda value: half_of(reorder(value, low, -1), 1 - sec, value.ndim - 1)
    branch_l = dot(active_l, local_down)
    arrived = swap(other_half(branch_l).astype(low16), "section", 1)
    final = absolute(hidden_l) + absolute(branch_l) + arrived.astype(f32)
    final = final.reshape(code_count, utts, frames, width // 2)
    final = jnp.where(valid, final, 0.0).astype(low16)
    output = jnp.transpose(final, (1, 2, 0, 3))

    returned = jnp.sum(
        lax.dynamic_index_in_dim(grad_codes, sec, 1, keepdims=False), axis=0
    ).astype(low16)
    top_g = row_gather(returned)
    grad_down_g = dot_tn(active_g, top_g).astype(low16)
    grad_lifted_g = gelu_grad(lifted_g, dot_nt(top_g, down_g)).astype(low16)
    grad_up_g = dot_tn(second_g, grad_lifted_g).astype(low16)
    grad_second_g = row_scatter(dot_nt(grad_lifted_g, up_g))
    through, gain2_g = norm_backward(hidden_g, r2, gain_g[1], grad_second_g)
    grad_hidden_g = returned.astype(f32) + through
    mid_g = row_gather(grad_hidden_g.astype(low16))
    grad_out_g = dot_tn(mixed_g, mid_g).astype(low16)
    grad_mixed_g = dot_nt(mid_g, out_g).astype(low16)
    grad_packed_g = global_attention_back(packed_g, probs_g, grad_mixed_g)
    grad_qkv_g = dot_tn(first_g, grad_packed_g).astype(low16)
    grad_first_g = row_scatter(dot_nt(grad_packed_g, qkv_g))
    through, gain1_g = norm_backward(start_g, r1, gain_g[0], grad_first_g)
    grad_start = grad_hidden_g + through

    other_start = swap(other_half(grad_start), "section", 1)
    own_start = absolute(grad_start)
    both_start = jnp.stack([choose(own_start, other_start), choose(other_start, own_start)])
    code_grad = absolute(grad_codes) + both_start[None]
    code_grad = jnp.transpose(code_grad, (1, 2, 0, 3))

    own_g = jnp.stack([gain1_g, gain2_g])
    total_g = own_g + swap(own_g, "section", 1)
    gain_total = reorder(choose(total_g, jnp.stack([gain1_l, gain2_l])), low, 1)
    for axis in ("tensor", "dp"):
        step = 1
        while step < lax.axis_size(axis):
            gain_total = gain_total + swap(gain_total, axis, step)
            step *= 2

    def local_unit(chunk, part, k, m):
        span = slice(m * block, (m + 1) * block)
        if chunk == 0:
            at = [
                grad_qkv_l[span, c * 4 * half_width + k * half_width :][:, :half_width]
                for c in range(3)
            ]
            if part == 0:
                return jnp.concatenate([at[0], at[1]], axis=1)
            mix = grad_out_l[k * half_width : (k + 1) * half_width, span]
            stacked = jnp.concatenate([mix[:, :half_width], mix[:, half_width:]], axis=0)
            return jnp.concatenate([at[2], stacked], axis=1)
        offset = k * half_hidden + part * (half_hidden // 2)
        if chunk == 1:
            return grad_up_l[span, offset : offset + half_hidden // 2]
        return grad_down_l[offset : offset + half_hidden // 2, span]

    def global_unit(chunk, part, half, m):
        span = slice(m * block, (m + 1) * block)
        if chunk == 0:
            at = [
                lax.dynamic_slice_in_dim(
                    grad_qkv_g[span], c * heads_width + half * half_width, half_width, 1
                )
                for c in range(3)
            ]
            if part == 0:
                return jnp.concatenate([at[0], at[1]], axis=1)
            mix = lax.dynamic_slice_in_dim(grad_out_g[:, span], half * half_width, half_width, 0)
            stacked = jnp.concatenate([mix[:, :half_width], mix[:, half_width:]], axis=0)
            return jnp.concatenate([at[2], stacked], axis=1)
        offset = half * half_hidden + part * (half_hidden // 2)
        if chunk == 1:
            return lax.dynamic_slice_in_dim(grad_up_g[span], offset, half_hidden // 2, 1)
        return lax.dynamic_slice_in_dim(grad_down_g[:, span], offset, half_hidden // 2, 0)

    finished = []
    for chunk in (2, 1, 0):
        tables_l = [
            [
                jnp.stack([local_unit(chunk, part, k, m) for k in range(4)])
                for m in range(QUARTERS)
            ]
            for part in range(2)
        ]
        piece_l = scatter_z(scatter_dp(*tables_l))
        away = jnp.stack(
            [
                jnp.stack([global_unit(chunk, part, 1 - sec, m) for m in range(QUARTERS)])
                for part in range(2)
            ]
        )
        own = jnp.stack(
            [
                jnp.stack([global_unit(chunk, part, sec, m) for m in range(QUARTERS)])
                for part in range(2)
            ]
        )
        both = add16(own, swap(away, "section", 1))
        piece_g = scatter_dp(
            [both[0, m] for m in range(QUARTERS)], [both[1, m] for m in range(QUARTERS)]
        )
        arrived = swap(choose(piece_l, piece_g), "section", 1)
        kept = choose(piece_g, piece_l)
        halves = jnp.stack([choose(kept, arrived), choose(arrived, kept)])
        finished.append(gather_dp(halves[:, 0], halves[:, 1]))
    tables_down, tables_up, tables_attn = finished

    def absolute_order(table):
        stacked = jnp.stack(table)
        return [
            lax.dynamic_index_in_dim(stacked, low ^ j, 0, keepdims=False)
            for j in range(QUARTERS)
        ]

    up_a, up_b = (absolute_order(table) for table in tables_up)
    up_grad = jnp.concatenate(
        [
            jnp.concatenate([up_a[j][0], up_b[j][0], up_a[j][1], up_b[j][1]], axis=1)
            for j in range(QUARTERS)
        ],
        axis=0,
    ).astype(f32)
    down_a, down_b = (absolute_order(table) for table in tables_down)
    down_grad = jnp.concatenate(
        [
            jnp.concatenate([down_a[j][0], down_b[j][0], down_a[j][1], down_b[j][1]], axis=0)
            for j in range(QUARTERS)
        ],
        axis=1,
    ).astype(f32)
    attn_a, attn_b = (absolute_order(table) for table in tables_attn)

    def part_of(unit_pair, start):
        return jnp.concatenate(
            [unit_pair[h][:, start * half_width : (start + 1) * half_width] for h in range(2)],
            axis=1,
        )

    qkv_grad = jnp.concatenate(
        [
            jnp.stack(
                [part_of(attn_a[j], 0), part_of(attn_a[j], 1), part_of(attn_b[j], 0)], axis=1
            )
            for j in range(QUARTERS)
        ],
        axis=0,
    ).astype(f32)

    def mix_of(stacked):
        stacked = stacked[:, half_width:]
        return jnp.concatenate([stacked[:half_width], stacked[half_width:]], axis=1)

    out_grad = jnp.concatenate(
        [
            jnp.concatenate([mix_of(attn_b[j][h]) for h in range(2)], axis=0)
            for j in range(QUARTERS)
        ],
        axis=1,
    ).astype(f32)
    return (
        output,
        code_grad,
        gain_total[None],
        qkv_grad[None],
        out_grad[None],
        up_grad[None],
        down_grad[None],
    )


def solution(mesh):
    in_specs = (
        P("dp", "tensor", None, None),
        P("dp"),
        P("section", None, None),
        P("section", None, None, "tensor"),
        P("section", "tensor", None),
        P("section", None, "tensor"),
        P("section", "tensor", None),
        P("dp", "tensor", None, None),
    )
    out_specs = (
        P("dp", "tensor", None, "section"),
        P("dp", "tensor", None, "section"),
        P("section", None, None),
        P("section", None, None, "tensor"),
        P("section", "tensor", None),
        P("section", None, "tensor"),
        P("section", "tensor", None),
    )
    return jax.shard_map(
        on_device, mesh=mesh, in_specs=in_specs, out_specs=out_specs, check_vma=False
    )
```

time: 1980 us -> 743 us (0.38)
  waiting for transfers between devices: 1460 us -> 242 us
  blocking collectives: 216 us -> 0 us
  other arithmetic: 84.3 us -> 198 us
  starting transfers between devices: 3.94 us -> 104 us
  local copies, waits for them, and re-layouts: 80.2 us -> 125 us
  matrix products: 90.8 us -> 60.7 us
    reduce_scatter x16 -> x0, waiting for transfers between devices: 555 us -> none  [the longest x1 142 us: on_device(): lax.psum_scatter(full_grads[3].astype(jnp.bfloat16), 'tensor', scatter_di...]
    all_gather x4 -> x0, waiting for transfers between devices: 457 us -> none  [the longest x1 149 us: on_device(): lax.all_gather(w_up, 'tensor', axis=2, tiled=True)]
    psum x1 -> x0, waiting for transfers between devices: 215 us -> none  [on_device(): weight_total = lax.psum(sharded, 'dp')]
    all_gather x10 -> x0, blocking collectives: 172 us -> none  [the longest x6 104 us: row_gather(): return lax.all_gather(values, 'tensor', axis=0, tiled=True)]
    concatenate x0 -> x24, other arithmetic: none -> 117 us  [the longest x1 68.1 us: assembled_t(): jnp.concatenate([jnp.concatenate([make(k, m) for m in range(QUARTERS)], a...]
    ppermute x2 -> x106, starting transfers between devices: 2.87 us -> 104 us  [swap(): return lax.ppermute(value, axis, [(i, i ^ flip) for i in range(count)])]
    psum x1 -> x0, blocking collectives: 44 us -> none  [on_device(): gain_total = lax.psum(totals[2], ('dp', 'tensor'))]
    dynamic_slice x0 -> x47, local copies, waits for them, and re-layouts: none -> 41 us  [the longest x20 26.5 us: global_unit(): lax.dynamic_slice_in_dim(grad_down_g[:, span], offset, half_hidden // 2, 0)]
  transfers between devices with their start and end apart: 23 -> 106, of which waited for: 18 -> 44; matrix products, arithmetic and copies ran while one was open for 6% -> 47% of each run, Pallas kernels for 0% -> 0%
where the time goes in v1:
time: 743 us; the launch traced here: 736 us
  waiting for transfers between devices  242 us (33%)
  other arithmetic  198 us (27%)
  local copies, waits for them, and re-layouts  125 us (17%)
  starting transfers between devices  104 us (14%)
  matrix products  60.7 us (8%)
    ppermute x106, waiting for transfers between devices, swap(): return lax.ppermute(value, axis, [(i, i ^ flip) for i in range(count)])  242 us
    ppermute x106, starting transfers between devices, swap(): return lax.ppermute(value, axis, [(i, i ^ flip) for i in range(count)])  104 us
    concatenate x1, other arithmetic, assembled_t(): jnp.concatenate([jnp.concatenate([make(k, m) for m in range(QUARTERS)], a...  68.1 us
    concatenate x1, other arithmetic, on_device(): local_qkv = jnp.concatenate([local_q, local_k, local_v], axis=1)  46 us
    unnamed x435, local copies, waits for them, and re-layouts  36.4 us
    dynamic_slice x20, local copies, waits for them, and re-layouts, global_unit(): lax.dynamic_slice_in_dim(grad_down_g[:, span], offset, half_hidden // 2, 0)  26.5 us
    dot_general x8, matrix products, dot(): return jnp.dot(a, b, preferred_element_type=f32)  23.4 us
    dot_general x8, matrix products, dot_nt(): lax.dot_general(a, b, (((1,), (1,)), ((), ())), preferred_element_type=f32)  16.1 us
  transfers between devices with their start and end apart: 106, of which 44 were waited for; matrix products, arithmetic and copies ran while one was open for 47% of the time, Pallas kernels for 0%

profile of v1, /device:TPU:0, one launch (start us, length us, event | category | flops | bytes accessed | tf_op | source)
XLA Modules:
  0.0 736.1 jit_solution(12862038032469040156)
XLA Ops:
  17.5 4.7 collective-permute-start.3
  26.0 2.8 broadcast_select_fusion.4
  29.0 4.9 collective-permute-done.2
  39.9 2.5 collective-permute-start.8
  49.6 11.8 %collective-permute-done.7 = bf16[64,1024]{1,0:T(8,128)(2,1)S(1)} collective-permute-done((bf16[64,1024]{1,0:T(8,128)(2,1)S(1)}, bf16[64,1024]{1,0:T(8,128)(2,1)S(1)}, u32[]{:S(2)}, u32[]{:S(2)}) %collective-permute-start.7) | collective-permute-done | bytes 131104 | tf_op jit(solution)/shard_map/ppermute | solution.py:17
  64.9 7.8 %collective-permute-done.18 = bf16[2,256,256]{1,2,0:T(8,128)(2,1)S(1)} collective-permute-done((bf16[2,256,256]{1,2,0:T(8,128)(2,1)S(1)}, bf16[2,256,256]{1,2,0:T(8,128)(2,1)S(1)}, u32[]{:S(2)}, u32[]{:S(2)}) %collective-permute-start.18) | collective-permute-done | bytes 262176 | tf_op jit(solution)/shard_map/ppermute | solution.py:17
  77.3 2.7 broadcast_select_fusion
  84.5 4.1 multiply_convert_fusion.4
  99.2 12.8 %collective-permute-done.15 = bf16[64,1024]{1,0:T(8,128)(2,1)S(1)} collective-permute-done((bf16[64,1024]{1,0:T(8,128)(2,1)S(1)}, bf16[64,1024]{1,0:T(8,128)(2,1)S(1)}, u32[]{:S(2)}, u32[]{:S(2)}) %collective-permute-start.15) | collective-permute-done | bytes 131104 | tf_op jit(solution)/shard_map/ppermute | solution.py:17
  112.2 5.4 collective-permute-done.25
  118.5 3.0 collective-permute-done.31
  158.5 11.6 %collective-permute-done.27 = bf16[3,256,256]{2,1,0:T(8,128)(2,1)S(1)} collective-permute-done((bf16[3,256,256]{2,1,0:T(8,128)(2,1)S(1)}, bf16[3,256,256]{2,1,0:T(8,128)(2,1)S(1)}, u32[]{:S(2)}, u32[]{:S(2)}) %collective-permute-start.27) | collective-permute-done | bytes 393248 | tf_op jit(solution)/shard_map/ppermute | solution.py:17
  172.3 7.7 %collective-permute-done.34 = bf16[3,256,256]{2,1,0:T(8,128)(2,1)S(1)} collective-permute-done((bf16[3,256,256]{2,1,0:T(8,128)(2,1)S(1)}, bf16[3,256,256]{2,1,0:T(8,128)(2,1)S(1)}, u32[]{:S(2)}, u32[]{:S(2)}) %collective-permute-start.34) | collective-permute-done | bytes 393248 | tf_op jit(solution)/shard_map/ppermute | solution.py:17
  196.5 46.0 %maximum_maximum_fusion.1 = bf16[1024,1536]{0,1:T(8,128)(2,1)} fusion(bf16[256,128]{0,1:T(8,128)(2,1)} %slice.2874, bf16[256,128]{0,1:T(8,128)(2,1)} %slice.2872, bf16[256,128]{0,1:T(8,128)(2,1)} %slice.2870, bf16[256,128]{0,1:T(8,128)(2,1)} %get-tuple-element.255, bf16[256,128]{0,1:T(8,128)(2,1)} %slice.2868, bf16[256,128]{0,1:T(8,128)(2,1)} %slice.2866, ...), kind=kLoop, calls=%fused_computation.8 | loop fusion | flops 150994944 | bytes 6291456 | tf_op jit(solution)/shard_map/concatenate | solution.py:317
  242.6 4.7 fusion.7
  247.3 4.8 reshape.1048
  252.1 6.5 fusion.197
  264.9 68.1 %maximum_maximum_fusion = bf16[2048,1024]{1,0:T(8,128)(2,1)S(1)} fusion(bf16[256,256]{1,0:T(8,128)(2,1)S(1)} %get-tuple-element.381, bf16[256,256]{1,0:T(8,128)(2,1)S(1)} %get-tuple-element.387, bf16[256,256]{1,0:T(8,128)(2,1)S(1)} %copy-done.49, bf16[256,256]{1,0:T(8,128)(2,1)S(1)} %get-tuple-element.388, bf16[256,256]{1,0:T(8,128)(2,1)S(1)} %get-tuple-element.382, ...), kind=kLoop, calls=%fused_computation.3 | loop fusion | flops 117440512 | bytes 8388608 | tf_op jit(solution)/shard_map/concatenate | solution.py:305
  337.0 9.4 %multiply_convert_fusion = (bf16[384,2048]{1,0:T(8,128)(2,1)S(1)}, f32[384,2048]{1,0:T(8,128)S(1)}, f32[384,2048]{1,0:T(8,128)}) fusion(bf16[256,2048]{1,0:T(8,128)(2,1)S(1)} %get-tuple-element.393, bf16[256,2048]{1,0:T(8,128)(2,1)S(1)} %constant_dynamic-update-slice_fusion.36, bf16[256,2048]{1,0:T(8,128)(2,1)S(1)} %get-tuple-element.392, ...), kind=kOutput, calls=%fused_computation.10 | convolution fusion | flops 1679687680 | bytes 13637120 | tf_op jit(solution)/shard_map/dot_general | solution.py:21
  346.4 5.4 add_convert_fusion
  351.9 5.9 convolution_convert_fusion.9
  400.3 14.9 %collective-permute-done.97 = bf16[2,4,256,256]{2,3,1,0:T(8,128)(2,1)S(1)} collective-permute-done((bf16[2,4,256,256]{2,3,1,0:T(8,128)(2,1)S(1)}, bf16[2,4,256,256]{2,3,1,0:T(8,128)(2,1)S(1)}, u32[]{:S(2)}, u32[]{:S(2)}) %collective-permute-start.97) | collective-permute-done | bytes 1048608 | tf_op jit(solution)/shard_map/ppermute | solution.py:17
  420.6 30.1 %collective-permute-done.82 = bf16[4,256,256]{1,2,0:T(8,128)(2,1)S(1)} collective-permute-done((bf16[4,256,256]{1,2,0:T(8,128)(2,1)S(1)}, bf16[4,256,256]{1,2,0:T(8,128)(2,1)S(1)}, u32[]{:S(2)}, u32[]{:S(2)}) %collective-permute-start.82) | collective-permute-done | bytes 524320 | tf_op jit(solution)/shard_map/ppermute | solution.py:17
  456.3 4.8 collective-permute-done.98
  461.1 2.8 collective-permute-start.41
  465.8 3.8 collective-permute-done.41
  528.0 16.1 %collective-permute-done.48 = bf16[64,1024]{1,0:T(8,128)(2,1)S(1)} collective-permute-done((bf16[64,1024]{1,0:T(8,128)(2,1)S(1)}, bf16[64,1024]{1,0:T(8,128)(2,1)S(1)}, u32[]{:S(2)}, u32[]{:S(2)}) %collective-permute-start.48) | collective-permute-done | bytes 131104 | tf_op jit(solution)/shard_map/ppermute | solution.py:17
  560.8 3.0 collective-permute-done.51
  565.3 3.9 collective-permute-done.50
  571.4 3.0 collective-permute-done.54
  575.4 3.7 collective-permute-done.55
  583.3 3.1 collective-permute-done.57
  599.3 20.3 %collective-permute-done.67 = bf16[2,2,256,256]{2,3,1,0:T(8,128)(2,1)S(1)} collective-permute-done((bf16[2,2,256,256]{2,3,1,0:T(8,128)(2,1)S(1)}, bf16[2,2,256,256]{2,3,1,0:T(8,128)(2,1)S(1)}, u32[]{:S(2)}, u32[]{:S(2)}) %collective-permute-start.67) | collective-permute-done | bytes 524320 | tf_op jit(solution)/shard_map/ppermute | solution.py:17
  622.0 4.7 collective-permute-done.75
  628.3 4.8 collective-permute-done.91
  635.3 3.0 collective-permute-done.76
  641.8 4.3 collective-permute-done.59
  647.6 3.4 collective-permute-done.78
  659.5 3.3 collective-permute-done.62
  668.2 4.1 collective-permute-done.88
  674.6 3.4 collective-permute-done.104
  679.6 4.0 collective-permute-done.72
  685.2 10.2 %collective-permute-done.89 = bf16[2,2,256,256]{2,3,1,0:T(8,128)(2,1)S(1)} collective-permute-done((bf16[2,2,256,256]{2,3,1,0:T(8,128)(2,1)S(1)}, bf16[2,2,256,256]{2,3,1,0:T(8,128)(2,1)S(1)}, u32[]{:S(2)}, u32[]{:S(2)}) %collective-permute-start.89) | collective-permute-done | bytes 524320 | tf_op jit(solution)/shard_map/ppermute | solution.py:17
  698.8 7.9 %collective-permute-done.105 = bf16[2,2,256,256]{2,3,1,0:T(8,128)(2,1)S(1)} collective-permute-done((bf16[2,2,256,256]{2,3,1,0:T(8,128)(2,1)S(1)}, bf16[2,2,256,256]{2,3,1,0:T(8,128)(2,1)S(1)}, u32[]{:S(2)}, u32[]{:S(2)}) %collective-permute-start.105) | collective-permute-done | bytes 524320 | tf_op jit(solution)/shard_map/ppermute | solution.py:17
  710.0 5.3 copy.259
  717.4 2.6 maximum_convert_fusion
  720.0 5.3 copy.258
  732.4 3.5 copy.256
  (1084 shorter events, 318.3 us)
Async XLA Ops:
  5.5 69.8 %collective-permute-start.13 = (bf16[1024,1024]{1,0:T(8,128)(2,1)}, bf16[1024,1024]{1,0:T(8,128)(2,1)}, u32[]{:S(2)}, u32[]{:S(2)}) collective-permute-start(bf16[1024,1024]{1,0:T(8,128)(2,1)} %bitcast.1426), channel_id=1, source_target_pairs={{0,16},{16,0},{1,17},{17,1},{2,18},{18,2},{3,19},{19,3},{4,20},{20... | collective-permute-start | bytes 6291464 | tf_op jit(solution)/shard_map/ppermute | solution.py:17
  5.6 71.7 %collective-permute-start.12 = (bf16[1024,1024]{1,0:T(8,128)(2,1)}, bf16[1024,1024]{1,0:T(8,128)(2,1)}, u32[]{:S(2)}, u32[]{:S(2)}) collective-permute-start(bf16[1024,1024]{1,0:T(8,128)(2,1)} %bitcast.1427), channel_id=1, source_target_pairs={{0,16},{16,0},{1,17},{17,1},{2,18},{18,2},{3,19},{19,3},{4,20},{20... | collective-permute-start | bytes 6291464 | tf_op jit(solution)/shard_map/ppermute | solution.py:17
  45.2 27.5 %collective-permute-start.18 = (bf16[2,256,256]{1,2,0:T(8,128)(2,1)S(1)}, bf16[2,256,256]{1,2,0:T(8,128)(2,1)S(1)}, u32[]{:S(2)}, u32[]{:S(2)}) collective-permute-start(bf16[2,256,256]{1,2,0:T(8,128)(2,1)S(1)} %get-tuple-element.585), channel_id=1, source_target_pairs={{0,2},{1,3},{2,0},{3,1},{4,6},{5,7},{6,4},{7,5},{8,10},{9,11},{10,... | collective-permute-start | bytes 786440 | tf_op jit(solution)/shard_map/ppermute | solution.py:17
  75.3 48.6 %collective-permute-start.19 = (bf16[2,2,256,256]{2,3,1,0:T(8,128)(2,1)S(1)}, bf16[2,2,256,256]{2,3,1,0:T(8,128)(2,1)S(1)}, u32[]{:S(2)}, u32[]{:S(2)}) collective-permute-start(bf16[2,2,256,256]{2,3,1,0:T(8,128)(2,1)S(1)} %pad_maximum_fusion.35), channel_id=1, source_target_pairs={{0,1},{1,0},{2,3},{3,2},{4,5},{5,4},{6,7},{7,6},{8,9},{9,8},{10,11... | collective-permute-start | bytes 1572872 | tf_op jit(solution)/shard_map/ppermute | solution.py:17
  93.1 24.6 %collective-permute-start.25 = (bf16[2,256,256]{2,1,0:T(8,128)(2,1)S(1)}, bf16[2,256,256]{2,1,0:T(8,128)(2,1)S(1)}, u32[]{:S(2)}, u32[]{:S(2)}) collective-permute-start(bf16[2,256,256]{2,1,0:T(8,128)(2,1)S(1)} %get-tuple-element.579), channel_id=1, source_target_pairs={{0,2},{1,3},{2,0},{3,1},{4,6},{5,7},{6,4},{7,5},{8,10},{9,11},{10,... | collective-permute-start | bytes 786440 | tf_op jit(solution)/shard_map/ppermute | solution.py:17
  95.1 26.3 %collective-permute-start.31 = (bf16[2,256,256]{2,1,0:T(8,128)(2,1)S(1)}, bf16[2,256,256]{2,1,0:T(8,128)(2,1)S(1)}, u32[]{:S(2)}, u32[]{:S(2)}) collective-permute-start(bf16[2,256,256]{2,1,0:T(8,128)(2,1)S(1)} %get-tuple-element.575), channel_id=1, source_target_pairs={{0,2},{1,3},{2,0},{3,1},{4,6},{5,7},{6,4},{7,5},{8,10},{9,11},{10,... | collective-permute-start | bytes 786440 | tf_op jit(solution)/shard_map/ppermute | solution.py:17
  118.5 30.0 %collective-permute-start.26 = (bf16[2,2,256,256]{3,2,1,0:T(8,128)(2,1)}, bf16[2,2,256,256]{3,2,1,0:T(8,128)(2,1)S(1)}, u32[]{:S(2)}, u32[]{:S(2)}) collective-permute-start(bf16[2,2,256,256]{3,2,1,0:T(8,128)(2,1)} %pad_maximum_fusion.36), channel_id=1, source_target_pairs={{0,1},{1,0},{2,3},{3,2},{4,5},{5,4},{6,7},{7,6},{8,9},{9,8},{10,11... | collective-permute-start | bytes 1572872 | tf_op jit(solution)/shard_map/ppermute | solution.py:17
  122.3 26.9 %collective-permute-start.32 = (bf16[2,2,256,256]{3,2,1,0:T(8,128)(2,1)}, bf16[2,2,256,256]{3,2,1,0:T(8,128)(2,1)}, u32[]{:S(2)}, u32[]{:S(2)}) collective-permute-start(bf16[2,2,256,256]{3,2,1,0:T(8,128)(2,1)} %pad_maximum_fusion.37), channel_id=1, source_target_pairs={{0,1},{1,0},{2,3},{3,2},{4,5},{5,4},{6,7},{7,6},{8,9},{9,8},{10,11... | collective-permute-start | bytes 1572872 | tf_op jit(solution)/shard_map/ppermute | solution.py:17
  143.9 44.1 %collective-permute-start.23 = (bf16[2,3,256,256]{2,3,1,0:T(8,128)(2,1)S(1)}, bf16[2,3,256,256]{2,3,1,0:T(8,128)(2,1)S(1)}, u32[]{:S(2)}, u32[]{:S(2)}) collective-permute-start(bf16[2,3,256,256]{2,3,1,0:T(8,128)(2,1)S(1)} %pad_maximum_fusion.25), channel_id=1, source_target_pairs={{0,4},{4,0},{8,12},{12,8},{1,5},{5,1},{9,13},{13,9},{2,6},{6,2},{1... | collective-permute-start | bytes 2359304 | tf_op jit(solution)/shard_map/ppermute | solution.py:17
  145.6 46.9 %collective-permute-start.21 = (bf16[2,3,256,256]{2,3,1,0:T(8,128)(2,1)S(1)}, bf16[2,3,256,256]{2,3,1,0:T(8,128)(2,1)S(1)}, u32[]{:S(2)}, u32[]{:S(2)}) collective-permute-start(bf16[2,3,256,256]{2,3,1,0:T(8,128)(2,1)S(1)} %pad_maximum_fusion.24), channel_id=1, source_target_pairs={{0,8},{4,12},{8,0},{12,4},{1,9},{5,13},{9,1},{13,5},{2,10},{6,14},... | collective-permute-start | bytes 2359304 | tf_op jit(solution)/shard_map/ppermute | solution.py:17
  148.6 36.3 %collective-permute-start.28 = (bf16[3,256,256]{2,1,0:T(8,128)(2,1)S(1)}, bf16[3,256,256]{2,1,0:T(8,128)(2,1)S(1)}, u32[]{:S(2)}, u32[]{:S(2)}) collective-permute-start(bf16[3,256,256]{2,1,0:T(8,128)(2,1)S(1)} %get-tuple-element.553), channel_id=1, source_target_pairs={{0,8},{4,12},{8,0},{12,4},{1,9},{5,13},{9,1},{13,5},{2,10},{6,14},... | collective-permute-start | bytes 1179656 | tf_op jit(solution)/shard_map/ppermute | solution.py:17
  151.1 28.8 %collective-permute-start.34 = (bf16[3,256,256]{2,1,0:T(8,128)(2,1)S(1)}, bf16[3,256,256]{2,1,0:T(8,128)(2,1)S(1)}, u32[]{:S(2)}, u32[]{:S(2)}) collective-permute-start(bf16[3,256,256]{2,1,0:T(8,128)(2,1)S(1)} %get-tuple-element.551), channel_id=1, source_target_pairs={{0,8},{4,12},{8,0},{12,4},{1,9},{5,13},{9,1},{13,5},{2,10},{6,14},... | collective-permute-start | bytes 1179656 | tf_op jit(solution)/shard_map/ppermute | solution.py:17
  180.0 153.0 %collective-permute-start.30 = (bf16[2,3,256,256]{3,2,1,0:T(8,128)(2,1)}, bf16[2,3,256,256]{3,2,1,0:T(8,128)(2,1)}, u32[]{:S(2)}, u32[]{:S(2)}) collective-permute-start(bf16[2,3,256,256]{3,2,1,0:T(8,128)(2,1)} %pad_maximum_fusion.27), channel_id=1, source_target_pairs={{0,8},{4,12},{8,0},{12,4},{1,9},{5,13},{9,1},{13,5},{2,10},{6,14},... | collective-permute-start | bytes 2359304 | tf_op jit(solution)/shard_map/ppermute | solution.py:17
  182.4 79.6 %collective-permute-start.35 = (bf16[2,3,256,256]{3,2,1,0:T(8,128)(2,1)}, bf16[2,3,256,256]{3,2,1,0:T(8,128)(2,1)}, u32[]{:S(2)}, u32[]{:S(2)}) collective-permute-start(bf16[2,3,256,256]{3,2,1,0:T(8,128)(2,1)} %pad_maximum_fusion.28), channel_id=1, source_target_pairs={{0,4},{4,0},{8,12},{12,8},{1,5},{5,1},{9,13},{13,9},{2,6},{6,2},{1... | collective-permute-start | bytes 2359304 | tf_op jit(solution)/shard_map/ppermute | solution.py:17
  184.9 78.5 %collective-permute-start.36 = (bf16[2,3,256,256]{3,2,1,0:T(8,128)(2,1)}, bf16[2,3,256,256]{3,2,1,0:T(8,128)(2,1)}, u32[]{:S(2)}, u32[]{:S(2)}) collective-permute-start(bf16[2,3,256,256]{3,2,1,0:T(8,128)(2,1)} %pad_maximum_fusion.29), channel_id=1, source_target_pairs={{0,8},{4,12},{8,0},{12,4},{1,9},{5,13},{9,1},{13,5},{2,10},{6,14},... | collective-permute-start | bytes 2359304 | tf_op jit(solution)/shard_map/ppermute | solution.py:17
  188.0 146.1 %collective-permute-start.29 = (bf16[2,3,256,256]{3,2,1,0:T(8,128)(2,1)}, bf16[2,3,256,256]{3,2,1,0:T(8,128)(2,1)S(1)}, u32[]{:S(2)}, u32[]{:S(2)}) collective-permute-start(bf16[2,3,256,256]{3,2,1,0:T(8,128)(2,1)} %pad_maximum_fusion.26), channel_id=1, source_target_pairs={{0,4},{4,0},{8,12},{12,8},{1,5},{5,1},{9,13},{13,9},{2,6},{6,2},{1... | collective-permute-start | bytes 2359304 | tf_op jit(solution)/shard_map/ppermute | solution.py:17
  262.0 74.4 %collective-permute-start.24 = (bf16[384,1024]{1,0:T(8,128)(2,1)S(1)}, bf16[384,1024]{1,0:T(8,128)(2,1)S(1)}, u32[]{:S(2)}, u32[]{:S(2)}) collective-permute-start(bf16[384,1024]{1,0:T(8,128)(2,1)S(1)} %convolution_convert_fusion.10), channel_id=1, source_target_pairs={{0,16},{16,0},{1,17},{17,1},{2,18},{18,2},{3,19},{19,3},{4,20},{20... | collective-permute-start | bytes 2359304 | tf_op jit(solution)/shard_map/ppermute | solution.py:17
  366.6 30.3 %collective-permute-start.81 = (bf16[2,4,256,256]{2,3,1,0:T(8,128)(2,1)S(1)}, bf16[2,4,256,256]{2,3,1,0:T(8,128)(2,1)S(1)}, u32[]{:S(2)}, u32[]{:S(2)}) collective-permute-start(bf16[2,4,256,256]{2,3,1,0:T(8,128)(2,1)S(1)} %pad_maximum_fusion.14), channel_id=1, source_target_pairs={{0,8},{4,12},{8,0},{12,4},{1,9},{5,13},{9,1},{13,5},{2,10},{6,14},... | collective-permute-start | bytes 3145736 | tf_op jit(solution)/shard_map/ppermute | solution.py:17
  368.5 30.1 %collective-permute-start.79 = (bf16[2,4,256,256]{2,3,1,0:T(8,128)(2,1)S(1)}, bf16[2,4,256,256]{2,3,1,0:T(8,128)(2,1)S(1)}, u32[]{:S(2)}, u32[]{:S(2)}) collective-permute-start(bf16[2,4,256,256]{2,3,1,0:T(8,128)(2,1)S(1)} %pad_maximum_fusion.13), channel_id=1, source_target_pairs={{0,4},{4,0},{8,12},{12,8},{1,5},{5,1},{9,13},{13,9},{2,6},{6,2},{1... | collective-permute-start | bytes 3145736 | tf_op jit(solution)/shard_map/ppermute | solution.py:17
  370.3 44.9 %collective-permute-start.97 = (bf16[2,4,256,256]{2,3,1,0:T(8,128)(2,1)S(1)}, bf16[2,4,256,256]{2,3,1,0:T(8,128)(2,1)S(1)}, u32[]{:S(2)}, u32[]{:S(2)}) collective-permute-start(bf16[2,4,256,256]{2,3,1,0:T(8,128)(2,1)S(1)} %pad_maximum_fusion.19), channel_id=1, source_target_pairs={{0,8},{4,12},{8,0},{12,4},{1,9},{5,13},{9,1},{13,5},{2,10},{6,14},... | collective-permute-start | bytes 3145736 | tf_op jit(solution)/shard_map/ppermute | solution.py:17
  371.3 45.7 %collective-permute-start.95 = (bf16[2,4,256,256]{2,3,1,0:T(8,128)(2,1)S(1)}, bf16[2,4,256,256]{2,3,1,0:T(8,128)(2,1)S(1)}, u32[]{:S(2)}, u32[]{:S(2)}) collective-permute-start(bf16[2,4,256,256]{2,3,1,0:T(8,128)(2,1)S(1)} %pad_maximum_fusion.18), channel_id=1, source_target_pairs={{0,4},{4,0},{8,12},{12,8},{1,5},{5,1},{9,13},{13,9},{2,6},{6,2},{1... | collective-permute-start | bytes 3145736 | tf_op jit(solution)/shard_map/ppermute | solution.py:17
  384.2 34.4 %collective-permute-start.39 = (bf16[384,1024]{1,0:T(8,128)(2,1)S(1)}, bf16[384,1024]{1,0:T(8,128)(2,1)S(1)}, u32[]{:S(2)}, u32[]{:S(2)}) collective-permute-start(bf16[384,1024]{1,0:T(8,128)(2,1)S(1)} %convolution_convert_fusion.8), channel_id=1, source_target_pairs={{0,16},{16,0},{1,17},{17,1},{2,18},{18,2},{3,19},{19,3},{4,20},{20... | collective-permute-start | bytes 2359304 | tf_op jit(solution)/shard_map/ppermute | solution.py:17
  396.9 124.3 %collective-permute-start.63 = (bf16[2,4,256,256]{2,3,1,0:T(8,128)(2,1)}, bf16[2,4,256,256]{2,3,1,0:T(8,128)(2,1)}, u32[]{:S(2)}, u32[]{:S(2)}) collective-permute-start(bf16[2,4,256,256]{2,3,1,0:T(8,128)(2,1)} %pad_maximum_fusion.8), channel_id=1, source_target_pairs={{0,4},{4,0},{8,12},{12,8},{1,5},{5,1},{9,13},{13,9},{2,6},{6,2},{1... | collective-permute-start | bytes 3145736 | tf_op jit(solution)/shard_map/ppermute | solution.py:17
  398.5 126.4 %collective-permute-start.65 = (bf16[2,4,256,256]{2,3,1,0:T(8,128)(2,1)}, bf16[2,4,256,256]{2,3,1,0:T(8,128)(2,1)}, u32[]{:S(2)}, u32[]{:S(2)}) collective-permute-start(bf16[2,4,256,256]{2,3,1,0:T(8,128)(2,1)} %pad_maximum_fusion.9), channel_id=1, source_target_pairs={{0,8},{4,12},{8,0},{12,4},{1,9},{5,13},{9,1},{13,5},{2,10},{6,14},... | collective-permute-start | bytes 3145736 | tf_op jit(solution)/shard_map/ppermute | solution.py:17
  415.1 35.6 %collective-permute-start.82 = (bf16[4,256,256]{1,2,0:T(8,128)(2,1)S(1)}, bf16[4,256,256]{1,2,0:T(8,128)(2,1)S(1)}, u32[]{:S(2)}, u32[]{:S(2)}) collective-permute-start(bf16[4,256,256]{1,2,0:T(8,128)(2,1)S(1)} %fusion.24), channel_id=1, source_target_pairs={{0,4},{4,0},{8,12},{12,8},{1,5},{5,1},{9,13},{13,9},{2,6},{6,2},{1... | collective-permute-start | bytes 1572872 | tf_op jit(solution)/shard_map/ppermute | solution.py:17
  417.0 34.5 %collective-permute-start.80 = (bf16[4,256,256]{1,2,0:T(8,128)(2,1)S(1)}, bf16[4,256,256]{1,2,0:T(8,128)(2,1)S(1)}, u32[]{:S(2)}, u32[]{:S(2)}) collective-permute-start(bf16[4,256,256]{1,2,0:T(8,128)(2,1)S(1)} %fusion.26), channel_id=1, source_target_pairs={{0,8},{4,12},{8,0},{12,4},{1,9},{5,13},{9,1},{13,5},{2,10},{6,14},... | collective-permute-start | bytes 1572872 | tf_op jit(solution)/shard_map/ppermute | solution.py:17
  418.6 42.5 %collective-permute-start.98 = (bf16[4,256,256]{1,2,0:T(8,128)(2,1)S(1)}, bf16[4,256,256]{1,2,0:T(8,128)(2,1)S(1)}, u32[]{:S(2)}, u32[]{:S(2)}) collective-permute-start(bf16[4,256,256]{1,2,0:T(8,128)(2,1)S(1)} %fusion.20), channel_id=1, source_target_pairs={{0,4},{4,0},{8,12},{12,8},{1,5},{5,1},{9,13},{13,9},{2,6},{6,2},{1... | collective-permute-start | bytes 1572872 | tf_op jit(solution)/shard_map/ppermute | solution.py:17
  473.3 40.9 %collective-permute-start.43 = (bf16[64,1024]{1,0:T(8,128)(2,1)}, bf16[64,1024]{1,0:T(8,128)(2,1)}, u32[]{:S(2)}, u32[]{:S(2)}) collective-permute-start(bf16[64,1024]{1,0:T(8,128)(2,1)} %get-tuple-element.477), channel_id=1, source_target_pairs={{0,1},{1,0},{2,3},{3,2},{4,5},{5,4},{6,7},{7,6},{8,9},{9,8},{10,11... | collective-permute-start | bytes 393224 | tf_op jit(solution)/shard_map/ppermute | solution.py:17
  474.5 41.8 %collective-permute-start.45 = (bf16[64,1024]{1,0:T(8,128)(2,1)}, bf16[64,1024]{1,0:T(8,128)(2,1)}, u32[]{:S(2)}, u32[]{:S(2)}) collective-permute-start(bf16[64,1024]{1,0:T(8,128)(2,1)} %get-tuple-element.478), channel_id=1, source_target_pairs={{0,3},{1,2},{2,1},{3,0},{4,7},{5,6},{6,5},{7,4},{8,11},{9,10},{10,... | collective-permute-start | bytes 393224 | tf_op jit(solution)/shard_map/ppermute | solution.py:17
  475.8 40.5 %collective-permute-start.44 = (bf16[64,1024]{1,0:T(8,128)(2,1)}, bf16[64,1024]{1,0:T(8,128)(2,1)}, u32[]{:S(2)}, u32[]{:S(2)}) collective-permute-start(bf16[64,1024]{1,0:T(8,128)(2,1)} %get-tuple-element.479), channel_id=1, source_target_pairs={{0,2},{1,3},{2,0},{3,1},{4,6},{5,7},{6,4},{7,5},{8,10},{9,11},{10,... | collective-permute-start | bytes 393224 | tf_op jit(solution)/shard_map/ppermute | solution.py:17
  514.2 42.0 %collective-permute-start.83 = (bf16[2,2,256,256]{2,3,1,0:T(8,128)(2,1)}, bf16[2,2,256,256]{2,3,1,0:T(8,128)(2,1)}, u32[]{:S(2)}, u32[]{:S(2)}) collective-permute-start(bf16[2,2,256,256]{2,3,1,0:T(8,128)(2,1)} %pad_maximum_fusion.43), channel_id=1, source_target_pairs={{0,1},{1,0},{2,3},{3,2},{4,5},{5,4},{6,7},{7,6},{8,9},{9,8},{10,11... | collective-permute-start | bytes 1572872 | tf_op jit(solution)/shard_map/ppermute | solution.py:17
  516.3 42.4 %collective-permute-start.99 = (bf16[2,2,256,256]{2,3,1,0:T(8,128)(2,1)}, bf16[2,2,256,256]{2,3,1,0:T(8,128)(2,1)}, u32[]{:S(2)}, u32[]{:S(2)}) collective-permute-start(bf16[2,2,256,256]{2,3,1,0:T(8,128)(2,1)} %pad_maximum_fusion.46), channel_id=1, source_target_pairs={{0,1},{1,0},{2,3},{3,2},{4,5},{5,4},{6,7},{7,6},{8,9},{9,8},{10,11... | collective-permute-start | bytes 1572872 | tf_op jit(solution)/shard_map/ppermute | solution.py:17
  519.6 24.5 %collective-permute-start.48 = (bf16[64,1024]{1,0:T(8,128)(2,1)S(1)}, bf16[64,1024]{1,0:T(8,128)(2,1)S(1)}, u32[]{:S(2)}, u32[]{:S(2)}) collective-permute-start(bf16[64,1024]{1,0:T(8,128)(2,1)S(1)} %get-tuple-element.49), channel_id=1, source_target_pairs={{0,3},{1,2},{2,1},{3,0},{4,7},{5,6},{6,5},{7,4},{8,11},{9,10},{10,... | collective-permute-start | bytes 393224 | tf_op jit(solution)/shard_map/ppermute | solution.py:17
  521.2 22.9 %collective-permute-start.47 = (bf16[64,1024]{1,0:T(8,128)(2,1)S(1)}, bf16[64,1024]{1,0:T(8,128)(2,1)S(1)}, u32[]{:S(2)}, u32[]{:S(2)}) collective-permute-start(bf16[64,1024]{1,0:T(8,128)(2,1)S(1)} %get-tuple-element.49), channel_id=1, source_target_pairs={{0,2},{1,3},{2,0},{3,1},{4,6},{5,7},{6,4},{7,5},{8,10},{9,11},{10,... | collective-permute-start | bytes 393224 | tf_op jit(solution)/shard_map/ppermute | solution.py:17
  544.1 50.7 %collective-permute-start.74 = (bf16[2,4,256,256]{2,3,1,0:T(8,128)(2,1)}, bf16[2,4,256,256]{2,3,1,0:T(8,128)(2,1)}, u32[]{:S(2)}, u32[]{:S(2)}) collective-permute-start(bf16[2,4,256,256]{2,3,1,0:T(8,128)(2,1)} %pad_maximum_fusion.12), channel_id=1, source_target_pairs={{0,16},{16,0},{1,17},{17,1},{2,18},{18,2},{3,19},{19,3},{4,20},{20... | collective-permute-start | bytes 3145736 | tf_op jit(solution)/shard_map/ppermute | solution.py:17
  544.1 52.8 %collective-permute-start.90 = (bf16[2,4,256,256]{2,3,1,0:T(8,128)(2,1)}, bf16[2,4,256,256]{2,3,1,0:T(8,128)(2,1)}, u32[]{:S(2)}, u32[]{:S(2)}) collective-permute-start(bf16[2,4,256,256]{2,3,1,0:T(8,128)(2,1)} %pad_maximum_fusion.17), channel_id=1, source_target_pairs={{0,16},{16,0},{1,17},{17,1},{2,18},{18,2},{3,19},{19,3},{4,20},{20... | collective-permute-start | bytes 3145736 | tf_op jit(solution)/shard_map/ppermute | solution.py:17
  560.2 28.9 %collective-permute-start.64 = (bf16[4,256,256]{1,2,0:T(8,128)(2,1)S(1)}, bf16[4,256,256]{1,2,0:T(8,128)(2,1)S(1)}, u32[]{:S(2)}, u32[]{:S(2)}) collective-permute-start(bf16[4,256,256]{1,2,0:T(8,128)(2,1)S(1)} %copy-done.52), channel_id=1, source_target_pairs={{0,8},{4,12},{8,0},{12,4},{1,9},{5,13},{9,1},{13,5},{2,10},{6,14},... | collective-permute-start | bytes 1572872 | tf_op jit(solution)/shard_map/ppermute | solution.py:17
  563.8 27.4 %collective-permute-start.66 = (bf16[4,256,256]{1,2,0:T(8,128)(2,1)S(1)}, bf16[4,256,256]{1,2,0:T(8,128)(2,1)S(1)}, u32[]{:S(2)}, u32[]{:S(2)}) collective-permute-start(bf16[4,256,256]{1,2,0:T(8,128)(2,1)S(1)} %copy-done.51), channel_id=1, source_target_pairs={{0,4},{4,0},{8,12},{12,8},{1,5},{5,1},{9,13},{13,9},{2,6},{6,2},{1... | collective-permute-start | bytes 1572872 | tf_op jit(solution)/shard_map/ppermute | solution.py:17
  587.7 33.4 %collective-permute-start.58 = (bf16[2,4,256,256]{2,3,1,0:T(8,128)(2,1)S(1)}, bf16[2,4,256,256]{2,3,1,0:T(8,128)(2,1)S(1)}, u32[]{:S(2)}, u32[]{:S(2)}) collective-permute-start(bf16[2,4,256,256]{2,3,1,0:T(8,128)(2,1)S(1)} %pad_maximum_fusion.7), channel_id=1, source_target_pairs={{0,16},{16,0},{1,17},{17,1},{2,18},{18,2},{3,19},{19,3},{4,20},{20... | collective-permute-start | bytes 3145736 | tf_op jit(solution)/shard_map/ppermute | solution.py:17
  589.1 63.5 %collective-permute-start.84 = (bf16[2,256,256]{1,2,0:T(8,128)(2,1)S(1)}, bf16[2,256,256]{1,2,0:T(8,128)(2,1)S(1)}, u32[]{:S(2)}, u32[]{:S(2)}) collective-permute-start(bf16[2,256,256]{1,2,0:T(8,128)(2,1)S(1)} %fusion.58), channel_id=1, source_target_pairs={{0,2},{1,3},{2,0},{3,1},{4,6},{5,7},{6,4},{7,5},{8,10},{9,11},{10,... | collective-permute-start | bytes 786440 | tf_op jit(solution)/shard_map/ppermute | solution.py:17
  591.2 67.1 %collective-permute-start.100 = (bf16[2,256,256]{1,2,0:T(8,128)(2,1)S(1)}, bf16[2,256,256]{1,2,0:T(8,128)(2,1)S(1)}, u32[]{:S(2)}, u32[]{:S(2)}) collective-permute-start(bf16[2,256,256]{1,2,0:T(8,128)(2,1)S(1)} %fusion.56), channel_id=1, source_target_pairs={{0,2},{1,3},{2,0},{3,1},{4,6},{5,7},{6,4},{7,5},{8,10},{9,11},{10,... | collective-permute-start | bytes 786440 | tf_op jit(solution)/shard_map/ppermute | solution.py:17
  594.8 24.8 %collective-permute-start.67 = (bf16[2,2,256,256]{2,3,1,0:T(8,128)(2,1)S(1)}, bf16[2,2,256,256]{2,3,1,0:T(8,128)(2,1)S(1)}, u32[]{:S(2)}, u32[]{:S(2)}) collective-permute-start(bf16[2,2,256,256]{2,3,1,0:T(8,128)(2,1)S(1)} %pad_maximum_fusion.40), channel_id=1, source_target_pairs={{0,1},{1,0},{2,3},{3,2},{4,5},{5,4},{6,7},{7,6},{8,9},{9,8},{10,11... | collective-permute-start | bytes 1572872 | tf_op jit(solution)/shard_map/ppermute | solution.py:17
  596.9 36.8 %collective-permute-start.77 = (bf16[2,256,256]{1,2,0:T(8,128)(2,1)S(1)}, bf16[2,256,256]{1,2,0:T(8,128)(2,1)S(1)}, u32[]{:S(2)}, u32[]{:S(2)}) collective-permute-start(bf16[2,256,256]{1,2,0:T(8,128)(2,1)S(1)} %pad_maximum_fusion.83), channel_id=1, source_target_pairs={{0,8},{4,12},{8,0},{12,4},{1,9},{5,13},{9,1},{13,5},{2,10},{6,14},... | collective-permute-start | bytes 786440 | tf_op jit(solution)/shard_map/ppermute | solution.py:17
  639.9 22.9 %collective-permute-start.68 = (bf16[2,256,256]{1,2,0:T(8,128)(2,1)S(1)}, bf16[2,256,256]{1,2,0:T(8,128)(2,1)S(1)}, u32[]{:S(2)}, u32[]{:S(2)}) collective-permute-start(bf16[2,256,256]{1,2,0:T(8,128)(2,1)S(1)} %fusion.60), channel_id=1, source_target_pairs={{0,2},{1,3},{2,0},{3,1},{4,6},{5,7},{6,4},{7,5},{8,10},{9,11},{10,... | collective-permute-start | bytes 786440 | tf_op jit(solution)/shard_map/ppermute | solution.py:17
  678.6 28.1 %collective-permute-start.105 = (bf16[2,2,256,256]{2,3,1,0:T(8,128)(2,1)S(1)}, bf16[2,2,256,256]{2,3,1,0:T(8,128)(2,1)S(1)}, u32[]{:S(2)}, u32[]{:S(2)}) collective-permute-start(bf16[2,2,256,256]{2,3,1,0:T(8,128)(2,1)S(1)} %pad_maximum_fusion.48), channel_id=1, source_target_pairs={{0,4},{4,0},{8,12},{12,8},{1,5},{5,1},{9,13},{13,9},{2,6},{6,2},{1... | collective-permute-start | bytes 1572872 | tf_op jit(solution)/shard_map/ppermute | solution.py:17
  683.6 23.3 %collective-permute-start.103 = (bf16[2,2,256,256]{2,3,1,0:T(8,128)(2,1)S(1)}, bf16[2,2,256,256]{2,3,1,0:T(8,128)(2,1)S(1)}, u32[]{:S(2)}, u32[]{:S(2)}) collective-permute-start(bf16[2,2,256,256]{2,3,1,0:T(8,128)(2,1)S(1)} %pad_maximum_fusion.47), channel_id=1, source_target_pairs={{0,8},{4,12},{8,0},{12,4},{1,9},{5,13},{9,1},{13,5},{2,10},{6,14},... | collective-permute-start | bytes 1572872 | tf_op jit(solution)/shard_map/ppermute | solution.py:17
  684.2 41.2 %collective-permute-start.73 = (bf16[2,2,256,256]{2,3,1,0:T(8,128)(2,1)S(1)}, bf16[2,2,256,256]{2,3,1,0:T(8,128)(2,1)}, u32[]{:S(2)}, u32[]{:S(2)}) collective-permute-start(bf16[2,2,256,256]{2,3,1,0:T(8,128)(2,1)S(1)} %pad_maximum_fusion.42), channel_id=1, source_target_pairs={{0,4},{4,0},{8,12},{12,8},{1,5},{5,1},{9,13},{13,9},{2,6},{6,2},{1... | collective-permute-start | bytes 1572872 | tf_op jit(solution)/shard_map/ppermute | solution.py:17
  695.4 33.0 %collective-permute-start.71 = (bf16[2,2,256,256]{2,3,1,0:T(8,128)(2,1)S(1)}, bf16[2,2,256,256]{2,3,1,0:T(8,128)(2,1)}, u32[]{:S(2)}, u32[]{:S(2)}) collective-permute-start(bf16[2,2,256,256]{2,3,1,0:T(8,128)(2,1)S(1)} %pad_maximum_fusion.41), channel_id=1, source_target_pairs={{0,8},{4,12},{8,0},{12,4},{1,9},{5,13},{9,1},{13,5},{2,10},{6,14},... | collective-permute-start | bytes 1572872 | tf_op jit(solution)/shard_map/ppermute | solution.py:17
  (254 other events, 2564.3 us)

commit v2 on v0

v2 whole, which is shorter than its diff:
```python
import functools

import jax
import jax.numpy as jnp
from jax import lax
from jax.experimental import pallas as pl
from jax.experimental.pallas import tpu as pltpu
from jax.sharding import PartitionSpec as P

HEAD_DIM = 64
SCALE = HEAD_DIM ** (-0.5)
QUARTERS = 4
UNIT = 256
epsilon = 1e-06
negative = -1e30
f32 = jnp.float32
low16 = jnp.bfloat16

VM = pl.BlockSpec(memory_space=pltpu.VMEM)
SM = pl.BlockSpec(memory_space=pltpu.SMEM)
ANY = pl.BlockSpec(memory_space=pl.ANY)
MIB = 1 << 20

LOW, SEC, SHARD, LENGTHS = 0, 1, 2, 3


def shape(dims, dtype):
    return jax.ShapeDtypeStruct(tuple(dims), dtype)


def call(body, outs, args, specs, scratch=(), limit=24, flops=0, moved=0, out_specs=None):
    return pl.pallas_call(
        body,
        out_shape=tuple(outs),
        in_specs=list(specs),
        out_specs=tuple(out_specs or [VM] * len(outs)),
        scratch_shapes=list(scratch),
        compiler_params=pltpu.CompilerParams(vmem_limit_bytes=limit * MIB),
        cost_estimate=pl.CostEstimate(flops=flops, bytes_accessed=moved, transcendentals=0),
    )(*args)


def swap(value, axis, flip):
    count = lax.axis_size(axis)
    return lax.ppermute(value, axis, [(i, i ^ flip) for i in range(count)])


def dot(a, b):
    return jnp.dot(a, b, preferred_element_type=f32)


def dot_tn(a, b):
    return lax.dot_general(a, b, (((0,), (0,)), ((), ())), preferred_element_type=f32)


def dot_nt(a, b):
    return lax.dot_general(a, b, (((1,), (1,)), ((), ())), preferred_element_type=f32)


def factor_of(values):
    return lax.rsqrt(jnp.mean(values * values, axis=-1, keepdims=True) + epsilon)


def norm_back(values, gain, upstream):
    factor = factor_of(values)
    weighted = upstream * gain
    inner = jnp.mean(weighted * values, axis=-1, keepdims=True)
    through = factor * weighted - values * (factor * factor * factor) * inner
    return through, jnp.sum(upstream * values * factor, axis=0, keepdims=True)


def normal_cdf(values):
    return 0.5 * (1.0 + lax.erf(values * (0.5**0.5)))


def gelu_slope(values, cdf):
    return cdf + values * (jnp.exp(-0.5 * values * values) * 0.3989422804014327)


def block_at(low, m):
    return pl.multiple_of((low ^ m) * UNIT, UNIT)


def span(m):
    return slice(m * UNIT, (m + 1) * UNIT)


class Copies:
    def __init__(self, sems):
        self.sems = sems
        self.made = []

    def start(self, src, dst):
        copy = pltpu.make_async_copy(src, dst, self.sems.at[len(self.made)])
        copy.start()
        self.made.append(copy)
        return copy

    def pick(self, own_first, sec, own, other, dst):
        sem = self.sems.at[len(self.made)]

        @pl.when((sec == 0) == own_first)
        def _():
            pltpu.make_async_copy(own, dst, sem).start()

        @pl.when((sec == 0) != own_first)
        def _():
            pltpu.make_async_copy(other, dst, sem).start()

        copy = pltpu.make_async_copy(own, dst, sem)
        self.made.append(copy)
        return copy

    def wait(self):
        for copy in self.made:
            copy.wait()


def start_kernel(info, codes, own_gain, other_gain, first, start, gain_g, gain_l):
    low, sec = info[LOW], info[SEC]
    for m in range(QUARTERS):
        at = pl.ds(block_at(low, m), UNIT)
        own, other = own_gain[:, at], other_gain[:, at]
        gain_g[:, span(m)] = jnp.where(sec == 0, own, other)
        gain_l[:, span(m)] = jnp.where(sec == 0, other, own)
        total = codes[sec, 0, :, at].astype(f32)
        for c in range(1, codes.shape[1]):
            total = total + codes[sec, c, :, at].astype(f32)
        start[:, span(m)] = total
    values = start[...]
    first[...] = (values * factor_of(values) * gain_g[0:1, :]).astype(low16)


def piece_kernel(quarters, info, own_qkv, other_qkv, own_out, other_out, own_up, other_up,
                 own_down, other_down, pieces, sems):
    low, sec = info[LOW], info[SEC]
    half = own_qkv.shape[2] // 2
    wide = own_up.shape[1] // 2

    def branch(half_index, qkv, out, up, down):
        made = Copies(sems)
        for place, m in enumerate(quarters):
            at = pl.ds(block_at(low, m), UNIT)
            at_right = pl.ds(pl.multiple_of(block_at(low, m) + half, half), half)
            at_left = pl.ds(block_at(low, m), half)
            lanes = slice(half_index * half, (half_index + 1) * half)
            target = pieces.at[place]
            made.start(qkv.at[0, at, lanes], target.at[0, :, 0:half])
            made.start(qkv.at[1, at, lanes], target.at[0, :, half : 2 * half])
            made.start(qkv.at[2, at, lanes], target.at[1, :, 0:half])
            made.start(out.at[lanes, at_left], target.at[1, 0:half, half : 2 * half])
            made.start(out.at[lanes, at_right], target.at[1, half : 2 * half, half : 2 * half])
            for part in range(2):
                begin = half_index * wide + part * UNIT
                hidden = slice(begin, begin + UNIT)
                made.start(up.at[at, hidden], target.at[2 + part])
                made.start(down.at[hidden, at], target.at[4 + part])
        made.wait()

    @pl.when(sec == 0)
    def _():
        branch(0, other_qkv, other_out, other_up, other_down)

    @pl.when(sec != 0)
    def _():
        branch(1, own_qkv, own_out, own_up, own_down)


def fetch_attention(made, low, sec, own_qkv, other_qkv, own_out, other_out, qkv, out):
    for m in range(QUARTERS):
        at = pl.ds(block_at(low, m), UNIT)
        made.pick(True, sec, own_qkv.at[:, at, :], other_qkv.at[:, at, :], qkv.at[:, span(m), :])
    for m in range(QUARTERS):
        at = pl.ds(block_at(low, m), UNIT)
        made.pick(True, sec, own_out.at[:, at], other_out.at[:, at], out.at[:, span(m)])


def global_attention_kernel(info, rows, own_qkv, other_qkv, own_out, other_out,
                            packed, probs, mixed, partial, qkv, out, sems):
    low, sec = info[LOW], info[SEC]
    made = Copies(sems)
    fetch_attention(made, low, sec, own_qkv, other_qkv, own_out, other_out, qkv, out)
    count = rows.shape[0]
    length = info[LENGTHS + sec]
    query_at = lax.broadcasted_iota(jnp.int32, (count, count), 0)
    key_at = lax.broadcasted_iota(jnp.int32, (count, count), 1)
    allowed = (key_at <= query_at) & (key_at < length)
    made.wait()
    values = rows[...]
    for c in range(3):
        packed[c] = dot(values, qkv[c]).astype(low16)
    heads = []
    for h in range(packed.shape[2] // HEAD_DIM):
        lanes = slice(h * HEAD_DIM, (h + 1) * HEAD_DIM)
        scores = dot_nt(packed[0, :, lanes], packed[1, :, lanes]) * SCALE
        scores = jnp.where(allowed, scores, negative)
        raised = jnp.exp(scores - jnp.max(scores, axis=-1, keepdims=True))
        exact = raised / jnp.sum(raised, axis=-1, keepdims=True)
        probs[h] = exact
        heads.append(dot(exact.astype(low16), packed[2, :, lanes]).astype(low16))
    mixed[...] = jnp.concatenate(heads, axis=1)
    partial[...] = dot(mixed[...], out[...]).astype(low16).reshape(partial.shape)


def total_of(arrived):
    total = arrived[0].astype(f32)
    for k in range(1, arrived.shape[0]):
        total = total + arrived[k].astype(f32)
    return total


def middle_kernel(start, arrived, gain, hidden, second):
    values = start[...] + total_of(arrived)
    hidden[...] = values
    second[...] = (values * factor_of(values) * gain[1:2, :]).astype(low16)


def fetch_feed(made, low, sec, own_up, other_up, own_down, other_down, up, down):
    for m in range(QUARTERS):
        at = pl.ds(block_at(low, m), UNIT)
        made.pick(True, sec, own_up.at[at, :], other_up.at[at, :], up.at[span(m), :])
    for m in range(QUARTERS):
        at = pl.ds(block_at(low, m), UNIT)
        made.pick(True, sec, own_down.at[:, at], other_down.at[:, at], down.at[:, span(m)])


def global_feed_kernel(info, rows, own_up, other_up, own_down, other_down,
                       lifted, active, partial, up, down, total, sems):
    made = Copies(sems)
    fetch_feed(made, info[LOW], info[SEC], own_up, other_up, own_down, other_down, up, down)
    made.wait()
    values = rows[...]
    for t in range(up.shape[1] // UNIT):
        tile = dot(values, up[:, span(t)])
        lifted[:, span(t)] = tile
        low_tile = (tile * normal_cdf(tile)).astype(low16)
        active[:, span(t)] = low_tile
        branch = dot(low_tile, down[span(t), :])
        total[...] = branch if t == 0 else total[...] + branch
    partial[...] = total[...].astype(low16).reshape(partial.shape)


def sent_kernel(hidden, arrived, sent):
    sent[...] = (hidden[...] + total_of(arrived)).astype(low16)


def global_feed_back_kernel(info, top, lifted, own_up, other_up, own_down, other_down,
                            grad_lifted, partial, up, down, total, sems):
    made = Copies(sems)
    fetch_feed(made, info[LOW], info[SEC], own_up, other_up, own_down, other_down, up, down)
    made.wait()
    values = top[...]
    for t in range(up.shape[1] // UNIT):
        tile = lifted[:, span(t)]
        grad = dot_nt(values, down[span(t), :]) * gelu_slope(tile, normal_cdf(tile))
        grad = grad.astype(low16)
        grad_lifted[:, span(t)] = grad
        back = dot_nt(grad, up[:, span(t)])
        total[...] = back if t == 0 else total[...] + back
    partial[...] = total[...].astype(low16).reshape(partial.shape)


def middle_back_kernel(arrived, hidden, gain, returned, grad_hidden, mid, gain_grad):
    through, gain_grad[...] = norm_back(hidden[...], gain[1:2, :], total_of(arrived))
    values = returned[...].astype(f32) + through
    grad_hidden[...] = values
    mid[...] = values.astype(low16)


def global_attention_back_kernel(info, mid, packed, probs, own_qkv, other_qkv, own_out, other_out,
                                 grads, partial, qkv, out, sems):
    low, sec = info[LOW], info[SEC]
    made = Copies(sems)
    fetch_attention(made, low, sec, own_qkv, other_qkv, own_out, other_out, qkv, out)
    made.wait()
    grad_mixed = dot_nt(mid[...], out[...]).astype(low16)
    columns = [[], [], []]
    for h in range(packed.shape[2] // HEAD_DIM):
        lanes = slice(h * HEAD_DIM, (h + 1) * HEAD_DIM)
        exact = probs[h]
        grad = grad_mixed[:, lanes]
        columns[2].append(dot_tn(exact.astype(low16), grad).astype(low16))
        grad_probs = dot_nt(grad, packed[2, :, lanes])
        center = jnp.sum(grad_probs * exact, axis=-1, keepdims=True)
        grad_scores = (exact * (grad_probs - center)).astype(low16)
        columns[0].append((dot(grad_scores, packed[1, :, lanes]) * SCALE).astype(low16))
        columns[1].append((dot_tn(grad_scores, packed[0, :, lanes]) * SCALE).astype(low16))
    total = None
    for c in range(3):
        grads[c] = jnp.concatenate(columns[c], axis=1)
        back = dot_nt(grads[c], qkv[c])
        total = back if c == 0 else total + back
    partial[...] = total.astype(low16).reshape(partial.shape)


def start_back_kernel(info, arrived, start, gain, grad_hidden, kept, given, gain_grad, values):
    low, sec = info[LOW], info[SEC]
    through, gain_grad[...] = norm_back(start[...], gain[0:1, :], total_of(arrived))
    values[...] = grad_hidden[...] + through
    for j in range(2):
        kept[:, span(j)] = values[:, pl.ds(block_at(low, 2 * sec + j), UNIT)]
        given[:, span(j)] = values[:, pl.ds(block_at(low, 2 * (1 - sec) + j), UNIT)]


class LocalWeights:
    def __init__(self, refs):
        self.refs = refs

    def unit(self, k, m, u):
        own, rest = self.refs[0], self.refs[1]
        if k == 0:
            return own.at[0, u] if m == 0 else rest.at[m - 1, u]
        base = self.refs[2 + 5 * (k - 1) : 7 + 5 * (k - 1)]
        if m < 3:
            return base[m].at[0, u]
        return base[3].at[0, u] if u < 3 else base[4].at[0, u - 3]


def pair_rows(a, b, size):
    return jnp.concatenate([a * b, a[size:] * b[: 2 * size], a[2 * size :] * b[:size]], axis=0)


def by_pair(stacked, size):
    names = [(0, 0), (1, 1), (2, 2), (1, 0), (2, 1), (2, 0)]
    return {name: stacked[n * size : (n + 1) * size] for n, name in enumerate(names)}


def from_pairs(pairs):
    names = [(0, 0), (1, 1), (2, 2), (1, 0), (2, 1), (2, 0)]
    return jnp.concatenate([pairs[name] for name in names], axis=0)


def head_sums(products, table):
    upper = products.astype(low16)
    lower = (products - upper.astype(f32)).astype(low16)
    return dot(upper, table) + dot(lower, table)


def head_table(width):
    row = lax.broadcasted_iota(jnp.int32, (width, width), 0) // HEAD_DIM
    column = lax.broadcasted_iota(jnp.int32, (width, width), 1) // HEAD_DIM
    return (row == column).astype(f32).astype(low16)


def gather_mix(weights, mix, k, half):
    for m in range(QUARTERS):
        begin = m * UNIT
        mix[k * half : (k + 1) * half, begin : begin + half] = weights[
            k, 1, begin : begin + half, half:
        ]
        mix[k * half : (k + 1) * half, begin + half : begin + UNIT] = weights[
            k, 1, begin + half : begin + UNIT, half:
        ]


def local_attention_kernel(info, codes, sent_own, sent_other, gain, *rest):
    refs, (start, first, query_keys, values_out, probs, mixed, partial, weights, mix, sems) = (
        rest[:17], rest[17:]
    )
    low, sec = info[LOW], info[SEC]
    local = LocalWeights(refs)
    made = Copies(sems)
    groups = []
    for k in range(4):
        groups.append(
            [
                made.start(local.unit(k, m, u), weights.at[k, u, span(m), :])
                for u in range(2)
                for m in range(QUARTERS)
            ]
        )
    utts, code_count, frames, _ = codes.shape
    for u in range(utts):
        sent = jnp.where(sec == u, sent_own[...], sent_other[...]).astype(f32)
        for c in range(code_count):
            row = (u * code_count + c) * frames
            for m in range(QUARTERS):
                code = codes[u, c, :, pl.ds(block_at(low, m), UNIT)].astype(f32)
                start[row : row + frames, span(m)] = sent[:, span(m)] + code
    values = start[...]
    first[...] = (values * factor_of(values) * gain[0:1, :]).astype(low16)
    half = values_out.shape[2]
    table = head_table(half)
    rows = first[...]
    size = frames
    group = code_count * frames
    for k in range(4):
        for copy in groups[k]:
            copy.wait()
        query_keys[k] = dot(rows, weights[k, 0]).astype(low16)
        values_out[k] = dot(rows, weights[k, 1, :, :half]).astype(low16)
        gather_mix(weights, mix, k, half)
        for u in range(utts):
            at = slice(u * group, (u + 1) * group)
            q = query_keys[k, at, :half].astype(f32)
            key = query_keys[k, at, half:].astype(f32)
            val = values_out[k, at, :].astype(f32)
            scores = by_pair(head_sums(pair_rows(q, key, size), table) * SCALE, size)
            exact = {}
            for i in range(3):
                peak = scores[(i, 0)]
                for j in range(1, i + 1):
                    peak = jnp.maximum(peak, scores[(i, j)])
                raised = [jnp.exp(scores[(i, j)] - peak) for j in range(i + 1)]
                whole = raised[0]
                for j in range(1, i + 1):
                    whole = whole + raised[j]
                for j in range(i + 1):
                    exact[(i, j)] = raised[j] / whole
            probs[k, u] = from_pairs(exact)
            for i in range(3):
                total = None
                for j in range(i + 1):
                    weight = exact[(i, j)].astype(low16).astype(f32)
                    term = weight * val[j * size : (j + 1) * size]
                    total = term if total is None else total + term
                begin = u * group + i * size
                mixed[begin : begin + size, k * half : (k + 1) * half] = total.astype(low16)
    partial[...] = dot(mixed[...], mix[...]).astype(low16)


def local_feed_kernel(info, start, own_part, other_part, gain, cotangent, *rest):
    refs = rest[:17]
    (hidden, second, top, active, grad_lifted, grad_second, branch_out,
     up, down, branch, back, sems) = rest[17:]
    low = info[LOW]
    local = LocalWeights(refs)
    tiles = active.shape[0]
    made = Copies(sems)
    for t in range(tiles):
        for m in range(QUARTERS):
            made.start(local.unit(t // 2, m, 2 + t % 2), up.at[t, span(m), :])
        for m in range(QUARTERS):
            made.start(local.unit(t // 2, m, 4 + t % 2), down.at[t, :, span(m)])
    utts, code_count, frames, _ = cotangent.shape
    frame_at = lax.broadcasted_iota(jnp.int32, (frames, 1), 0) + info[SHARD] * frames
    for u in range(utts):
        valid = frame_at < info[LENGTHS + u]
        for c in range(code_count):
            row = (u * code_count + c) * frames
            for m in range(QUARTERS):
                part = cotangent[u, c, :, pl.ds(block_at(low, m), UNIT)].astype(f32)
                top[row : row + frames, span(m)] = jnp.where(valid, part, 0.0).astype(low16)
    values = start[...] + (own_part[...].astype(f32) + other_part[...].astype(f32))
    hidden[...] = values
    second[...] = (values * factor_of(values) * gain[1:2, :]).astype(low16)
    branch[...] = jnp.zeros_like(branch)
    back[...] = jnp.zeros_like(back)

    @pl.loop(0, tiles)
    def _(t):
        for m in range(QUARTERS):
            pltpu.make_async_copy(
                refs[0].at[0, 0], up.at[t, span(m), :], sems.at[8 * t + m]
            ).wait()
        for m in range(QUARTERS):
            pltpu.make_async_copy(
                refs[0].at[0, 0], down.at[t, :, span(m)], sems.at[8 * t + 4 + m]
            ).wait()
        tile = dot(second[...], up[t])
        cdf = normal_cdf(tile)
        low_tile = (tile * cdf).astype(low16)
        active[t] = low_tile
        branch[...] += dot(low_tile, down[t])
        grad = (dot_nt(top[...], down[t]) * gelu_slope(tile, cdf)).astype(low16)
        grad_lifted[t] = grad
        back[...] += dot_nt(grad, up[t])

    branch_out[...] = branch[...].astype(low16)
    grad_second[...] = back[...].astype(low16)


def local_attention_back_kernel(hidden, own_back, other_back, top, gain, query_keys, values_in,
                                probs, *rest):
    refs = rest[:17]
    (grad_hidden, mid, grad_query_keys, grad_values, grad_first, gain_grad,
     weights, mix, total, sems) = rest[17:]
    local = LocalWeights(refs)
    made = Copies(sems)
    groups = []
    for k in range(4):
        groups.append(
            [
                made.start(local.unit(k, m, u), weights.at[k, u, span(m), :])
                for u in range(2)
                for m in range(QUARTERS)
            ]
        )
    upstream = own_back[...].astype(f32) + other_back[...].astype(f32)
    through, gain_grad[...] = norm_back(hidden[...], gain[1:2, :], upstream)
    grads = top[...].astype(f32) + through
    grad_hidden[...] = grads
    mid[...] = grads.astype(low16)
    utts = probs.shape[1]
    half = values_in.shape[2]
    group = query_keys.shape[1] // utts
    size = group // 3
    table = head_table(half)
    for k in range(4):
        for copy in groups[k]:
            copy.wait()
        gather_mix(weights, mix, k, half)
        grad_mixed = dot_nt(mid[...], mix[k * half : (k + 1) * half, :]).astype(low16)
        grad_mixed = grad_mixed.astype(f32)
        for u in range(utts):
            at = slice(u * group, (u + 1) * group)
            q = query_keys[k, at, :half].astype(f32)
            key = query_keys[k, at, half:].astype(f32)
            val = values_in[k, at, :].astype(f32)
            grad = grad_mixed[at]
            exact = by_pair(probs[k, u], size)
            grad_probs = by_pair(head_sums(pair_rows(grad, val, size), table), size)
            scored = {}
            for i in range(3):
                center = grad_probs[(i, 0)] * exact[(i, 0)]
                for j in range(1, i + 1):
                    center = center + grad_probs[(i, j)] * exact[(i, j)]
                for j in range(i + 1):
                    score = exact[(i, j)] * (grad_probs[(i, j)] - center)
                    scored[(i, j)] = score.astype(low16).astype(f32)

            def rows_of(array, n):
                return array[n * size : (n + 1) * size]

            for i in range(3):
                begin = u * group + i * size
                to_query = sum(scored[(i, j)] * rows_of(key, j) for j in range(i + 1))
                to_key = sum(scored[(n, i)] * rows_of(q, n) for n in range(i, 3))
                to_value = sum(
                    exact[(n, i)].astype(low16).astype(f32) * rows_of(grad, n)
                    for n in range(i, 3)
                )
                grad_query_keys[k, begin : begin + size, :half] = (to_query * SCALE).astype(low16)
                grad_query_keys[k, begin : begin + size, half:] = (to_key * SCALE).astype(low16)
                grad_values[k, begin : begin + size, :] = to_value.astype(low16)
        back = dot_nt(grad_query_keys[k], weights[k, 0])
        back = back + dot_nt(grad_values[k], weights[k, 1, :, :half])
        total[...] = back if k == 0 else total[...] + back
    grad_first[...] = total[...].astype(low16)


def local_end_kernel(info, own_back, other_back, start, grad_hidden, gain,
                     returned, code_part, gain_grad, values):
    low, sec = info[LOW], info[SEC]
    upstream = own_back[...].astype(f32) + other_back[...].astype(f32)
    through, gain_grad[...] = norm_back(start[...], gain[0:1, :], upstream)
    values[...] = grad_hidden[...] + through
    utts, code_count, frames, _ = code_part.shape
    total = None
    for c in range(code_count):
        begin = pl.multiple_of((sec * code_count + c) * frames, frames)
        part = values[pl.ds(begin, frames), :]
        total = part if total is None else total + part
    returned[...] = total.astype(low16)
    for u in range(utts):
        for c in range(code_count):
            row = (u * code_count + c) * frames
            for j in range(2):
                at = pl.ds(block_at(low, 2 * sec + j), UNIT)
                code_part[u, c, :, span(j)] = values[row : row + frames, at]


def output_kernel(info, hidden, own_part, other_part, output):
    low, sec = info[LOW], info[SEC]
    utts, code_count, frames, _ = output.shape
    frame_at = lax.broadcasted_iota(jnp.int32, (frames, 1), 0) + info[SHARD] * frames
    for u in range(utts):
        valid = frame_at < info[LENGTHS + u]
        for c in range(code_count):
            row = (u * code_count + c) * frames
            rows = slice(row, row + frames)
            for j in range(2):
                at = pl.ds(block_at(low, 2 * sec + j), UNIT)
                value = hidden[rows, at] + (
                    own_part[rows, at].astype(f32) + other_part[rows, at].astype(f32)
                )
                output[u, c, :, span(j)] = jnp.where(valid, value, 0.0).astype(low16)


SEND_A, KEEP_A, SEND_B, KEEP_B = (1, 3), (0, 2), (2, 3), (0, 1)


def local_up_kernel(second, grad_lifted, send_a, send_b, keep_a, keep_b, turned):
    turned[...] = jnp.transpose(second[...])
    for k in range(4):
        for part, pairs in enumerate(
            (((send_a, SEND_A), (keep_a, KEEP_A)), ((send_b, SEND_B), (keep_b, KEEP_B)))
        ):
            right = grad_lifted[2 * k + part]
            for target, order in pairs:
                for place, m in enumerate(order):
                    target[place, k] = dot(turned[span(m), :], right).astype(low16)


def local_down_kernel(active, top, send_a, send_b, keep_a, keep_b):
    for k in range(4):
        for part, pairs in enumerate(
            (((send_a, SEND_A), (keep_a, KEEP_A)), ((send_b, SEND_B), (keep_b, KEEP_B)))
        ):
            left = jnp.transpose(active[2 * k + part])
            for target, order in pairs:
                for place, m in enumerate(order):
                    target[place, k] = dot(left, top[:, span(m)]).astype(low16)


def local_mix_kernel(first, grad_query_keys, grad_values, mixed, mid,
                     send_a, send_b, keep_a, keep_b, turned):
    turned[...] = jnp.transpose(first[...])
    half = grad_values.shape[2]
    for k in range(4):
        left = jnp.transpose(mixed[:, k * half : (k + 1) * half])
        for target, order in ((send_a, SEND_A), (keep_a, KEEP_A)):
            for place, m in enumerate(order):
                target[place, k] = dot(turned[span(m), :], grad_query_keys[k]).astype(low16)
        for target, order in ((send_b, SEND_B), (keep_b, KEEP_B)):
            for place, m in enumerate(order):
                value = dot(turned[span(m), :], grad_values[k]).astype(low16)
                out = dot(left, mid[:, span(m)]).astype(low16)
                target[place, k, :, :half] = value
                target[place, k, :half, half:] = out[:, :half]
                target[place, k, half:, half:] = out[:, half:]


def global_feed_grad_kernel(info, second, grad_lifted, active, top, away, kept, turned):
    sec = info[SEC]
    turned[...] = jnp.transpose(second[...])
    wide = active.shape[1] // 2
    for target, half in ((away, 1 - sec), (kept, sec)):
        for part in range(2):
            at = pl.ds(pl.multiple_of(half * wide + part * UNIT, UNIT), UNIT)
            right = grad_lifted[:, at]
            left = jnp.transpose(active[:, at])
            for m in range(QUARTERS):
                target[m, part, 0] = dot(turned[span(m), :], right).astype(low16)
                target[m, part, 1] = dot(left, top[:, span(m)]).astype(low16)


def global_mix_grad_kernel(info, first, grads, mixed, mid, away, kept, turned):
    sec = info[SEC]
    turned[...] = jnp.transpose(first[...])
    width = mixed.shape[1] // 2
    for target, half in ((away, 1 - sec), (kept, sec)):
        at = pl.ds(pl.multiple_of(half * width, width), width)
        left = jnp.transpose(mixed[:, at])
        for m in range(QUARTERS):
            for c in range(2):
                target[m, 0, 0, :, c * width : (c + 1) * width] = dot(
                    turned[span(m), :], grads[c, :, at]
                ).astype(low16)
            target[m, 1, 0, :, :width] = dot(turned[span(m), :], grads[2, :, at]).astype(low16)
            out = dot(left, mid[:, span(m)]).astype(low16)
            target[m, 1, 0, :width, width:] = out[:, :width]
            target[m, 1, 0, width:, width:] = out[:, width:]


def add16(a, b):
    return (a.astype(f32) + b.astype(f32)).astype(low16)


def merge_kernel(kept, arrived, send_a, send_b, keep_a, keep_b):
    for part, pairs in enumerate(
        (((send_a, SEND_A), (keep_a, KEEP_A)), ((send_b, SEND_B), (keep_b, KEEP_B)))
    ):
        for target, order in pairs:
            for place, m in enumerate(order):
                target[place] = add16(kept[m, part], arrived[m, part])


def pick_kernel(info, *refs):
    sec = info[SEC]
    *units, given, kept = refs
    half = len(units) // 2
    place = 0
    for mine, theirs in zip(units[:half], units[half:]):
        for n in range(mine.shape[0]):
            local, world = mine[n], theirs[n]
            given[place] = jnp.where(sec == 0, local, world)
            kept[place] = jnp.where(sec == 0, world, local)
            place += 1


def whole_quarters(refs):
    own, x_part, y_part, far_kept, far_arrived = refs
    count = own.shape[0] // 2

    def unit(m, index):
        if m < 3:
            return (own, x_part, y_part)[m][index]
        return far_kept[index] if index < count else far_arrived[index - count]

    return unit, count


def feed_final_kernel(info, own, x_part, y_part, far_kept, far_arrived, up, down):
    low, sec = info[LOW], info[SEC]
    unit, count = whole_quarters((own, x_part, y_part, far_kept, far_arrived))
    wide = up.shape[1] // 2
    for m in range(QUARTERS):
        at = pl.ds(block_at(low, m), UNIT)
        for source, half in ((0, sec), (count, 1 - sec)):
            for part in range(2):
                hidden = pl.ds(pl.multiple_of(half * wide + part * UNIT, UNIT), UNIT)
                up[at, hidden] = unit(m, source + part).astype(f32)
                down[hidden, at] = unit(m, source + 2 + part).astype(f32)


def mix_final_kernel(info, own, x_part, y_part, far_kept, far_arrived, qkv, out):
    low, sec = info[LOW], info[SEC]
    unit, count = whole_quarters((own, x_part, y_part, far_kept, far_arrived))
    width = out.shape[0] // 2
    for m in range(QUARTERS):
        at = pl.ds(block_at(low, m), UNIT)
        at_left = pl.ds(block_at(low, m), width)
        at_right = pl.ds(pl.multiple_of(block_at(low, m) + width, width), width)
        for source, half in ((0, sec), (count, 1 - sec)):
            lanes = pl.ds(pl.multiple_of(half * width, width), width)
            query_keys = unit(m, source).astype(f32)
            qkv[0, at, lanes] = query_keys[:, :width]
            qkv[1, at, lanes] = query_keys[:, width:]
            rest = unit(m, source + 1).astype(f32)
            qkv[2, at, lanes] = rest[:, :width]
            out[lanes, at_left] = rest[:width, width:]
            out[lanes, at_right] = rest[width:, width:]


def sum_rest(value):
    step = QUARTERS
    while step < lax.axis_size("dp"):
        value = add16(value, swap(value, "dp", step))
        step *= 2
    return value


def reduce_dp(send_a, send_b, keep_a, keep_b):
    from_x = swap(send_a, "dp", 1)
    from_y = swap(send_b, "dp", 2)
    own_a, far_a = add16(keep_a[0], from_x[0]), add16(keep_a[1], from_x[1])
    own_b, far_b = add16(keep_b[0], from_y[0]), add16(keep_b[1], from_y[1])
    from_y = swap(far_a, "dp", 2)
    from_x = swap(far_b, "dp", 1)
    return sum_rest(add16(own_a, from_y)), sum_rest(add16(own_b, from_x))


def reduce_tensor(a, b):
    total = jnp.stack([a[0], b[0]]).astype(f32)
    for k in (1, 2, 3):
        total = total + swap(jnp.stack([a[k], b[k]]), "tensor", k).astype(f32)
    return total.astype(low16)


def gather_dp(units):
    count = units.shape[0] // 2
    x_part = swap(units, "dp", 1)
    y_part = swap(units, "dp", 2)
    far_kept = swap(x_part[:count], "dp", 2)
    far_arrived = swap(y_part[count:], "dp", 1)
    return units, x_part, y_part, far_kept, far_arrived


def on_device(codes, lengths, gains, w_qkv, w_out, w_up, w_down, cotangent):
    sec = lax.axis_index("section")
    low = lax.axis_index("dp") % QUARTERS
    z = lax.axis_index("tensor")
    first_core = sec == 0
    utts, frames, code_count, width = codes.shape
    heads_width = w_out.shape[1]
    half = heads_width // 2
    wide = w_up.shape[2]
    rows_g = 4 * frames
    rows_l = utts * code_count * frames
    tiles = 2 * wide // UNIT
    info = jnp.concatenate([jnp.stack([low, sec, z]).astype(jnp.int32), lengths])

    code_rows = jnp.transpose(codes, (0, 2, 1, 3))
    cot_rows = jnp.transpose(cotangent, (0, 2, 1, 3))
    own_w = (jnp.transpose(w_qkv[0], (1, 0, 2)), w_out[0], w_up[0], w_down[0])

    def sem(count):
        return pltpu.SemaphoreType.DMA((count,))

    other_gain = swap(gains[0], "section", 1)
    other_w = tuple(swap(w, "section", 1) for w in own_w)
    both_w = tuple(w for pair in zip(own_w, other_w) for w in pair)
    attention_w, feed_w = both_w[:4], both_w[4:]

    first_rows, start_g, gain_g, gain_l = call(
        start_kernel,
        [
            shape((frames, width), low16),
            shape((frames, width), f32),
            shape((2, width), f32),
            shape((2, width), f32),
        ],
        (info, code_rows, gains[0], other_gain),
        [SM, VM, VM, VM],
        moved=2 * MIB,
    )

    def pieces(quarters):
        return call(
            functools.partial(piece_kernel, quarters),
            [shape((len(quarters), 6, UNIT, UNIT), low16)],
            (info,) + both_w,
            [SM] + [ANY] * 8,
            [sem(9 * len(quarters))],
            out_specs=[ANY],
            moved=2 * len(quarters) * MIB,
        )[0]

    own_piece = pieces((0,))
    rest_pieces = pieces((1, 2, 3))
    by_z = {1: swap(own_piece, "tensor", 1), 2: swap(own_piece, "tensor", 2)}
    by_z[3] = swap(by_z[2], "tensor", 1)
    local_w = [own_piece, rest_pieces]
    for k in (1, 2, 3):
        x_part = swap(by_z[k], "dp", 1)
        y_part = swap(by_z[k], "dp", 2)
        local_w += [
            by_z[k],
            x_part,
            y_part,
            swap(x_part[:, :3], "dp", 2),
            swap(y_part[:, 3:], "dp", 1),
        ]
    local_w = tuple(local_w)

    def gather(rows):
        return lax.all_gather(rows, "tensor", axis=0, tiled=True)

    def scatter(partial):
        return lax.all_to_all(partial, "tensor", 0, 0)

    first_g = gather(first_rows)
    packed_g, probs_g, mixed_g, partial = call(
        global_attention_kernel,
        [
            shape((3, rows_g, heads_width), low16),
            shape((heads_width // HEAD_DIM, rows_g, rows_g), f32),
            shape((rows_g, heads_width), low16),
            shape((4, frames, width), low16),
        ],
        (info, first_g) + attention_w,
        [SM, VM] + [ANY] * 4,
        [
            pltpu.VMEM((3, width, heads_width), low16),
            pltpu.VMEM((heads_width, width), low16),
            sem(8),
        ],
        flops=2 * 10**9,
        moved=8 * MIB,
    )
    hidden_g, second_rows = call(
        middle_kernel,
        [shape((frames, width), f32), shape((frames, width), low16)],
        (start_g, scatter(partial), gain_g),
        [VM] * 3,
        moved=2 * MIB,
    )
    second_g = gather(second_rows)
    lifted_g, active_g, partial = call(
        global_feed_kernel,
        [
            shape((rows_g, wide), f32),
            shape((rows_g, wide), low16),
            shape((4, frames, width), low16),
        ],
        (info, second_g) + feed_w,
        [SM, VM] + [ANY] * 4,
        [
            pltpu.VMEM((width, wide), low16),
            pltpu.VMEM((wide, width), low16),
            pltpu.VMEM((rows_g, width), f32),
            sem(8),
        ],
        flops=2 * 10**9,
        moved=8 * MIB,
    )
    sent = call(
        sent_kernel,
        [shape((frames, width), low16)],
        (hidden_g, scatter(partial)),
        [VM] * 2,
        moved=MIB,
    )[0]

    start_l, first_l, query_keys, values_l, probs_l, mixed_l, partial = call(
        local_attention_kernel,
        [
            shape((rows_l, width), f32),
            shape((rows_l, width), low16),
            shape((4, rows_l, 2 * half), low16),
            shape((4, rows_l, half), low16),
            shape((4, utts, 2 * rows_l // utts, half), f32),
            shape((rows_l, 4 * half), low16),
            shape((rows_l, width), low16),
        ],
        (info, code_rows, sent, swap(sent, "section", 1), gain_l) + local_w,
        [SM] + [VM] * 4 + [ANY] * 17,
        [
            pltpu.VMEM((4, 2, width, UNIT), low16),
            pltpu.VMEM((4 * half, width), low16),
            sem(32),
        ],
        limit=40,
        flops=4 * 10**9,
        moved=20 * MIB,
    )
    hidden_l, second_l, top_l, active_l, grad_lifted_l, back, branch_l = call(
        local_feed_kernel,
        [
            shape((rows_l, width), f32),
            shape((rows_l, width), low16),
            shape((rows_l, width), low16),
            shape((tiles, rows_l, UNIT), low16),
            shape((tiles, rows_l, UNIT), low16),
            shape((rows_l, width), low16),
            shape((rows_l, width), low16),
        ],
        (info, start_l, partial, swap(partial, "section", 1), gain_l, cot_rows) + local_w,
        [SM] + [VM] * 5 + [ANY] * 17,
        [
            pltpu.VMEM((tiles, width, UNIT), low16),
            pltpu.VMEM((tiles, UNIT, width), low16),
            pltpu.VMEM((rows_l, width), f32),
            pltpu.VMEM((rows_l, width), f32),
            sem(8 * tiles),
        ],
        limit=48,
        flops=10 * 10**9,
        moved=24 * MIB,
    )

    send_shape = shape((2, 4, UNIT, UNIT), low16)
    turned_l = pltpu.VMEM((width, rows_l), low16)
    down_units = call(
        local_down_kernel,
        [send_shape] * 4,
        (active_l, top_l),
        [VM] * 2,
        flops=3 * 10**9,
        moved=8 * MIB,
    )
    up_units = call(
        local_up_kernel,
        [send_shape] * 4,
        (second_l, grad_lifted_l),
        [VM] * 2,
        [turned_l],
        flops=3 * 10**9,
        moved=8 * MIB,
    )
    grad_hidden_l, mid_l, grad_query_keys, grad_values, back, gain2_l = call(
        local_attention_back_kernel,
        [
            shape((rows_l, width), f32),
            shape((rows_l, width), low16),
            shape((4, rows_l, 2 * half), low16),
            shape((4, rows_l, half), low16),
            shape((rows_l, width), low16),
            shape((1, width), f32),
        ],
        (hidden_l, back, swap(back, "section", 1), top_l, gain_l, query_keys, values_l, probs_l)
        + local_w,
        [VM] * 8 + [ANY] * 17,
        [
            pltpu.VMEM((4, 2, width, UNIT), low16),
            pltpu.VMEM((4 * half, width), low16),
            pltpu.VMEM((rows_l, width), f32),
            sem(32),
        ],
        limit=40,
        flops=5 * 10**9,
        moved=20 * MIB,
    )
    mix_units = call(
        local_mix_kernel,
        [send_shape] * 4,
        (first_l, grad_query_keys, grad_values, mixed_l, mid_l),
        [VM] * 5,
        [turned_l],
        flops=3 * 10**9,
        moved=8 * MIB,
    )
    returned, code_part, gain1_l = call(
        local_end_kernel,
        [
            shape((frames, width), low16),
            shape((utts, code_count, frames, width // 2), f32),
            shape((1, width), f32),
        ],
        (info, back, swap(back, "section", 1), start_l, grad_hidden_l, gain_l),
        [SM] + [VM] * 5,
        [pltpu.VMEM((rows_l, width), f32)],
        moved=6 * MIB,
    )
    output = call(
        output_kernel,
        [shape((utts, code_count, frames, width // 2), low16)],
        (info, hidden_l, branch_l, swap(branch_l, "section", 1)),
        [SM] + [VM] * 3,
        moved=4 * MIB,
    )[0]

    top_g = gather(returned)
    grad_lifted_g, partial = call(
        global_feed_back_kernel,
        [shape((rows_g, wide), low16), shape((4, frames, width), low16)],
        (info, top_g, lifted_g) + feed_w,
        [SM, VM, VM] + [ANY] * 4,
        [
            pltpu.VMEM((width, wide), low16),
            pltpu.VMEM((wide, width), low16),
            pltpu.VMEM((rows_g, width), f32),
            sem(8),
        ],
        flops=2 * 10**9,
        moved=8 * MIB,
    )
    grad_hidden_g, mid_rows, gain2_g = call(
        middle_back_kernel,
        [shape((frames, width), f32), shape((frames, width), low16), shape((1, width), f32)],
        (scatter(partial), hidden_g, gain_g, returned),
        [VM] * 4,
        moved=2 * MIB,
    )
    away_feed, kept_feed = call(
        global_feed_grad_kernel,
        [shape((QUARTERS, 2, 2, UNIT, UNIT), low16)] * 2,
        (info, second_g, grad_lifted_g, active_g, top_g),
        [SM] + [VM] * 4,
        [pltpu.VMEM((width, rows_g), low16)],
        flops=4 * 10**9,
        moved=8 * MIB,
    )
    mid_g = gather(mid_rows)
    grads_g, partial = call(
        global_attention_back_kernel,
        [shape((3, rows_g, heads_width), low16), shape((4, frames, width), low16)],
        (info, mid_g, packed_g, probs_g) + attention_w,
        [SM, VM, VM, VM] + [ANY] * 4,
        [
            pltpu.VMEM((3, width, heads_width), low16),
            pltpu.VMEM((heads_width, width), low16),
            sem(8),
        ],
        flops=2 * 10**9,
        moved=8 * MIB,
    )
    away_mix, kept_mix = call(
        global_mix_grad_kernel,
        [shape((QUARTERS, 2, 1, UNIT, UNIT), low16)] * 2,
        (info, first_g, grads_g, mixed_g, mid_g),
        [SM] + [VM] * 4,
        [pltpu.VMEM((width, rows_g), low16)],
        flops=2 * 10**9,
        moved=4 * MIB,
    )
    kept_start, given_start, gain1_g = call(
        start_back_kernel,
        [
            shape((frames, width // 2), f32),
            shape((frames, width // 2), f32),
            shape((1, width), f32),
        ],
        (info, scatter(partial), start_g, gain_g, grad_hidden_g),
        [SM] + [VM] * 4,
        [pltpu.VMEM((frames, width), f32)],
        moved=2 * MIB,
    )
    arrived_start = swap(given_start, "section", 1)
    both_start = jnp.stack(
        [
            jnp.where(first_core, kept_start, arrived_start),
            jnp.where(first_core, arrived_start, kept_start),
        ]
    )
    code_grad = jnp.transpose(code_part + both_start[:, None], (0, 2, 1, 3))

    own_gain = jnp.concatenate([gain1_g, gain2_g], axis=0)
    total_gain = own_gain + swap(own_gain, "section", 1)
    local_gain = jnp.concatenate([gain1_l, gain2_l], axis=0)
    gain_total = jnp.where(first_core, total_gain, local_gain)
    gain_total = jnp.concatenate(
        [
            lax.dynamic_slice_in_dim(gain_total, (low ^ m) * UNIT, UNIT, 1)
            for m in range(QUARTERS)
        ],
        axis=1,
    )
    for axis in ("tensor", "dp"):
        step = 1
        while step < lax.axis_size(axis):
            gain_total = gain_total + swap(gain_total, axis, step)
            step *= 2

    local_down = reduce_tensor(*reduce_dp(*down_units))
    local_up = reduce_tensor(*reduce_dp(*up_units))
    local_mix = reduce_tensor(*reduce_dp(*mix_units))

    def global_sum(away, kept, count):
        units = call(
            merge_kernel,
            [shape((2, count, UNIT, UNIT), low16)] * 4,
            (kept, swap(away, "section", 1)),
            [VM] * 2,
            moved=2 * count * MIB,
        )
        return reduce_dp(*units)

    def finish(local_units, global_units, body, outs):
        count = sum(unit.shape[0] for unit in local_units)
        given, kept = call(
            pick_kernel,
            [shape((count, UNIT, UNIT), low16)] * 2,
            (info,) + tuple(local_units) + tuple(global_units),
            [SM] + [VM] * (len(local_units) + len(global_units)),
            moved=2 * MIB,
        )
        arrived = swap(given, "section", 1)
        return call(
            body,
            outs,
            (info,) + gather_dp(jnp.concatenate([kept, arrived])),
            [SM] + [VM] * 5,
            limit=32,
            moved=16 * MIB,
        )

    feed_a, feed_b = global_sum(away_feed, kept_feed, 2)
    mix_a, mix_b = global_sum(away_mix, kept_mix, 1)
    global_up = jnp.stack([feed_a[0], feed_b[0]])
    global_down = jnp.stack([feed_a[1], feed_b[1]])
    up_grad, down_grad = finish(
        (local_up, local_down),
        (global_up, global_down),
        feed_final_kernel,
        [shape((width, wide), f32), shape((wide, width), f32)],
    )
    qkv_grad, out_grad = finish(
        (local_mix,),
        (jnp.concatenate([mix_a, mix_b]),),
        mix_final_kernel,
        [shape((3, width, heads_width), f32), shape((heads_width, width), f32)],
    )
    return (
        jnp.transpose(output, (0, 2, 1, 3)),
        code_grad,
        gain_total[None],
        jnp.transpose(qkv_grad, (1, 0, 2))[None],
        out_grad[None],
        up_grad[None],
        down_grad[None],
    )


def solution(mesh):
    in_specs = (
        P("dp", "tensor", None, None),
        P("dp"),
        P("section", None, None),
        P("section", None, None, "tensor"),
        P("section", "tensor", None),
        P("section", None, "tensor"),
        P("section", "tensor", None),
        P("dp", "tensor", None, None),
    )
    out_specs = (
        P("dp", "tensor", None, "section"),
        P("dp", "tensor", None, "section"),
        P("section", None, None),
        P("section", None, None, "tensor"),
        P("section", "tensor", None),
        P("section", None, "tensor"),
        P("section", "tensor", None),
    )
    return jax.shard_map(
        on_device, mesh=mesh, in_specs=in_specs, out_specs=out_specs, check_vma=False
    )
```

time: 1980 us -> 541 us (0.27)
  waiting for transfers between devices: 1460 us -> 175 us
  blocking collectives: 216 us -> 105 us
  matrix products: 90.8 us -> 0 us
  Pallas kernels: 0 us -> 85.7 us
  starting transfers between devices: 3.94 us -> 85.5 us
  other arithmetic: 84.3 us -> 28.2 us
  local copies, waits for them, and re-layouts: 80.2 us -> 52.6 us
    reduce_scatter x16 -> x0, waiting for transfers between devices: 555 us -> none  [the longest x1 142 us: on_device(): lax.psum_scatter(full_grads[3].astype(jnp.bfloat16), 'tensor', scatter_di...]
    all_gather x4 -> x0, waiting for transfers between devices: 457 us -> none  [the longest x1 149 us: on_device(): lax.all_gather(w_up, 'tensor', axis=2, tiled=True)]
    psum x1 -> x0, waiting for transfers between devices: 215 us -> none  [on_device(): weight_total = lax.psum(sharded, 'dp')]
    dot_general x46 -> x0, matrix products: 87.8 us -> none  [the longest x2 10.4 us: feed_forward(): branch = jnp.dot(active, w_drop, preferred_element_type=jnp.float32)]
    pallas_call x0 -> x27, Pallas kernels: none -> 85.7 us  [call(): pl.pallas_call(body, out_shape=tuple(outs), in_specs=list(specs), out_spe...]
    ppermute x2 -> x72, waiting for transfers between devices: 234 us -> 165 us  [swap(): return lax.ppermute(value, axis, [(i, i ^ flip) for i in range(count)])]
    all_gather x10 -> x4, blocking collectives: 172 us -> 105 us  [gather(): return lax.all_gather(rows, 'tensor', axis=0, tiled=True)]
    ppermute x2 -> x72, starting transfers between devices: 2.87 us -> 69.9 us  [swap(): return lax.ppermute(value, axis, [(i, i ^ flip) for i in range(count)])]
  transfers between devices with their start and end apart: 23 -> 76, of which waited for: 18 -> 28; matrix products, arithmetic and copies ran while one was open for 6% -> 7% of each run, Pallas kernels for 0% -> 10%
where the time goes in v2:
time: 541 us; the launch traced here: 534 us
  waiting for transfers between devices  175 us (32%)
  blocking collectives  105 us (19%)
  Pallas kernels  85.7 us (16%)
  starting transfers between devices  85.5 us (16%)
  local copies, waits for them, and re-layouts  52.6 us (10%)
  other arithmetic  28.2 us (5%)
    ppermute x72, waiting for transfers between devices, swap(): return lax.ppermute(value, axis, [(i, i ^ flip) for i in range(count)])  165 us
    all_gather x4, blocking collectives, gather(): return lax.all_gather(rows, 'tensor', axis=0, tiled=True)  105 us
    pallas_call x27, Pallas kernels, call(): pl.pallas_call(body, out_shape=tuple(outs), in_specs=list(specs), out_spe...  85.7 us
    ppermute x72, starting transfers between devices, swap(): return lax.ppermute(value, axis, [(i, i ^ flip) for i in range(count)])  69.9 us
    unnamed x242, local copies, waits for them, and re-layouts  42.7 us
    convert_element_type x20, other arithmetic, add16(): return (a.astype(f32) + b.astype(f32)).astype(low16)  17.9 us
    all_to_all x4, starting transfers between devices, scatter(): return lax.all_to_all(partial, 'tensor', 0, 0)  15.6 us
  transfers between devices with their start and end apart: 76, of which 28 were waited for; matrix products, arithmetic and copies ran while one was open for 7% of the time, Pallas kernels for 10%

profile of v2, /device:TPU:0, one launch (start us, length us, event | category | flops | bytes accessed | tf_op | source)
XLA Modules:
  0.0 533.9 jit_solution(6884320323932015341)
XLA Ops:
  2.9 6.0 %collective-permute-done.other_gain = f32[2,1024]{1,0:T(2,128)S(1)} collective-permute-done((f32[2,1024]{1,0:T(2,128)}, f32[2,1024]{1,0:T(2,128)S(1)}, u32[]{:S(2)}, u32[]{:S(2)}) %collective-permute-start) | collective-permute-done | bytes 8224 | tf_op jit(solution)/shard_map/ppermute | solution.py:45
  12.2 2.5 copy-done
  20.4 3.0 collective-permute-start.6
  23.5 2.6 collective-permute-start.11
  26.0 45.3 %all_gather.12.rows.first = bf16[256,1024]{1,0:T(8,128)(2,1)S(1)} all-gather(bf16[64,1024]{1,0:T(8,128)(2,1)S(1)} %get-tuple-element.86), channel_id=1, replica_groups=mesh['section'=2,'dp'=4,'tensor'=4] {'tensor'}, dimensions={0}, use_global_device_ids=true | all-gather | bytes 655360 | tf_op jit(solution)/shard_map/all_gather | solution.py:828
  71.4 2.9 shard_map.136
  77.6 3.6 all-to-all-start
  84.7 6.5 %all-to-all-done.arrived = bf16[4,64,1024]{2,1,0:T(8,128)(2,1)S(1)} async-done(((bf16[4,64,1024]{2,1,0:T(8,128)(2,1)}), bf16[4,64,1024]{2,1,0:T(8,128)(2,1)S(1)}, u32[]{:S(2)}, u32[]{:S(2)}) %all-to-all-start) | async-done | bytes 524320 | tf_op jit(solution)/shard_map/all_to_all | solution.py:831
  94.5 25.6 %all_gather.13.rows.second = bf16[256,1024]{1,0:T(8,128)(2,1)S(1)} all-gather(bf16[64,1024]{1,0:T(8,128)(2,1)S(1)} %get-tuple-element.90), channel_id=1, replica_groups=mesh['section'=2,'dp'=4,'tensor'=4] {'tensor'}, dimensions={0}, use_global_device_ids=true | all-gather | bytes 655360 | tf_op jit(solution)/shard_map/all_gather | solution.py:828
  123.3 2.7 shard_map.138
  128.5 4.2 all-to-all-start.1
  140.0 3.0 all-to-all-done.1.arrived
  145.3 8.3 %collective-permute-done.12.rest_8_ = bf16[1,6,256,256]{3,2,1,0:T(8,128)(2,1)} collective-permute-done((bf16[1,6,256,256]{3,2,1,0:T(8,128)(2,1)}, bf16[1,6,256,256]{3,2,1,0:T(8,128)(2,1)}, u32[]{:S(2)}, u32[]{:S(2)}) %collective-permute-start.12) | collective-permute-done | bytes 786464 | tf_op jit(solution)/shard_map/ppermute | solution.py:45
  158.2 9.3 %collective-permute-done.17.rest_13_ = bf16[1,6,256,256]{3,2,1,0:T(8,128)(2,1)} collective-permute-done((bf16[1,6,256,256]{3,2,1,0:T(8,128)(2,1)}, bf16[1,6,256,256]{3,2,1,0:T(8,128)(2,1)}, u32[]{:S(2)}, u32[]{:S(2)}) %collective-permute-start.17) | collective-permute-done | bytes 786464 | tf_op jit(solution)/shard_map/ppermute | solution.py:45
  174.9 5.4 %collective-permute-done.9.rest_5_ = bf16[1,3,256,256]{3,2,1,0:T(8,128)(2,1)} collective-permute-done((bf16[1,3,256,256]{3,2,1,0:T(8,128)(2,1)}, bf16[1,3,256,256]{3,2,1,0:T(8,128)(2,1)}, u32[]{:S(2)}, u32[]{:S(2)}) %collective-permute-start.9) | collective-permute-done | bytes 393248 | tf_op jit(solution)/shard_map/ppermute | solution.py:45
  187.1 2.5 collective-permute-done.19.rest_15_
  189.6 7.7 %shard_map.142 = (f32[384,1024]{1,0:T(8,128)}, bf16[384,1024]{1,0:T(8,128)(2,1)S(1)}, bf16[4,384,256]{2,1,0:T(8,128)(2,1)S(1)}, bf16[4,384,128]{2,1,0:T(8,128)(2...) custom-call(s32[5]{0:T(128)S(1)} %pad_add_fusion.info, ...), custom_call_target="tpu_custom_call" | custom-call | flops 4000000000 | bytes 20971520 | tf_op jit(solution)/shard_map/pallas_call | solution.py:32
  203.1 17.8 %shard_map.143 = (f32[384,1024]{1,0:T(8,128)}, bf16[384,1024]{1,0:T(8,128)(2,1)S(1)}, bf16[384,1024]{1,0:T(8,128)(2,1)S(1)}, bf16[8,384,256]{2,1,0:T(8,128)(2,1)...) custom-call(s32[5]{0:T(128)S(1)} %pad_add_fusion.info, ...), custom_call_target="tpu_custom_call" | custom-call | flops 10000000000 | bytes 25165824 | tf_op jit(solution)/shard_map/pallas_call | solution.py:32
  222.6 3.2 shard_map.156
  236.8 11.6 %shard_map.145 = (f32[384,1024]{1,0:T(8,128)}, bf16[384,1024]{1,0:T(8,128)(2,1)S(1)}, bf16[4,384,256]{2,1,0:T(8,128)(2,1)S(1)}, bf16[4,384,128]{2,1,0:T(8,128)(2...) custom-call(f32[384,1024]{1,0:T(8,128)} %get-tuple-element.95.hidden, ...), custom_call_target="tpu_custom_call" | custom-call | flops 5000000000 | bytes 20971520 | tf_op jit(solution)/shard_map/pallas_call | solution.py:32
  248.6 3.6 shard_map.151
  252.2 2.9 collective-permute-done.50
  261.5 15.9 %collective-permute-done.57 = bf16[2,4,256,256]{3,2,1,0:T(8,128)(2,1)S(1)} collective-permute-done((bf16[2,4,256,256]{3,2,1,0:T(8,128)(2,1)S(1)}, bf16[2,4,256,256]{3,2,1,0:T(8,128)(2,1)S(1)}, u32[]{:S(2)}, u32[]{:S(2)}) %collective-permute-start.57) | collective-permute-done | bytes 1048608 | tf_op jit(solution)/shard_map/ppermute | solution.py:45
  284.6 16.0 %all_gather.14.top = bf16[256,1024]{1,0:T(8,128)(2,1)S(1)} all-gather(bf16[64,1024]{1,0:T(8,128)(2,1)S(1)} %get-tuple-element.105.returned), channel_id=1, replica_groups=mesh['section'=2,'dp'=4,'tensor'=4] {'tensor'}, dimensions={0}, use_global_device_ids=true | all-gather | bytes 655360 | tf_op jit(solution)/shard_map/all_gather | solution.py:828
  300.6 2.7 shard_map.147
  304.9 4.1 all-to-all-start.2
  309.0 3.8 collective-permute-done.51
  316.6 3.5 collective-permute-start.54
  320.2 2.9 collective-permute-done.58
  323.1 2.5 collective-permute-start.53
  331.5 2.8 shard_map.158
  341.2 15.2 %collective-permute-done.53 = bf16[2,256,256]{2,1,0:T(8,128)(2,1)S(1)} collective-permute-done((bf16[2,256,256]{2,1,0:T(8,128)(2,1)S(1)}, bf16[2,256,256]{2,1,0:T(8,128)(2,1)S(1)}, u32[]{:S(2)}, u32[]{:S(2)}) %collective-permute-start.53) | collective-permute-done | bytes 262176 | tf_op jit(solution)/shard_map/ppermute | solution.py:45
  358.5 18.1 %all_gather.15.mid = bf16[256,1024]{1,0:T(8,128)(2,1)S(1)} all-gather(bf16[64,1024]{1,0:T(8,128)(2,1)S(1)} %get-tuple-element.108), channel_id=1, replica_groups=mesh['section'=2,'dp'=4,'tensor'=4] {'tensor'}, dimensions={0}, use_global_device_ids=true | all-gather | bytes 655360 | tf_op jit(solution)/shard_map/all_gather | solution.py:828
  379.0 3.8 shard_map.149
  384.3 3.8 all-to-all-start.3
  410.7 2.7 collective-permute-done.37
  413.4 15.1 %collective-permute-done.36 = bf16[2,256,256]{2,1,0:T(8,128)(2,1)} collective-permute-done((bf16[2,256,256]{2,1,0:T(8,128)(2,1)}, bf16[2,256,256]{2,1,0:T(8,128)(2,1)}, u32[]{:S(2)}, u32[]{:S(2)}) %collective-permute-start.36) | collective-permute-done | bytes 262176 | tf_op jit(solution)/shard_map/ppermute | solution.py:45
  434.5 8.8 %collective-permute-done.65 = bf16[2,2,256,256]{3,2,1,0:T(8,128)(2,1)S(1)} collective-permute-done((bf16[2,2,256,256]{3,2,1,0:T(8,128)(2,1)S(1)}, bf16[2,2,256,256]{3,2,1,0:T(8,128)(2,1)S(1)}, u32[]{:S(2)}, u32[]{:S(2)}) %collective-permute-start.65) | collective-permute-done | bytes 524320 | tf_op jit(solution)/shard_map/ppermute | solution.py:45
  444.4 3.4 collective-permute-done.41
  450.0 9.2 %collective-permute-done.66 = bf16[2,256,256]{2,1,0:T(8,128)(2,1)S(1)} collective-permute-done((bf16[2,256,256]{2,1,0:T(8,128)(2,1)S(1)}, bf16[2,256,256]{2,1,0:T(8,128)(2,1)S(1)}, u32[]{:S(2)}, u32[]{:S(2)}) %collective-permute-start.66) | collective-permute-done | bytes 262176 | tf_op jit(solution)/shard_map/ppermute | solution.py:45
  460.1 5.5 %collective-permute-done.64 = bf16[2,256,256]{2,1,0:T(8,128)(2,1)S(1)} collective-permute-done((bf16[2,256,256]{2,1,0:T(8,128)(2,1)S(1)}, bf16[2,256,256]{2,1,0:T(8,128)(2,1)S(1)}, u32[]{:S(2)}, u32[]{:S(2)}) %collective-permute-start.64) | collective-permute-done | bytes 262176 | tf_op jit(solution)/shard_map/ppermute | solution.py:45
  469.9 3.0 collective-permute-done.40
  473.7 4.5 collective-permute-done.28
  480.8 13.0 %collective-permute-done.29 = f32[2,1024]{1,0:T(2,128)S(1)} collective-permute-done((f32[2,1024]{1,0:T(2,128)S(1)}, f32[2,1024]{1,0:T(2,128)S(1)}, u32[]{:S(2)}, u32[]{:S(2)}) %collective-permute-start.29) | collective-permute-done | bytes 8224 | tf_op jit(solution)/shard_map/ppermute | solution.py:45
  501.4 8.1 %collective-permute-done.44.x_part = bf16[4,256,256]{2,1,0:T(8,128)(2,1)S(1)} collective-permute-done((bf16[4,256,256]{2,1,0:T(8,128)(2,1)S(1)}, bf16[4,256,256]{2,1,0:T(8,128)(2,1)S(1)}, u32[]{:S(2)}, u32[]{:S(2)}) %collective-permute-start.44) | collective-permute-done | bytes 524320 | tf_op jit(solution)/shard_map/ppermute | solution.py:45
  514.5 11.8 %collective-permute-done.46.far_kept = bf16[2,256,256]{2,1,0:T(8,128)(2,1)S(1)} collective-permute-done((bf16[2,256,256]{2,1,0:T(8,128)(2,1)S(1)}, bf16[2,256,256]{2,1,0:T(8,128)(2,1)S(1)}, u32[]{:S(2)}, u32[]{:S(2)}) %collective-permute-start.46) | collective-permute-done | bytes 262176 | tf_op jit(solution)/shard_map/ppermute | solution.py:45
  526.3 2.9 shard_map.155
  529.2 4.5 shard_map.161
  (443 shorter events, 163.9 us)
Async XLA Ops:
  20.4 62.7 %collective-permute-start.6 = (bf16[1,6,256,256]{3,2,1,0:T(8,128)(2,1)S(1)}, bf16[1,6,256,256]{3,2,1,0:T(8,128)(2,1)}, u32[]{:S(2)}, u32[]{:S(2)}) collective-permute-start(bf16[1,6,256,256]{3,2,1,0:T(8,128)(2,1)S(1)} %shard_map.140.rest_0_), channel_id=1, source_target_pairs={{0,1},{1,0},{2,3},{3,2},{4,5},{5,4},{6,7},{7,6},{8,9},{9,8},{10,11... | collective-permute-start | bytes 2359304 | tf_op jit(solution)/shard_map/ppermute | solution.py:45
  23.5 57.7 %collective-permute-start.11 = (bf16[1,6,256,256]{3,2,1,0:T(8,128)(2,1)S(1)}, bf16[1,6,256,256]{3,2,1,0:T(8,128)(2,1)}, u32[]{:S(2)}, u32[]{:S(2)}) collective-permute-start(bf16[1,6,256,256]{3,2,1,0:T(8,128)(2,1)S(1)} %shard_map.140.rest_0_), channel_id=1, source_target_pairs={{0,2},{1,3},{2,0},{3,1},{4,6},{5,7},{6,4},{7,5},{8,10},{9,11},{10,... | collective-permute-start | bytes 2359304 | tf_op jit(solution)/shard_map/ppermute | solution.py:45
  81.2 54.6 %collective-permute-start.16 = (bf16[1,6,256,256]{3,2,1,0:T(8,128)(2,1)}, bf16[1,6,256,256]{3,2,1,0:T(8,128)(2,1)}, u32[]{:S(2)}, u32[]{:S(2)}) collective-permute-start(bf16[1,6,256,256]{3,2,1,0:T(8,128)(2,1)} %collective-permute-done.11.rest_7_), channel_id=1, source_target_pairs={{0,1},{1,0},{2,3},{3,2},{4,5},{5,4},{6,7},{7,6},{8,9},{9,8},{10,11... | collective-permute-start | bytes 2359304 | tf_op jit(solution)/shard_map/ppermute | solution.py:45
  83.2 53.0 %collective-permute-start.7 = (bf16[1,6,256,256]{3,2,1,0:T(8,128)(2,1)}, bf16[1,6,256,256]{3,2,1,0:T(8,128)(2,1)}, u32[]{:S(2)}, u32[]{:S(2)}) collective-permute-start(bf16[1,6,256,256]{3,2,1,0:T(8,128)(2,1)} %collective-permute-done.6.rest_2_), channel_id=1, source_target_pairs={{0,4},{4,0},{8,12},{12,8},{1,5},{5,1},{9,13},{13,9},{2,6},{6,2},{1... | collective-permute-start | bytes 2359304 | tf_op jit(solution)/shard_map/ppermute | solution.py:45
  93.0 45.6 %collective-permute-start.8 = (bf16[1,6,256,256]{3,2,1,0:T(8,128)(2,1)}, bf16[1,6,256,256]{3,2,1,0:T(8,128)(2,1)}, u32[]{:S(2)}, u32[]{:S(2)}) collective-permute-start(bf16[1,6,256,256]{3,2,1,0:T(8,128)(2,1)} %collective-permute-done.6.rest_2_), channel_id=1, source_target_pairs={{0,8},{4,12},{8,0},{12,4},{1,9},{5,13},{9,1},{13,5},{2,10},{6,14},... | collective-permute-start | bytes 2359304 | tf_op jit(solution)/shard_map/ppermute | solution.py:45
  132.7 20.9 %collective-permute-start.12 = (bf16[1,6,256,256]{3,2,1,0:T(8,128)(2,1)}, bf16[1,6,256,256]{3,2,1,0:T(8,128)(2,1)}, u32[]{:S(2)}, u32[]{:S(2)}) collective-permute-start(bf16[1,6,256,256]{3,2,1,0:T(8,128)(2,1)} %collective-permute-done.11.rest_7_), channel_id=1, source_target_pairs={{0,4},{4,0},{8,12},{12,8},{1,5},{5,1},{9,13},{13,9},{2,6},{6,2},{1... | collective-permute-start | bytes 2359304 | tf_op jit(solution)/shard_map/ppermute | solution.py:45
  134.2 21.4 %collective-permute-start.13 = (bf16[1,6,256,256]{3,2,1,0:T(8,128)(2,1)}, bf16[1,6,256,256]{3,2,1,0:T(8,128)(2,1)}, u32[]{:S(2)}, u32[]{:S(2)}) collective-permute-start(bf16[1,6,256,256]{3,2,1,0:T(8,128)(2,1)} %collective-permute-done.11.rest_7_), channel_id=1, source_target_pairs={{0,8},{4,12},{8,0},{12,4},{1,9},{5,13},{9,1},{13,5},{2,10},{6,14},... | collective-permute-start | bytes 2359304 | tf_op jit(solution)/shard_map/ppermute | solution.py:45
  135.8 31.8 %collective-permute-start.17 = (bf16[1,6,256,256]{3,2,1,0:T(8,128)(2,1)}, bf16[1,6,256,256]{3,2,1,0:T(8,128)(2,1)}, u32[]{:S(2)}, u32[]{:S(2)}) collective-permute-start(bf16[1,6,256,256]{3,2,1,0:T(8,128)(2,1)} %collective-permute-done.16.rest_12_), channel_id=1, source_target_pairs={{0,4},{4,0},{8,12},{12,8},{1,5},{5,1},{9,13},{13,9},{2,6},{6,2},{1... | collective-permute-start | bytes 2359304 | tf_op jit(solution)/shard_map/ppermute | solution.py:45
  136.2 35.7 %collective-permute-start.18 = (bf16[1,6,256,256]{3,2,1,0:T(8,128)(2,1)}, bf16[1,6,256,256]{3,2,1,0:T(8,128)(2,1)}, u32[]{:S(2)}, u32[]{:S(2)}) collective-permute-start(bf16[1,6,256,256]{3,2,1,0:T(8,128)(2,1)} %collective-permute-done.16.rest_12_), channel_id=1, source_target_pairs={{0,8},{4,12},{8,0},{12,4},{1,9},{5,13},{9,1},{13,5},{2,10},{6,14},... | collective-permute-start | bytes 2359304 | tf_op jit(solution)/shard_map/ppermute | solution.py:45
  138.6 41.7 %collective-permute-start.9 = (bf16[1,3,256,256]{3,2,1,0:T(8,128)(2,1)}, bf16[1,3,256,256]{3,2,1,0:T(8,128)(2,1)}, u32[]{:S(2)}, u32[]{:S(2)}) collective-permute-start(bf16[1,3,256,256]{3,2,1,0:T(8,128)(2,1)} %slice.312), channel_id=1, source_target_pairs={{0,8},{4,12},{8,0},{12,4},{1,9},{5,13},{9,1},{13,5},{2,10},{6,14},... | collective-permute-start | bytes 1179656 | tf_op jit(solution)/shard_map/ppermute | solution.py:45
  153.6 19.9 %collective-permute-start.5 = (bf16[64,1024]{1,0:T(8,128)(2,1)S(1)}, bf16[64,1024]{1,0:T(8,128)(2,1)S(1)}, u32[]{:S(2)}, u32[]{:S(2)}) collective-permute-start(bf16[64,1024]{1,0:T(8,128)(2,1)S(1)} %shard_map.139.sent_own), channel_id=1, source_target_pairs={{0,16},{16,0},{1,17},{17,1},{2,18},{18,2},{3,19},{19,3},{4,20},{20... | collective-permute-start | bytes 393224 | tf_op jit(solution)/shard_map/ppermute | solution.py:45
  155.6 31.5 %collective-permute-start.10 = (bf16[1,3,256,256]{3,2,1,0:T(8,128)(2,1)S(1)}, bf16[1,3,256,256]{3,2,1,0:T(8,128)(2,1)S(1)}, u32[]{:S(2)}, u32[]{:S(2)}) collective-permute-start(bf16[1,3,256,256]{3,2,1,0:T(8,128)(2,1)S(1)} %slice.313), channel_id=1, source_target_pairs={{0,4},{4,0},{8,12},{12,8},{1,5},{5,1},{9,13},{13,9},{2,6},{6,2},{1... | collective-permute-start | bytes 1179656 | tf_op jit(solution)/shard_map/ppermute | solution.py:45
  167.5 19.6 %collective-permute-start.14 = (bf16[1,3,256,256]{3,2,1,0:T(8,128)(2,1)S(1)}, bf16[1,3,256,256]{3,2,1,0:T(8,128)(2,1)S(1)}, u32[]{:S(2)}, u32[]{:S(2)}) collective-permute-start(bf16[1,3,256,256]{3,2,1,0:T(8,128)(2,1)S(1)} %slice.314), channel_id=1, source_target_pairs={{0,8},{4,12},{8,0},{12,4},{1,9},{5,13},{9,1},{13,5},{2,10},{6,14},... | collective-permute-start | bytes 1179656 | tf_op jit(solution)/shard_map/ppermute | solution.py:45
  228.8 26.3 %collective-permute-start.50 = (bf16[2,4,256,256]{3,2,1,0:T(8,128)(2,1)}, bf16[2,4,256,256]{3,2,1,0:T(8,128)(2,1)}, u32[]{:S(2)}, u32[]{:S(2)}) collective-permute-start(bf16[2,4,256,256]{3,2,1,0:T(8,128)(2,1)} %get-tuple-element.145), channel_id=1, source_target_pairs={{0,8},{4,12},{8,0},{12,4},{1,9},{5,13},{9,1},{13,5},{2,10},{6,14},... | collective-permute-start | bytes 3145736 | tf_op jit(solution)/shard_map/ppermute | solution.py:45
  230.3 28.3 %collective-permute-start.48 = (bf16[2,4,256,256]{3,2,1,0:T(8,128)(2,1)}, bf16[2,4,256,256]{3,2,1,0:T(8,128)(2,1)}, u32[]{:S(2)}, u32[]{:S(2)}) collective-permute-start(bf16[2,4,256,256]{3,2,1,0:T(8,128)(2,1)} %copy-done.90), channel_id=1, source_target_pairs={{0,4},{4,0},{8,12},{12,8},{1,5},{5,1},{9,13},{13,9},{2,6},{6,2},{1... | collective-permute-start | bytes 3145736 | tf_op jit(solution)/shard_map/ppermute | solution.py:45
  235.0 42.5 %collective-permute-start.57 = (bf16[2,4,256,256]{3,2,1,0:T(8,128)(2,1)S(1)}, bf16[2,4,256,256]{3,2,1,0:T(8,128)(2,1)S(1)}, u32[]{:S(2)}, u32[]{:S(2)}) collective-permute-start(bf16[2,4,256,256]{3,2,1,0:T(8,128)(2,1)S(1)} %get-tuple-element.150), channel_id=1, source_target_pairs={{0,8},{4,12},{8,0},{12,4},{1,9},{5,13},{9,1},{13,5},{2,10},{6,14},... | collective-permute-start | bytes 3145736 | tf_op jit(solution)/shard_map/ppermute | solution.py:45
  235.4 43.7 %collective-permute-start.55 = (bf16[2,4,256,256]{3,2,1,0:T(8,128)(2,1)S(1)}, bf16[2,4,256,256]{3,2,1,0:T(8,128)(2,1)S(1)}, u32[]{:S(2)}, u32[]{:S(2)}) collective-permute-start(bf16[2,4,256,256]{3,2,1,0:T(8,128)(2,1)S(1)} %get-tuple-element.148), channel_id=1, source_target_pairs={{0,4},{4,0},{8,12},{12,8},{1,5},{5,1},{9,13},{13,9},{2,6},{6,2},{1... | collective-permute-start | bytes 3145736 | tf_op jit(solution)/shard_map/ppermute | solution.py:45
  248.5 33.3 %collective-permute-start.24 = (bf16[384,1024]{1,0:T(8,128)(2,1)S(1)}, bf16[384,1024]{1,0:T(8,128)(2,1)S(1)}, u32[]{:S(2)}, u32[]{:S(2)}) collective-permute-start(bf16[384,1024]{1,0:T(8,128)(2,1)S(1)} %get-tuple-element.102.own_back), channel_id=1, source_target_pairs={{0,16},{16,0},{1,17},{17,1},{2,18},{18,2},{3,19},{19,3},{4,20},{20... | collective-permute-start | bytes 2359304 | tf_op jit(solution)/shard_map/ppermute | solution.py:45
  255.1 79.9 %collective-permute-start.33 = (bf16[2,4,256,256]{3,2,1,0:T(8,128)(2,1)}, bf16[2,4,256,256]{3,2,1,0:T(8,128)(2,1)}, u32[]{:S(2)}, u32[]{:S(2)}) collective-permute-start(bf16[2,4,256,256]{3,2,1,0:T(8,128)(2,1)} %get-tuple-element.127), channel_id=1, source_target_pairs={{0,8},{4,12},{8,0},{12,4},{1,9},{5,13},{9,1},{13,5},{2,10},{6,14},... | collective-permute-start | bytes 3145736 | tf_op jit(solution)/shard_map/ppermute | solution.py:45
  258.6 79.1 %collective-permute-start.31 = (bf16[2,4,256,256]{3,2,1,0:T(8,128)(2,1)}, bf16[2,4,256,256]{3,2,1,0:T(8,128)(2,1)}, u32[]{:S(2)}, u32[]{:S(2)}) collective-permute-start(bf16[2,4,256,256]{3,2,1,0:T(8,128)(2,1)} %get-tuple-element.125), channel_id=1, source_target_pairs={{0,4},{4,0},{8,12},{12,8},{1,5},{5,1},{9,13},{13,9},{2,6},{6,2},{1... | collective-permute-start | bytes 3145736 | tf_op jit(solution)/shard_map/ppermute | solution.py:45
  277.4 35.4 %collective-permute-start.51 = (bf16[4,256,256]{2,1,0:T(8,128)(2,1)}, bf16[4,256,256]{2,1,0:T(8,128)(2,1)}, u32[]{:S(2)}, u32[]{:S(2)}) collective-permute-start(bf16[4,256,256]{2,1,0:T(8,128)(2,1)} %fusion.13), channel_id=1, source_target_pairs={{0,4},{4,0},{8,12},{12,8},{1,5},{5,1},{9,13},{13,9},{2,6},{6,2},{1... | collective-permute-start | bytes 1572872 | tf_op jit(solution)/shard_map/ppermute | solution.py:45
  279.1 35.9 %collective-permute-start.49 = (bf16[4,256,256]{2,1,0:T(8,128)(2,1)}, bf16[4,256,256]{2,1,0:T(8,128)(2,1)}, u32[]{:S(2)}, u32[]{:S(2)}) collective-permute-start(bf16[4,256,256]{2,1,0:T(8,128)(2,1)} %fusion.11), channel_id=1, source_target_pairs={{0,8},{4,12},{8,0},{12,4},{1,9},{5,13},{9,1},{13,5},{2,10},{6,14},... | collective-permute-start | bytes 1572872 | tf_op jit(solution)/shard_map/ppermute | solution.py:45
  281.8 41.3 %collective-permute-start.58 = (bf16[4,256,256]{2,1,0:T(8,128)(2,1)}, bf16[4,256,256]{2,1,0:T(8,128)(2,1)}, u32[]{:S(2)}, u32[]{:S(2)}) collective-permute-start(bf16[4,256,256]{2,1,0:T(8,128)(2,1)} %fusion.17), channel_id=1, source_target_pairs={{0,4},{4,0},{8,12},{12,8},{1,5},{5,1},{9,13},{13,9},{2,6},{6,2},{1... | collective-permute-start | bytes 1572872 | tf_op jit(solution)/shard_map/ppermute | solution.py:45
  304.9 53.3 %all-to-all-start.2 = ((bf16[4,64,1024]{2,1,0:T(8,128)(2,1)}), bf16[4,64,1024]{2,1,0:T(8,128)(2,1)S(1)}, u32[]{:S(2)}, u32[]{:S(2)}) async-start(bf16[4,64,1024]{2,1,0:T(8,128)(2,1)} %copy-done.67), calls=%async_computation.2 | async-start | bytes 1048576 | tf_op jit(solution)/shard_map/all_to_all | solution.py:831
  316.6 24.6 %collective-permute-start.54 = (bf16[2,256,256]{2,1,0:T(8,128)(2,1)S(1)}, bf16[2,256,256]{2,1,0:T(8,128)(2,1)S(1)}, u32[]{:S(2)}, u32[]{:S(2)}) collective-permute-start(bf16[2,256,256]{2,1,0:T(8,128)(2,1)S(1)} %pad_maximum_fusion.7), channel_id=1, source_target_pairs={{0,3},{1,2},{2,1},{3,0},{4,7},{5,6},{6,5},{7,4},{8,11},{9,10},{10,... | collective-permute-start | bytes 786440 | tf_op jit(solution)/shard_map/ppermute | solution.py:45
  323.1 33.3 %collective-permute-start.53 = (bf16[2,256,256]{2,1,0:T(8,128)(2,1)S(1)}, bf16[2,256,256]{2,1,0:T(8,128)(2,1)S(1)}, u32[]{:S(2)}, u32[]{:S(2)}) collective-permute-start(bf16[2,256,256]{2,1,0:T(8,128)(2,1)S(1)} %pad_maximum_fusion.6), channel_id=1, source_target_pairs={{0,2},{1,3},{2,0},{3,1},{4,6},{5,7},{6,4},{7,5},{8,10},{9,11},{10,... | collective-permute-start | bytes 786440 | tf_op jit(solution)/shard_map/ppermute | solution.py:45
  326.9 30.4 %collective-permute-start.52 = (bf16[2,256,256]{2,1,0:T(8,128)(2,1)S(1)}, bf16[2,256,256]{2,1,0:T(8,128)(2,1)S(1)}, u32[]{:S(2)}, u32[]{:S(2)}) collective-permute-start(bf16[2,256,256]{2,1,0:T(8,128)(2,1)S(1)} %pad_maximum_fusion.5), channel_id=1, source_target_pairs={{0,1},{1,0},{2,3},{3,2},{4,5},{5,4},{6,7},{7,6},{8,9},{9,8},{10,11... | collective-permute-start | bytes 786440 | tf_op jit(solution)/shard_map/ppermute | solution.py:45
  335.0 67.0 %collective-permute-start.61 = (bf16[2,256,256]{2,1,0:T(8,128)(2,1)}, bf16[2,256,256]{2,1,0:T(8,128)(2,1)}, u32[]{:S(2)}, u32[]{:S(2)}) collective-permute-start(bf16[2,256,256]{2,1,0:T(8,128)(2,1)} %pad_maximum_fusion.10), channel_id=1, source_target_pairs={{0,3},{1,2},{2,1},{3,0},{4,7},{5,6},{6,5},{7,4},{8,11},{9,10},{10,... | collective-permute-start | bytes 786440 | tf_op jit(solution)/shard_map/ppermute | solution.py:45
  337.7 66.7 %collective-permute-start.60 = (bf16[2,256,256]{2,1,0:T(8,128)(2,1)}, bf16[2,256,256]{2,1,0:T(8,128)(2,1)}, u32[]{:S(2)}, u32[]{:S(2)}) collective-permute-start(bf16[2,256,256]{2,1,0:T(8,128)(2,1)} %pad_maximum_fusion.9), channel_id=1, source_target_pairs={{0,2},{1,3},{2,0},{3,1},{4,6},{5,7},{6,4},{7,5},{8,10},{9,11},{10,... | collective-permute-start | bytes 786440 | tf_op jit(solution)/shard_map/ppermute | solution.py:45
  341.2 67.2 %collective-permute-start.62 = (bf16[4,2,2,256,256]{4,3,2,1,0:T(8,128)(2,1)}, bf16[4,2,2,256,256]{4,3,2,1,0:T(8,128)(2,1)}, u32[]{:S(2)}, u32[]{:S(2)}) collective-permute-start(bf16[4,2,2,256,256]{4,3,2,1,0:T(8,128)(2,1)} %get-tuple-element.154), channel_id=1, source_target_pairs={{0,16},{16,0},{1,17},{17,1},{2,18},{18,2},{3,19},{19,3},{4,20},{20... | collective-permute-start | bytes 6291464 | tf_op jit(solution)/shard_map/ppermute | solution.py:45
  356.4 37.0 %collective-permute-start.34 = (bf16[4,256,256]{2,1,0:T(8,128)(2,1)}, bf16[4,256,256]{2,1,0:T(8,128)(2,1)}, u32[]{:S(2)}, u32[]{:S(2)}) collective-permute-start(bf16[4,256,256]{2,1,0:T(8,128)(2,1)} %fusion.9), channel_id=1, source_target_pairs={{0,4},{4,0},{8,12},{12,8},{1,5},{5,1},{9,13},{13,9},{2,6},{6,2},{1... | collective-permute-start | bytes 1572872 | tf_op jit(solution)/shard_map/ppermute | solution.py:45
  357.3 40.3 %collective-permute-start.32 = (bf16[4,256,256]{2,1,0:T(8,128)(2,1)}, bf16[4,256,256]{2,1,0:T(8,128)(2,1)}, u32[]{:S(2)}, u32[]{:S(2)}) collective-permute-start(bf16[4,256,256]{2,1,0:T(8,128)(2,1)} %fusion.7), channel_id=1, source_target_pairs={{0,8},{4,12},{8,0},{12,4},{1,9},{5,13},{9,1},{13,5},{2,10},{6,14},... | collective-permute-start | bytes 1572872 | tf_op jit(solution)/shard_map/ppermute | solution.py:45
  384.3 23.2 %all-to-all-start.3 = ((bf16[4,64,1024]{2,1,0:T(8,128)(2,1)}), bf16[4,64,1024]{2,1,0:T(8,128)(2,1)S(1)}, u32[]{:S(2)}, u32[]{:S(2)}) async-start(bf16[4,64,1024]{2,1,0:T(8,128)(2,1)} %copy-done.68), calls=%async_computation.3 | async-start | bytes 1048576 | tf_op jit(solution)/shard_map/all_to_all | solution.py:831
  397.6 33.0 %collective-permute-start.38 = (bf16[4,2,1,256,256]{4,3,2,1,0:T(8,128)(2,1)}, bf16[4,2,1,256,256]{4,3,2,1,0:T(8,128)(2,1)}, u32[]{:S(2)}, u32[]{:S(2)}) collective-permute-start(bf16[4,2,1,256,256]{4,3,2,1,0:T(8,128)(2,1)} %get-tuple-element.131), channel_id=1, source_target_pairs={{0,16},{16,0},{1,17},{17,1},{2,18},{18,2},{3,19},{19,3},{4,20},{20... | collective-permute-start | bytes 3145736 | tf_op jit(solution)/shard_map/ppermute | solution.py:45
  404.4 24.0 %collective-permute-start.36 = (bf16[2,256,256]{2,1,0:T(8,128)(2,1)}, bf16[2,256,256]{2,1,0:T(8,128)(2,1)}, u32[]{:S(2)}, u32[]{:S(2)}) collective-permute-start(bf16[2,256,256]{2,1,0:T(8,128)(2,1)} %pad_maximum_fusion.2), channel_id=1, source_target_pairs={{0,2},{1,3},{2,0},{3,1},{4,6},{5,7},{6,4},{7,5},{8,10},{9,11},{10,... | collective-permute-start | bytes 786440 | tf_op jit(solution)/shard_map/ppermute | solution.py:45
  404.5 24.8 %collective-permute-start.35 = (bf16[2,256,256]{2,1,0:T(8,128)(2,1)}, bf16[2,256,256]{2,1,0:T(8,128)(2,1)}, u32[]{:S(2)}, u32[]{:S(2)}) collective-permute-start(bf16[2,256,256]{2,1,0:T(8,128)(2,1)} %pad_maximum_fusion.1), channel_id=1, source_target_pairs={{0,1},{1,0},{2,3},{3,2},{4,5},{5,4},{6,7},{7,6},{8,9},{9,8},{10,11... | collective-permute-start | bytes 786440 | tf_op jit(solution)/shard_map/ppermute | solution.py:45
  408.4 70.9 %collective-permute-start.22 = (bf16[384,1024]{1,0:T(8,128)(2,1)}, bf16[384,1024]{1,0:T(8,128)(2,1)S(1)}, u32[]{:S(2)}, u32[]{:S(2)}) collective-permute-start(bf16[384,1024]{1,0:T(8,128)(2,1)} %copy-done.61), channel_id=1, source_target_pairs={{0,16},{16,0},{1,17},{17,1},{2,18},{18,2},{3,19},{19,3},{4,20},{20... | collective-permute-start | bytes 2359304 | tf_op jit(solution)/shard_map/ppermute | solution.py:45
  413.4 17.1 %collective-permute-start.26 = (f32[2,1024]{1,0:T(2,128)S(1)}, f32[2,1024]{1,0:T(2,128)S(1)}, u32[]{:S(2)}, u32[]{:S(2)}) collective-permute-start(f32[2,1024]{1,0:T(2,128)S(1)} %pad_maximum_fusion.13), channel_id=1, source_target_pairs={{0,16},{16,0},{1,17},{17,1},{2,18},{18,2},{3,19},{19,3},{4,20},{20... | collective-permute-start | bytes 24584 | tf_op jit(solution)/shard_map/ppermute | solution.py:45
  434.5 39.2 %collective-permute-start.27 = (f32[2,1024]{1,0:T(2,128)S(1)}, f32[2,1024]{1,0:T(2,128)S(1)}, u32[]{:S(2)}, u32[]{:S(2)}) collective-permute-start(f32[2,1024]{1,0:T(2,128)S(1)} %pad_maximum_fusion.14), channel_id=1, source_target_pairs={{0,1},{1,0},{2,3},{3,2},{4,5},{5,4},{6,7},{7,6},{8,9},{9,8},{10,11... | collective-permute-start | bytes 24584 | tf_op jit(solution)/shard_map/ppermute | solution.py:45
  443.3 23.2 %collective-permute-start.39 = (bf16[2,1,256,256]{3,2,1,0:T(8,128)(2,1)S(1)}, bf16[2,1,256,256]{3,2,1,0:T(8,128)(2,1)S(1)}, u32[]{:S(2)}, u32[]{:S(2)}) collective-permute-start(bf16[2,1,256,256]{3,2,1,0:T(8,128)(2,1)S(1)} %get-tuple-element.133), channel_id=1, source_target_pairs={{0,4},{4,0},{8,12},{12,8},{1,5},{5,1},{9,13},{13,9},{2,6},{6,2},{1... | collective-permute-start | bytes 786440 | tf_op jit(solution)/shard_map/ppermute | solution.py:45
  448.9 18.4 %collective-permute-start.42 = (bf16[1,256,256]{2,1,0:T(8,128)(2,1)S(1)}, bf16[1,256,256]{2,1,0:T(8,128)(2,1)S(1)}, u32[]{:S(2)}, u32[]{:S(2)}) collective-permute-start(bf16[1,256,256]{2,1,0:T(8,128)(2,1)S(1)} %fusion.29), channel_id=1, source_target_pairs={{0,4},{4,0},{8,12},{12,8},{1,5},{5,1},{9,13},{13,9},{2,6},{6,2},{1... | collective-permute-start | bytes 393224 | tf_op jit(solution)/shard_map/ppermute | solution.py:45
  468.4 30.5 %collective-permute-start.68 = (bf16[8,256,256]{2,1,0:T(8,128)(2,1)S(1)}, bf16[8,256,256]{2,1,0:T(8,128)(2,1)S(1)}, u32[]{:S(2)}, u32[]{:S(2)}) collective-permute-start(bf16[8,256,256]{2,1,0:T(8,128)(2,1)S(1)} %constant_dynamic-update-slice_fusion.2.own), channel_id=1, source_target_pairs={{0,4},{4,0},{8,12},{12,8},{1,5},{5,1},{9,13},{13,9},{2,6},{6,2},{1... | collective-permute-start | bytes 3145736 | tf_op jit(solution)/shard_map/ppermute | solution.py:45
  469.5 30.7 %collective-permute-start.69 = (bf16[8,256,256]{2,1,0:T(8,128)(2,1)S(1)}, bf16[8,256,256]{2,1,0:T(8,128)(2,1)S(1)}, u32[]{:S(2)}, u32[]{:S(2)}) collective-permute-start(bf16[8,256,256]{2,1,0:T(8,128)(2,1)S(1)} %constant_dynamic-update-slice_fusion.2.own), channel_id=1, source_target_pairs={{0,8},{4,12},{8,0},{12,4},{1,9},{5,13},{9,1},{13,5},{2,10},{6,14},... | collective-permute-start | bytes 3145736 | tf_op jit(solution)/shard_map/ppermute | solution.py:45
  473.6 21.0 %collective-permute-start.43 = (bf16[2,256,256]{2,1,0:T(8,128)(2,1)S(1)}, bf16[2,256,256]{2,1,0:T(8,128)(2,1)S(1)}, u32[]{:S(2)}, u32[]{:S(2)}) collective-permute-start(bf16[2,256,256]{2,1,0:T(8,128)(2,1)S(1)} %get-tuple-element.137), channel_id=1, source_target_pairs={{0,16},{16,0},{1,17},{17,1},{2,18},{18,2},{3,19},{19,3},{4,20},{20... | collective-permute-start | bytes 786440 | tf_op jit(solution)/shard_map/ppermute | solution.py:45
  480.8 20.6 %collective-permute-start.25 = (f32[64,512]{1,0:T(8,128)S(1)}, f32[64,512]{1,0:T(8,128)S(1)}, u32[]{:S(2)}, u32[]{:S(2)}) collective-permute-start(f32[64,512]{1,0:T(8,128)S(1)} %get-tuple-element.114), channel_id=1, source_target_pairs={{0,16},{16,0},{1,17},{17,1},{2,18},{18,2},{3,19},{19,3},{4,20},{20... | collective-permute-start | bytes 393224 | tf_op jit(solution)/shard_map/ppermute | solution.py:45
  498.9 30.3 %collective-permute-start.70 = (bf16[4,256,256]{2,1,0:T(8,128)(2,1)S(1)}, bf16[4,256,256]{2,1,0:T(8,128)(2,1)S(1)}, u32[]{:S(2)}, u32[]{:S(2)}) collective-permute-start(bf16[4,256,256]{2,1,0:T(8,128)(2,1)S(1)} %slice.368), channel_id=1, source_target_pairs={{0,8},{4,12},{8,0},{12,4},{1,9},{5,13},{9,1},{13,5},{2,10},{6,14},... | collective-permute-start | bytes 1572872 | tf_op jit(solution)/shard_map/ppermute | solution.py:45
  500.3 29.0 %collective-permute-start.71 = (bf16[4,256,256]{2,1,0:T(8,128)(2,1)S(1)}, bf16[4,256,256]{2,1,0:T(8,128)(2,1)S(1)}, u32[]{:S(2)}, u32[]{:S(2)}) collective-permute-start(bf16[4,256,256]{2,1,0:T(8,128)(2,1)S(1)} %slice.369), channel_id=1, source_target_pairs={{0,4},{4,0},{8,12},{12,8},{1,5},{5,1},{9,13},{13,9},{2,6},{6,2},{1... | collective-permute-start | bytes 1572872 | tf_op jit(solution)/shard_map/ppermute | solution.py:45
  509.6 16.7 %collective-permute-start.46 = (bf16[2,256,256]{2,1,0:T(8,128)(2,1)S(1)}, bf16[2,256,256]{2,1,0:T(8,128)(2,1)S(1)}, u32[]{:S(2)}, u32[]{:S(2)}) collective-permute-start(bf16[2,256,256]{2,1,0:T(8,128)(2,1)S(1)} %slice.334), channel_id=1, source_target_pairs={{0,8},{4,12},{8,0},{12,4},{1,9},{5,13},{9,1},{13,5},{2,10},{6,14},... | collective-permute-start | bytes 786440 | tf_op jit(solution)/shard_map/ppermute | solution.py:45
  (148 other events, 1822.3 us)

commit v3 on v2

--- a/solution.py
+++ b/solution.py
@@ -18,7 +18,7 @@
 
 VM = pl.BlockSpec(memory_space=pltpu.VMEM)
 SM = pl.BlockSpec(memory_space=pltpu.SMEM)
-ANY = pl.BlockSpec(memory_space=pl.ANY)
+ANY = pl.BlockSpec(memory_space=pltpu.HBM)
 MIB = 1 << 20
 
 LOW, SEC, SHARD, LENGTHS = 0, 1, 2, 3
@@ -28,21 +28,41 @@
     return jax.ShapeDtypeStruct(tuple(dims), dtype)
 
 
-def call(body, outs, args, specs, scratch=(), limit=24, flops=0, moved=0, out_specs=None):
-    return pl.pallas_call(
-        body,
-        out_shape=tuple(outs),
-        in_specs=list(specs),
-        out_specs=tuple(out_specs or [VM] * len(outs)),
-        scratch_shapes=list(scratch),
-        compiler_params=pltpu.CompilerParams(vmem_limit_bytes=limit * MIB),
-        cost_estimate=pl.CostEstimate(flops=flops, bytes_accessed=moved, transcendentals=0),
-    )(*args)
+class Order:
+    def __init__(self):
+        self.token = None
+
+    def after(self, value):
+        if self.token is None:
+            return value
+        return lax.optimization_barrier((value, self.token))[0]
+
+    def call(self, body, outs, args, specs, scratch=(), limit=56, flops=0, moved=0, grid=()):
+        args = (self.after(args[0]),) + tuple(args[1:])
+        results = pl.pallas_call(
+            body,
+            out_shape=tuple(outs),
+            grid=grid,
+            in_specs=list(specs),
+            out_specs=tuple(VM for _ in outs),
+            scratch_shapes=list(scratch),
+            compiler_params=pltpu.CompilerParams(vmem_limit_bytes=limit * MIB),
+            cost_estimate=pl.CostEstimate(flops=flops, bytes_accessed=moved, transcendentals=0),
+        )(*args)
+        self.token = results[-1]
+        return results
 
 
 def swap(value, axis, flip):
     count = lax.axis_size(axis)
     return lax.ppermute(value, axis, [(i, i ^ flip) for i in range(count)])
+
+
+def swap_one(value, axis, flip, section):
+    count = lax.axis_size(axis)
+    base = section * count
+    pairs = [(base + i, base + (i ^ flip)) for i in range(count)]
+    return lax.ppermute(value, ("section", axis), pairs)
 
 
 def dot(a, b):
@@ -111,8 +131,8 @@
         self.made.append(copy)
         return copy
 
-    def wait(self):
-        for copy in self.made:
+    def wait(self, begin=0, end=None):
+        for copy in self.made[begin:end]:
             copy.wait()
 
 
@@ -131,39 +151,56 @@
     first[...] = (values * factor_of(values) * gain_g[0:1, :]).astype(low16)
 
 
-def piece_kernel(quarters, info, own_qkv, other_qkv, own_out, other_out, own_up, other_up,
-                 own_down, other_down, pieces, sems):
+def from_local(sec, own, other, branch):
+    @pl.when(sec == 0)
+    def _():
+        branch(0, *other)
+
+    @pl.when(sec != 0)
+    def _():
+        branch(1, *own)
+
+
+def mix_piece_kernel(info, own_qkv, other_qkv, own_out, other_out, piece, whole, sems):
     low, sec = info[LOW], info[SEC]
     half = own_qkv.shape[2] // 2
-    wide = own_up.shape[1] // 2
-
-    def branch(half_index, qkv, out, up, down):
+
+    def branch(half_index, qkv, out):
         made = Copies(sems)
-        for place, m in enumerate(quarters):
+        for m in range(QUARTERS):
             at = pl.ds(block_at(low, m), UNIT)
             at_right = pl.ds(pl.multiple_of(block_at(low, m) + half, half), half)
             at_left = pl.ds(block_at(low, m), half)
             lanes = slice(half_index * half, (half_index + 1) * half)
-            target = pieces.at[place]
+            target = whole.at[m]
             made.start(qkv.at[0, at, lanes], target.at[0, :, 0:half])
             made.start(qkv.at[1, at, lanes], target.at[0, :, half : 2 * half])
             made.start(qkv.at[2, at, lanes], target.at[1, :, 0:half])
             made.start(out.at[lanes, at_left], target.at[1, 0:half, half : 2 * half])
             made.start(out.at[lanes, at_right], target.at[1, half : 2 * half, half : 2 * half])
+        made.wait()
+
+    from_local(sec, (own_qkv, own_out), (other_qkv, other_out), branch)
+    piece[...] = whole[0]
+
+
+def feed_piece_kernel(info, own_up, other_up, own_down, other_down, piece, whole, sems):
+    low, sec = info[LOW], info[SEC]
+    wide = own_up.shape[1] // 2
+
+    def branch(half_index, up, down):
+        made = Copies(sems)
+        for m in range(QUARTERS):
+            at = pl.ds(block_at(low, m), UNIT)
             for part in range(2):
                 begin = half_index * wide + part * UNIT
                 hidden = slice(begin, begin + UNIT)
-                made.start(up.at[at, hidden], target.at[2 + part])
-                made.start(down.at[hidden, at], target.at[4 + part])
+                made.start(up.at[at, hidden], whole.at[m, part])
+                made.start(down.at[hidden, at], whole.at[m, 2 + part])
         made.wait()
 
-    @pl.when(sec == 0)
-    def _():
-        branch(0, other_qkv, other_out, other_up, other_down)
-
-    @pl.when(sec != 0)
-    def _():
-        branch(1, own_qkv, own_out, own_up, own_down)
+    from_local(sec, (own_up, own_down), (other_up, other_down), branch)
+    piece[...] = whole[0]
 
 
 def fetch_attention(made, low, sec, own_qkv, other_qkv, own_out, other_out, qkv, out):
@@ -185,7 +222,7 @@
     query_at = lax.broadcasted_iota(jnp.int32, (count, count), 0)
     key_at = lax.broadcasted_iota(jnp.int32, (count, count), 1)
     allowed = (key_at <= query_at) & (key_at < length)
-    made.wait()
+    made.wait(0, QUARTERS)
     values = rows[...]
     for c in range(3):
         packed[c] = dot(values, qkv[c]).astype(low16)
@@ -199,6 +236,7 @@
         probs[h] = exact
         heads.append(dot(exact.astype(low16), packed[2, :, lanes]).astype(low16))
     mixed[...] = jnp.concatenate(heads, axis=1)
+    made.wait(QUARTERS)
     partial[...] = dot(mixed[...], out[...]).astype(low16).reshape(partial.shape)
 
 
@@ -228,13 +266,15 @@
                        lifted, active, partial, up, down, total, sems):
     made = Copies(sems)
     fetch_feed(made, info[LOW], info[SEC], own_up, other_up, own_down, other_down, up, down)
-    made.wait()
+    made.wait(0, QUARTERS)
     values = rows[...]
     for t in range(up.shape[1] // UNIT):
         tile = dot(values, up[:, span(t)])
         lifted[:, span(t)] = tile
         low_tile = (tile * normal_cdf(tile)).astype(low16)
         active[:, span(t)] = low_tile
+        if t == 0:
+            made.wait(QUARTERS)
         branch = dot(low_tile, down[span(t), :])
         total[...] = branch if t == 0 else total[...] + branch
     partial[...] = total[...].astype(low16).reshape(partial.shape)
@@ -248,13 +288,15 @@
                             grad_lifted, partial, up, down, total, sems):
     made = Copies(sems)
     fetch_feed(made, info[LOW], info[SEC], own_up, other_up, own_down, other_down, up, down)
-    made.wait()
+    made.wait(QUARTERS)
     values = top[...]
     for t in range(up.shape[1] // UNIT):
         tile = lifted[:, span(t)]
         grad = dot_nt(values, down[span(t), :]) * gelu_slope(tile, normal_cdf(tile))
         grad = grad.astype(low16)
         grad_lifted[:, span(t)] = grad
+        if t == 0:
+            made.wait(0, QUARTERS)
         back = dot_nt(grad, up[:, span(t)])
         total[...] = back if t == 0 else total[...] + back
     partial[...] = total[...].astype(low16).reshape(partial.shape)
@@ -272,7 +314,7 @@
     low, sec = info[LOW], info[SEC]
     made = Copies(sems)
     fetch_attention(made, low, sec, own_qkv, other_qkv, own_out, other_out, qkv, out)
-    made.wait()
+    made.wait(QUARTERS)
     grad_mixed = dot_nt(mid[...], out[...]).astype(low16)
     columns = [[], [], []]
     for h in range(packed.shape[2] // HEAD_DIM):
@@ -286,6 +328,7 @@
         columns[0].append((dot(grad_scores, packed[1, :, lanes]) * SCALE).astype(low16))
         columns[1].append((dot_tn(grad_scores, packed[0, :, lanes]) * SCALE).astype(low16))
     total = None
+    made.wait(0, QUARTERS)
     for c in range(3):
         grads[c] = jnp.concatenate(columns[c], axis=1)
         back = dot_nt(grads[c], qkv[c])
@@ -302,18 +345,27 @@
         given[:, span(j)] = values[:, pl.ds(block_at(low, 2 * (1 - sec) + j), UNIT)]
 
 
-class LocalWeights:
-    def __init__(self, refs):
-        self.refs = refs
-
-    def unit(self, k, m, u):
-        own, rest = self.refs[0], self.refs[1]
-        if k == 0:
-            return own.at[0, u] if m == 0 else rest.at[m - 1, u]
-        base = self.refs[2 + 5 * (k - 1) : 7 + 5 * (k - 1)]
-        if m < 3:
-            return base[m].at[0, u]
-        return base[3].at[0, u] if u < 3 else base[4].at[0, u - 3]
+def mix_unit(refs, k, m, u):
+    whole, near, x_part, y_part, far = refs[0], refs[1:4], refs[4], refs[5], refs[6:8]
+    if k == 0:
+        return whole.at[m, u]
+    if m == 0:
+        return near[k - 1].at[u]
+    if m == 3:
+        return far[u].at[k - 1]
+    return (x_part if m == 1 else y_part).at[k - 1, u]
+
+
+def feed_unit(refs, k, m, u):
+    if k == 0:
+        return refs[0].at[m, u]
+    base = refs[5 * k - 4 : 5 * k + 1]
+    if m < 3:
+        return base[m].at[u]
+    return base[3].at[u] if u < 2 else base[4].at[u - 2]
+
+
+MIX_REFS, FEED_REFS = 8, 16
 
 
 def pair_rows(a, b, size):
@@ -355,16 +407,15 @@
 
 def local_attention_kernel(info, codes, sent_own, sent_other, gain, *rest):
     refs, (start, first, query_keys, values_out, probs, mixed, partial, weights, mix, sems) = (
-        rest[:17], rest[17:]
+        rest[:MIX_REFS], rest[MIX_REFS:]
     )
     low, sec = info[LOW], info[SEC]
-    local = LocalWeights(refs)
     made = Copies(sems)
     groups = []
     for k in range(4):
         groups.append(
             [
-                made.start(local.unit(k, m, u), weights.at[k, u, span(m), :])
+                made.start(mix_unit(refs, k, m, u), weights.at[k, u, span(m), :])
                 for u in range(2)
                 for m in range(QUARTERS)
             ]
@@ -420,18 +471,17 @@
 
 
 def local_feed_kernel(info, start, own_part, other_part, gain, cotangent, *rest):
-    refs = rest[:17]
-    (hidden, second, top, active, grad_lifted, grad_second, branch_out,
-     up, down, branch, back, sems) = rest[17:]
+    refs = rest[:FEED_REFS]
+    (hidden, second, top, active, grad_lifted, grad_second,
+     up, down, back, sems) = rest[FEED_REFS:]
     low = info[LOW]
-    local = LocalWeights(refs)
     tiles = active.shape[0]
     made = Copies(sems)
     for t in range(tiles):
         for m in range(QUARTERS):
-            made.start(local.unit(t // 2, m, 2 + t % 2), up.at[t, span(m), :])
+            made.start(feed_unit(refs, t // 2, m, t % 2), up.at[t, span(m), :])
         for m in range(QUARTERS):
-            made.start(local.unit(t // 2, m, 4 + t % 2), down.at[t, :, span(m)])
+            made.start(feed_unit(refs, t // 2, m, 2 + t % 2), down.at[t, :, span(m)])
     utts, code_count, frames, _ = cotangent.shape
     frame_at = lax.broadcasted_iota(jnp.int32, (frames, 1), 0) + info[SHARD] * frames
     for u in range(utts):
@@ -444,7 +494,6 @@
     values = start[...] + (own_part[...].astype(f32) + other_part[...].astype(f32))
     hidden[...] = values
     second[...] = (values * factor_of(values) * gain[1:2, :]).astype(low16)
-    branch[...] = jnp.zeros_like(branch)
     back[...] = jnp.zeros_like(back)
 
     @pl.loop(0, tiles)
@@ -461,27 +510,24 @@
         cdf = normal_cdf(tile)
         low_tile = (tile * cdf).astype(low16)
         active[t] = low_tile
-        branch[...] += dot(low_tile, down[t])
         grad = (dot_nt(top[...], down[t]) * gelu_slope(tile, cdf)).astype(low16)
         grad_lifted[t] = grad
         back[...] += dot_nt(grad, up[t])
 
-    branch_out[...] = branch[...].astype(low16)
     grad_second[...] = back[...].astype(low16)
 
 
 def local_attention_back_kernel(hidden, own_back, other_back, top, gain, query_keys, values_in,
                                 probs, *rest):
-    refs = rest[:17]
+    refs = rest[:MIX_REFS]
     (grad_hidden, mid, grad_query_keys, grad_values, grad_first, gain_grad,
-     weights, mix, total, sems) = rest[17:]
-    local = LocalWeights(refs)
+     weights, mix, total, sems) = rest[MIX_REFS:]
     made = Copies(sems)
     groups = []
     for k in range(4):
         groups.append(
             [
-                made.start(local.unit(k, m, u), weights.at[k, u, span(m), :])
+                made.start(mix_unit(refs, k, m, u), weights.at[k, u, span(m), :])
                 for u in range(2)
                 for m in range(QUARTERS)
             ]
@@ -580,27 +626,39 @@
 SEND_A, KEEP_A, SEND_B, KEEP_B = (1, 3), (0, 2), (2, 3), (0, 1)
 
 
-def local_up_kernel(second, grad_lifted, send_a, send_b, keep_a, keep_b, turned):
+def local_drop_kernel(active, *rest):
+    refs, (branch_out, down, branch, sems) = rest[:FEED_REFS], rest[FEED_REFS:]
+    tiles = active.shape[0]
+    made = Copies(sems)
+    for t in range(tiles):
+        for m in range(QUARTERS):
+            made.start(feed_unit(refs, t // 2, m, 2 + t % 2), down.at[t, :, span(m)])
+    branch[...] = jnp.zeros_like(branch)
+
+    @pl.loop(0, tiles)
+    def _(t):
+        for m in range(QUARTERS):
+            pltpu.make_async_copy(
+                refs[0].at[0, 0], down.at[t, :, span(m)], sems.at[QUARTERS * t + m]
+            ).wait()
+        branch[...] += dot(active[t], down[t])
+
+    branch_out[...] = branch[...].astype(low16)
+
+
+def local_feed_grad_kernel(second, grad_lifted, active, top,
+                           send_a, send_b, keep_a, keep_b, turned):
     turned[...] = jnp.transpose(second[...])
     for k in range(4):
         for part, pairs in enumerate(
             (((send_a, SEND_A), (keep_a, KEEP_A)), ((send_b, SEND_B), (keep_b, KEEP_B)))
         ):
             right = grad_lifted[2 * k + part]
-            for target, order in pairs:
-                for place, m in enumerate(order):
-                    target[place, k] = dot(turned[span(m), :], right).astype(low16)
-
-
-def local_down_kernel(active, top, send_a, send_b, keep_a, keep_b):
-    for k in range(4):
-        for part, pairs in enumerate(
-            (((send_a, SEND_A), (keep_a, KEEP_A)), ((send_b, SEND_B), (keep_b, KEEP_B)))
-        ):
             left = jnp.transpose(active[2 * k + part])
             for target, order in pairs:
                 for place, m in enumerate(order):
-                    target[place, k] = dot(left, top[:, span(m)]).astype(low16)
+                    target[place, 2 * k] = dot(turned[span(m), :], right).astype(low16)
+                    target[place, 2 * k + 1] = dot(left, top[:, span(m)]).astype(low16)
 
 
 def local_mix_kernel(first, grad_query_keys, grad_values, mixed, mid,
@@ -666,61 +724,88 @@
                 target[place] = add16(kept[m, part], arrived[m, part])
 
 
-def pick_kernel(info, *refs):
-    sec = info[SEC]
-    *units, given, kept = refs
-    half = len(units) // 2
-    place = 0
-    for mine, theirs in zip(units[:half], units[half:]):
-        for n in range(mine.shape[0]):
-            local, world = mine[n], theirs[n]
-            given[place] = jnp.where(sec == 0, local, world)
-            kept[place] = jnp.where(sec == 0, world, local)
-            place += 1
-
-
-def whole_quarters(refs):
-    own, x_part, y_part, far_kept, far_arrived = refs
-    count = own.shape[0] // 2
-
-    def unit(m, index):
-        if m < 3:
-            return (own, x_part, y_part)[m][index]
-        return far_kept[index] if index < count else far_arrived[index - count]
-
-    return unit, count
-
-
-def feed_final_kernel(info, own, x_part, y_part, far_kept, far_arrived, up, down):
+def far_kernel(keep_a, from_x, keep_b, from_y, far_a, far_b):
+    far_a[...] = add16(keep_a[0], from_x[0])
+    far_b[...] = add16(keep_b[0], from_y[0])
+
+
+def sum_kernel(*refs):
+    parts, outs = (refs[:3], refs[3:6]), refs[6:]
+    for part, (keep, once, twice) in enumerate(parts):
+        total = keep[0].astype(f32) + once[0].astype(f32) + twice[...].astype(f32)
+        total = total.astype(low16)
+        if len(outs) == 1:
+            count = total.shape[0]
+            outs[0][part * count : (part + 1) * count] = total
+        else:
+            count = total.shape[0] // 4
+            for k in range(4):
+                outs[(k + 1) % 2][k // 2, part * count : (part + 1) * count] = total[
+                    k * count : (k + 1) * count
+                ]
+
+
+def far_tensor_kernel(keep, arrived, far):
+    far[...] = add16(keep[0], arrived[0])
+
+
+def total_kernel(keep, once, twice, total):
+    for n in range(total.shape[0]):
+        value = keep[0, n].astype(f32) + once[0, n].astype(f32) + twice[n].astype(f32)
+        total[n] = value.astype(low16)
+
+
+def half_at(index, count):
+    return pl.BlockSpec(
+        (1, count, UNIT, UNIT), lambda i: (index, 0, 0, 0), memory_space=pltpu.VMEM
+    )
+
+
+def fetch_quarters(sec, refs, target, sems):
+    made = Copies(sems)
+    count = target.shape[1]
+    for index in range(3):
+        made.pick(True, sec, refs[index], refs[5 + index], target.at[index])
+    for index in range(2):
+        at = pl.ds(index * (count // 2), count // 2)
+        made.pick(True, sec, refs[3 + index], refs[8 + index], target.at[3, at])
+    return made
+
+
+def feed_final_kernel(info, *rest):
+    refs, (up, down, units, sems) = rest[:10], rest[10:]
     low, sec = info[LOW], info[SEC]
-    unit, count = whole_quarters((own, x_part, y_part, far_kept, far_arrived))
+    fetch_quarters(sec, refs, units, sems).wait()
     wide = up.shape[1] // 2
+    count = units.shape[1] // 2
     for m in range(QUARTERS):
         at = pl.ds(block_at(low, m), UNIT)
         for source, half in ((0, sec), (count, 1 - sec)):
             for part in range(2):
                 hidden = pl.ds(pl.multiple_of(half * wide + part * UNIT, UNIT), UNIT)
-                up[at, hidden] = unit(m, source + part).astype(f32)
-                down[hidden, at] = unit(m, source + 2 + part).astype(f32)
-
-
-def mix_final_kernel(info, own, x_part, y_part, far_kept, far_arrived, qkv, out):
+                up[at, hidden] = units[m, source + 2 * part].astype(f32)
+                down[hidden, at] = units[m, source + 2 * part + 1].astype(f32)
+
+
+def mix_final_kernel(info, *rest):
+    refs, (qkv, out, units, sems) = rest[:10], rest[10:]
     low, sec = info[LOW], info[SEC]
-    unit, count = whole_quarters((own, x_part, y_part, far_kept, far_arrived))
+    fetch_quarters(sec, refs, units, sems).wait()
     width = out.shape[0] // 2
+    count = units.shape[1] // 2
     for m in range(QUARTERS):
         at = pl.ds(block_at(low, m), UNIT)
         at_left = pl.ds(block_at(low, m), width)
         at_right = pl.ds(pl.multiple_of(block_at(low, m) + width, width), width)
         for source, half in ((0, sec), (count, 1 - sec)):
             lanes = pl.ds(pl.multiple_of(half * width, width), width)
-            query_keys = unit(m, source).astype(f32)
+            query_keys = units[m, source].astype(f32)
             qkv[0, at, lanes] = query_keys[:, :width]
             qkv[1, at, lanes] = query_keys[:, width:]
-            rest = unit(m, source + 1).astype(f32)
-            qkv[2, at, lanes] = rest[:, :width]
-            out[lanes, at_left] = rest[:width, width:]
-            out[lanes, at_right] = rest[width:, width:]
+            rest_unit = units[m, source + 1].astype(f32)
+            qkv[2, at, lanes] = rest_unit[:, :width]
+            out[lanes, at_left] = rest_unit[:width, width:]
+            out[lanes, at_right] = rest_unit[width:, width:]
 
 
 def sum_rest(value):
@@ -731,29 +816,77 @@
     return value
 
 
-def reduce_dp(send_a, send_b, keep_a, keep_b):
-    from_x = swap(send_a, "dp", 1)
-    from_y = swap(send_b, "dp", 2)
-    own_a, far_a = add16(keep_a[0], from_x[0]), add16(keep_a[1], from_x[1])
-    own_b, far_b = add16(keep_b[0], from_y[0]), add16(keep_b[1], from_y[1])
-    from_y = swap(far_a, "dp", 2)
-    from_x = swap(far_b, "dp", 1)
-    return sum_rest(add16(own_a, from_y)), sum_rest(add16(own_b, from_x))
-
-
-def reduce_tensor(a, b):
-    total = jnp.stack([a[0], b[0]]).astype(f32)
-    for k in (1, 2, 3):
-        total = total + swap(jnp.stack([a[k], b[k]]), "tensor", k).astype(f32)
-    return total.astype(low16)
-
-
-def gather_dp(units):
-    count = units.shape[0] // 2
-    x_part = swap(units, "dp", 1)
-    y_part = swap(units, "dp", 2)
-    far_kept = swap(x_part[:count], "dp", 2)
-    far_arrived = swap(y_part[count:], "dp", 1)
+class Sum:
+    def __init__(self, order, send_a, send_b, keep_a, keep_b, split):
+        self.order, self.split = order, split
+        self.keep = (keep_a, keep_b)
+        self.count = keep_a.shape[1]
+        self.once = (swap(send_a, "dp", 1), swap(send_b, "dp", 2))
+
+    def second(self):
+        far = half_at(1, self.count)
+        far_a, far_b = self.order.call(
+            far_kernel,
+            [shape((self.count, UNIT, UNIT), low16)] * 2,
+            (self.keep[0], self.once[0], self.keep[1], self.once[1]),
+            [far] * 4,
+            moved=self.count * MIB,
+            grid=(1,),
+        )
+        self.twice = (swap(far_a, "dp", 2), swap(far_b, "dp", 1))
+
+    def third(self):
+        if self.split:
+            outs = [shape((2, self.count // 2, UNIT, UNIT), low16)] * 2
+        else:
+            outs = [shape((2 * self.count, UNIT, UNIT), low16)]
+        near = half_at(0, self.count)
+        totals = self.order.call(
+            sum_kernel,
+            outs,
+            (self.keep[0], self.once[0], self.twice[0], self.keep[1], self.once[1], self.twice[1]),
+            [near, near, VM] * 2,
+            moved=self.count * MIB,
+            grid=(1,),
+        )
+        totals = [sum_rest(total) for total in totals]
+        if not self.split:
+            return totals[0]
+        self.keep = totals[1]
+        self.count = self.keep.shape[1]
+        self.once = swap(totals[0], "tensor", 1)
+
+    def fourth(self):
+        far = self.order.call(
+            far_tensor_kernel,
+            [shape((self.count, UNIT, UNIT), low16)],
+            (self.keep, self.once),
+            [half_at(1, self.count)] * 2,
+            moved=self.count * MIB // 2,
+            grid=(1,),
+        )[0]
+        self.twice = swap(far, "tensor", 2)
+
+    def last(self):
+        near = half_at(0, self.count)
+        return self.order.call(
+            total_kernel,
+            [shape((self.count, UNIT, UNIT), low16)],
+            (self.keep, self.once, self.twice),
+            [near, near, VM],
+            moved=self.count * MIB // 2,
+            grid=(1,),
+        )[0]
+
+
+def gather_dp(kept, section):
+    arrived = lax.ppermute(kept, "section", [(1 - section, section)])
+    units = jnp.concatenate([kept, arrived])
+    count = kept.shape[0]
+    x_part = swap_one(units, "dp", 1, section)
+    y_part = swap_one(units, "dp", 2, section)
+    far_kept = swap_one(x_part[:count], "dp", 2, section)
+    far_arrived = swap_one(y_part[count:], "dp", 1, section)
     return units, x_part, y_part, far_kept, far_arrived
 
 
@@ -770,6 +903,8 @@
     rows_l = utts * code_count * frames
     tiles = 2 * wide // UNIT
     info = jnp.concatenate([jnp.stack([low, sec, z]).astype(jnp.int32), lengths])
+    order = Order()
+    call = order.call
 
     code_rows = jnp.transpose(codes, (0, 2, 1, 3))
     cot_rows = jnp.transpose(cotangent, (0, 2, 1, 3))
@@ -778,7 +913,16 @@
     def sem(count):
         return pltpu.SemaphoreType.DMA((count,))
 
+    def gather(rows):
+        gathered = lax.all_gather(rows, "tensor", axis=0, tiled=True)
+        order.token = gathered
+        return gathered
+
+    def scatter(partial):
+        return lax.all_to_all(partial, "tensor", 0, 0)
+
     other_gain = swap(gains[0], "section", 1)
+    own_w, other_gain = lax.optimization_barrier((own_w, other_gain))
     other_w = tuple(swap(w, "section", 1) for w in own_w)
     both_w = tuple(w for pair in zip(own_w, other_w) for w in pair)
     attention_w, feed_w = both_w[:4], both_w[4:]
@@ -795,42 +939,19 @@
         [SM, VM, VM, VM],
         moved=2 * MIB,
     )
-
-    def pieces(quarters):
-        return call(
-            functools.partial(piece_kernel, quarters),
-            [shape((len(quarters), 6, UNIT, UNIT), low16)],
-            (info,) + both_w,
-            [SM] + [ANY] * 8,
-            [sem(9 * len(quarters))],
-            out_specs=[ANY],
-            moved=2 * len(quarters) * MIB,
-        )[0]
-
-    own_piece = pieces((0,))
-    rest_pieces = pieces((1, 2, 3))
-    by_z = {1: swap(own_piece, "tensor", 1), 2: swap(own_piece, "tensor", 2)}
-    by_z[3] = swap(by_z[2], "tensor", 1)
-    local_w = [own_piece, rest_pieces]
-    for k in (1, 2, 3):
-        x_part = swap(by_z[k], "dp", 1)
-        y_part = swap(by_z[k], "dp", 2)
-        local_w += [
-            by_z[k],
-            x_part,
-            y_part,
-            swap(x_part[:, :3], "dp", 2),
-            swap(y_part[:, 3:], "dp", 1),
-        ]
-    local_w = tuple(local_w)
-
-    def gather(rows):
-        return lax.all_gather(rows, "tensor", axis=0, tiled=True)
-
-    def scatter(partial):
-        return lax.all_to_all(partial, "tensor", 0, 0)
-
     first_g = gather(first_rows)
+
+    mix_piece, mix_whole = call(
+        mix_piece_kernel,
+        [shape((2, UNIT, UNIT), low16), shape((QUARTERS, 2, UNIT, UNIT), low16)],
+        (info,) + attention_w,
+        [SM] + [ANY] * 4,
+        [sem(5 * QUARTERS)],
+        moved=2 * MIB,
+    )
+    mix_z1 = swap(mix_piece, "tensor", 1)
+    mix_z2 = swap(mix_piece, "tensor", 2)
+
     packed_g, probs_g, mixed_g, partial = call(
         global_attention_kernel,
         [
@@ -849,14 +970,48 @@
         flops=2 * 10**9,
         moved=8 * MIB,
     )
+    arrived = scatter(partial)
+    feed_piece, feed_whole = call(
+        feed_piece_kernel,
+        [shape((4, UNIT, UNIT), low16), shape((QUARTERS, 4, UNIT, UNIT), low16)],
+        (info,) + feed_w,
+        [SM] + [ANY] * 4,
+        [sem(4 * QUARTERS)],
+        moved=4 * MIB,
+    )
+    feed_z1 = swap(feed_piece, "tensor", 1)
+    mix_z3 = swap(mix_z2, "tensor", 1)
+    mix_far = jnp.stack([mix_z1, mix_z2, mix_z3])
+    mix_x = swap(mix_far, "dp", 1)
+    mix_y = swap(mix_far, "dp", 2)
+    mix_w = (
+        mix_whole,
+        mix_z1,
+        mix_z2,
+        mix_z3,
+        mix_x,
+        mix_y,
+        swap(mix_x[:, 0], "dp", 2),
+        swap(mix_y[:, 1], "dp", 1),
+    )
     hidden_g, second_rows = call(
         middle_kernel,
         [shape((frames, width), f32), shape((frames, width), low16)],
-        (start_g, scatter(partial), gain_g),
+        (start_g, arrived, gain_g),
         [VM] * 3,
         moved=2 * MIB,
     )
     second_g = gather(second_rows)
+    feed_z2 = swap(order.after(feed_piece), "tensor", 2)
+    feed_z3 = swap(feed_z2, "tensor", 1)
+    feed_l = [feed_whole]
+    for part in (feed_z1, feed_z2, feed_z3):
+        x_part = swap(part, "dp", 1)
+        y_part = swap(part, "dp", 2)
+        feed_l += [
+            part, x_part, y_part, swap(x_part[:2], "dp", 2), swap(y_part[2:], "dp", 1)
+        ]
+    feed_l = tuple(feed_l)
     lifted_g, active_g, partial = call(
         global_feed_kernel,
         [
@@ -894,18 +1049,17 @@
             shape((rows_l, 4 * half), low16),
             shape((rows_l, width), low16),
         ],
-        (info, code_rows, sent, swap(sent, "section", 1), gain_l) + local_w,
-        [SM] + [VM] * 4 + [ANY] * 17,
+        (info, code_rows, sent, swap(sent, "section", 1), gain_l) + mix_w,
+        [SM] + [VM] * 4 + [ANY] * MIX_REFS,
         [
             pltpu.VMEM((4, 2, width, UNIT), low16),
             pltpu.VMEM((4 * half, width), low16),
             sem(32),
         ],
-        limit=40,
         flops=4 * 10**9,
         moved=20 * MIB,
     )
-    hidden_l, second_l, top_l, active_l, grad_lifted_l, back, branch_l = call(
+    hidden_l, second_l, top_l, active_l, grad_lifted_l, back = call(
         local_feed_kernel,
         [
             shape((rows_l, width), f32),
@@ -914,40 +1068,32 @@
             shape((tiles, rows_l, UNIT), low16),
             shape((tiles, rows_l, UNIT), low16),
             shape((rows_l, width), low16),
-            shape((rows_l, width), low16),
-        ],
-        (info, start_l, partial, swap(partial, "section", 1), gain_l, cot_rows) + local_w,
-        [SM] + [VM] * 5 + [ANY] * 17,
+        ],
+        (info, start_l, partial, swap(partial, "section", 1), gain_l, cot_rows) + feed_l,
+        [SM] + [VM] * 5 + [ANY] * FEED_REFS,
         [
             pltpu.VMEM((tiles, width, UNIT), low16),
             pltpu.VMEM((tiles, UNIT, width), low16),
             pltpu.VMEM((rows_l, width), f32),
-            pltpu.VMEM((rows_l, width), f32),
             sem(8 * tiles),
         ],
-        limit=48,
         flops=10 * 10**9,
         moved=24 * MIB,
     )
-
-    send_shape = shape((2, 4, UNIT, UNIT), low16)
+    other_back = swap(back, "section", 1)
     turned_l = pltpu.VMEM((width, rows_l), low16)
-    down_units = call(
-        local_down_kernel,
-        [send_shape] * 4,
-        (active_l, top_l),
-        [VM] * 2,
-        flops=3 * 10**9,
-        moved=8 * MIB,
-    )
-    up_units = call(
-        local_up_kernel,
-        [send_shape] * 4,
-        (second_l, grad_lifted_l),
-        [VM] * 2,
-        [turned_l],
-        flops=3 * 10**9,
-        moved=8 * MIB,
+    local_feed = Sum(
+        order,
+        *call(
+            local_feed_grad_kernel,
+            [shape((2, 8, UNIT, UNIT), low16)] * 4,
+            (second_l, grad_lifted_l, active_l, top_l),
+            [VM] * 4,
+            [turned_l],
+            flops=6 * 10**9,
+            moved=16 * MIB,
+        ),
+        True,
     )
     grad_hidden_l, mid_l, grad_query_keys, grad_values, back, gain2_l = call(
         local_attention_back_kernel,
@@ -959,27 +1105,30 @@
             shape((rows_l, width), low16),
             shape((1, width), f32),
         ],
-        (hidden_l, back, swap(back, "section", 1), top_l, gain_l, query_keys, values_l, probs_l)
-        + local_w,
-        [VM] * 8 + [ANY] * 17,
+        (hidden_l, back, other_back, top_l, gain_l, query_keys, values_l, probs_l) + mix_w,
+        [VM] * 8 + [ANY] * MIX_REFS,
         [
             pltpu.VMEM((4, 2, width, UNIT), low16),
             pltpu.VMEM((4 * half, width), low16),
             pltpu.VMEM((rows_l, width), f32),
             sem(32),
         ],
-        limit=40,
         flops=5 * 10**9,
         moved=20 * MIB,
     )
-    mix_units = call(
-        local_mix_kernel,
-        [send_shape] * 4,
-        (first_l, grad_query_keys, grad_values, mixed_l, mid_l),
-        [VM] * 5,
-        [turned_l],
-        flops=3 * 10**9,
-        moved=8 * MIB,
+    other_back = swap(back, "section", 1)
+    local_mix = Sum(
+        order,
+        *call(
+            local_mix_kernel,
+            [shape((2, 4, UNIT, UNIT), low16)] * 4,
+            (first_l, grad_query_keys, grad_values, mixed_l, mid_l),
+            [VM] * 5,
+            [turned_l],
+            flops=3 * 10**9,
+            moved=8 * MIB,
+        ),
+        True,
     )
     returned, code_part, gain1_l = call(
         local_end_kernel,
@@ -988,18 +1137,11 @@
             shape((utts, code_count, frames, width // 2), f32),
             shape((1, width), f32),
         ],
-        (info, back, swap(back, "section", 1), start_l, grad_hidden_l, gain_l),
+        (info, back, other_back, start_l, grad_hidden_l, gain_l),
         [SM] + [VM] * 5,
         [pltpu.VMEM((rows_l, width), f32)],
         moved=6 * MIB,
     )
-    output = call(
-        output_kernel,
-        [shape((utts, code_count, frames, width // 2), low16)],
-        (info, hidden_l, branch_l, swap(branch_l, "section", 1)),
-        [SM] + [VM] * 3,
-        moved=4 * MIB,
-    )[0]
 
     top_g = gather(returned)
     grad_lifted_g, partial = call(
@@ -1016,13 +1158,7 @@
         flops=2 * 10**9,
         moved=8 * MIB,
     )
-    grad_hidden_g, mid_rows, gain2_g = call(
-        middle_back_kernel,
-        [shape((frames, width), f32), shape((frames, width), low16), shape((1, width), f32)],
-        (scatter(partial), hidden_g, gain_g, returned),
-        [VM] * 4,
-        moved=2 * MIB,
-    )
+    arrived = scatter(partial)
     away_feed, kept_feed = call(
         global_feed_grad_kernel,
         [shape((QUARTERS, 2, 2, UNIT, UNIT), low16)] * 2,
@@ -1032,6 +1168,15 @@
         flops=4 * 10**9,
         moved=8 * MIB,
     )
+    away_feed = swap(away_feed, "section", 1)
+    local_feed.second()
+    grad_hidden_g, mid_rows, gain2_g = call(
+        middle_back_kernel,
+        [shape((frames, width), f32), shape((frames, width), low16), shape((1, width), f32)],
+        (arrived, hidden_g, gain_g, returned),
+        [VM] * 4,
+        moved=2 * MIB,
+    )
     mid_g = gather(mid_rows)
     grads_g, partial = call(
         global_attention_back_kernel,
@@ -1046,6 +1191,20 @@
         flops=2 * 10**9,
         moved=8 * MIB,
     )
+    arrived = scatter(partial)
+    local_mix.second()
+
+    def merged(away, kept, count):
+        units = call(
+            merge_kernel,
+            [shape((2, count, UNIT, UNIT), low16)] * 4,
+            (kept, away),
+            [VM] * 2,
+            moved=2 * count * MIB,
+        )
+        return Sum(order, *units, False)
+
+    global_feed = merged(away_feed, kept_feed, 2)
     away_mix, kept_mix = call(
         global_mix_grad_kernel,
         [shape((QUARTERS, 2, 1, UNIT, UNIT), low16)] * 2,
@@ -1055,6 +1214,9 @@
         flops=2 * 10**9,
         moved=4 * MIB,
     )
+    away_mix = swap(away_mix, "section", 1)
+    local_feed.third()
+    global_mix = merged(away_mix, kept_mix, 1)
     kept_start, given_start, gain1_g = call(
         start_back_kernel,
         [
@@ -1062,11 +1224,14 @@
             shape((frames, width // 2), f32),
             shape((1, width), f32),
         ],
-        (info, scatter(partial), start_g, gain_g, grad_hidden_g),
+        (info, arrived, start_g, gain_g, grad_hidden_g),
         [SM] + [VM] * 4,
         [pltpu.VMEM((frames, width), f32)],
         moved=2 * MIB,
     )
+    local_mix.third()
+    global_feed.second()
+    global_mix.second()
     arrived_start = swap(given_start, "section", 1)
     both_start = jnp.stack(
         [
@@ -1093,54 +1258,47 @@
             gain_total = gain_total + swap(gain_total, axis, step)
             step *= 2
 
-    local_down = reduce_tensor(*reduce_dp(*down_units))
-    local_up = reduce_tensor(*reduce_dp(*up_units))
-    local_mix = reduce_tensor(*reduce_dp(*mix_units))
-
-    def global_sum(away, kept, count):
-        units = call(
-            merge_kernel,
-            [shape((2, count, UNIT, UNIT), low16)] * 4,
-            (kept, swap(away, "section", 1)),
-            [VM] * 2,
-            moved=2 * count * MIB,
-        )
-        return reduce_dp(*units)
-
-    def finish(local_units, global_units, body, outs):
-        count = sum(unit.shape[0] for unit in local_units)
-        given, kept = call(
-            pick_kernel,
-            [shape((count, UNIT, UNIT), low16)] * 2,
-            (info,) + tuple(local_units) + tuple(global_units),
-            [SM] + [VM] * (len(local_units) + len(global_units)),
-            moved=2 * MIB,
-        )
-        arrived = swap(given, "section", 1)
-        return call(
-            body,
-            outs,
-            (info,) + gather_dp(jnp.concatenate([kept, arrived])),
-            [SM] + [VM] * 5,
-            limit=32,
-            moved=16 * MIB,
-        )
-
-    feed_a, feed_b = global_sum(away_feed, kept_feed, 2)
-    mix_a, mix_b = global_sum(away_mix, kept_mix, 1)
-    global_up = jnp.stack([feed_a[0], feed_b[0]])
-    global_down = jnp.stack([feed_a[1], feed_b[1]])
-    up_grad, down_grad = finish(
-        (local_up, local_down),
-        (global_up, global_down),
+    branch_l = call(
+        local_drop_kernel,
+        [shape((rows_l, width), low16)],
+        (active_l,) + feed_l,
+        [VM] + [ANY] * FEED_REFS,
+        [
+            pltpu.VMEM((tiles, UNIT, width), low16),
+            pltpu.VMEM((rows_l, width), f32),
+            sem(QUARTERS * tiles),
+        ],
+        flops=2 * 10**9,
+        moved=8 * MIB,
+    )[0]
+    global_feed = gather_dp(global_feed.third(), 0)
+    global_mix = gather_dp(global_mix.third(), 0)
+    local_feed.fourth()
+    output = call(
+        output_kernel,
+        [shape((utts, code_count, frames, width // 2), low16)],
+        (info, hidden_l, branch_l, swap(branch_l, "section", 1)),
+        [SM] + [VM] * 3,
+        moved=4 * MIB,
+    )[0]
+    local_mix.fourth()
+    local_feed = gather_dp(local_feed.last(), 1)
+    local_mix = gather_dp(local_mix.last(), 1)
+    up_grad, down_grad = call(
         feed_final_kernel,
         [shape((width, wide), f32), shape((wide, width), f32)],
-    )
-    qkv_grad, out_grad = finish(
-        (local_mix,),
-        (jnp.concatenate([mix_a, mix_b]),),
+        (info,) + global_feed + local_feed,
+        [SM] + [ANY] * 10,
+        [pltpu.VMEM((QUARTERS, 8, UNIT, UNIT), low16), sem(5)],
+        moved=16 * MIB,
+    )
+    qkv_grad, out_grad = call(
         mix_final_kernel,
         [shape((3, width, heads_width), f32), shape((heads_width, width), f32)],
+        (info,) + global_mix + local_mix,
+        [SM] + [ANY] * 10,
+        [pltpu.VMEM((QUARTERS, 4, UNIT, UNIT), low16), sem(5)],
+        moved=8 * MIB,
     )
     return (
         jnp.transpose(output, (0, 2, 1, 3)),

time: 541 us -> 502 us (0.928)
  Pallas kernels: 85.7 us -> 160 us
  waiting for transfers between devices: 175 us -> 122 us
  blocking collectives: 105 us -> 75.6 us
  local copies, waits for them, and re-layouts: 52.6 us -> 27.8 us
  other arithmetic: 28.2 us -> 5.15 us
  starting transfers between devices: 85.5 us -> 103 us
    pallas_call x27 -> x37, Pallas kernels: 85.7 us -> 160 us  [call(): pl.pallas_call(body, out_shape=tuple(outs), grid=grid, in_specs=list(spec...]
    ppermute x72 -> x60, waiting for transfers between devices: 165 us -> 102 us  [swap(): return lax.ppermute(value, axis, [(i, i ^ flip) for i in range(count)])]
    ppermute x0 -> x20, starting transfers between devices: none -> 37.9 us  [the longest x16 28.7 us: swap_one(): return lax.ppermute(value, ('section', axis), pairs)]
    all_gather x4, blocking collectives: 105 us -> 75.6 us  [gather(): gathered = lax.all_gather(rows, 'tensor', axis=0, tiled=True)]
    convert_element_type x23 -> x0, other arithmetic: 21.2 us -> none  [the longest x20 17.9 us: add16(): return (a.astype(f32) + b.astype(f32)).astype(low16)]
    unnamed x242 -> x156, local copies, waits for them, and re-layouts: 42.7 us -> 21.6 us
    ppermute x72 -> x60, starting transfers between devices: 69.9 us -> 49.2 us  [swap(): return lax.ppermute(value, axis, [(i, i ^ flip) for i in range(count)])]
    ppermute x0 -> x20, waiting for transfers between devices: none -> 12.2 us  [the longest x16 10.6 us: swap_one(): return lax.ppermute(value, ('section', axis), pairs)]
  transfers between devices with their start and end apart: 76 -> 84, of which waited for: 28 -> 27; matrix products, arithmetic and copies ran while one was open for 7% -> 2% of each run, Pallas kernels for 10% -> 26%
where the time goes in v3:
time: 502 us; the launch traced here: 495 us
  Pallas kernels  160 us (32%)
  waiting for transfers between devices  122 us (24%)
  starting transfers between devices  103 us (21%)
  blocking collectives  75.6 us (15%)
  local copies, waits for them, and re-layouts  27.8 us (6%)
  other arithmetic  5.15 us (1%)
    pallas_call x37, Pallas kernels, call(): pl.pallas_call(body, out_shape=tuple(outs), grid=grid, in_specs=list(spec...  160 us
    ppermute x60, waiting for transfers between devices, swap(): return lax.ppermute(value, axis, [(i, i ^ flip) for i in range(count)])  102 us
    all_gather x4, blocking collectives, gather(): gathered = lax.all_gather(rows, 'tensor', axis=0, tiled=True)  75.6 us
    ppermute x60, starting transfers between devices, swap(): return lax.ppermute(value, axis, [(i, i ^ flip) for i in range(count)])  49.2 us
    ppermute x16, starting transfers between devices, swap_one(): return lax.ppermute(value, ('section', axis), pairs)  28.7 us
    unnamed x156, local copies, waits for them, and re-layouts  21.6 us
    all_to_all x4, starting transfers between devices, scatter(): return lax.all_to_all(partial, 'tensor', 0, 0)  15.6 us
    ppermute x16, waiting for transfers between devices, swap_one(): return lax.ppermute(value, ('section', axis), pairs)  10.6 us
  transfers between devices with their start and end apart: 84, of which 27 were waited for; matrix products, arithmetic and copies ran while one was open for 2% of the time, Pallas kernels for 26%

profile of v3, /device:TPU:0, one launch (start us, length us, event | category | flops | bytes accessed | tf_op | source)
XLA Modules:
  0.0 495.4 jit_solution(4412045450185036814)
XLA Ops:
  6.4 19.5 %all_gather.12.rows.first = bf16[256,1024]{1,0:T(8,128)(2,1)} all-gather(bf16[64,1024]{1,0:T(8,128)(2,1)} %get-tuple-element.136), channel_id=1, replica_groups=mesh['section'=2,'dp'=4,'tensor'=4] {'tensor'}, dimensions={0}, use_global_device_ids=true | all-gather | bytes 655360 | tf_op jit(solution)/shard_map/all_gather | solution.py:917
  26.7 3.1 shard_map.136
  30.7 5.5 %shard_map.137 = (bf16[3,256,256]{2,1,0:T(8,128)(2,1)}, f32[4,256,256]{2,1,0:T(8,128)}, bf16[256,256]{1,0:T(8,128)(2,1)}, bf16[4,64,1024]{2,1,0:T(8,128)(2,1)}) custom-call(s32[5]{0:T(128)} %pad_add_fusion.info, bf16[256,1024]{1,0:T(8,128)(2,1)} %all_gather.12.rows.first, bf16[3,1024,256]{2,1,0:T(8,128)(2,1)} %bitcast.46, ...), custom_call_target="tpu_custom_call" | custom-call | flops 2000000000 | bytes 8388608 | tf_op jit(solution)/shard_map/pallas_call | solution.py:42
  36.2 3.5 all-to-all-start
  44.2 12.6 %collective-permute-done.6.rest_1_ = bf16[2,256,256]{2,1,0:T(8,128)(2,1)S(1)} collective-permute-done((bf16[2,256,256]{2,1,0:T(8,128)(2,1)}, bf16[2,256,256]{2,1,0:T(8,128)(2,1)S(1)}, u32[]{:S(2)}, u32[]{:S(2)}) %collective-permute-start.6) | collective-permute-done | bytes 262176 | tf_op jit(solution)/shard_map/ppermute | solution.py:58
  56.8 5.4 %collective-permute-done.8.rest_3_ = bf16[2,256,256]{2,1,0:T(8,128)(2,1)S(1)} collective-permute-done((bf16[2,256,256]{2,1,0:T(8,128)(2,1)S(1)}, bf16[2,256,256]{2,1,0:T(8,128)(2,1)S(1)}, u32[]{:S(2)}, u32[]{:S(2)}) %collective-permute-start.8) | collective-permute-done | bytes 262176 | tf_op jit(solution)/shard_map/ppermute | solution.py:58
  68.2 3.9 shard_map.138
  75.0 23.7 %all_gather.13.rows.second = bf16[256,1024]{1,0:T(8,128)(2,1)} all-gather(bf16[64,1024]{1,0:T(8,128)(2,1)} %get-tuple-element.150), channel_id=1, replica_groups=mesh['section'=2,'dp'=4,'tensor'=4] {'tensor'}, dimensions={0}, use_global_device_ids=true | all-gather | bytes 655360 | tf_op jit(solution)/shard_map/all_gather | solution.py:917
  99.5 5.6 %shard_map.140 = (f32[256,1024]{1,0:T(8,128)}, bf16[256,1024]{1,0:T(8,128)(2,1)}, bf16[4,64,1024]{2,1,0:T(8,128)(2,1)}) custom-call(s32[5]{0:T(128)} %pad_add_fusion.info, bf16[256,1024]{1,0:T(8,128)(2,1)} %all_gather.13.rows.second, bf16[1024,1024]{1,0:T(8,128)(2,1)} %bitcast.38, bf16[1024,1024]{1,0:T(8,128)(2,1)} %copy-done, bf16[1024,1024]{1,0:T(8,128)(2,1)} %bitcast.42, ...), custom_call_target="tpu_custom_call" | custom-call | flops 2000000000 | bytes 8388608 | tf_op jit(solution)/shard_map/pallas_call | solution.py:42
  105.1 4.3 all-to-all-start.1
  111.3 15.0 %collective-permute-done.19.rest_6_ = bf16[4,256,256]{2,1,0:T(8,128)(2,1)S(1)} collective-permute-done((bf16[4,256,256]{2,1,0:T(8,128)(2,1)}, bf16[4,256,256]{2,1,0:T(8,128)(2,1)S(1)}, u32[]{:S(2)}, u32[]{:S(2)}) %collective-permute-start.19) | collective-permute-done | bytes 524320 | tf_op jit(solution)/shard_map/ppermute | solution.py:58
  138.8 4.0 collective-permute-done.24.rest_11_
  143.8 8.9 %shard_map.142 = (f32[384,1024]{1,0:T(8,128)}, bf16[384,1024]{1,0:T(8,128)(2,1)}, bf16[4,384,256]{2,1,0:T(8,128)(2,1)}, bf16[4,384,128]{2,1,0:T(8,128)(2,1)}, f3...) custom-call(s32[5]{0:T(128)} %pad_add_fusion.info, ...), custom_call_target="tpu_custom_call" | custom-call | flops 4000000000 | bytes 20971520 | tf_op jit(solution)/shard_map/pallas_call | solution.py:42
  156.1 7.6 %collective-permute-done.25.rest_12_ = bf16[4,256,256]{2,1,0:T(8,128)(2,1)S(1)} collective-permute-done((bf16[4,256,256]{2,1,0:T(8,128)(2,1)}, bf16[4,256,256]{2,1,0:T(8,128)(2,1)S(1)}, u32[]{:S(2)}, u32[]{:S(2)}) %collective-permute-start.25) | collective-permute-done | bytes 524320 | tf_op jit(solution)/shard_map/ppermute | solution.py:58
  167.1 4.0 collective-permute-done.17.rest_4_
  173.2 3.5 collective-permute-done.22.rest_9_
  176.7 4.6 collective-permute-done.27.rest_14_
  182.1 13.6 %shard_map.143 = (f32[384,1024]{1,0:T(8,128)}, bf16[384,1024]{1,0:T(8,128)(2,1)}, bf16[384,1024]{1,0:T(8,128)(2,1)}, bf16[8,384,256]{2,1,0:T(8,128)(2,1)}, bf16[...) custom-call(s32[5]{0:T(128)} %pad_add_fusion.info, f32[384,1024]{1,0:T(8,128)} %get-tuple-element.159.start, ...), custom_call_target="tpu_custom_call" | custom-call | flops 10000000000 | bytes 25165824 | tf_op jit(solution)/shard_map/pallas_call | solution.py:42
  195.7 9.3 %shard_map.144 = (bf16[2,8,256,256]{3,2,1,0:T(8,128)(2,1)}, bf16[2,8,256,256]{3,2,1,0:T(8,128)(2,1)}, bf16[2,8,256,256]{3,2,1,0:T(8,128)(2,1)}, bf16[2,8,256,256]{3,2,1,0:T(8,128)(2,1)}) custom-call(bf16[384,1024]{1,0:T(8,128)(2,1)} %get-tuple-element.164.second, bf16[8,384,256]{2,1,0:T(8,128)(2,1)} %get-tuple-element.165.grad_lifted, ...), custom_call_target="tpu_custom_call" | custom-call | flops 6000000000 | bytes 16777216 | tf_op jit(solution)/shard_map/pallas_call | solution.py:42
  206.0 11.1 %shard_map.145 = (f32[384,1024]{1,0:T(8,128)}, bf16[384,1024]{1,0:T(8,128)(2,1)}, bf16[4,384,256]{2,1,0:T(8,128)(2,1)}, bf16[4,384,128]{2,1,0:T(8,128)(2,1)}, bf...) custom-call(f32[384,1024]{1,0:T(8,128)} %get-tuple-element.172.hidden, bf16[384,1024]{1,0:T(8,128)(2,1)} %get-tuple-element.163.own_back, ...), custom_call_target="tpu_custom_call" | custom-call | flops 5000000000 | bytes 20971520 | tf_op jit(solution)/shard_map/pallas_call | solution.py:42
  219.7 6.1 %shard_map.146 = (bf16[2,4,256,256]{3,2,1,0:T(8,128)(2,1)}, bf16[2,4,256,256]{3,2,1,0:T(8,128)(2,1)}, bf16[2,4,256,256]{3,2,1,0:T(8,128)(2,1)}, bf16[2,4,256,256]{3,2,1,0:T(8,128)(2,1)}) custom-call(bf16[384,1024]{1,0:T(8,128)(2,1)} %get-tuple-element.177.first, bf16[4,384,256]{2,1,0:T(8,128)(2,1)} %get-tuple-element.178.grad_query_keys, ...), custom_call_target="tpu_custom_call" | custom-call | flops 3000000000 | bytes 8388608 | tf_op jit(solution)/shard_map/pallas_call | solution.py:42
  226.7 4.4 shard_map.147
  231.1 16.3 %all_gather.14.top = bf16[256,1024]{1,0:T(8,128)(2,1)} all-gather(bf16[64,1024]{1,0:T(8,128)(2,1)} %get-tuple-element.186.returned), channel_id=1, replica_groups=mesh['section'=2,'dp'=4,'tensor'=4] {'tensor'}, dimensions={0}, use_global_device_ids=true | all-gather | bytes 655360 | tf_op jit(solution)/shard_map/all_gather | solution.py:917
  247.4 6.3 %shard_map.148 = (bf16[256,1024]{1,0:T(8,128)(2,1)}, bf16[4,64,1024]{2,1,0:T(8,128)(2,1)}) custom-call(s32[5]{0:T(128)} %pad_add_fusion.info, bf16[256,1024]{1,0:T(8,128)(2,1)} %all_gather.14.top, f32[256,1024]{1,0:T(8,128)} %get-tuple-element.188.lifted, bf16[1024,1024]{1,0:T(8,128)(2,1)} %bitcast.39, bf16[1024,1024]{1,0:T(8,128)(2,1)} %copy-done, ...), custom_call_target="tpu_custom_call" | custom-call | flops 2000000000 | bytes 8388608 | tf_op jit(solution)/shard_map/pallas_call | solution.py:42
  253.7 4.3 shard_map.149
  258.0 4.1 all-to-all-start.2
  267.8 3.7 shard_map.150
  273.0 4.6 all-to-all-done.2.arrived
  279.8 16.1 %all_gather.15.mid = bf16[256,1024]{1,0:T(8,128)(2,1)} all-gather(bf16[64,1024]{1,0:T(8,128)(2,1)} %get-tuple-element.200), channel_id=1, replica_groups=mesh['section'=2,'dp'=4,'tensor'=4] {'tensor'}, dimensions={0}, use_global_device_ids=true | all-gather | bytes 655360 | tf_op jit(solution)/shard_map/all_gather | solution.py:917
  295.9 6.8 %shard_map.152 = (bf16[3,256,256]{2,1,0:T(8,128)(2,1)}, bf16[4,64,1024]{2,1,0:T(8,128)(2,1)}) custom-call(s32[5]{0:T(128)} %pad_add_fusion.info, bf16[256,1024]{1,0:T(8,128)(2,1)} %all_gather.15.mid, bf16[3,256,256]{2,1,0:T(8,128)(2,1)} %get-tuple-element.202.packed, f32[4,256,256]{2,1,0:T(8,128)} %get-tuple-element.203.probs, ...), custom_call_target="tpu_custom_call" | custom-call | flops 2000000000 | bytes 8388608 | tf_op jit(solution)/shard_map/pallas_call | solution.py:42
  306.2 3.7 shard_map.154
  309.9 3.5 shard_map.155
  313.4 3.7 all-to-all-start.3
  320.1 4.8 shard_map.156
  337.4 3.1 shard_map.159
  340.6 4.4 collective-permute-done.41.from_x.refs_1_
  353.1 6.8 %shard_map.162.own_part = bf16[384,1024]{1,0:T(8,128)(2,1)} custom-call(bf16[8,384,256]{2,1,0:T(8,128)(2,1)} %get-tuple-element.238.active, bf16[4,4,256,256]{3,2,1,0:T(8,128)(2,1)} %get-tuple-element.146.rest_0_, bf16[4,256,256]{2,1,0:T(8,128)(2,1)} %copy-done.45, bf16[4,256,256]{2,1,0:T(8,128)(2,1)} %copy-done.24, bf16[4,256,256]{2,1,0:T(8,128)(2,1)} %copy-done.25, ...), custom_call_target="tpu_custom_call" | custom-call | flops 2000000000 | bytes 8388608 | tf_op jit(solution)/shard_map/pallas_call | solution.py:42
  384.9 14.6 %collective-permute-done.58.twice = bf16[4,256,256]{2,1,0:T(8,128)(2,1)S(1)} collective-permute-done((bf16[4,256,256]{2,1,0:T(8,128)(2,1)}, bf16[4,256,256]{2,1,0:T(8,128)(2,1)S(1)}, u32[]{:S(2)}, u32[]{:S(2)}) %collective-permute-start.58) | collective-permute-done | bytes 524320 | tf_op jit(solution)/shard_map/ppermute | solution.py:58
  411.4 3.3 collective-permute-start.59
  415.9 5.9 %collective-permute-done.54 = f32[2,1024]{1,0:T(2,128)S(1)} collective-permute-done((f32[2,1024]{1,0:T(2,128)S(1)}, f32[2,1024]{1,0:T(2,128)S(1)}, u32[]{:S(2)}, u32[]{:S(2)}) %collective-permute-start.54) | collective-permute-done | bytes 8224 | tf_op jit(solution)/shard_map/ppermute | solution.py:58
  422.5 6.7 %collective-permute-done.55 = f32[2,1024]{1,0:T(2,128)S(1)} collective-permute-done((f32[2,1024]{1,0:T(2,128)S(1)}, f32[2,1024]{1,0:T(2,128)S(1)}, u32[]{:S(2)}, u32[]{:S(2)}) %collective-permute-start.55) | collective-permute-done | bytes 8224 | tf_op jit(solution)/shard_map/ppermute | solution.py:58
  429.2 3.6 collective-permute-done.56
  437.1 5.2 %collective-permute-start.75 = (bf16[2,256,256]{2,1,0:T(8,128)(2,1)}, bf16[2,256,256]{2,1,0:T(8,128)(2,1)S(1)}, u32[]{:S(2)}, u32[]{:S(2)}) collective-permute-start(bf16[2,256,256]{2,1,0:T(8,128)(2,1)} %shard_map.169), channel_id=1, source_target_pairs={{0,16},{1,17},{2,18},{3,19},{4,20},{5,21},{6,22},{7,23},{8,24},{9,... | collective-permute-start | bytes 786440 | tf_op jit(solution)/shard_map/ppermute | solution.py:883
  453.2 5.2 %collective-permute-done.71.rest_1_ = bf16[4,256,256]{2,1,0:T(8,128)(2,1)S(1)} collective-permute-done((bf16[4,256,256]{2,1,0:T(8,128)(2,1)S(1)}, bf16[4,256,256]{2,1,0:T(8,128)(2,1)S(1)}, u32[]{:S(2)}, u32[]{:S(2)}) %collective-permute-start.71) | collective-permute-done | bytes 524320 | tf_op jit(solution)/shard_map/ppermute | solution.py:65
  458.3 3.3 collective-permute-start.63
  469.6 5.5 %collective-permute-done.63.rest_3_ = bf16[4,256,256]{2,1,0:T(8,128)(2,1)S(1)} collective-permute-done((bf16[4,256,256]{2,1,0:T(8,128)(2,1)S(1)}, bf16[4,256,256]{2,1,0:T(8,128)(2,1)S(1)}, u32[]{:S(2)}, u32[]{:S(2)}) %collective-permute-start.63) | collective-permute-done | bytes 524320 | tf_op jit(solution)/shard_map/ppermute | solution.py:65
  482.0 6.8 %shard_map.170 = (f32[1024,1024]{1,0:T(8,128)}, f32[1024,1024]{1,0:T(8,128)}) custom-call(s32[5]{0:T(128)} %pad_add_fusion.info, bf16[8,256,256]{2,1,0:T(8,128)(2,1)} %copy-done.3, bf16[8,256,256]{2,1,0:T(8,128)(2,1)} %copy-done.6, bf16[8,256,256]{2,1,0:T(8,128)(2,1)} %copy-done.7, bf16[4,256,256]{2,1,0:T(8,128)(2,1)} %copy-done.39, ...), custom_call_target="tpu_custom_call" | custom-call | bytes 16777216 | tf_op jit(solution)/shard_map/pallas_call | solution.py:42
  490.4 4.5 shard_map.171
  (352 shorter events, 157.1 us)
Async XLA Ops:
  2.2 23.7 %collective-permute-start.1 = (bf16[3,1024,256]{2,1,0:T(8,128)(2,1)}, bf16[3,1024,256]{2,1,0:T(8,128)(2,1)}, u32[]{:S(2)}, u32[]{:S(2)}) collective-permute-start(bf16[3,1024,256]{2,1,0:T(8,128)(2,1)} %bitcast.44), channel_id=1, source_target_pairs={{0,16},{16,0},{1,17},{17,1},{2,18},{18,2},{3,19},{19,3},{4,20},{20... | collective-permute-start | bytes 4718600 | tf_op jit(solution)/shard_map/ppermute | solution.py:58
  2.5 64.3 %collective-permute-start.3 = (bf16[1024,1024]{1,0:T(8,128)(2,1)}, bf16[1024,1024]{1,0:T(8,128)(2,1)S(1)}, u32[]{:S(2)}, u32[]{:S(2)}) collective-permute-start(bf16[1024,1024]{1,0:T(8,128)(2,1)} %bitcast.36), channel_id=1, source_target_pairs={{0,16},{16,0},{1,17},{17,1},{2,18},{18,2},{3,19},{19,3},{4,20},{20... | collective-permute-start | bytes 6291464 | tf_op jit(solution)/shard_map/ppermute | solution.py:58
  2.7 64.2 %collective-permute-start.4 = (bf16[1024,1024]{1,0:T(8,128)(2,1)}, bf16[1024,1024]{1,0:T(8,128)(2,1)}, u32[]{:S(2)}, u32[]{:S(2)}) collective-permute-start(bf16[1024,1024]{1,0:T(8,128)(2,1)} %bitcast.40), channel_id=1, source_target_pairs={{0,16},{16,0},{1,17},{17,1},{2,18},{18,2},{3,19},{19,3},{4,20},{20... | collective-permute-start | bytes 6291464 | tf_op jit(solution)/shard_map/ppermute | solution.py:58
  3.0 22.9 %collective-permute-start.2 = (bf16[256,1024]{1,0:T(8,128)(2,1)}, bf16[256,1024]{1,0:T(8,128)(2,1)S(1)}, u32[]{:S(2)}, u32[]{:S(2)}) collective-permute-start(bf16[256,1024]{1,0:T(8,128)(2,1)} %bitcast.50), channel_id=1, source_target_pairs={{0,16},{16,0},{1,17},{17,1},{2,18},{18,2},{3,19},{19,3},{4,20},{20... | collective-permute-start | bytes 1572872 | tf_op jit(solution)/shard_map/ppermute | solution.py:58
  36.2 36.0 %all-to-all-start = ((bf16[4,64,1024]{2,1,0:T(8,128)(2,1)}), bf16[4,64,1024]{2,1,0:T(8,128)(2,1)S(1)}, u32[]{:S(2)}, u32[]{:S(2)}) async-start(bf16[4,64,1024]{2,1,0:T(8,128)(2,1)} %get-tuple-element.142), calls=%async_computation | async-start | bytes 1048576 | tf_op jit(solution)/shard_map/all_to_all | solution.py:922
  39.7 17.1 %collective-permute-start.6 = (bf16[2,256,256]{2,1,0:T(8,128)(2,1)}, bf16[2,256,256]{2,1,0:T(8,128)(2,1)S(1)}, u32[]{:S(2)}, u32[]{:S(2)}) collective-permute-start(bf16[2,256,256]{2,1,0:T(8,128)(2,1)} %get-tuple-element.156), channel_id=1, source_target_pairs={{0,1},{1,0},{2,3},{3,2},{4,5},{5,4},{6,7},{7,6},{8,9},{9,8},{10,11... | collective-permute-start | bytes 786440 | tf_op jit(solution)/shard_map/ppermute | solution.py:58
  44.2 18.0 %collective-permute-start.8 = (bf16[2,256,256]{2,1,0:T(8,128)(2,1)S(1)}, bf16[2,256,256]{2,1,0:T(8,128)(2,1)S(1)}, u32[]{:S(2)}, u32[]{:S(2)}) collective-permute-start(bf16[2,256,256]{2,1,0:T(8,128)(2,1)S(1)} %collective-permute-done.7.rest_2_), channel_id=1, source_target_pairs={{0,1},{1,0},{2,3},{3,2},{4,5},{5,4},{6,7},{7,6},{8,9},{9,8},{10,11... | collective-permute-start | bytes 786440 | tf_op jit(solution)/shard_map/ppermute | solution.py:58
  63.8 46.2 %collective-permute-start.9 = (bf16[3,2,256,256]{3,2,0,1:T(8,128)(2,1)}, bf16[3,2,256,256]{3,2,0,1:T(8,128)(2,1)S(1)}, u32[]{:S(2)}, u32[]{:S(2)}) collective-permute-start(bf16[3,2,256,256]{3,2,0,1:T(8,128)(2,1)} %pad_maximum_fusion.2), channel_id=1, source_target_pairs={{0,4},{4,0},{8,12},{12,8},{1,5},{5,1},{9,13},{13,9},{2,6},{6,2},{1... | collective-permute-start | bytes 2359304 | tf_op jit(solution)/shard_map/ppermute | solution.py:58
  65.3 61.0 %collective-permute-start.10 = (bf16[3,2,256,256]{3,2,0,1:T(8,128)(2,1)}, bf16[3,2,256,256]{3,2,0,1:T(8,128)(2,1)}, u32[]{:S(2)}, u32[]{:S(2)}) collective-permute-start(bf16[3,2,256,256]{3,2,0,1:T(8,128)(2,1)} %pad_maximum_fusion.2), channel_id=1, source_target_pairs={{0,8},{4,12},{8,0},{12,4},{1,9},{5,13},{9,1},{13,5},{2,10},{6,14},... | collective-permute-start | bytes 2359304 | tf_op jit(solution)/shard_map/ppermute | solution.py:58
  72.1 37.2 %collective-permute-start.14 = (bf16[4,256,256]{2,1,0:T(8,128)(2,1)}, bf16[4,256,256]{2,1,0:T(8,128)(2,1)S(1)}, u32[]{:S(2)}, u32[]{:S(2)}) collective-permute-start(bf16[4,256,256]{2,1,0:T(8,128)(2,1)} %get-tuple-element.161), channel_id=1, source_target_pairs={{0,1},{1,0},{2,3},{3,2},{4,5},{5,4},{6,7},{7,6},{8,9},{9,8},{10,11... | collective-permute-start | bytes 1572872 | tf_op jit(solution)/shard_map/ppermute | solution.py:58
  98.7 27.6 %collective-permute-start.19 = (bf16[4,256,256]{2,1,0:T(8,128)(2,1)}, bf16[4,256,256]{2,1,0:T(8,128)(2,1)S(1)}, u32[]{:S(2)}, u32[]{:S(2)}) collective-permute-start(bf16[4,256,256]{2,1,0:T(8,128)(2,1)} %get-tuple-element.161), channel_id=1, source_target_pairs={{0,2},{1,3},{2,0},{3,1},{4,6},{5,7},{6,4},{7,5},{8,10},{9,11},{10,... | collective-permute-start | bytes 1572872 | tf_op jit(solution)/shard_map/ppermute | solution.py:58
  105.1 26.8 %all-to-all-start.1 = ((bf16[4,64,1024]{2,1,0:T(8,128)(2,1)}), bf16[4,64,1024]{2,1,0:T(8,128)(2,1)S(1)}, u32[]{:S(2)}, u32[]{:S(2)}) async-start(bf16[4,64,1024]{2,1,0:T(8,128)(2,1)} %get-tuple-element.152), calls=%async_computation.1 | async-start | bytes 1048576 | tf_op jit(solution)/shard_map/all_to_all | solution.py:922
  109.4 25.1 %collective-permute-start.15 = (bf16[4,256,256]{2,1,0:T(8,128)(2,1)S(1)}, bf16[4,256,256]{2,1,0:T(8,128)(2,1)S(1)}, u32[]{:S(2)}, u32[]{:S(2)}) collective-permute-start(bf16[4,256,256]{2,1,0:T(8,128)(2,1)S(1)} %collective-permute-done.14.rest_1_), channel_id=1, source_target_pairs={{0,4},{4,0},{8,12},{12,8},{1,5},{5,1},{9,13},{13,9},{2,6},{6,2},{1... | collective-permute-start | bytes 1572872 | tf_op jit(solution)/shard_map/ppermute | solution.py:58
  110.8 27.3 %collective-permute-start.11 = (bf16[3,256,256]{2,1,0:T(8,128)(2,1)}, bf16[3,256,256]{2,1,0:T(8,128)(2,1)}, u32[]{:S(2)}, u32[]{:S(2)}) collective-permute-start(bf16[3,256,256]{2,1,0:T(8,128)(2,1)} %slice_bitcast_fusion.1), channel_id=1, source_target_pairs={{0,8},{4,12},{8,0},{12,4},{1,9},{5,13},{9,1},{13,5},{2,10},{6,14},... | collective-permute-start | bytes 1179656 | tf_op jit(solution)/shard_map/ppermute | solution.py:58
  126.3 16.5 %collective-permute-start.24 = (bf16[4,256,256]{2,1,0:T(8,128)(2,1)S(1)}, bf16[4,256,256]{2,1,0:T(8,128)(2,1)}, u32[]{:S(2)}, u32[]{:S(2)}) collective-permute-start(bf16[4,256,256]{2,1,0:T(8,128)(2,1)S(1)} %collective-permute-done.19.rest_6_), channel_id=1, source_target_pairs={{0,1},{1,0},{2,3},{3,2},{4,5},{5,4},{6,7},{7,6},{8,9},{9,8},{10,11... | collective-permute-start | bytes 1572872 | tf_op jit(solution)/shard_map/ppermute | solution.py:58
  128.6 24.1 %collective-permute-start.16 = (bf16[4,256,256]{2,1,0:T(8,128)(2,1)S(1)}, bf16[4,256,256]{2,1,0:T(8,128)(2,1)S(1)}, u32[]{:S(2)}, u32[]{:S(2)}) collective-permute-start(bf16[4,256,256]{2,1,0:T(8,128)(2,1)S(1)} %collective-permute-done.14.rest_1_), channel_id=1, source_target_pairs={{0,8},{4,12},{8,0},{12,4},{1,9},{5,13},{9,1},{13,5},{2,10},{6,14},... | collective-permute-start | bytes 1572872 | tf_op jit(solution)/shard_map/ppermute | solution.py:58
  138.1 16.3 %collective-permute-start.21 = (bf16[4,256,256]{2,1,0:T(8,128)(2,1)S(1)}, bf16[4,256,256]{2,1,0:T(8,128)(2,1)S(1)}, u32[]{:S(2)}, u32[]{:S(2)}) collective-permute-start(bf16[4,256,256]{2,1,0:T(8,128)(2,1)S(1)} %collective-permute-done.19.rest_6_), channel_id=1, source_target_pairs={{0,8},{4,12},{8,0},{12,4},{1,9},{5,13},{9,1},{13,5},{2,10},{6,14},... | collective-permute-start | bytes 1572872 | tf_op jit(solution)/shard_map/ppermute | solution.py:58
  142.8 20.9 %collective-permute-start.25 = (bf16[4,256,256]{2,1,0:T(8,128)(2,1)}, bf16[4,256,256]{2,1,0:T(8,128)(2,1)S(1)}, u32[]{:S(2)}, u32[]{:S(2)}) collective-permute-start(bf16[4,256,256]{2,1,0:T(8,128)(2,1)} %collective-permute-done.24.rest_11_), channel_id=1, source_target_pairs={{0,4},{4,0},{8,12},{12,8},{1,5},{5,1},{9,13},{13,9},{2,6},{6,2},{1... | collective-permute-start | bytes 1572872 | tf_op jit(solution)/shard_map/ppermute | solution.py:58
  143.2 22.3 %collective-permute-start.26 = (bf16[4,256,256]{2,1,0:T(8,128)(2,1)}, bf16[4,256,256]{2,1,0:T(8,128)(2,1)S(1)}, u32[]{:S(2)}, u32[]{:S(2)}) collective-permute-start(bf16[4,256,256]{2,1,0:T(8,128)(2,1)} %collective-permute-done.24.rest_11_), channel_id=1, source_target_pairs={{0,8},{4,12},{8,0},{12,4},{1,9},{5,13},{9,1},{13,5},{2,10},{6,14},... | collective-permute-start | bytes 1572872 | tf_op jit(solution)/shard_map/ppermute | solution.py:58
  152.8 24.0 %collective-permute-start.13 = (bf16[384,1024]{1,0:T(8,128)(2,1)}, bf16[384,1024]{1,0:T(8,128)(2,1)S(1)}, u32[]{:S(2)}, u32[]{:S(2)}) collective-permute-start(bf16[384,1024]{1,0:T(8,128)(2,1)} %get-tuple-element.157.own_part), channel_id=1, source_target_pairs={{0,16},{16,0},{1,17},{17,1},{2,18},{18,2},{3,19},{19,3},{4,20},{20... | collective-permute-start | bytes 2359304 | tf_op jit(solution)/shard_map/ppermute | solution.py:58
  152.9 18.2 %collective-permute-start.17 = (bf16[2,256,256]{2,1,0:T(8,128)(2,1)S(1)}, bf16[2,256,256]{2,1,0:T(8,128)(2,1)S(1)}, u32[]{:S(2)}, u32[]{:S(2)}) collective-permute-start(bf16[2,256,256]{2,1,0:T(8,128)(2,1)S(1)} %slice.66), channel_id=1, source_target_pairs={{0,8},{4,12},{8,0},{12,4},{1,9},{5,13},{9,1},{13,5},{2,10},{6,14},... | collective-permute-start | bytes 786440 | tf_op jit(solution)/shard_map/ppermute | solution.py:58
  154.4 17.3 %collective-permute-start.18 = (bf16[2,256,256]{2,1,0:T(8,128)(2,1)S(1)}, bf16[2,256,256]{2,1,0:T(8,128)(2,1)S(1)}, u32[]{:S(2)}, u32[]{:S(2)}) collective-permute-start(bf16[2,256,256]{2,1,0:T(8,128)(2,1)S(1)} %slice.67), channel_id=1, source_target_pairs={{0,4},{4,0},{8,12},{12,8},{1,5},{5,1},{9,13},{13,9},{2,6},{6,2},{1... | collective-permute-start | bytes 786440 | tf_op jit(solution)/shard_map/ppermute | solution.py:58
  217.6 47.9 %collective-permute-start.31 = (bf16[2,8,256,256]{3,2,1,0:T(8,128)(2,1)}, bf16[2,8,256,256]{3,2,1,0:T(8,128)(2,1)S(1)}, u32[]{:S(2)}, u32[]{:S(2)}) collective-permute-start(bf16[2,8,256,256]{3,2,1,0:T(8,128)(2,1)} %get-tuple-element.196), channel_id=1, source_target_pairs={{0,4},{4,0},{8,12},{12,8},{1,5},{5,1},{9,13},{13,9},{2,6},{6,2},{1... | collective-permute-start | bytes 6291464 | tf_op jit(solution)/shard_map/ppermute | solution.py:58
  219.2 48.6 %collective-permute-start.32 = (bf16[2,8,256,256]{3,2,1,0:T(8,128)(2,1)}, bf16[2,8,256,256]{3,2,1,0:T(8,128)(2,1)}, u32[]{:S(2)}, u32[]{:S(2)}) collective-permute-start(bf16[2,8,256,256]{3,2,1,0:T(8,128)(2,1)} %get-tuple-element.197), channel_id=1, source_target_pairs={{0,8},{4,12},{8,0},{12,4},{1,9},{5,13},{9,1},{13,5},{2,10},{6,14},... | collective-permute-start | bytes 6291464 | tf_op jit(solution)/shard_map/ppermute | solution.py:58
  258.0 48.2 %collective-permute-start.35 = (bf16[4,2,2,256,256]{4,3,2,1,0:T(8,128)(2,1)}, bf16[4,2,2,256,256]{4,3,2,1,0:T(8,128)(2,1)}, u32[]{:S(2)}, u32[]{:S(2)}) collective-permute-start(bf16[4,2,2,256,256]{4,3,2,1,0:T(8,128)(2,1)} %get-tuple-element.210), channel_id=1, source_target_pairs={{0,16},{16,0},{1,17},{17,1},{2,18},{18,2},{3,19},{19,3},{4,20},{20... | collective-permute-start | bytes 6291464 | tf_op jit(solution)/shard_map/ppermute | solution.py:58
  258.0 19.6 %all-to-all-start.2 = ((bf16[4,64,1024]{2,1,0:T(8,128)(2,1)}), bf16[4,64,1024]{2,1,0:T(8,128)(2,1)}, u32[]{:S(2)}, u32[]{:S(2)}) async-start(bf16[4,64,1024]{2,1,0:T(8,128)(2,1)} %get-tuple-element.189), calls=%async_computation.2 | async-start | bytes 1048576 | tf_op jit(solution)/shard_map/all_to_all | solution.py:922
  262.2 40.5 %collective-permute-start.33 = (bf16[2,4,256,256]{3,2,1,0:T(8,128)(2,1)}, bf16[2,4,256,256]{3,2,1,0:T(8,128)(2,1)S(1)}, u32[]{:S(2)}, u32[]{:S(2)}) collective-permute-start(bf16[2,4,256,256]{3,2,1,0:T(8,128)(2,1)} %get-tuple-element.206), channel_id=1, source_target_pairs={{0,4},{4,0},{8,12},{12,8},{1,5},{5,1},{9,13},{13,9},{2,6},{6,2},{1... | collective-permute-start | bytes 3145736 | tf_op jit(solution)/shard_map/ppermute | solution.py:58
  262.8 39.9 %collective-permute-start.34 = (bf16[2,4,256,256]{3,2,1,0:T(8,128)(2,1)}, bf16[2,4,256,256]{3,2,1,0:T(8,128)(2,1)}, u32[]{:S(2)}, u32[]{:S(2)}) collective-permute-start(bf16[2,4,256,256]{3,2,1,0:T(8,128)(2,1)} %get-tuple-element.207), channel_id=1, source_target_pairs={{0,8},{4,12},{8,0},{12,4},{1,9},{5,13},{9,1},{13,5},{2,10},{6,14},... | collective-permute-start | bytes 3145736 | tf_op jit(solution)/shard_map/ppermute | solution.py:58
  271.5 47.6 %collective-permute-start.36 = (bf16[8,256,256]{2,1,0:T(8,128)(2,1)}, bf16[8,256,256]{2,1,0:T(8,128)(2,1)S(1)}, u32[]{:S(2)}, u32[]{:S(2)}) collective-permute-start(bf16[8,256,256]{2,1,0:T(8,128)(2,1)} %get-tuple-element.217), channel_id=1, source_target_pairs={{0,8},{4,12},{8,0},{12,4},{1,9},{5,13},{9,1},{13,5},{2,10},{6,14},... | collective-permute-start | bytes 3145736 | tf_op jit(solution)/shard_map/ppermute | solution.py:58
  271.5 47.6 %collective-permute-start.37 = (bf16[8,256,256]{2,1,0:T(8,128)(2,1)}, bf16[8,256,256]{2,1,0:T(8,128)(2,1)}, u32[]{:S(2)}, u32[]{:S(2)}) collective-permute-start(bf16[8,256,256]{2,1,0:T(8,128)(2,1)} %get-tuple-element.198), channel_id=1, source_target_pairs={{0,4},{4,0},{8,12},{12,8},{1,5},{5,1},{9,13},{13,9},{2,6},{6,2},{1... | collective-permute-start | bytes 3145736 | tf_op jit(solution)/shard_map/ppermute | solution.py:58
  313.4 21.1 %all-to-all-start.3 = ((bf16[4,64,1024]{2,1,0:T(8,128)(2,1)}), bf16[4,64,1024]{2,1,0:T(8,128)(2,1)S(1)}, u32[]{:S(2)}, u32[]{:S(2)}) async-start(bf16[4,64,1024]{2,1,0:T(8,128)(2,1)} %get-tuple-element.204), calls=%async_computation.3 | async-start | bytes 1048576 | tf_op jit(solution)/shard_map/all_to_all | solution.py:922
  324.8 45.8 %collective-permute-start.49 = (bf16[2,4,256,256]{3,2,1,0:T(8,128)(2,1)}, bf16[2,4,256,256]{3,2,1,0:T(8,128)(2,1)S(1)}, u32[]{:S(2)}, u32[]{:S(2)}) collective-permute-start(bf16[2,4,256,256]{3,2,1,0:T(8,128)(2,1)} %get-tuple-element.244), channel_id=1, source_target_pairs={{0,1},{1,0},{2,3},{3,2},{4,5},{5,4},{6,7},{7,6},{8,9},{9,8},{10,11... | collective-permute-start | bytes 3145736 | tf_op jit(solution)/shard_map/ppermute | solution.py:58
  326.8 18.1 %collective-permute-start.41 = (bf16[2,2,256,256]{3,2,1,0:T(8,128)(2,1)}, bf16[2,2,256,256]{3,2,1,0:T(8,128)(2,1)S(1)}, u32[]{:S(2)}, u32[]{:S(2)}) collective-permute-start(bf16[2,2,256,256]{3,2,1,0:T(8,128)(2,1)} %get-tuple-element.231), channel_id=1, source_target_pairs={{0,4},{4,0},{8,12},{12,8},{1,5},{5,1},{9,13},{13,9},{2,6},{6,2},{1... | collective-permute-start | bytes 1572872 | tf_op jit(solution)/shard_map/ppermute | solution.py:58
  332.6 17.3 %collective-permute-start.43 = (bf16[2,1,256,256]{3,2,1,0:T(8,128)(2,1)}, bf16[2,1,256,256]{3,2,1,0:T(8,128)(2,1)S(1)}, u32[]{:S(2)}, u32[]{:S(2)}) collective-permute-start(bf16[2,1,256,256]{3,2,1,0:T(8,128)(2,1)} %get-tuple-element.235), channel_id=1, source_target_pairs={{0,4},{4,0},{8,12},{12,8},{1,5},{5,1},{9,13},{13,9},{2,6},{6,2},{1... | collective-permute-start | bytes 786440 | tf_op jit(solution)/shard_map/ppermute | solution.py:58
  333.7 16.2 %collective-permute-start.44 = (bf16[2,1,256,256]{3,2,1,0:T(8,128)(2,1)}, bf16[2,1,256,256]{3,2,1,0:T(8,128)(2,1)S(1)}, u32[]{:S(2)}, u32[]{:S(2)}) collective-permute-start(bf16[2,1,256,256]{3,2,1,0:T(8,128)(2,1)} %get-tuple-element.236), channel_id=1, source_target_pairs={{0,8},{4,12},{8,0},{12,4},{1,9},{5,13},{9,1},{13,5},{2,10},{6,14},... | collective-permute-start | bytes 786440 | tf_op jit(solution)/shard_map/ppermute | solution.py:58
  359.9 18.7 %collective-permute-start.50 = (bf16[384,1024]{1,0:T(8,128)(2,1)}, bf16[384,1024]{1,0:T(8,128)(2,1)S(1)}, u32[]{:S(2)}, u32[]{:S(2)}) collective-permute-start(bf16[384,1024]{1,0:T(8,128)(2,1)} %shard_map.162.own_part), channel_id=1, source_target_pairs={{0,16},{16,0},{1,17},{17,1},{2,18},{18,2},{3,19},{19,3},{4,20},{20... | collective-permute-start | bytes 2359304 | tf_op jit(solution)/shard_map/ppermute | solution.py:58
  362.9 19.4 %collective-permute-start.57 = (bf16[2,2,256,256]{3,2,1,0:T(8,128)(2,1)}, bf16[2,2,256,256]{3,2,1,0:T(8,128)(2,1)S(1)}, u32[]{:S(2)}, u32[]{:S(2)}) collective-permute-start(bf16[2,2,256,256]{3,2,1,0:T(8,128)(2,1)} %get-tuple-element.252), channel_id=1, source_target_pairs={{0,1},{1,0},{2,3},{3,2},{4,5},{5,4},{6,7},{7,6},{8,9},{9,8},{10,11... | collective-permute-start | bytes 1572872 | tf_op jit(solution)/shard_map/ppermute | solution.py:58
  373.8 25.8 %collective-permute-start.58 = (bf16[4,256,256]{2,1,0:T(8,128)(2,1)}, bf16[4,256,256]{2,1,0:T(8,128)(2,1)S(1)}, u32[]{:S(2)}, u32[]{:S(2)}) collective-permute-start(bf16[4,256,256]{2,1,0:T(8,128)(2,1)} %shard_map.165), channel_id=1, source_target_pairs={{0,2},{1,3},{2,0},{3,1},{4,6},{5,7},{6,4},{7,5},{8,10},{9,11},{10,... | collective-permute-start | bytes 1572872 | tf_op jit(solution)/shard_map/ppermute | solution.py:58
  376.1 28.1 %collective-permute-start.60 = (bf16[4,256,256]{2,1,0:T(8,128)(2,1)S(1)}, bf16[4,256,256]{2,1,0:T(8,128)(2,1)S(1)}, u32[]{:S(2)}, u32[]{:S(2)}) collective-permute-start(bf16[4,256,256]{2,1,0:T(8,128)(2,1)S(1)} %copy-done.18), channel_id=1, source_target_pairs={{16,0},{17,1},{18,2},{19,3},{20,4},{21,5},{22,6},{23,7},{24,8},{25... | collective-permute-start | bytes 1572872 | tf_op jit(solution)/shard_map/ppermute | solution.py:883
  377.5 26.7 %collective-permute-start.52 = (f32[2,1024]{1,0:T(2,128)S(1)}, f32[2,1024]{1,0:T(2,128)S(1)}, u32[]{:S(2)}, u32[]{:S(2)}) collective-permute-start(f32[2,1024]{1,0:T(2,128)S(1)} %pad_maximum_fusion.6), channel_id=1, source_target_pairs={{0,16},{16,0},{1,17},{17,1},{2,18},{18,2},{3,19},{19,3},{4,20},{20... | collective-permute-start | bytes 24584 | tf_op jit(solution)/shard_map/ppermute | solution.py:58
  404.3 42.2 %collective-permute-start.61 = (bf16[8,256,256]{2,1,0:T(8,128)(2,1)S(1)}, bf16[8,256,256]{2,1,0:T(8,128)(2,1)S(1)}, u32[]{:S(2)}, u32[]{:S(2)}) collective-permute-start(bf16[8,256,256]{2,1,0:T(8,128)(2,1)S(1)} %pad_maximum_fusion.rest_0_), channel_id=1, source_target_pairs={{0,4},{4,0},{8,12},{12,8},{1,5},{5,1},{9,13},{13,9},{2,6},{6,2},{1... | collective-permute-start | bytes 3145736 | tf_op jit(solution)/shard_map/ppermute | solution.py:65
  408.3 42.0 %collective-permute-start.62 = (bf16[8,256,256]{2,1,0:T(8,128)(2,1)S(1)}, bf16[8,256,256]{2,1,0:T(8,128)(2,1)S(1)}, u32[]{:S(2)}, u32[]{:S(2)}) collective-permute-start(bf16[8,256,256]{2,1,0:T(8,128)(2,1)S(1)} %pad_maximum_fusion.rest_0_), channel_id=1, source_target_pairs={{0,8},{4,12},{8,0},{12,4},{1,9},{5,13},{9,1},{13,5},{2,10},{6,14},... | collective-permute-start | bytes 3145736 | tf_op jit(solution)/shard_map/ppermute | solution.py:65
  411.4 22.7 %collective-permute-start.59 = (bf16[2,256,256]{2,1,0:T(8,128)(2,1)S(1)}, bf16[2,256,256]{2,1,0:T(8,128)(2,1)S(1)}, u32[]{:S(2)}, u32[]{:S(2)}) collective-permute-start(bf16[2,256,256]{2,1,0:T(8,128)(2,1)S(1)} %copy-done.47), channel_id=1, source_target_pairs={{0,2},{1,3},{2,0},{3,1},{4,6},{5,7},{6,4},{7,5},{8,10},{9,11},{10,... | collective-permute-start | bytes 786440 | tf_op jit(solution)/shard_map/ppermute | solution.py:58
  414.9 36.1 %collective-permute-start.66 = (bf16[8,256,256]{2,1,0:T(8,128)(2,1)S(1)}, bf16[8,256,256]{2,1,0:T(8,128)(2,1)S(1)}, u32[]{:S(2)}, u32[]{:S(2)}) collective-permute-start(bf16[8,256,256]{2,1,0:T(8,128)(2,1)S(1)} %pad_maximum_fusion.1.rest_5_), channel_id=1, source_target_pairs={{16,20},{20,16},{24,28},{28,24},{17,21},{21,17},{25,29},{29,25},{1... | collective-permute-start | bytes 3145736 | tf_op jit(solution)/shard_map/ppermute | solution.py:65
  434.1 29.9 %collective-permute-start.67 = (bf16[8,256,256]{2,1,0:T(8,128)(2,1)S(1)}, bf16[8,256,256]{2,1,0:T(8,128)(2,1)S(1)}, u32[]{:S(2)}, u32[]{:S(2)}) collective-permute-start(bf16[8,256,256]{2,1,0:T(8,128)(2,1)S(1)} %pad_maximum_fusion.1.rest_5_), channel_id=1, source_target_pairs={{16,24},{20,28},{24,16},{28,20},{17,25},{21,29},{25,17},{29,21},{1... | collective-permute-start | bytes 3145736 | tf_op jit(solution)/shard_map/ppermute | solution.py:65
  458.3 16.7 %collective-permute-start.63 = (bf16[4,256,256]{2,1,0:T(8,128)(2,1)S(1)}, bf16[4,256,256]{2,1,0:T(8,128)(2,1)S(1)}, u32[]{:S(2)}, u32[]{:S(2)}) collective-permute-start(bf16[4,256,256]{2,1,0:T(8,128)(2,1)S(1)} %slice.72), channel_id=1, source_target_pairs={{0,8},{4,12},{8,0},{12,4},{1,9},{5,13},{9,1},{13,5},{2,10},{6,14},... | collective-permute-start | bytes 1572872 | tf_op jit(solution)/shard_map/ppermute | solution.py:65
  461.6 17.2 %collective-permute-start.64 = (bf16[4,256,256]{2,1,0:T(8,128)(2,1)S(1)}, bf16[4,256,256]{2,1,0:T(8,128)(2,1)}, u32[]{:S(2)}, u32[]{:S(2)}) collective-permute-start(bf16[4,256,256]{2,1,0:T(8,128)(2,1)S(1)} %slice.73), channel_id=1, source_target_pairs={{0,4},{4,0},{8,12},{12,8},{1,5},{5,1},{9,13},{13,9},{2,6},{6,2},{1... | collective-permute-start | bytes 1572872 | tf_op jit(solution)/shard_map/ppermute | solution.py:65
  466.5 22.4 %collective-permute-start.73 = (bf16[2,256,256]{2,1,0:T(8,128)(2,1)S(1)}, bf16[2,256,256]{2,1,0:T(8,128)(2,1)S(1)}, u32[]{:S(2)}, u32[]{:S(2)}) collective-permute-start(bf16[2,256,256]{2,1,0:T(8,128)(2,1)S(1)} %slice.76), channel_id=1, source_target_pairs={{0,8},{4,12},{8,0},{12,4},{1,9},{5,13},{9,1},{13,5},{2,10},{6,14},... | collective-permute-start | bytes 786440 | tf_op jit(solution)/shard_map/ppermute | solution.py:65
  (114 other events, 1080.5 us)

commit v4 on v3

--- a/solution.py
+++ b/solution.py
@@ -20,6 +20,7 @@
 SM = pl.BlockSpec(memory_space=pltpu.SMEM)
 ANY = pl.BlockSpec(memory_space=pltpu.HBM)
 MIB = 1 << 20
+PACE = 2 * 10**8
 
 LOW, SEC, SHARD, LENGTHS = 0, 1, 2, 3
 
@@ -30,14 +31,17 @@
 
 class Order:
     def __init__(self):
-        self.token = None
+        self.tokens = ()
 
     def after(self, value):
-        if self.token is None:
+        if not self.tokens:
             return value
-        return lax.optimization_barrier((value, self.token))[0]
-
-    def call(self, body, outs, args, specs, scratch=(), limit=56, flops=0, moved=0, grid=()):
+        return lax.optimization_barrier((value,) + self.tokens)[0]
+
+    def until(self, *values):
+        self.tokens += values
+
+    def call(self, body, outs, args, specs, scratch=(), limit=56, us=2.0, grid=()):
         args = (self.after(args[0]),) + tuple(args[1:])
         results = pl.pallas_call(
             body,
@@ -47,22 +51,17 @@
             out_specs=tuple(VM for _ in outs),
             scratch_shapes=list(scratch),
             compiler_params=pltpu.CompilerParams(vmem_limit_bytes=limit * MIB),
-            cost_estimate=pl.CostEstimate(flops=flops, bytes_accessed=moved, transcendentals=0),
+            cost_estimate=pl.CostEstimate(
+                flops=int(us * PACE), bytes_accessed=0, transcendentals=0
+            ),
         )(*args)
-        self.token = results[-1]
+        self.tokens = (results[-1],)
         return results
 
 
 def swap(value, axis, flip):
     count = lax.axis_size(axis)
     return lax.ppermute(value, axis, [(i, i ^ flip) for i in range(count)])
-
-
-def swap_one(value, axis, flip, section):
-    count = lax.axis_size(axis)
-    base = section * count
-    pairs = [(base + i, base + (i ^ flip)) for i in range(count)]
-    return lax.ppermute(value, ("section", axis), pairs)
 
 
 def dot(a, b):
@@ -212,18 +211,41 @@
         made.pick(True, sec, own_out.at[:, at], other_out.at[:, at], out.at[:, span(m)])
 
 
-def global_attention_kernel(info, rows, own_qkv, other_qkv, own_out, other_out,
-                            packed, probs, mixed, partial, qkv, out, sems):
+def by_shard(info, blocks):
+    count = blocks.shape[0]
+    return jnp.concatenate([blocks[info[SHARD] ^ k] for k in range(count)], axis=0)
+
+
+def other_half(info, width):
+    half = width // 2
+    return pl.ds(pl.multiple_of((1 - info[SEC]) * half, half), half)
+
+
+def spread_blocks(info, target, values):
+    frames = target.shape[1]
+    for k in range(target.shape[0]):
+        target[info[SHARD] ^ k] = values[k * frames : (k + 1) * frames].astype(low16)
+
+
+def row_places(info, count, frames, dimension):
+    at = lax.broadcasted_iota(jnp.int32, (count, count), dimension)
+    return (lax.div(at, frames) ^ info[SHARD]) * frames + lax.rem(at, frames)
+
+
+def global_attention_kernel(info, *rest):
+    (blocks, own_qkv, other_qkv, own_out, other_out,
+     rows, packed, probs, mixed, given, partial, qkv, out, sems) = rest
     low, sec = info[LOW], info[SEC]
     made = Copies(sems)
     fetch_attention(made, low, sec, own_qkv, other_qkv, own_out, other_out, qkv, out)
-    count = rows.shape[0]
+    count, frames = rows.shape[0], blocks.shape[1]
     length = info[LENGTHS + sec]
-    query_at = lax.broadcasted_iota(jnp.int32, (count, count), 0)
-    key_at = lax.broadcasted_iota(jnp.int32, (count, count), 1)
+    query_at = row_places(info, count, frames, 0)
+    key_at = row_places(info, count, frames, 1)
     allowed = (key_at <= query_at) & (key_at < length)
+    values = by_shard(info, blocks)
+    rows[...] = values
     made.wait(0, QUARTERS)
-    values = rows[...]
     for c in range(3):
         packed[c] = dot(values, qkv[c]).astype(low16)
     heads = []
@@ -236,8 +258,9 @@
         probs[h] = exact
         heads.append(dot(exact.astype(low16), packed[2, :, lanes]).astype(low16))
     mixed[...] = jnp.concatenate(heads, axis=1)
+    given[...] = mixed[:, other_half(info, mixed.shape[1])]
     made.wait(QUARTERS)
-    partial[...] = dot(mixed[...], out[...]).astype(low16).reshape(partial.shape)
+    spread_blocks(info, partial, dot(mixed[...], out[...]))
 
 
 def total_of(arrived):
@@ -262,12 +285,14 @@
         made.pick(True, sec, own_down.at[:, at], other_down.at[:, at], down.at[:, span(m)])
 
 
-def global_feed_kernel(info, rows, own_up, other_up, own_down, other_down,
-                       lifted, active, partial, up, down, total, sems):
+def global_feed_kernel(info, *rest):
+    (blocks, own_up, other_up, own_down, other_down,
+     rows, lifted, active, given, partial, up, down, total, sems) = rest
     made = Copies(sems)
     fetch_feed(made, info[LOW], info[SEC], own_up, other_up, own_down, other_down, up, down)
+    values = by_shard(info, blocks)
+    rows[...] = values
     made.wait(0, QUARTERS)
-    values = rows[...]
     for t in range(up.shape[1] // UNIT):
         tile = dot(values, up[:, span(t)])
         lifted[:, span(t)] = tile
@@ -277,19 +302,22 @@
             made.wait(QUARTERS)
         branch = dot(low_tile, down[span(t), :])
         total[...] = branch if t == 0 else total[...] + branch
-    partial[...] = total[...].astype(low16).reshape(partial.shape)
+    spread_blocks(info, partial, total[...])
+    given[...] = active[:, other_half(info, active.shape[1])]
 
 
 def sent_kernel(hidden, arrived, sent):
     sent[...] = (hidden[...] + total_of(arrived)).astype(low16)
 
 
-def global_feed_back_kernel(info, top, lifted, own_up, other_up, own_down, other_down,
-                            grad_lifted, partial, up, down, total, sems):
+def global_feed_back_kernel(info, *rest):
+    (blocks, lifted, own_up, other_up, own_down, other_down,
+     rows, grad_lifted, given, partial, up, down, total, sems) = rest
     made = Copies(sems)
     fetch_feed(made, info[LOW], info[SEC], own_up, other_up, own_down, other_down, up, down)
+    values = by_shard(info, blocks)
+    rows[...] = values
     made.wait(QUARTERS)
-    values = top[...]
     for t in range(up.shape[1] // UNIT):
         tile = lifted[:, span(t)]
         grad = dot_nt(values, down[span(t), :]) * gelu_slope(tile, normal_cdf(tile))
@@ -299,7 +327,8 @@
             made.wait(0, QUARTERS)
         back = dot_nt(grad, up[:, span(t)])
         total[...] = back if t == 0 else total[...] + back
-    partial[...] = total[...].astype(low16).reshape(partial.shape)
+    spread_blocks(info, partial, total[...])
+    given[...] = grad_lifted[:, other_half(info, grad_lifted.shape[1])]
 
 
 def middle_back_kernel(arrived, hidden, gain, returned, grad_hidden, mid, gain_grad):
@@ -309,13 +338,16 @@
     mid[...] = values.astype(low16)
 
 
-def global_attention_back_kernel(info, mid, packed, probs, own_qkv, other_qkv, own_out, other_out,
-                                 grads, partial, qkv, out, sems):
+def global_attention_back_kernel(info, *rest):
+    (blocks, packed, probs, own_qkv, other_qkv, own_out, other_out,
+     rows, grads, given, partial, qkv, out, sems) = rest
     low, sec = info[LOW], info[SEC]
     made = Copies(sems)
     fetch_attention(made, low, sec, own_qkv, other_qkv, own_out, other_out, qkv, out)
+    values = by_shard(info, blocks)
+    rows[...] = values
     made.wait(QUARTERS)
-    grad_mixed = dot_nt(mid[...], out[...]).astype(low16)
+    grad_mixed = dot_nt(values, out[...]).astype(low16)
     columns = [[], [], []]
     for h in range(packed.shape[2] // HEAD_DIM):
         lanes = slice(h * HEAD_DIM, (h + 1) * HEAD_DIM)
@@ -333,7 +365,8 @@
         grads[c] = jnp.concatenate(columns[c], axis=1)
         back = dot_nt(grads[c], qkv[c])
         total = back if c == 0 else total + back
-    partial[...] = total.astype(low16).reshape(partial.shape)
+    spread_blocks(info, partial, total)
+    given[...] = grads[:, :, other_half(info, grads.shape[2])]
 
 
 def start_back_kernel(info, arrived, start, gain, grad_hidden, kept, given, gain_grad, values):
@@ -346,26 +379,27 @@
 
 
 def mix_unit(refs, k, m, u):
-    whole, near, x_part, y_part, far = refs[0], refs[1:4], refs[4], refs[5], refs[6:8]
+    whole, near = refs[0], refs[1:4]
+    both = refs[4:8]
+    last = refs[8:12]
     if k == 0:
         return whole.at[m, u]
     if m == 0:
         return near[k - 1].at[u]
-    if m == 3:
-        return far[u].at[k - 1]
-    return (x_part if m == 1 else y_part).at[k - 1, u]
+    if k == 3:
+        return last[m - 1].at[u] if m < 3 else last[2 + u].at[0]
+    return both[m - 1].at[k - 1, u] if m < 3 else both[2 + u].at[k - 1]
 
 
 def feed_unit(refs, k, m, u):
     if k == 0:
         return refs[0].at[m, u]
-    base = refs[5 * k - 4 : 5 * k + 1]
     if m < 3:
-        return base[m].at[u]
-    return base[3].at[u] if u < 2 else base[4].at[u - 2]
-
-
-MIX_REFS, FEED_REFS = 8, 16
+        return refs[1 + m].at[u]
+    return refs[4].at[u] if u < 2 else refs[5].at[u - 2]
+
+
+MIX_REFS, FEED_REFS = 12, 6
 
 
 def pair_rows(a, b, size):
@@ -470,11 +504,30 @@
     partial[...] = dot(mixed[...], mix[...]).astype(low16)
 
 
-def local_feed_kernel(info, start, own_part, other_part, gain, cotangent, *rest):
-    refs = rest[:FEED_REFS]
-    (hidden, second, top, active, grad_lifted, grad_second,
-     up, down, back, sems) = rest[FEED_REFS:]
-    low = info[LOW]
+def local_top_kernel(info, cotangent, top, given):
+    low, sec = info[LOW], info[SEC]
+    utts, code_count, frames, _ = cotangent.shape
+    group = code_count * frames
+    frame_at = lax.broadcasted_iota(jnp.int32, (frames, 1), 0) + info[SHARD] * frames
+    for u in range(utts):
+        valid = frame_at < info[LENGTHS + u]
+        for c in range(code_count):
+            row = u * group + c * frames
+            for m in range(QUARTERS):
+                part = cotangent[u, c, :, pl.ds(block_at(low, m), UNIT)].astype(f32)
+                top[row : row + frames, span(m)] = jnp.where(valid, part, 0.0).astype(low16)
+    given[...] = top[pl.ds(pl.multiple_of(sec * group, group), group), :]
+
+
+def local_norm_kernel(info, start, own_part, other_part, gain, hidden, second, given):
+    values = start[...] + (own_part[...].astype(f32) + other_part[...].astype(f32))
+    hidden[...] = values
+    second[...] = (values * factor_of(values) * gain[1:2, :]).astype(low16)
+    group = given.shape[0]
+    given[...] = second[pl.ds(pl.multiple_of(info[SEC] * group, group), group), :]
+
+
+def feed_tiles(refs, second, top, active, grad_lifted, up, down, back, sems):
     tiles = active.shape[0]
     made = Copies(sems)
     for t in range(tiles):
@@ -482,18 +535,6 @@
             made.start(feed_unit(refs, t // 2, m, t % 2), up.at[t, span(m), :])
         for m in range(QUARTERS):
             made.start(feed_unit(refs, t // 2, m, 2 + t % 2), down.at[t, :, span(m)])
-    utts, code_count, frames, _ = cotangent.shape
-    frame_at = lax.broadcasted_iota(jnp.int32, (frames, 1), 0) + info[SHARD] * frames
-    for u in range(utts):
-        valid = frame_at < info[LENGTHS + u]
-        for c in range(code_count):
-            row = (u * code_count + c) * frames
-            for m in range(QUARTERS):
-                part = cotangent[u, c, :, pl.ds(block_at(low, m), UNIT)].astype(f32)
-                top[row : row + frames, span(m)] = jnp.where(valid, part, 0.0).astype(low16)
-    values = start[...] + (own_part[...].astype(f32) + other_part[...].astype(f32))
-    hidden[...] = values
-    second[...] = (values * factor_of(values) * gain[1:2, :]).astype(low16)
     back[...] = jnp.zeros_like(back)
 
     @pl.loop(0, tiles)
@@ -508,17 +549,49 @@
             ).wait()
         tile = dot(second[...], up[t])
         cdf = normal_cdf(tile)
-        low_tile = (tile * cdf).astype(low16)
-        active[t] = low_tile
+        active[t] = (tile * cdf).astype(low16)
         grad = (dot_nt(top[...], down[t]) * gelu_slope(tile, cdf)).astype(low16)
         grad_lifted[t] = grad
         back[...] += dot_nt(grad, up[t])
 
+
+def local_feed_kernel(second, top, *rest):
+    refs, (active, grad_lifted, grad_second, up, down, back, sems) = (
+        rest[:FEED_REFS], rest[FEED_REFS:]
+    )
+    feed_tiles(refs, second, top, active, grad_lifted, up, down, back, sems)
     grad_second[...] = back[...].astype(low16)
 
 
-def local_attention_back_kernel(hidden, own_back, other_back, top, gain, query_keys, values_in,
-                                probs, *rest):
+def far_feed_kernel(second_same, second_cross, top_same, top_cross, *rest):
+    refs = rest[:FEED_REFS]
+    (active, grad_lifted, second, top, same, cross, up, down, back, sems) = rest[FEED_REFS:]
+    group = same.shape[0]
+    second[:group] = second_same[...]
+    second[group:] = second_cross[...]
+    top[:group] = top_same[...]
+    top[group:] = top_cross[...]
+    feed_tiles(refs, second, top, active, grad_lifted, up, down, back, sems)
+    same[...] = back[:group].astype(low16)
+    cross[...] = back[group:].astype(low16)
+
+
+def pair_kernel(a, b, total):
+    total[...] = add16(a[...], b[...])
+
+
+def with_far(sec, rows, own, other, far_same, far_cross):
+    group = far_same.shape[0]
+    parts = []
+    for u in range(rows // group):
+        at = slice(u * group, (u + 1) * group)
+        far = jnp.where(sec == u, far_same[...], far_cross[...]).astype(f32)
+        parts.append(own[at, :].astype(f32) + other[at, :].astype(f32) + far)
+    return jnp.concatenate(parts, axis=0)
+
+
+def local_attention_back_kernel(info, hidden, own_back, other_back, far_same, far_cross, top, gain,
+                                query_keys, values_in, probs, *rest):
     refs = rest[:MIX_REFS]
     (grad_hidden, mid, grad_query_keys, grad_values, grad_first, gain_grad,
      weights, mix, total, sems) = rest[MIX_REFS:]
@@ -532,7 +605,7 @@
                 for m in range(QUARTERS)
             ]
         )
-    upstream = own_back[...].astype(f32) + other_back[...].astype(f32)
+    upstream = with_far(info[SEC], hidden.shape[0], own_back, other_back, far_same, far_cross)
     through, gain_grad[...] = norm_back(hidden[...], gain[1:2, :], upstream)
     grads = top[...].astype(f32) + through
     grad_hidden[...] = grads
@@ -606,19 +679,23 @@
                 code_part[u, c, :, span(j)] = values[row : row + frames, at]
 
 
-def output_kernel(info, hidden, own_part, other_part, output):
+def output_kernel(info, hidden, own_part, other_part, far_same, far_cross, output):
     low, sec = info[LOW], info[SEC]
     utts, code_count, frames, _ = output.shape
+    group = code_count * frames
     frame_at = lax.broadcasted_iota(jnp.int32, (frames, 1), 0) + info[SHARD] * frames
     for u in range(utts):
         valid = frame_at < info[LENGTHS + u]
         for c in range(code_count):
-            row = (u * code_count + c) * frames
-            rows = slice(row, row + frames)
+            rows = slice(u * group + c * frames, u * group + (c + 1) * frames)
+            inner = slice(c * frames, (c + 1) * frames)
             for j in range(2):
                 at = pl.ds(block_at(low, 2 * sec + j), UNIT)
+                far = jnp.where(sec == u, far_same[inner, at], far_cross[inner, at])
                 value = hidden[rows, at] + (
-                    own_part[rows, at].astype(f32) + other_part[rows, at].astype(f32)
+                    own_part[rows, at].astype(f32)
+                    + other_part[rows, at].astype(f32)
+                    + far.astype(f32)
                 )
                 output[u, c, :, span(j)] = jnp.where(valid, value, 0.0).astype(low16)
 
@@ -626,9 +703,9 @@
 SEND_A, KEEP_A, SEND_B, KEEP_B = (1, 3), (0, 2), (2, 3), (0, 1)
 
 
-def local_drop_kernel(active, *rest):
-    refs, (branch_out, down, branch, sems) = rest[:FEED_REFS], rest[FEED_REFS:]
-    tiles = active.shape[0]
+def local_drop_kernel(own_active, far_active, *rest):
+    refs, (own_branch, same, cross, down, branch, sems) = rest[:FEED_REFS], rest[FEED_REFS:]
+    tiles, count, _ = own_active.shape
     made = Copies(sems)
     for t in range(tiles):
         for m in range(QUARTERS):
@@ -641,24 +718,35 @@
             pltpu.make_async_copy(
                 refs[0].at[0, 0], down.at[t, :, span(m)], sems.at[QUARTERS * t + m]
             ).wait()
-        branch[...] += dot(active[t], down[t])
-
-    branch_out[...] = branch[...].astype(low16)
-
-
-def local_feed_grad_kernel(second, grad_lifted, active, top,
-                           send_a, send_b, keep_a, keep_b, turned):
-    turned[...] = jnp.transpose(second[...])
-    for k in range(4):
+        branch[:count] += dot(own_active[t], down[t])
+        branch[count:] += dot(far_active[t], down[t])
+
+    own_branch[...] = branch[:count].astype(low16)
+    group = same.shape[0]
+    same[...] = branch[count : count + group].astype(low16)
+    cross[...] = branch[count + group :].astype(low16)
+
+
+def local_feed_grad_kernel(second, far_second, own_lifted, far_lifted, own_active, far_active,
+                           top, far_top, send_a, send_b, keep_a, keep_b, turned, tops):
+    count = second.shape[0]
+    turned[:, :count] = jnp.transpose(second[...])
+    turned[:, count:] = jnp.transpose(far_second[...])
+    tops[:count] = top[...]
+    tops[count:] = far_top[...]
+    for k in range(2):
         for part, pairs in enumerate(
             (((send_a, SEND_A), (keep_a, KEEP_A)), ((send_b, SEND_B), (keep_b, KEEP_B)))
         ):
-            right = grad_lifted[2 * k + part]
-            left = jnp.transpose(active[2 * k + part])
+            t = 2 * k + part
+            right = jnp.concatenate([own_lifted[t], far_lifted[t]], axis=0)
+            left = jnp.concatenate(
+                [jnp.transpose(own_active[t]), jnp.transpose(far_active[t])], axis=1
+            )
             for target, order in pairs:
                 for place, m in enumerate(order):
                     target[place, 2 * k] = dot(turned[span(m), :], right).astype(low16)
-                    target[place, 2 * k + 1] = dot(left, top[:, span(m)]).astype(low16)
+                    target[place, 2 * k + 1] = dot(left, tops[:, span(m)]).astype(low16)
 
 
 def local_mix_kernel(first, grad_query_keys, grad_values, mixed, mid,
@@ -679,49 +767,62 @@
                 target[place, k, half:, half:] = out[:, half:]
 
 
-def global_feed_grad_kernel(info, second, grad_lifted, active, top, away, kept, turned):
-    sec = info[SEC]
-    turned[...] = jnp.transpose(second[...])
+def by_order(send_a, send_b, keep_a, keep_b):
+    return (
+        (0, ((send_a, SEND_A), (keep_a, KEEP_A))),
+        (1, ((send_b, SEND_B), (keep_b, KEEP_B))),
+    )
+
+
+def global_feed_grad_kernel(info, second, far_second, grad_lifted, far_lifted, active, far_active,
+                            top, far_top, send_a, send_b, keep_a, keep_b, turned, tops):
+    sec, count = info[SEC], second.shape[0]
+    turned[:, :count] = jnp.transpose(second[...])
+    turned[:, count:] = jnp.transpose(far_second[...])
+    tops[:count] = top[...]
+    tops[count:] = far_top[...]
     wide = active.shape[1] // 2
-    for target, half in ((away, 1 - sec), (kept, sec)):
-        for part in range(2):
-            at = pl.ds(pl.multiple_of(half * wide + part * UNIT, UNIT), UNIT)
-            right = grad_lifted[:, at]
-            left = jnp.transpose(active[:, at])
-            for m in range(QUARTERS):
-                target[m, part, 0] = dot(turned[span(m), :], right).astype(low16)
-                target[m, part, 1] = dot(left, top[:, span(m)]).astype(low16)
-
-
-def global_mix_grad_kernel(info, first, grads, mixed, mid, away, kept, turned):
-    sec = info[SEC]
-    turned[...] = jnp.transpose(first[...])
+    for part, pairs in by_order(send_a, send_b, keep_a, keep_b):
+        at = pl.ds(pl.multiple_of(sec * wide + part * UNIT, UNIT), UNIT)
+        right = jnp.concatenate([grad_lifted[:, at], far_lifted[:, span(part)]], axis=0)
+        left = jnp.concatenate(
+            [jnp.transpose(active[:, at]), jnp.transpose(far_active[:, span(part)])], axis=1
+        )
+        for target, order in pairs:
+            for place, m in enumerate(order):
+                target[place, 0] = dot(turned[span(m), :], right).astype(low16)
+                target[place, 1] = dot(left, tops[:, span(m)]).astype(low16)
+
+
+def global_mix_grad_kernel(info, first, far_first, grads, far_grads, mixed, far_mixed, mid,
+                           far_mid, send_a, send_b, keep_a, keep_b, turned, mids):
+    sec, count = info[SEC], first.shape[0]
+    turned[:, :count] = jnp.transpose(first[...])
+    turned[:, count:] = jnp.transpose(far_first[...])
+    mids[:count] = mid[...]
+    mids[count:] = far_mid[...]
     width = mixed.shape[1] // 2
-    for target, half in ((away, 1 - sec), (kept, sec)):
-        at = pl.ds(pl.multiple_of(half * width, width), width)
-        left = jnp.transpose(mixed[:, at])
-        for m in range(QUARTERS):
-            for c in range(2):
-                target[m, 0, 0, :, c * width : (c + 1) * width] = dot(
-                    turned[span(m), :], grads[c, :, at]
-                ).astype(low16)
-            target[m, 1, 0, :, :width] = dot(turned[span(m), :], grads[2, :, at]).astype(low16)
-            out = dot(left, mid[:, span(m)]).astype(low16)
-            target[m, 1, 0, :width, width:] = out[:, :width]
-            target[m, 1, 0, width:, width:] = out[:, width:]
+    at = pl.ds(pl.multiple_of(sec * width, width), width)
+    right = [jnp.concatenate([grads[c, :, at], far_grads[c]], axis=0) for c in range(3)]
+    left = jnp.concatenate([jnp.transpose(mixed[:, at]), jnp.transpose(far_mixed[...])], axis=1)
+    for part, pairs in by_order(send_a, send_b, keep_a, keep_b):
+        for target, order in pairs:
+            for place, m in enumerate(order):
+                rows = turned[span(m), :]
+                if part == 0:
+                    for c in range(2):
+                        target[place, 0, :, c * width : (c + 1) * width] = dot(
+                            rows, right[c]
+                        ).astype(low16)
+                else:
+                    target[place, 0, :, :width] = dot(rows, right[2]).astype(low16)
+                    out = dot(left, mids[:, span(m)]).astype(low16)
+                    target[place, 0, :width, width:] = out[:, :width]
+                    target[place, 0, width:, width:] = out[:, width:]
 
 
 def add16(a, b):
     return (a.astype(f32) + b.astype(f32)).astype(low16)
-
-
-def merge_kernel(kept, arrived, send_a, send_b, keep_a, keep_b):
-    for part, pairs in enumerate(
-        (((send_a, SEND_A), (keep_a, KEEP_A)), ((send_b, SEND_B), (keep_b, KEEP_B)))
-    ):
-        for target, order in pairs:
-            for place, m in enumerate(order):
-                target[place] = add16(kept[m, part], arrived[m, part])
 
 
 def far_kernel(keep_a, from_x, keep_b, from_y, far_a, far_b):
@@ -729,30 +830,37 @@
     far_b[...] = add16(keep_b[0], from_y[0])
 
 
-def sum_kernel(*refs):
+def sum_kernel(shards, *refs):
     parts, outs = (refs[:3], refs[3:6]), refs[6:]
     for part, (keep, once, twice) in enumerate(parts):
         total = keep[0].astype(f32) + once[0].astype(f32) + twice[...].astype(f32)
         total = total.astype(low16)
-        if len(outs) == 1:
-            count = total.shape[0]
-            outs[0][part * count : (part + 1) * count] = total
+        count = total.shape[0] // shards
+        at = slice(part * count, (part + 1) * count)
+        if shards == 1:
+            outs[0][at] = total
+        elif shards == 2:
+            outs[1][0, at] = total[:count]
+            outs[0][0, at] = total[count:]
         else:
-            count = total.shape[0] // 4
             for k in range(4):
-                outs[(k + 1) % 2][k // 2, part * count : (part + 1) * count] = total[
-                    k * count : (k + 1) * count
-                ]
+                outs[(k + 1) % 2][k // 2, at] = total[k * count : (k + 1) * count]
 
 
 def far_tensor_kernel(keep, arrived, far):
     far[...] = add16(keep[0], arrived[0])
 
 
-def total_kernel(keep, once, twice, total):
-    for n in range(total.shape[0]):
-        value = keep[0, n].astype(f32) + once[0, n].astype(f32) + twice[n].astype(f32)
-        total[n] = value.astype(low16)
+def pick_kernel(info, *refs):
+    *terms, world, given, kept = refs
+    sec = info[SEC]
+    local = terms[0][0].astype(f32)
+    for term in terms[1:]:
+        local = local + (term[0] if len(term.shape) == 4 else term[...]).astype(f32)
+    local = local.astype(low16)
+    other = world[...]
+    given[...] = jnp.where(sec == 0, local, other)
+    kept[...] = jnp.where(sec == 0, other, local)
 
 
 def half_at(index, count):
@@ -761,48 +869,43 @@
     )
 
 
-def fetch_quarters(sec, refs, target, sems):
-    made = Copies(sems)
-    count = target.shape[1]
-    for index in range(3):
-        made.pick(True, sec, refs[index], refs[5 + index], target.at[index])
-    for index in range(2):
-        at = pl.ds(index * (count // 2), count // 2)
-        made.pick(True, sec, refs[3 + index], refs[8 + index], target.at[3, at])
-    return made
+def quarter_unit(refs, m, index):
+    own, x_part, y_part, far_kept, far_arrived = refs
+    count = own.shape[0] // 2
+    if m < 3:
+        return (own, x_part, y_part)[m][index].astype(f32)
+    return (far_kept[index] if index < count else far_arrived[index - count]).astype(f32)
 
 
 def feed_final_kernel(info, *rest):
-    refs, (up, down, units, sems) = rest[:10], rest[10:]
+    refs, (up, down) = rest[:5], rest[5:]
     low, sec = info[LOW], info[SEC]
-    fetch_quarters(sec, refs, units, sems).wait()
     wide = up.shape[1] // 2
-    count = units.shape[1] // 2
+    count = refs[0].shape[0] // 2
     for m in range(QUARTERS):
         at = pl.ds(block_at(low, m), UNIT)
         for source, half in ((0, sec), (count, 1 - sec)):
             for part in range(2):
                 hidden = pl.ds(pl.multiple_of(half * wide + part * UNIT, UNIT), UNIT)
-                up[at, hidden] = units[m, source + 2 * part].astype(f32)
-                down[hidden, at] = units[m, source + 2 * part + 1].astype(f32)
+                up[at, hidden] = quarter_unit(refs, m, source + 2 * part)
+                down[hidden, at] = quarter_unit(refs, m, source + 2 * part + 1)
 
 
 def mix_final_kernel(info, *rest):
-    refs, (qkv, out, units, sems) = rest[:10], rest[10:]
+    refs, (qkv, out) = rest[:5], rest[5:]
     low, sec = info[LOW], info[SEC]
-    fetch_quarters(sec, refs, units, sems).wait()
     width = out.shape[0] // 2
-    count = units.shape[1] // 2
+    count = refs[0].shape[0] // 2
     for m in range(QUARTERS):
         at = pl.ds(block_at(low, m), UNIT)
         at_left = pl.ds(block_at(low, m), width)
         at_right = pl.ds(pl.multiple_of(block_at(low, m) + width, width), width)
         for source, half in ((0, sec), (count, 1 - sec)):
             lanes = pl.ds(pl.multiple_of(half * width, width), width)
-            query_keys = units[m, source].astype(f32)
+            query_keys = quarter_unit(refs, m, source)
             qkv[0, at, lanes] = query_keys[:, :width]
             qkv[1, at, lanes] = query_keys[:, width:]
-            rest_unit = units[m, source + 1].astype(f32)
+            rest_unit = quarter_unit(refs, m, source + 1)
             qkv[2, at, lanes] = rest_unit[:, :width]
             out[lanes, at_left] = rest_unit[:width, width:]
             out[lanes, at_right] = rest_unit[width:, width:]
@@ -817,8 +920,8 @@
 
 
 class Sum:
-    def __init__(self, order, send_a, send_b, keep_a, keep_b, split):
-        self.order, self.split = order, split
+    def __init__(self, order, shards, send_a, send_b, keep_a, keep_b):
+        self.order, self.shards = order, shards
         self.keep = (keep_a, keep_b)
         self.count = keep_a.shape[1]
         self.once = (swap(send_a, "dp", 1), swap(send_b, "dp", 2))
@@ -830,31 +933,33 @@
             [shape((self.count, UNIT, UNIT), low16)] * 2,
             (self.keep[0], self.once[0], self.keep[1], self.once[1]),
             [far] * 4,
-            moved=self.count * MIB,
             grid=(1,),
         )
         self.twice = (swap(far_a, "dp", 2), swap(far_b, "dp", 1))
 
     def third(self):
-        if self.split:
-            outs = [shape((2, self.count // 2, UNIT, UNIT), low16)] * 2
+        count = 2 * self.count // self.shards
+        if self.shards == 1:
+            outs = [shape((count, UNIT, UNIT), low16)]
         else:
-            outs = [shape((2 * self.count, UNIT, UNIT), low16)]
+            outs = [shape((self.shards // 2, count, UNIT, UNIT), low16)] * 2
         near = half_at(0, self.count)
         totals = self.order.call(
-            sum_kernel,
+            functools.partial(sum_kernel, self.shards),
             outs,
             (self.keep[0], self.once[0], self.twice[0], self.keep[1], self.once[1], self.twice[1]),
             [near, near, VM] * 2,
-            moved=self.count * MIB,
             grid=(1,),
         )
         totals = [sum_rest(total) for total in totals]
-        if not self.split:
+        self.count = count
+        if self.shards == 1:
             return totals[0]
         self.keep = totals[1]
-        self.count = self.keep.shape[1]
-        self.once = swap(totals[0], "tensor", 1)
+        if self.shards == 2:
+            self.terms = (self.keep, swap(totals[0], "tensor", 2))
+        else:
+            self.once = swap(totals[0], "tensor", 1)
 
     def fourth(self):
         far = self.order.call(
@@ -862,32 +967,35 @@
             [shape((self.count, UNIT, UNIT), low16)],
             (self.keep, self.once),
             [half_at(1, self.count)] * 2,
-            moved=self.count * MIB // 2,
             grid=(1,),
         )[0]
-        self.twice = swap(far, "tensor", 2)
-
-    def last(self):
+        self.terms = (self.keep, self.once, swap(far, "tensor", 2))
+
+    def gathered(self, info, world):
         near = half_at(0, self.count)
-        return self.order.call(
-            total_kernel,
-            [shape((self.count, UNIT, UNIT), low16)],
-            (self.keep, self.once, self.twice),
-            [near, near, VM],
-            moved=self.count * MIB // 2,
+        given, kept = self.order.call(
+            pick_kernel,
+            [shape((self.count, UNIT, UNIT), low16)] * 2,
+            (info,) + self.terms + (world,),
+            [SM] + [near if term.ndim == 4 else VM for term in self.terms] + [VM],
             grid=(1,),
-        )[0]
-
-
-def gather_dp(kept, section):
-    arrived = lax.ppermute(kept, "section", [(1 - section, section)])
-    units = jnp.concatenate([kept, arrived])
-    count = kept.shape[0]
-    x_part = swap_one(units, "dp", 1, section)
-    y_part = swap_one(units, "dp", 2, section)
-    far_kept = swap_one(x_part[:count], "dp", 2, section)
-    far_arrived = swap_one(y_part[count:], "dp", 1, section)
-    return units, x_part, y_part, far_kept, far_arrived
+        )
+        units = jnp.concatenate([kept, swap(given, "section", 1)])
+        return Gather(units)
+
+
+class Gather:
+    def __init__(self, units):
+        self.units = units
+        self.count = units.shape[0] // 2
+        self.near = (swap(units, "dp", 1), swap(units, "dp", 2))
+
+    def far(self):
+        x_part, y_part = self.near
+        self.rest = (
+            swap(x_part[: self.count], "dp", 2), swap(y_part[self.count :], "dp", 1)
+        )
+        return (self.units,) + self.near + self.rest
 
 
 def on_device(codes, lengths, gains, w_qkv, w_out, w_up, w_down, cotangent):
@@ -901,7 +1009,7 @@
     wide = w_up.shape[2]
     rows_g = 4 * frames
     rows_l = utts * code_count * frames
-    tiles = 2 * wide // UNIT
+    tiles = wide // UNIT
     info = jnp.concatenate([jnp.stack([low, sec, z]).astype(jnp.int32), lengths])
     order = Order()
     call = order.call
@@ -914,8 +1022,8 @@
         return pltpu.SemaphoreType.DMA((count,))
 
     def gather(rows):
-        gathered = lax.all_gather(rows, "tensor", axis=0, tiled=True)
-        order.token = gathered
+        gathered = lax.all_gather(rows, "tensor")
+        order.tokens = (gathered,)
         return gathered
 
     def scatter(partial):
@@ -923,9 +1031,11 @@
 
     other_gain = swap(gains[0], "section", 1)
     own_w, other_gain = lax.optimization_barrier((own_w, other_gain))
-    other_w = tuple(swap(w, "section", 1) for w in own_w)
-    both_w = tuple(w for pair in zip(own_w, other_w) for w in pair)
-    attention_w, feed_w = both_w[:4], both_w[4:]
+
+    def with_other(weights):
+        return tuple(w for own in weights for w in (own, swap(own, "section", 1)))
+
+    attention_w = with_other(own_w[:2])
 
     first_rows, start_g, gain_g, gain_l = call(
         start_kernel,
@@ -937,9 +1047,9 @@
         ],
         (info, code_rows, gains[0], other_gain),
         [SM, VM, VM, VM],
-        moved=2 * MIB,
-    )
-    first_g = gather(first_rows)
+        us=2,
+    )
+    first_blocks = gather(first_rows)
 
     mix_piece, mix_whole = call(
         mix_piece_kernel,
@@ -947,43 +1057,66 @@
         (info,) + attention_w,
         [SM] + [ANY] * 4,
         [sem(5 * QUARTERS)],
-        moved=2 * MIB,
+        us=3.2,
     )
     mix_z1 = swap(mix_piece, "tensor", 1)
     mix_z2 = swap(mix_piece, "tensor", 2)
-
-    packed_g, probs_g, mixed_g, partial = call(
+    feed_w = with_other(order.after(own_w[2:]))
+
+    first_g, packed_g, probs_g, mixed_g, mixed_given, partial = call(
         global_attention_kernel,
         [
+            shape((rows_g, width), low16),
             shape((3, rows_g, heads_width), low16),
             shape((heads_width // HEAD_DIM, rows_g, rows_g), f32),
             shape((rows_g, heads_width), low16),
+            shape((rows_g, half), low16),
             shape((4, frames, width), low16),
         ],
-        (info, first_g) + attention_w,
+        (info, first_blocks) + attention_w,
         [SM, VM] + [ANY] * 4,
         [
             pltpu.VMEM((3, width, heads_width), low16),
             pltpu.VMEM((heads_width, width), low16),
             sem(8),
         ],
-        flops=2 * 10**9,
-        moved=8 * MIB,
-    )
+        us=5.7,
+    )
+    partial, mix_z1, mix_z2 = lax.optimization_barrier((partial, mix_z1, mix_z2))
     arrived = scatter(partial)
+    mix_z3 = swap(order.after(mix_z2), "tensor", 1)
+    top_l, top_given = call(
+        local_top_kernel,
+        [shape((rows_l, width), low16), shape((rows_l // utts, width), low16)],
+        (info, cot_rows),
+        [SM, VM],
+        us=2.3,
+    )
+    mix_near = jnp.stack(order.after([mix_z1, mix_z2]))
+    mix_x = swap(mix_near, "dp", 1)
+    mix_y = swap(mix_near, "dp", 2)
     feed_piece, feed_whole = call(
         feed_piece_kernel,
         [shape((4, UNIT, UNIT), low16), shape((QUARTERS, 4, UNIT, UNIT), low16)],
         (info,) + feed_w,
         [SM] + [ANY] * 4,
         [sem(4 * QUARTERS)],
-        moved=4 * MIB,
-    )
-    feed_z1 = swap(feed_piece, "tensor", 1)
-    mix_z3 = swap(mix_z2, "tensor", 1)
-    mix_far = jnp.stack([mix_z1, mix_z2, mix_z3])
-    mix_x = swap(mix_far, "dp", 1)
-    mix_y = swap(mix_far, "dp", 2)
+        us=4,
+    )
+    feed_z2 = swap(feed_piece, "tensor", 2)
+    hidden_g, second_rows = call(
+        middle_kernel,
+        [shape((frames, width), f32), shape((frames, width), low16)],
+        (start_g, arrived, gain_g),
+        [VM] * 3,
+        us=2,
+    )
+    mix_z3 = order.after(mix_z3)
+    mix_x3 = swap(mix_z3, "dp", 1)
+    mix_y3 = swap(mix_z3, "dp", 2)
+    second_blocks = gather(second_rows)
+    order.until(feed_z2, mix_x, mix_y, mix_x3, mix_y3)
+    feed_z2, mix_x, mix_y, mix_x3, mix_y3 = order.after((feed_z2, mix_x, mix_y, mix_x3, mix_y3))
     mix_w = (
         mix_whole,
         mix_z1,
@@ -993,33 +1126,23 @@
         mix_y,
         swap(mix_x[:, 0], "dp", 2),
         swap(mix_y[:, 1], "dp", 1),
-    )
-    hidden_g, second_rows = call(
-        middle_kernel,
-        [shape((frames, width), f32), shape((frames, width), low16)],
-        (start_g, arrived, gain_g),
-        [VM] * 3,
-        moved=2 * MIB,
-    )
-    second_g = gather(second_rows)
-    feed_z2 = swap(order.after(feed_piece), "tensor", 2)
-    feed_z3 = swap(feed_z2, "tensor", 1)
-    feed_l = [feed_whole]
-    for part in (feed_z1, feed_z2, feed_z3):
-        x_part = swap(part, "dp", 1)
-        y_part = swap(part, "dp", 2)
-        feed_l += [
-            part, x_part, y_part, swap(x_part[:2], "dp", 2), swap(y_part[2:], "dp", 1)
-        ]
-    feed_l = tuple(feed_l)
-    lifted_g, active_g, partial = call(
+        mix_x3,
+        mix_y3,
+        swap(mix_x3[:1], "dp", 2),
+        swap(mix_y3[1:], "dp", 1),
+    )
+    feed_x = swap(feed_z2, "dp", 1)
+    feed_y = swap(feed_z2, "dp", 2)
+    second_g, lifted_g, active_g, active_given, partial = call(
         global_feed_kernel,
         [
+            shape((rows_g, width), low16),
             shape((rows_g, wide), f32),
             shape((rows_g, wide), low16),
+            shape((rows_g, wide // 2), low16),
             shape((4, frames, width), low16),
         ],
-        (info, second_g) + feed_w,
+        (info, second_blocks) + feed_w,
         [SM, VM] + [ANY] * 4,
         [
             pltpu.VMEM((width, wide), low16),
@@ -1027,16 +1150,28 @@
             pltpu.VMEM((rows_g, width), f32),
             sem(8),
         ],
-        flops=2 * 10**9,
-        moved=8 * MIB,
-    )
+        us=5.6,
+    )
+    arrived = scatter(partial)
+    order.until(feed_x, feed_y)
     sent = call(
         sent_kernel,
         [shape((frames, width), low16)],
-        (hidden_g, scatter(partial)),
+        (hidden_g, arrived),
         [VM] * 2,
-        moved=MIB,
+        us=1.9,
     )[0]
+    other_sent = swap(sent, "section", 1)
+    feed_x, feed_y = order.after((feed_x, feed_y))
+    feed_l = (
+        feed_whole,
+        feed_z2,
+        feed_x,
+        feed_y,
+        swap(feed_x[:2], "dp", 2),
+        swap(feed_y[2:], "dp", 1),
+    )
+    top_same = swap(order.after(top_given), "tensor", 1)
 
     start_l, first_l, query_keys, values_l, probs_l, mixed_l, partial = call(
         local_attention_kernel,
@@ -1049,51 +1184,86 @@
             shape((rows_l, 4 * half), low16),
             shape((rows_l, width), low16),
         ],
-        (info, code_rows, sent, swap(sent, "section", 1), gain_l) + mix_w,
+        (info, code_rows, sent, other_sent, gain_l) + mix_w,
         [SM] + [VM] * 4 + [ANY] * MIX_REFS,
         [
             pltpu.VMEM((4, 2, width, UNIT), low16),
             pltpu.VMEM((4 * half, width), low16),
             sem(32),
         ],
-        flops=4 * 10**9,
-        moved=20 * MIB,
-    )
-    hidden_l, second_l, top_l, active_l, grad_lifted_l, back = call(
-        local_feed_kernel,
+        us=9,
+    )
+    order.until(*feed_l, top_same)
+    hidden_l, second_l, second_given = call(
+        local_norm_kernel,
         [
             shape((rows_l, width), f32),
             shape((rows_l, width), low16),
-            shape((rows_l, width), low16),
-            shape((tiles, rows_l, UNIT), low16),
-            shape((tiles, rows_l, UNIT), low16),
-            shape((rows_l, width), low16),
-        ],
-        (info, start_l, partial, swap(partial, "section", 1), gain_l, cot_rows) + feed_l,
-        [SM] + [VM] * 5 + [ANY] * FEED_REFS,
-        [
-            pltpu.VMEM((tiles, width, UNIT), low16),
-            pltpu.VMEM((tiles, UNIT, width), low16),
-            pltpu.VMEM((rows_l, width), f32),
-            sem(8 * tiles),
-        ],
-        flops=10 * 10**9,
-        moved=24 * MIB,
+            shape((rows_l // utts, width), low16),
+        ],
+        (info, start_l, partial, swap(partial, "section", 1), gain_l),
+        [SM] + [VM] * 4,
+        us=3.7,
+    )
+    second_same = swap(second_given, "tensor", 1)
+    top_cross = swap(order.after(top_same), "section", 1)
+    feed_scratch = [
+        pltpu.VMEM((tiles, width, UNIT), low16),
+        pltpu.VMEM((tiles, UNIT, width), low16),
+        pltpu.VMEM((rows_l, width), f32),
+        sem(8 * tiles),
+    ]
+    wide_rows = shape((rows_l, width), low16)
+    half_rows = shape((rows_l // utts, width), low16)
+    tiled_rows = shape((tiles, rows_l, UNIT), low16)
+    active_l, grad_lifted_l, back = call(
+        local_feed_kernel,
+        [tiled_rows, tiled_rows, wide_rows],
+        (second_l, top_l) + feed_l,
+        [VM] * 2 + [ANY] * FEED_REFS,
+        feed_scratch,
+        us=7.9,
     )
     other_back = swap(back, "section", 1)
+    second_same = order.after(second_same)
+    second_cross = swap(second_same, "section", 1)
+    far_active, far_lifted, far_second, far_top, same, cross = call(
+        far_feed_kernel,
+        [tiled_rows, tiled_rows, wide_rows, wide_rows, half_rows, half_rows],
+        (second_same, second_cross, top_same, top_cross) + feed_l,
+        [VM] * 4 + [ANY] * FEED_REFS,
+        feed_scratch,
+        us=8.2,
+    )
+
+    def from_neighbour(same, cross):
+        total = call(
+            pair_kernel, [half_rows], (same, swap(cross, "section", 1)), [VM] * 2
+        )[0]
+        return swap(total, "tensor", 1)
+
+    far_same = from_neighbour(same, cross)
     turned_l = pltpu.VMEM((width, rows_l), low16)
     local_feed = Sum(
         order,
+        2,
         *call(
             local_feed_grad_kernel,
-            [shape((2, 8, UNIT, UNIT), low16)] * 4,
-            (second_l, grad_lifted_l, active_l, top_l),
-            [VM] * 4,
-            [turned_l],
-            flops=6 * 10**9,
-            moved=16 * MIB,
+            [shape((2, 4, UNIT, UNIT), low16)] * 4,
+            (
+                second_l, far_second, grad_lifted_l, far_lifted, active_l, far_active, top_l,
+                far_top,
+            ),
+            [VM] * 8,
+            [pltpu.VMEM((width, 2 * rows_l), low16), pltpu.VMEM((2 * rows_l, width), low16)],
+            us=7.6,
         ),
-        True,
+    )
+    far_same = order.after(far_same)
+    far_back = (far_same, swap(far_same, "section", 1))
+    far_first, far_mixed, far_second_g, far_active_g = (
+        swap(order.after(value), "section", 1)
+        for value in (first_g, mixed_given, second_g, active_given)
     )
     grad_hidden_l, mid_l, grad_query_keys, grad_values, back, gain2_l = call(
         local_attention_back_kernel,
@@ -1105,30 +1275,31 @@
             shape((rows_l, width), low16),
             shape((1, width), f32),
         ],
-        (hidden_l, back, other_back, top_l, gain_l, query_keys, values_l, probs_l) + mix_w,
-        [VM] * 8 + [ANY] * MIX_REFS,
+        (info, hidden_l, back, other_back)
+        + far_back
+        + (top_l, gain_l, query_keys, values_l, probs_l)
+        + mix_w,
+        [SM] + [VM] * 10 + [ANY] * MIX_REFS,
         [
             pltpu.VMEM((4, 2, width, UNIT), low16),
             pltpu.VMEM((4 * half, width), low16),
             pltpu.VMEM((rows_l, width), f32),
             sem(32),
         ],
-        flops=5 * 10**9,
-        moved=20 * MIB,
+        us=11.4,
     )
     other_back = swap(back, "section", 1)
     local_mix = Sum(
         order,
+        4,
         *call(
             local_mix_kernel,
             [shape((2, 4, UNIT, UNIT), low16)] * 4,
             (first_l, grad_query_keys, grad_values, mixed_l, mid_l),
             [VM] * 5,
             [turned_l],
-            flops=3 * 10**9,
-            moved=8 * MIB,
+            us=6,
         ),
-        True,
     )
     returned, code_part, gain1_l = call(
         local_end_kernel,
@@ -1140,83 +1311,94 @@
         (info, back, other_back, start_l, grad_hidden_l, gain_l),
         [SM] + [VM] * 5,
         [pltpu.VMEM((rows_l, width), f32)],
-        moved=6 * MIB,
-    )
-
-    top_g = gather(returned)
-    grad_lifted_g, partial = call(
+        us=4.4,
+    )
+
+    top_blocks = gather(returned)
+    local_feed.second()
+    order.until(*local_mix.once, far_first, far_mixed, far_second_g, far_active_g)
+    top_g, grad_lifted_g, lifted_given, partial = call(
         global_feed_back_kernel,
-        [shape((rows_g, wide), low16), shape((4, frames, width), low16)],
-        (info, top_g, lifted_g) + feed_w,
-        [SM, VM, VM] + [ANY] * 4,
+        [
+            shape((rows_g, width), low16),
+            shape((rows_g, wide), low16),
+            shape((rows_g, wide // 2), low16),
+            shape((4, frames, width), low16),
+        ],
+        (info, top_blocks, lifted_g) + feed_w,
+        [SM] + [VM] * 2 + [ANY] * 4,
         [
             pltpu.VMEM((width, wide), low16),
             pltpu.VMEM((wide, width), low16),
             pltpu.VMEM((rows_g, width), f32),
             sem(8),
         ],
-        flops=2 * 10**9,
-        moved=8 * MIB,
+        us=6.3,
     )
     arrived = scatter(partial)
-    away_feed, kept_feed = call(
-        global_feed_grad_kernel,
-        [shape((QUARTERS, 2, 2, UNIT, UNIT), low16)] * 2,
-        (info, second_g, grad_lifted_g, active_g, top_g),
-        [SM] + [VM] * 4,
-        [pltpu.VMEM((width, rows_g), low16)],
-        flops=4 * 10**9,
-        moved=8 * MIB,
-    )
-    away_feed = swap(away_feed, "section", 1)
-    local_feed.second()
+    far_top_g, far_lifted_g = swap(top_g, "section", 1), swap(lifted_given, "section", 1)
+    local_feed.third()
+    local_mix.second()
+    global_feed = Sum(
+        order,
+        1,
+        *call(
+            global_feed_grad_kernel,
+            [shape((2, 2, UNIT, UNIT), low16)] * 4,
+            (
+                info, second_g, far_second_g, grad_lifted_g, far_lifted_g, active_g, far_active_g,
+                top_g, far_top_g,
+            ),
+            [SM] + [VM] * 8,
+            [pltpu.VMEM((width, 2 * rows_g), low16), pltpu.VMEM((2 * rows_g, width), low16)],
+            us=3.5,
+        ),
+    )
     grad_hidden_g, mid_rows, gain2_g = call(
         middle_back_kernel,
         [shape((frames, width), f32), shape((frames, width), low16), shape((1, width), f32)],
         (arrived, hidden_g, gain_g, returned),
         [VM] * 4,
-        moved=2 * MIB,
-    )
-    mid_g = gather(mid_rows)
-    grads_g, partial = call(
+        us=2.1,
+    )
+    mid_blocks = gather(mid_rows)
+    order.until(*local_mix.twice)
+    mid_g, grads_g, grads_given, partial = call(
         global_attention_back_kernel,
-        [shape((3, rows_g, heads_width), low16), shape((4, frames, width), low16)],
-        (info, mid_g, packed_g, probs_g) + attention_w,
-        [SM, VM, VM, VM] + [ANY] * 4,
+        [
+            shape((rows_g, width), low16),
+            shape((3, rows_g, heads_width), low16),
+            shape((3, rows_g, half), low16),
+            shape((4, frames, width), low16),
+        ],
+        (info, mid_blocks, packed_g, probs_g) + attention_w,
+        [SM] + [VM] * 3 + [ANY] * 4,
         [
             pltpu.VMEM((3, width, heads_width), low16),
             pltpu.VMEM((heads_width, width), low16),
             sem(8),
         ],
-        flops=2 * 10**9,
-        moved=8 * MIB,
+        us=6.8,
     )
     arrived = scatter(partial)
-    local_mix.second()
-
-    def merged(away, kept, count):
-        units = call(
-            merge_kernel,
-            [shape((2, count, UNIT, UNIT), low16)] * 4,
-            (kept, away),
-            [VM] * 2,
-            moved=2 * count * MIB,
-        )
-        return Sum(order, *units, False)
-
-    global_feed = merged(away_feed, kept_feed, 2)
-    away_mix, kept_mix = call(
-        global_mix_grad_kernel,
-        [shape((QUARTERS, 2, 1, UNIT, UNIT), low16)] * 2,
-        (info, first_g, grads_g, mixed_g, mid_g),
-        [SM] + [VM] * 4,
-        [pltpu.VMEM((width, rows_g), low16)],
-        flops=2 * 10**9,
-        moved=4 * MIB,
-    )
-    away_mix = swap(away_mix, "section", 1)
-    local_feed.third()
-    global_mix = merged(away_mix, kept_mix, 1)
+    far_mid_g, far_grads_g = swap(mid_g, "section", 1), swap(grads_given, "section", 1)
+    global_feed.second()
+    local_mix.third()
+    global_mix = Sum(
+        order,
+        1,
+        *call(
+            global_mix_grad_kernel,
+            [shape((2, 1, UNIT, UNIT), low16)] * 4,
+            (
+                info, first_g, far_first, grads_g, far_grads_g, mixed_g, far_mixed, mid_g,
+                far_mid_g,
+            ),
+            [SM] + [VM] * 8,
+            [pltpu.VMEM((width, 2 * rows_g), low16), pltpu.VMEM((2 * rows_g, width), low16)],
+            us=3,
+        ),
+    )
     kept_start, given_start, gain1_g = call(
         start_back_kernel,
         [
@@ -1227,11 +1409,24 @@
         (info, arrived, start_g, gain_g, grad_hidden_g),
         [SM] + [VM] * 4,
         [pltpu.VMEM((frames, width), f32)],
-        moved=2 * MIB,
-    )
-    local_mix.third()
-    global_feed.second()
+        us=2.1,
+    )
+    local_mix.fourth()
+    feed_sum = local_feed.gathered(info, global_feed.third())
     global_mix.second()
+    own_branch, same, cross = call(
+        local_drop_kernel,
+        [wide_rows, half_rows, half_rows],
+        (active_l, far_active) + feed_l,
+        [VM] * 2 + [ANY] * FEED_REFS,
+        [
+            pltpu.VMEM((tiles, UNIT, width), low16),
+            pltpu.VMEM((2 * rows_l, width), f32),
+            sem(QUARTERS * tiles),
+        ],
+        us=6.1,
+    )
+    other_branch = swap(own_branch, "section", 1)
     arrived_start = swap(given_start, "section", 1)
     both_start = jnp.stack(
         [
@@ -1240,6 +1435,8 @@
         ]
     )
     code_grad = jnp.transpose(code_part + both_start[:, None], (0, 2, 1, 3))
+    far_branch = from_neighbour(same, cross)
+    far_branch = (far_branch, swap(far_branch, "section", 1))
 
     own_gain = jnp.concatenate([gain1_g, gain2_g], axis=0)
     total_gain = own_gain + swap(own_gain, "section", 1)
@@ -1252,53 +1449,38 @@
         ],
         axis=1,
     )
-    for axis in ("tensor", "dp"):
-        step = 1
-        while step < lax.axis_size(axis):
-            gain_total = gain_total + swap(gain_total, axis, step)
-            step *= 2
-
-    branch_l = call(
-        local_drop_kernel,
-        [shape((rows_l, width), low16)],
-        (active_l,) + feed_l,
-        [VM] + [ANY] * FEED_REFS,
-        [
-            pltpu.VMEM((tiles, UNIT, width), low16),
-            pltpu.VMEM((rows_l, width), f32),
-            sem(QUARTERS * tiles),
-        ],
-        flops=2 * 10**9,
-        moved=8 * MIB,
-    )[0]
-    global_feed = gather_dp(global_feed.third(), 0)
-    global_mix = gather_dp(global_mix.third(), 0)
-    local_feed.fourth()
+    def over(value, axis):
+        copies = jnp.broadcast_to(value, (lax.axis_size(axis),) + value.shape)
+        return jnp.sum(lax.all_to_all(order.after(copies), axis, 0, 0), axis=0)
+
+    gain_total = over(gain_total, "tensor")
+    order.until(gain_total)
+
+    mix_sum = local_mix.gathered(info, global_mix.third())
     output = call(
         output_kernel,
         [shape((utts, code_count, frames, width // 2), low16)],
-        (info, hidden_l, branch_l, swap(branch_l, "section", 1)),
-        [SM] + [VM] * 3,
-        moved=4 * MIB,
+        (info, hidden_l, own_branch, other_branch) + far_branch,
+        [SM] + [VM] * 5,
+        us=3.1,
     )[0]
-    local_mix.fourth()
-    local_feed = gather_dp(local_feed.last(), 1)
-    local_mix = gather_dp(local_mix.last(), 1)
+    feed_parts = feed_sum.far()
+    gain_total = over(gain_total, "dp")
+    order.until(gain_total)
+    mix_parts = mix_sum.far()
     up_grad, down_grad = call(
         feed_final_kernel,
         [shape((width, wide), f32), shape((wide, width), f32)],
-        (info,) + global_feed + local_feed,
-        [SM] + [ANY] * 10,
-        [pltpu.VMEM((QUARTERS, 8, UNIT, UNIT), low16), sem(5)],
-        moved=16 * MIB,
+        (info,) + feed_parts,
+        [SM] + [VM] * 5,
+        us=6.8,
     )
     qkv_grad, out_grad = call(
         mix_final_kernel,
         [shape((3, width, heads_width), f32), shape((heads_width, width), f32)],
-        (info,) + global_mix + local_mix,
-        [SM] + [ANY] * 10,
-        [pltpu.VMEM((QUARTERS, 4, UNIT, UNIT), low16), sem(5)],
-        moved=8 * MIB,
+        (info,) + mix_parts,
+        [SM] + [VM] * 5,
+        us=4.5,
     )
     return (
         jnp.transpose(output, (0, 2, 1, 3)),

time: 502 us -> 448 us (0.89)
  waiting for transfers between devices: 122 us -> 71.8 us
  starting transfers between devices: 103 us -> 80.4 us
  blocking collectives: 75.6 us -> 91.9 us
    ppermute x20 -> x0, starting transfers between devices: 37.9 us -> none  [the longest x16 28.7 us: swap_one(): return lax.ppermute(value, ('section', axis), pairs)]
    ppermute x60 -> x75, waiting for transfers between devices: 102 us -> 64.9 us  [swap(): return lax.ppermute(value, axis, [(i, i ^ flip) for i in range(count)])]
    ppermute x20 -> x0, waiting for transfers between devices: 12.2 us -> none  [the longest x16 10.6 us: swap_one(): return lax.ppermute(value, ('section', axis), pairs)]
    ppermute x60 -> x75, starting transfers between devices: 49.2 us -> 61.3 us  [swap(): return lax.ppermute(value, axis, [(i, i ^ flip) for i in range(count)])]
    all_to_all x0 -> x1, blocking collectives: none -> 9.72 us  [over(): return jnp.sum(lax.all_to_all(order.after(copies), axis, 0, 0), axis=0)]
    all_to_all x4, waiting for transfers between devices: 7.17 us -> 0.01 us  [scatter(): return lax.all_to_all(partial, 'tensor', 0, 0)]
    all_to_all x0 -> x1, waiting for transfers between devices: none -> 6.93 us  [over(): return jnp.sum(lax.all_to_all(order.after(copies), axis, 0, 0), axis=0)]
    all_gather x4, blocking collectives: 75.6 us -> 82.2 us  [gather(): gathered = lax.all_gather(rows, 'tensor')]
  transfers between devices with their start and end apart: 84 -> 80, of which waited for: 27 -> 24; matrix products, arithmetic and copies ran while one was open for 2% -> 3% of each run, Pallas kernels for 26% -> 28%
where the time goes in v4:
time: 448 us; the launch traced here: 442 us
  Pallas kernels  161 us (36%)
  blocking collectives  91.9 us (21%)
  starting transfers between devices  80.4 us (18%)
  waiting for transfers between devices  71.8 us (16%)
  local copies, waits for them, and re-layouts  30.6 us (7%)
    pallas_call x39, Pallas kernels, call(): pl.pallas_call(body, out_shape=tuple(outs), grid=grid, in_specs=list(spec...  161 us
    all_gather x4, blocking collectives, gather(): gathered = lax.all_gather(rows, 'tensor')  82.2 us
    ppermute x75, waiting for transfers between devices, swap(): return lax.ppermute(value, axis, [(i, i ^ flip) for i in range(count)])  64.9 us
    ppermute x75, starting transfers between devices, swap(): return lax.ppermute(value, axis, [(i, i ^ flip) for i in range(count)])  61.3 us
    unnamed x170, local copies, waits for them, and re-layouts  23.6 us
    all_to_all x4, starting transfers between devices, scatter(): return lax.all_to_all(partial, 'tensor', 0, 0)  15.9 us
    all_to_all x1, blocking collectives, over(): return jnp.sum(lax.all_to_all(order.after(copies), axis, 0, 0), axis=0)  9.72 us
  transfers between devices with their start and end apart: 80, of which 24 were waited for; matrix products, arithmetic and copies ran while one was open for 3% of the time, Pallas kernels for 28%

profile of v4, /device:TPU:0, one launch (start us, length us, event | category | flops | bytes accessed | tf_op | source)
XLA Modules:
  0.0 441.5 jit_solution(12288488867637698611)
XLA Ops:
  6.0 19.4 %all-gather = bf16[256,1024]{1,0:T(8,128)(2,1)} all-gather(bf16[64,1024]{1,0:T(8,128)(2,1)} %get-tuple-element.182), channel_id=2, replica_groups=mesh['section'=2,'dp'=4,'tensor'=4] {'tensor'}, dimensions={0}, use_global_device_ids=true | all-gather | bytes 655360 | tf_op jit(solution)/shard_map/all_gather | solution.py:1025
  26.3 3.3 shard_map.136
  30.4 2.5 collective-permute-start.6
  33.0 5.7 %shard_map.137 = (bf16[256,1024]{1,0:T(8,128)(2,1)}, bf16[3,256,256]{2,1,0:T(8,128)(2,1)}, f32[4,256,256]{2,1,0:T(8,128)}, bf16[256,256]{1,0:T(8,128)(2,1)}, bf1...) custom-call(s32[5]{0:T(128)} %pad_add_fusion.info, bf16[4,64,1024]{2,1,0:T(8,128)(2,1)} %bitcast.49, ...), custom_call_target="tpu_custom_call" | custom-call | flops 1140000000 | tf_op jit(solution)/shard_map/pallas_call | solution.py:46
  38.7 5.2 %collective-permute-done.5.rest_1_ = bf16[2,256,256]{2,1,0:T(8,128)(2,1)S(1)} collective-permute-done((bf16[2,256,256]{2,1,0:T(8,128)(2,1)}, bf16[2,256,256]{2,1,0:T(8,128)(2,1)S(1)}, u32[]{:S(2)}, u32[]{:S(2)}) %collective-permute-start.5) | collective-permute-done | bytes 262176 | tf_op jit(solution)/shard_map/ppermute | solution.py:64
  45.2 4.1 all-to-all-start
  49.4 2.4 shard_map.138
  57.6 3.9 shard_map.139
  61.5 2.4 collective-permute-start.7
  71.7 26.2 %all-gather.1 = bf16[256,1024]{1,0:T(8,128)(2,1)} all-gather(bf16[64,1024]{1,0:T(8,128)(2,1)} %get-tuple-element.202), channel_id=3, replica_groups=mesh['section'=2,'dp'=4,'tensor'=4] {'tensor'}, dimensions={0}, use_global_device_ids=true | all-gather | bytes 655360 | tf_op jit(solution)/shard_map/all_gather | solution.py:1025
  98.0 6.1 %shard_map.141 = (bf16[256,1024]{1,0:T(8,128)(2,1)}, f32[256,1024]{1,0:T(8,128)}, bf16[256,1024]{1,0:T(8,128)(2,1)}, bf16[256,512]{1,0:T(8,128)(2,1)}, bf16[4,64,1024]{2,1,0:T(8,128)(2,1)}) custom-call(s32[5]{0:T(128)} %pad_add_fusion.info, bf16[4,64,1024]{2,1,0:T(8,128)(2,1)} %bitcast.50, bf16[1024,1024]{1,0:T(8,128)(2,1)} %bitcast.37, ...), custom_call_target="tpu_custom_call" | custom-call | flops 1120000000 | tf_op jit(solution)/shard_map/pallas_call | solution.py:46
  104.1 4.0 all-to-all-start.1
  114.0 7.7 %collective-permute-done.13.rest_2_ = bf16[4,256,256]{2,1,0:T(8,128)(2,1)S(1)} collective-permute-done((bf16[4,256,256]{2,1,0:T(8,128)(2,1)}, bf16[4,256,256]{2,1,0:T(8,128)(2,1)S(1)}, u32[]{:S(2)}, u32[]{:S(2)}) %collective-permute-start.13) | collective-permute-done | bytes 524320 | tf_op jit(solution)/shard_map/ppermute | solution.py:64
  127.6 9.0 %shard_map.143 = (f32[384,1024]{1,0:T(8,128)}, bf16[384,1024]{1,0:T(8,128)(2,1)}, bf16[4,384,256]{2,1,0:T(8,128)(2,1)}, bf16[4,384,128]{2,1,0:T(8,128)(2,1)}, f3...) custom-call(s32[5]{0:T(128)} %pad_add_fusion.info, ...), custom_call_target="tpu_custom_call" | custom-call | flops 1800000000 | tf_op jit(solution)/shard_map/pallas_call | solution.py:46
  141.4 5.6 %collective-permute-done.20.rest_4_ = bf16[2,256,256]{2,1,0:T(8,128)(2,1)S(1)} collective-permute-done((bf16[2,256,256]{2,1,0:T(8,128)(2,1)S(1)}, bf16[2,256,256]{2,1,0:T(8,128)(2,1)S(1)}, u32[]{:S(2)}, u32[]{:S(2)}) %collective-permute-start.20) | collective-permute-done | bytes 262176 | tf_op jit(solution)/shard_map/ppermute | solution.py:64
  149.4 3.7 shard_map.144
  154.6 7.9 %shard_map.145 = (bf16[4,384,256]{2,1,0:T(8,128)(2,1)}, bf16[4,384,256]{2,1,0:T(8,128)(2,1)}, bf16[384,1024]{1,0:T(8,128)(2,1)}) custom-call(bf16[384,1024]{1,0:T(8,128)(2,1)} %get-tuple-element.238.second, bf16[384,1024]{1,0:T(8,128)(2,1)} %get-tuple-element.230.top, bf16[4,4,256,256]{3,2,1,0:T(8,128)(2,1)} %get-tuple-element.196.rest_0_, ...), custom_call_target="tpu_custom_call" | custom-call | flops 1580000000 | tf_op jit(solution)/shard_map/pallas_call | solution.py:46
  166.3 8.1 %shard_map.146 = (bf16[4,384,256]{2,1,0:T(8,128)(2,1)}, bf16[4,384,256]{2,1,0:T(8,128)(2,1)}, bf16[384,1024]{1,0:T(8,128)(2,1)}, bf16[384,1024]{1,0:T(8,128)(2,1...) custom-call(bf16[192,1024]{1,0:T(8,128)(2,1)} %copy-done.70, bf16[192,1024]{1,0:T(8,128)(2,1)} %copy-done.72, ...), custom_call_target="tpu_custom_call" | custom-call | flops 1640000000 | tf_op jit(solution)/shard_map/pallas_call | solution.py:46
  180.8 7.6 %shard_map.148 = (bf16[2,4,256,256]{3,2,1,0:T(8,128)(2,1)}, bf16[2,4,256,256]{3,2,1,0:T(8,128)(2,1)}, bf16[2,4,256,256]{3,2,1,0:T(8,128)(2,1)}, bf16[2,4,256,256]{3,2,1,0:T(8,128)(2,1)}) custom-call(bf16[384,1024]{1,0:T(8,128)(2,1)} %get-tuple-element.238.second, bf16[384,1024]{1,0:T(8,128)(2,1)} %get-tuple-element.239.far_second, ...), custom_call_target="tpu_custom_call" | custom-call | flops 1520000000 | tf_op jit(solution)/shard_map/pallas_call | solution.py:46
  194.2 11.5 %shard_map.149 = (f32[384,1024]{1,0:T(8,128)}, bf16[384,1024]{1,0:T(8,128)(2,1)}, bf16[4,384,256]{2,1,0:T(8,128)(2,1)}, bf16[4,384,128]{2,1,0:T(8,128)(2,1)}, bf...) custom-call(s32[5]{0:T(128)} %pad_add_fusion.info, f32[384,1024]{1,0:T(8,128)} %get-tuple-element.247.hidden, ...), custom_call_target="tpu_custom_call" | custom-call | flops 2280000000 | tf_op jit(solution)/shard_map/pallas_call | solution.py:46
  206.2 6.2 %shard_map.150 = (bf16[2,4,256,256]{3,2,1,0:T(8,128)(2,1)}, bf16[2,4,256,256]{3,2,1,0:T(8,128)(2,1)}, bf16[2,4,256,256]{3,2,1,0:T(8,128)(2,1)}, bf16[2,4,256,256]{3,2,1,0:T(8,128)(2,1)}) custom-call(bf16[384,1024]{1,0:T(8,128)(2,1)} %get-tuple-element.253.first, bf16[4,384,256]{2,1,0:T(8,128)(2,1)} %get-tuple-element.254.grad_query_keys, ...), custom_call_target="tpu_custom_call" | custom-call | flops 1200000000 | tf_op jit(solution)/shard_map/pallas_call | solution.py:46
  213.8 2.9 collective-permute-done.32.from_x.refs_1_
  218.6 4.2 shard_map.151
  222.8 18.4 %all-gather.2 = bf16[256,1024]{1,0:T(8,128)(2,1)} all-gather(bf16[64,1024]{1,0:T(8,128)(2,1)} %get-tuple-element.264.returned), channel_id=4, replica_groups=mesh['section'=2,'dp'=4,'tensor'=4] {'tensor'}, dimensions={0}, use_global_device_ids=true | all-gather | bytes 655360 | tf_op jit(solution)/shard_map/all_gather | solution.py:1025
  241.2 2.6 shard_map.152
  247.3 7.2 %shard_map.153 = (bf16[256,1024]{1,0:T(8,128)(2,1)}, bf16[256,1024]{1,0:T(8,128)(2,1)}, bf16[256,512]{1,0:T(8,128)(2,1)}, bf16[4,64,1024]{2,1,0:T(8,128)(2,1)}) custom-call(s32[5]{0:T(128)} %pad_add_fusion.info, bf16[4,64,1024]{2,1,0:T(8,128)(2,1)} %bitcast.48, f32[256,1024]{1,0:T(8,128)} %get-tuple-element.280.rest_1_, bf16[1024,1024]{1,0:T(8,128)(2,1)} %bitcast.38, ...), custom_call_target="tpu_custom_call" | custom-call | flops 1260000000 | tf_op jit(solution)/shard_map/pallas_call | solution.py:46
  254.5 3.7 all-to-all-start.2
  260.3 3.1 shard_map.154
  263.4 2.6 shard_map.155
  268.3 4.2 shard_map.156
  278.2 18.1 %all-gather.3 = bf16[256,1024]{1,0:T(8,128)(2,1)} all-gather(bf16[64,1024]{1,0:T(8,128)(2,1)} %get-tuple-element.295), channel_id=5, replica_groups=mesh['section'=2,'dp'=4,'tensor'=4] {'tensor'}, dimensions={0}, use_global_device_ids=true | all-gather | bytes 655360 | tf_op jit(solution)/shard_map/all_gather | solution.py:1025
  296.3 7.2 %shard_map.158 = (bf16[256,1024]{1,0:T(8,128)(2,1)}, bf16[3,256,256]{2,1,0:T(8,128)(2,1)}, bf16[3,256,128]{2,1,0:T(8,128)(2,1)}, bf16[4,64,1024]{2,1,0:T(8,128)(2,1)}) custom-call(s32[5]{0:T(128)} %pad_add_fusion.info, bf16[4,64,1024]{2,1,0:T(8,128)(2,1)} %bitcast.51, bf16[3,256,256]{2,1,0:T(8,128)(2,1)} %get-tuple-element.298.rest_1_, ...), custom_call_target="tpu_custom_call" | custom-call | flops 1360000000 | tf_op jit(solution)/shard_map/pallas_call | solution.py:46
  303.6 4.0 all-to-all-start.3
  311.3 3.2 shard_map.160
  316.6 2.4 collective-permute-start.53
  322.1 3.6 shard_map.161
  329.8 11.7 %collective-permute-done.50.arrived.refs_1_ = bf16[2,2,256,256]{3,2,1,0:T(8,128)(2,1)S(1)} collective-permute-done((bf16[2,2,256,256]{3,2,1,0:T(8,128)(2,1)}, bf16[2,2,256,256]{3,2,1,0:T(8,128)(2,1)S(1)}, u32[]{:S(2)}, u32[]{:S(2)}) %collective-permute-start.50) | collective-permute-done | bytes 524320 | tf_op jit(solution)/shard_map/ppermute | solution.py:64
  345.5 2.3 shard_map.164.refs_2_
  348.6 2.5 shard_map.165
  354.5 6.2 %shard_map.167 = (bf16[384,1024]{1,0:T(8,128)(2,1)}, bf16[192,1024]{1,0:T(8,128)(2,1)}, bf16[192,1024]{1,0:T(8,128)(2,1)}) custom-call(bf16[4,384,256]{2,1,0:T(8,128)(2,1)} %get-tuple-element.328.own_active, bf16[4,384,256]{2,1,0:T(8,128)(2,1)} %get-tuple-element.243.far_active, bf16[4,4,256,256]{3,2,1,0:T(8,128)(2,1)} %get-tuple-element.196.rest_0_, ...), custom_call_target="tpu_custom_call" | custom-call | flops 1220000000 | tf_op jit(solution)/shard_map/pallas_call | solution.py:46
  366.4 4.1 collective-permute-done.58.refs_2_
  373.6 9.7 %all_to_all.30 = f32[4,2,1024]{2,1,0:T(2,128)S(1)} all-to-all(f32[4,2,1024]{2,1,0:T(2,128)S(1)} %broadcast_in_dim.22), channel_id=1, replica_groups=mesh['section'=2,'dp'=4,'tensor'=4] {'tensor'}, dimensions={0} | all-to-all | bytes 65536 | tf_op jit(solution)/shard_map/all_to_all | solution.py:1454
  383.4 7.7 %collective-permute-done.59.refs_5_ = bf16[1,256,256]{2,1,0:T(8,128)(2,1)S(1)} collective-permute-done((bf16[1,256,256]{2,1,0:T(8,128)(2,1)}, bf16[1,256,256]{2,1,0:T(8,128)(2,1)S(1)}, u32[]{:S(2)}, u32[]{:S(2)}) %collective-permute-start.59) | collective-permute-done | bytes 131104 | tf_op jit(solution)/shard_map/ppermute | solution.py:64
  408.8 3.1 shard_map.171
  412.6 3.3 all-to-all-start.5
  422.4 6.9 %all-to-all-done.5 = f32[4,2,1024]{2,1,0:T(2,128)S(1)} async-done(((f32[4,2,1024]{2,1,0:T(2,128)}), f32[4,2,1024]{2,1,0:T(2,128)S(1)}, u32[]{:S(2)}, u32[]{:S(2)}) %all-to-all-start.5) | async-done | bytes 32800 | tf_op jit(solution)/shard_map/all_to_all | solution.py:1454
  429.9 6.1 %shard_map.172 = (f32[1024,1024]{1,0:T(8,128)}, f32[1024,1024]{1,0:T(8,128)}) custom-call(s32[5]{0:T(128)} %pad_add_fusion.info, bf16[8,256,256]{2,1,0:T(8,128)(2,1)} %constant_dynamic-update-slice_fusion.rest_0_, bf16[8,256,256]{2,1,0:T(8,128)(2,1)} %copy-done.49, bf16[8,256,256]{2,1,0:T(8,128)(2,1)} %collective-permute-done.67.rest_2_, ...), custom_call_target="tpu_custom_call" | custom-call | flops 1360000000 | tf_op jit(solution)/shard_map/pallas_call | solution.py:46
  437.4 3.9 shard_map.173
  (351 shorter events, 132.2 us)
Async XLA Ops:
  2.2 23.3 %collective-permute-start.1 = (bf16[3,1024,256]{2,1,0:T(8,128)(2,1)}, bf16[3,1024,256]{2,1,0:T(8,128)(2,1)}, u32[]{:S(2)}, u32[]{:S(2)}) collective-permute-start(bf16[3,1024,256]{2,1,0:T(8,128)(2,1)} %bitcast.40), channel_id=1, source_target_pairs={{0,16},{16,0},{1,17},{17,1},{2,18},{18,2},{3,19},{19,3},{4,20},{20... | collective-permute-start | bytes 4718600 | tf_op jit(solution)/shard_map/ppermute | solution.py:64
  2.5 22.9 %collective-permute-start.2 = (bf16[256,1024]{1,0:T(8,128)(2,1)}, bf16[256,1024]{1,0:T(8,128)(2,1)S(1)}, u32[]{:S(2)}, u32[]{:S(2)}) collective-permute-start(bf16[256,1024]{1,0:T(8,128)(2,1)} %bitcast.44), channel_id=1, source_target_pairs={{0,16},{16,0},{1,17},{17,1},{2,18},{18,2},{3,19},{19,3},{4,20},{20... | collective-permute-start | bytes 1572872 | tf_op jit(solution)/shard_map/ppermute | solution.py:64
  29.5 28.1 %collective-permute-start.3 = (bf16[1024,1024]{1,0:T(8,128)(2,1)S(1)}, bf16[1024,1024]{1,0:T(8,128)(2,1)}, u32[]{:S(2)}, u32[]{:S(2)}) collective-permute-start(bf16[1024,1024]{1,0:T(8,128)(2,1)S(1)} %bitcast.39), channel_id=1, source_target_pairs={{0,16},{16,0},{1,17},{17,1},{2,18},{18,2},{3,19},{19,3},{4,20},{20... | collective-permute-start | bytes 6291464 | tf_op jit(solution)/shard_map/ppermute | solution.py:64
  29.6 28.0 %collective-permute-start.4 = (bf16[1024,1024]{1,0:T(8,128)(2,1)}, bf16[1024,1024]{1,0:T(8,128)(2,1)}, u32[]{:S(2)}, u32[]{:S(2)}) collective-permute-start(bf16[1024,1024]{1,0:T(8,128)(2,1)} %bitcast.9.own_down.rest_3_.rest_4_), channel_id=1, source_target_pairs={{0,16},{16,0},{1,17},{17,1},{2,18},{18,2},{3,19},{19,3},{4,20},{20... | collective-permute-start | bytes 6291464 | tf_op jit(solution)/shard_map/ppermute | solution.py:64
  30.1 13.8 %collective-permute-start.5 = (bf16[2,256,256]{2,1,0:T(8,128)(2,1)}, bf16[2,256,256]{2,1,0:T(8,128)(2,1)S(1)}, u32[]{:S(2)}, u32[]{:S(2)}) collective-permute-start(bf16[2,256,256]{2,1,0:T(8,128)(2,1)} %get-tuple-element.198), channel_id=1, source_target_pairs={{0,1},{1,0},{2,3},{3,2},{4,5},{5,4},{6,7},{7,6},{8,9},{9,8},{10,11... | collective-permute-start | bytes 786440 | tf_op jit(solution)/shard_map/ppermute | solution.py:64
  30.4 14.8 %collective-permute-start.6 = (bf16[2,256,256]{2,1,0:T(8,128)(2,1)}, bf16[2,256,256]{2,1,0:T(8,128)(2,1)S(1)}, u32[]{:S(2)}, u32[]{:S(2)}) collective-permute-start(bf16[2,256,256]{2,1,0:T(8,128)(2,1)} %get-tuple-element.198), channel_id=1, source_target_pairs={{0,2},{1,3},{2,0},{3,1},{4,6},{5,7},{6,4},{7,5},{8,10},{9,11},{10,... | collective-permute-start | bytes 786440 | tf_op jit(solution)/shard_map/ppermute | solution.py:64
  45.2 18.7 %all-to-all-start = ((bf16[4,64,1024]{2,1,0:T(8,128)(2,1)}), bf16[4,64,1024]{2,1,0:T(8,128)(2,1)}, u32[]{:S(2)}, u32[]{:S(2)}) async-start(bf16[4,64,1024]{2,1,0:T(8,128)(2,1)} %get-tuple-element.199), calls=%async_computation | async-start | bytes 1048576 | tf_op jit(solution)/shard_map/all_to_all | solution.py:1030
  52.6 45.4 %collective-permute-start.8 = (bf16[2,2,256,256]{3,2,1,0:T(8,128)(2,1)}, bf16[2,2,256,256]{3,2,1,0:T(8,128)(2,1)S(1)}, u32[]{:S(2)}, u32[]{:S(2)}) collective-permute-start(bf16[2,2,256,256]{3,2,1,0:T(8,128)(2,1)} %pad_maximum_fusion), channel_id=1, source_target_pairs={{0,4},{4,0},{8,12},{12,8},{1,5},{5,1},{9,13},{13,9},{2,6},{6,2},{1... | collective-permute-start | bytes 1572872 | tf_op jit(solution)/shard_map/ppermute | solution.py:64
  54.1 43.9 %collective-permute-start.9 = (bf16[2,2,256,256]{3,2,1,0:T(8,128)(2,1)}, bf16[2,2,256,256]{3,2,1,0:T(8,128)(2,1)S(1)}, u32[]{:S(2)}, u32[]{:S(2)}) collective-permute-start(bf16[2,2,256,256]{3,2,1,0:T(8,128)(2,1)} %pad_maximum_fusion), channel_id=1, source_target_pairs={{0,8},{4,12},{8,0},{12,4},{1,9},{5,13},{9,1},{13,5},{2,10},{6,14},... | collective-permute-start | bytes 1572872 | tf_op jit(solution)/shard_map/ppermute | solution.py:64
  61.5 36.5 %collective-permute-start.7 = (bf16[4,256,256]{2,1,0:T(8,128)(2,1)}, bf16[4,256,256]{2,1,0:T(8,128)(2,1)}, u32[]{:S(2)}, u32[]{:S(2)}) collective-permute-start(bf16[4,256,256]{2,1,0:T(8,128)(2,1)} %get-tuple-element.203), channel_id=1, source_target_pairs={{0,2},{1,3},{2,0},{3,1},{4,6},{5,7},{6,4},{7,5},{8,10},{9,11},{10,... | collective-permute-start | bytes 1572872 | tf_op jit(solution)/shard_map/ppermute | solution.py:64
  68.2 29.8 %collective-permute-start.11 = (bf16[2,256,256]{2,1,0:T(8,128)(2,1)}, bf16[2,256,256]{2,1,0:T(8,128)(2,1)S(1)}, u32[]{:S(2)}, u32[]{:S(2)}) collective-permute-start(bf16[2,256,256]{2,1,0:T(8,128)(2,1)} %collective-permute-done.10.rest_3_), channel_id=1, source_target_pairs={{0,4},{4,0},{8,12},{12,8},{1,5},{5,1},{9,13},{13,9},{2,6},{6,2},{1... | collective-permute-start | bytes 786440 | tf_op jit(solution)/shard_map/ppermute | solution.py:64
  70.2 27.8 %collective-permute-start.12 = (bf16[2,256,256]{2,1,0:T(8,128)(2,1)}, bf16[2,256,256]{2,1,0:T(8,128)(2,1)S(1)}, u32[]{:S(2)}, u32[]{:S(2)}) collective-permute-start(bf16[2,256,256]{2,1,0:T(8,128)(2,1)} %collective-permute-done.10.rest_3_), channel_id=1, source_target_pairs={{0,8},{4,12},{8,0},{12,4},{1,9},{5,13},{9,1},{13,5},{2,10},{6,14},... | collective-permute-start | bytes 786440 | tf_op jit(solution)/shard_map/ppermute | solution.py:64
  104.1 18.4 %all-to-all-start.1 = ((bf16[4,64,1024]{2,1,0:T(8,128)(2,1)}), bf16[4,64,1024]{2,1,0:T(8,128)(2,1)S(1)}, u32[]{:S(2)}, u32[]{:S(2)}) async-start(bf16[4,64,1024]{2,1,0:T(8,128)(2,1)} %get-tuple-element.211), calls=%async_computation.1 | async-start | bytes 1048576 | tf_op jit(solution)/shard_map/all_to_all | solution.py:1030
  110.7 16.0 %collective-permute-start.16 = (bf16[2,256,256]{2,1,0:T(8,128)(2,1)S(1)}, bf16[2,256,256]{2,1,0:T(8,128)(2,1)S(1)}, u32[]{:S(2)}, u32[]{:S(2)}) collective-permute-start(bf16[2,256,256]{2,1,0:T(8,128)(2,1)S(1)} %slice_bitcast_fusion.1), channel_id=1, source_target_pairs={{0,8},{4,12},{8,0},{12,4},{1,9},{5,13},{9,1},{13,5},{2,10},{6,14},... | collective-permute-start | bytes 786440 | tf_op jit(solution)/shard_map/ppermute | solution.py:64
  111.8 14.9 %collective-permute-start.17 = (bf16[2,256,256]{2,1,0:T(8,128)(2,1)}, bf16[2,256,256]{2,1,0:T(8,128)(2,1)S(1)}, u32[]{:S(2)}, u32[]{:S(2)}) collective-permute-start(bf16[2,256,256]{2,1,0:T(8,128)(2,1)} %slice_bitcast_fusion), channel_id=1, source_target_pairs={{0,4},{4,0},{8,12},{12,8},{1,5},{5,1},{9,13},{13,9},{2,6},{6,2},{1... | collective-permute-start | bytes 786440 | tf_op jit(solution)/shard_map/ppermute | solution.py:64
  190.4 26.2 %collective-permute-start.32 = (bf16[2,4,256,256]{3,2,1,0:T(8,128)(2,1)}, bf16[2,4,256,256]{3,2,1,0:T(8,128)(2,1)S(1)}, u32[]{:S(2)}, u32[]{:S(2)}) collective-permute-start(bf16[2,4,256,256]{3,2,1,0:T(8,128)(2,1)} %get-tuple-element.266), channel_id=1, source_target_pairs={{0,4},{4,0},{8,12},{12,8},{1,5},{5,1},{9,13},{13,9},{2,6},{6,2},{1... | collective-permute-start | bytes 3145736 | tf_op jit(solution)/shard_map/ppermute | solution.py:64
  191.4 26.2 %collective-permute-start.33 = (bf16[2,4,256,256]{3,2,1,0:T(8,128)(2,1)}, bf16[2,4,256,256]{3,2,1,0:T(8,128)(2,1)S(1)}, u32[]{:S(2)}, u32[]{:S(2)}) collective-permute-start(bf16[2,4,256,256]{3,2,1,0:T(8,128)(2,1)} %get-tuple-element.267), channel_id=1, source_target_pairs={{0,8},{4,12},{8,0},{12,4},{1,9},{5,13},{9,1},{13,5},{2,10},{6,14},... | collective-permute-start | bytes 3145736 | tf_op jit(solution)/shard_map/ppermute | solution.py:64
  193.1 20.2 %collective-permute-start.37 = (bf16[256,128]{1,0:T(8,128)(2,1)S(1)}, bf16[256,128]{1,0:T(8,128)(2,1)S(1)}, u32[]{:S(2)}, u32[]{:S(2)}) collective-permute-start(bf16[256,128]{1,0:T(8,128)(2,1)S(1)} %copy-done.82), channel_id=1, source_target_pairs={{0,16},{16,0},{1,17},{17,1},{2,18},{18,2},{3,19},{19,3},{4,20},{20... | collective-permute-start | bytes 196616 | tf_op jit(solution)/shard_map/ppermute | solution.py:64
  212.4 34.9 %collective-permute-start.34 = (bf16[2,4,256,256]{3,2,1,0:T(8,128)(2,1)}, bf16[2,4,256,256]{3,2,1,0:T(8,128)(2,1)S(1)}, u32[]{:S(2)}, u32[]{:S(2)}) collective-permute-start(bf16[2,4,256,256]{3,2,1,0:T(8,128)(2,1)} %get-tuple-element.269), channel_id=1, source_target_pairs={{0,4},{4,0},{8,12},{12,8},{1,5},{5,1},{9,13},{13,9},{2,6},{6,2},{1... | collective-permute-start | bytes 3145736 | tf_op jit(solution)/shard_map/ppermute | solution.py:64
  213.3 34.0 %collective-permute-start.35 = (bf16[2,4,256,256]{3,2,1,0:T(8,128)(2,1)}, bf16[2,4,256,256]{3,2,1,0:T(8,128)(2,1)S(1)}, u32[]{:S(2)}, u32[]{:S(2)}) collective-permute-start(bf16[2,4,256,256]{3,2,1,0:T(8,128)(2,1)} %get-tuple-element.270), channel_id=1, source_target_pairs={{0,8},{4,12},{8,0},{12,4},{1,9},{5,13},{9,1},{13,5},{2,10},{6,14},... | collective-permute-start | bytes 3145736 | tf_op jit(solution)/shard_map/ppermute | solution.py:64
  216.6 28.9 %collective-permute-start.36 = (bf16[256,1024]{1,0:T(8,128)(2,1)S(1)}, bf16[256,1024]{1,0:T(8,128)(2,1)S(1)}, u32[]{:S(2)}, u32[]{:S(2)}) collective-permute-start(bf16[256,1024]{1,0:T(8,128)(2,1)S(1)} %copy-done.33), channel_id=1, source_target_pairs={{0,16},{16,0},{1,17},{17,1},{2,18},{18,2},{3,19},{19,3},{4,20},{20... | collective-permute-start | bytes 1572872 | tf_op jit(solution)/shard_map/ppermute | solution.py:64
  217.6 29.7 %collective-permute-start.38 = (bf16[256,1024]{1,0:T(8,128)(2,1)S(1)}, bf16[256,1024]{1,0:T(8,128)(2,1)S(1)}, u32[]{:S(2)}, u32[]{:S(2)}) collective-permute-start(bf16[256,1024]{1,0:T(8,128)(2,1)S(1)} %copy-done.34), channel_id=1, source_target_pairs={{0,16},{16,0},{1,17},{17,1},{2,18},{18,2},{3,19},{19,3},{4,20},{20... | collective-permute-start | bytes 1572872 | tf_op jit(solution)/shard_map/ppermute | solution.py:64
  217.6 26.2 %collective-permute-start.39 = (bf16[256,512]{1,0:T(8,128)(2,1)S(1)}, bf16[256,512]{1,0:T(8,128)(2,1)S(1)}, u32[]{:S(2)}, u32[]{:S(2)}) collective-permute-start(bf16[256,512]{1,0:T(8,128)(2,1)S(1)} %copy-done.74), channel_id=1, source_target_pairs={{0,16},{16,0},{1,17},{17,1},{2,18},{18,2},{3,19},{19,3},{4,20},{20... | collective-permute-start | bytes 786440 | tf_op jit(solution)/shard_map/ppermute | solution.py:64
  243.8 14.9 %collective-permute-start.40 = (bf16[4,256,256]{2,1,0:T(8,128)(2,1)}, bf16[4,256,256]{2,1,0:T(8,128)(2,1)S(1)}, u32[]{:S(2)}, u32[]{:S(2)}) collective-permute-start(bf16[4,256,256]{2,1,0:T(8,128)(2,1)} %get-tuple-element.283), channel_id=1, source_target_pairs={{0,8},{4,12},{8,0},{12,4},{1,9},{5,13},{9,1},{13,5},{2,10},{6,14},... | collective-permute-start | bytes 1572872 | tf_op jit(solution)/shard_map/ppermute | solution.py:64
  254.5 20.7 %all-to-all-start.2 = ((bf16[4,64,1024]{2,1,0:T(8,128)(2,1)}), bf16[4,64,1024]{2,1,0:T(8,128)(2,1)S(1)}, u32[]{:S(2)}, u32[]{:S(2)}) async-start(bf16[4,64,1024]{2,1,0:T(8,128)(2,1)} %get-tuple-element.281), calls=%async_computation.2 | async-start | bytes 1048576 | tf_op jit(solution)/shard_map/all_to_all | solution.py:1030
  266.0 30.3 %collective-permute-start.44 = (bf16[4,256,256]{2,1,0:T(8,128)(2,1)}, bf16[4,256,256]{2,1,0:T(8,128)(2,1)S(1)}, u32[]{:S(2)}, u32[]{:S(2)}) collective-permute-start(bf16[4,256,256]{2,1,0:T(8,128)(2,1)} %get-tuple-element.296), channel_id=1, source_target_pairs={{0,8},{4,12},{8,0},{12,4},{1,9},{5,13},{9,1},{13,5},{2,10},{6,14},... | collective-permute-start | bytes 1572872 | tf_op jit(solution)/shard_map/ppermute | solution.py:64
  266.5 29.8 %collective-permute-start.45 = (bf16[4,256,256]{2,1,0:T(8,128)(2,1)}, bf16[4,256,256]{2,1,0:T(8,128)(2,1)S(1)}, u32[]{:S(2)}, u32[]{:S(2)}) collective-permute-start(bf16[4,256,256]{2,1,0:T(8,128)(2,1)} %get-tuple-element.286), channel_id=1, source_target_pairs={{0,4},{4,0},{8,12},{12,8},{1,5},{5,1},{9,13},{13,9},{2,6},{6,2},{1... | collective-permute-start | bytes 1572872 | tf_op jit(solution)/shard_map/ppermute | solution.py:64
  272.5 35.1 %collective-permute-start.46 = (bf16[2,2,256,256]{3,2,1,0:T(8,128)(2,1)}, bf16[2,2,256,256]{3,2,1,0:T(8,128)(2,1)S(1)}, u32[]{:S(2)}, u32[]{:S(2)}) collective-permute-start(bf16[2,2,256,256]{3,2,1,0:T(8,128)(2,1)} %get-tuple-element.302), channel_id=1, source_target_pairs={{0,4},{4,0},{8,12},{12,8},{1,5},{5,1},{9,13},{13,9},{2,6},{6,2},{1... | collective-permute-start | bytes 1572872 | tf_op jit(solution)/shard_map/ppermute | solution.py:64
  273.6 34.1 %collective-permute-start.47 = (bf16[2,2,256,256]{3,2,1,0:T(8,128)(2,1)}, bf16[2,2,256,256]{3,2,1,0:T(8,128)(2,1)S(1)}, u32[]{:S(2)}, u32[]{:S(2)}) collective-permute-start(bf16[2,2,256,256]{3,2,1,0:T(8,128)(2,1)} %get-tuple-element.303), channel_id=1, source_target_pairs={{0,8},{4,12},{8,0},{12,4},{1,9},{5,13},{9,1},{13,5},{2,10},{6,14},... | collective-permute-start | bytes 1572872 | tf_op jit(solution)/shard_map/ppermute | solution.py:64
  303.6 23.3 %all-to-all-start.3 = ((bf16[4,64,1024]{2,1,0:T(8,128)(2,1)}), bf16[4,64,1024]{2,1,0:T(8,128)(2,1)S(1)}, u32[]{:S(2)}, u32[]{:S(2)}) async-start(bf16[4,64,1024]{2,1,0:T(8,128)(2,1)} %get-tuple-element.300), calls=%async_computation.3 | async-start | bytes 1048576 | tf_op jit(solution)/shard_map/all_to_all | solution.py:1030
  307.6 13.7 %collective-permute-start.49 = (bf16[256,1024]{1,0:T(8,128)(2,1)}, bf16[256,1024]{1,0:T(8,128)(2,1)S(1)}, u32[]{:S(2)}, u32[]{:S(2)}) collective-permute-start(bf16[256,1024]{1,0:T(8,128)(2,1)} %get-tuple-element.311.mid), channel_id=1, source_target_pairs={{0,16},{16,0},{1,17},{17,1},{2,18},{18,2},{3,19},{19,3},{4,20},{20... | collective-permute-start | bytes 1572872 | tf_op jit(solution)/shard_map/ppermute | solution.py:64
  314.5 26.9 %collective-permute-start.50 = (bf16[2,2,256,256]{3,2,1,0:T(8,128)(2,1)}, bf16[2,2,256,256]{3,2,1,0:T(8,128)(2,1)S(1)}, u32[]{:S(2)}, u32[]{:S(2)}) collective-permute-start(bf16[2,2,256,256]{3,2,1,0:T(8,128)(2,1)} %get-tuple-element.318), channel_id=1, source_target_pairs={{0,1},{1,0},{2,3},{3,2},{4,5},{5,4},{6,7},{7,6},{8,9},{9,8},{10,11... | collective-permute-start | bytes 1572872 | tf_op jit(solution)/shard_map/ppermute | solution.py:64
  316.6 31.3 %collective-permute-start.53 = (bf16[1,4,256,256]{3,2,1,0:T(8,128)(2,1)S(1)}, bf16[1,4,256,256]{3,2,1,0:T(8,128)(2,1)S(1)}, u32[]{:S(2)}, u32[]{:S(2)}) collective-permute-start(bf16[1,4,256,256]{3,2,1,0:T(8,128)(2,1)S(1)} %copy-done.66), channel_id=1, source_target_pairs={{0,2},{1,3},{2,0},{3,1},{4,6},{5,7},{6,4},{7,5},{8,10},{9,11},{10,... | collective-permute-start | bytes 1572872 | tf_op jit(solution)/shard_map/ppermute | solution.py:64
  318.9 25.2 %collective-permute-start.51 = (bf16[2,256,256]{2,1,0:T(8,128)(2,1)}, bf16[2,256,256]{2,1,0:T(8,128)(2,1)S(1)}, u32[]{:S(2)}, u32[]{:S(2)}) collective-permute-start(bf16[2,256,256]{2,1,0:T(8,128)(2,1)} %get-tuple-element.320), channel_id=1, source_target_pairs={{0,8},{4,12},{8,0},{12,4},{1,9},{5,13},{9,1},{13,5},{2,10},{6,14},... | collective-permute-start | bytes 786440 | tf_op jit(solution)/shard_map/ppermute | solution.py:64
  320.4 23.7 %collective-permute-start.52 = (bf16[2,256,256]{2,1,0:T(8,128)(2,1)S(1)}, bf16[2,256,256]{2,1,0:T(8,128)(2,1)S(1)}, u32[]{:S(2)}, u32[]{:S(2)}) collective-permute-start(bf16[2,256,256]{2,1,0:T(8,128)(2,1)S(1)} %copy-done.75), channel_id=1, source_target_pairs={{0,4},{4,0},{8,12},{12,8},{1,5},{5,1},{9,13},{13,9},{2,6},{6,2},{1... | collective-permute-start | bytes 786440 | tf_op jit(solution)/shard_map/ppermute | solution.py:64
  325.7 25.6 %collective-permute-start.54 = (bf16[2,1,256,256]{3,2,1,0:T(8,128)(2,1)}, bf16[2,1,256,256]{3,2,1,0:T(8,128)(2,1)S(1)}, u32[]{:S(2)}, u32[]{:S(2)}) collective-permute-start(bf16[2,1,256,256]{3,2,1,0:T(8,128)(2,1)} %get-tuple-element.325), channel_id=1, source_target_pairs={{0,4},{4,0},{8,12},{12,8},{1,5},{5,1},{9,13},{13,9},{2,6},{6,2},{1... | collective-permute-start | bytes 786440 | tf_op jit(solution)/shard_map/ppermute | solution.py:64
  362.9 39.8 %collective-permute-start.66 = (bf16[8,256,256]{2,1,0:T(8,128)(2,1)}, bf16[8,256,256]{2,1,0:T(8,128)(2,1)S(1)}, u32[]{:S(2)}, u32[]{:S(2)}) collective-permute-start(bf16[8,256,256]{2,1,0:T(8,128)(2,1)} %constant_dynamic-update-slice_fusion.rest_0_), channel_id=1, source_target_pairs={{0,4},{4,0},{8,12},{12,8},{1,5},{5,1},{9,13},{13,9},{2,6},{6,2},{1... | collective-permute-start | bytes 3145736 | tf_op jit(solution)/shard_map/ppermute | solution.py:64
  364.0 29.7 %collective-permute-start.60 = (bf16[2,256,256]{2,1,0:T(8,128)(2,1)}, bf16[2,256,256]{2,1,0:T(8,128)(2,1)S(1)}, u32[]{:S(2)}, u32[]{:S(2)}) collective-permute-start(bf16[2,256,256]{2,1,0:T(8,128)(2,1)} %shard_map.163), channel_id=1, source_target_pairs={{0,2},{1,3},{2,0},{3,1},{4,6},{5,7},{6,4},{7,5},{8,10},{9,11},{10,... | collective-permute-start | bytes 786440 | tf_op jit(solution)/shard_map/ppermute | solution.py:64
  365.4 38.3 %collective-permute-start.67 = (bf16[8,256,256]{2,1,0:T(8,128)(2,1)}, bf16[8,256,256]{2,1,0:T(8,128)(2,1)}, u32[]{:S(2)}, u32[]{:S(2)}) collective-permute-start(bf16[8,256,256]{2,1,0:T(8,128)(2,1)} %constant_dynamic-update-slice_fusion.rest_0_), channel_id=1, source_target_pairs={{0,8},{4,12},{8,0},{12,4},{1,9},{5,13},{9,1},{13,5},{2,10},{6,14},... | collective-permute-start | bytes 3145736 | tf_op jit(solution)/shard_map/ppermute | solution.py:64
  370.5 36.5 %collective-permute-start.61 = (bf16[384,1024]{1,0:T(8,128)(2,1)S(1)}, bf16[384,1024]{1,0:T(8,128)(2,1)S(1)}, u32[]{:S(2)}, u32[]{:S(2)}) collective-permute-start(bf16[384,1024]{1,0:T(8,128)(2,1)S(1)} %copy-done.15), channel_id=1, source_target_pairs={{0,16},{16,0},{1,17},{17,1},{2,18},{18,2},{3,19},{19,3},{4,20},{20... | collective-permute-start | bytes 2359304 | tf_op jit(solution)/shard_map/ppermute | solution.py:64
  370.6 20.5 %collective-permute-start.59 = (bf16[1,256,256]{2,1,0:T(8,128)(2,1)}, bf16[1,256,256]{2,1,0:T(8,128)(2,1)S(1)}, u32[]{:S(2)}, u32[]{:S(2)}) collective-permute-start(bf16[1,256,256]{2,1,0:T(8,128)(2,1)} %get-tuple-element.327), channel_id=1, source_target_pairs={{0,4},{4,0},{8,12},{12,8},{1,5},{5,1},{9,13},{13,9},{2,6},{6,2},{1... | collective-permute-start | bytes 393224 | tf_op jit(solution)/shard_map/ppermute | solution.py:64
  401.7 15.2 %collective-permute-start.71 = (bf16[4,256,256]{2,1,0:T(8,128)(2,1)}, bf16[4,256,256]{2,1,0:T(8,128)(2,1)}, u32[]{:S(2)}, u32[]{:S(2)}) collective-permute-start(bf16[4,256,256]{2,1,0:T(8,128)(2,1)} %constant_dynamic-update-slice_fusion.2.rest_0_), channel_id=1, source_target_pairs={{0,4},{4,0},{8,12},{12,8},{1,5},{5,1},{9,13},{13,9},{2,6},{6,2},{1... | collective-permute-start | bytes 1572872 | tf_op jit(solution)/shard_map/ppermute | solution.py:64
  402.7 16.3 %collective-permute-start.72 = (bf16[4,256,256]{2,1,0:T(8,128)(2,1)}, bf16[4,256,256]{2,1,0:T(8,128)(2,1)}, u32[]{:S(2)}, u32[]{:S(2)}) collective-permute-start(bf16[4,256,256]{2,1,0:T(8,128)(2,1)} %constant_dynamic-update-slice_fusion.2.rest_0_), channel_id=1, source_target_pairs={{0,8},{4,12},{8,0},{12,4},{1,9},{5,13},{9,1},{13,5},{2,10},{6,14},... | collective-permute-start | bytes 1572872 | tf_op jit(solution)/shard_map/ppermute | solution.py:64
  405.9 24.0 %collective-permute-start.68 = (bf16[4,256,256]{2,1,0:T(8,128)(2,1)S(1)}, bf16[4,256,256]{2,1,0:T(8,128)(2,1)}, u32[]{:S(2)}, u32[]{:S(2)}) collective-permute-start(bf16[4,256,256]{2,1,0:T(8,128)(2,1)S(1)} %slice.40), channel_id=1, source_target_pairs={{0,8},{4,12},{8,0},{12,4},{1,9},{5,13},{9,1},{13,5},{2,10},{6,14},... | collective-permute-start | bytes 1572872 | tf_op jit(solution)/shard_map/ppermute | solution.py:64
  407.0 22.9 %collective-permute-start.69 = (bf16[4,256,256]{2,1,0:T(8,128)(2,1)S(1)}, bf16[4,256,256]{2,1,0:T(8,128)(2,1)}, u32[]{:S(2)}, u32[]{:S(2)}) collective-permute-start(bf16[4,256,256]{2,1,0:T(8,128)(2,1)S(1)} %slice.41), channel_id=1, source_target_pairs={{0,4},{4,0},{8,12},{12,8},{1,5},{5,1},{9,13},{13,9},{2,6},{6,2},{1... | collective-permute-start | bytes 1572872 | tf_op jit(solution)/shard_map/ppermute | solution.py:64
  412.6 16.7 %all-to-all-start.5 = ((f32[4,2,1024]{2,1,0:T(2,128)}), f32[4,2,1024]{2,1,0:T(2,128)S(1)}, u32[]{:S(2)}, u32[]{:S(2)}) async-start(f32[4,2,1024]{2,1,0:T(2,128)} %broadcast_in_dim.23), calls=%async_computation.5 | async-start | bytes 65536 | tf_op jit(solution)/shard_map/all_to_all | solution.py:1454
  417.8 18.2 %collective-permute-start.73 = (bf16[2,256,256]{2,1,0:T(8,128)(2,1)S(1)}, bf16[2,256,256]{2,1,0:T(8,128)(2,1)S(1)}, u32[]{:S(2)}, u32[]{:S(2)}) collective-permute-start(bf16[2,256,256]{2,1,0:T(8,128)(2,1)S(1)} %slice.42), channel_id=1, source_target_pairs={{0,8},{4,12},{8,0},{12,4},{1,9},{5,13},{9,1},{13,5},{2,10},{6,14},... | collective-permute-start | bytes 786440 | tf_op jit(solution)/shard_map/ppermute | solution.py:64
  419.9 16.1 %collective-permute-start.74 = (bf16[2,256,256]{2,1,0:T(8,128)(2,1)S(1)}, bf16[2,256,256]{2,1,0:T(8,128)(2,1)S(1)}, u32[]{:S(2)}, u32[]{:S(2)}) collective-permute-start(bf16[2,256,256]{2,1,0:T(8,128)(2,1)S(1)} %slice.43), channel_id=1, source_target_pairs={{0,4},{4,0},{8,12},{12,8},{1,5},{5,1},{9,13},{13,9},{2,6},{6,2},{1... | collective-permute-start | bytes 786440 | tf_op jit(solution)/shard_map/ppermute | solution.py:64
  (116 other events, 767.3 us)

commit v5 on v4

--- a/solution.py
+++ b/solution.py
@@ -1104,6 +1104,7 @@
         us=4,
     )
     feed_z2 = swap(feed_piece, "tensor", 2)
+    top_same = swap(order.after(top_given), "tensor", 1)
     hidden_g, second_rows = call(
         middle_kernel,
         [shape((frames, width), f32), shape((frames, width), low16)],
@@ -1115,7 +1116,7 @@
     mix_x3 = swap(mix_z3, "dp", 1)
     mix_y3 = swap(mix_z3, "dp", 2)
     second_blocks = gather(second_rows)
-    order.until(feed_z2, mix_x, mix_y, mix_x3, mix_y3)
+    order.until(feed_z2, mix_x, mix_y, mix_x3, mix_y3, top_same)
     feed_z2, mix_x, mix_y, mix_x3, mix_y3 = order.after((feed_z2, mix_x, mix_y, mix_x3, mix_y3))
     mix_w = (
         mix_whole,
@@ -1153,7 +1154,7 @@
         us=5.6,
     )
     arrived = scatter(partial)
-    order.until(feed_x, feed_y)
+    order.until(feed_x, feed_y, mix_w[6], mix_w[7], mix_w[10], mix_w[11])
     sent = call(
         sent_kernel,
         [shape((frames, width), low16)],
@@ -1162,7 +1163,6 @@
         us=1.9,
     )[0]
     other_sent = swap(sent, "section", 1)
-    feed_x, feed_y = order.after((feed_x, feed_y))
     feed_l = (
         feed_whole,
         feed_z2,
@@ -1171,7 +1171,8 @@
         swap(feed_x[:2], "dp", 2),
         swap(feed_y[2:], "dp", 1),
     )
-    top_same = swap(order.after(top_given), "tensor", 1)
+
+    order.until(*feed_l)
 
     start_l, first_l, query_keys, values_l, probs_l, mixed_l, partial = call(
         local_attention_kernel,
@@ -1193,7 +1194,6 @@
         ],
         us=9,
     )
-    order.until(*feed_l, top_same)
     hidden_l, second_l, second_given = call(
         local_norm_kernel,
         [
@@ -1238,11 +1238,11 @@
 
     def from_neighbour(same, cross):
         total = call(
-            pair_kernel, [half_rows], (same, swap(cross, "section", 1)), [VM] * 2
+            pair_kernel, [half_rows], (same, cross), [VM] * 2
         )[0]
         return swap(total, "tensor", 1)
 
-    far_same = from_neighbour(same, cross)
+    far_same = from_neighbour(same, swap(cross, "section", 1))
     turned_l = pltpu.VMEM((width, rows_l), low16)
     local_feed = Sum(
         order,
@@ -1411,9 +1411,11 @@
         [pltpu.VMEM((frames, width), f32)],
         us=2.1,
     )
+    world_feed = global_feed.third()
+    global_mix.second()
     local_mix.fourth()
-    feed_sum = local_feed.gathered(info, global_feed.third())
-    global_mix.second()
+    world_mix = global_mix.third()
+    feed_sum = local_feed.gathered(info, world_feed)
     own_branch, same, cross = call(
         local_drop_kernel,
         [wide_rows, half_rows, half_rows],
@@ -1427,6 +1429,7 @@
         us=6.1,
     )
     other_branch = swap(own_branch, "section", 1)
+    branch_cross = swap(cross, "section", 1)
     arrived_start = swap(given_start, "section", 1)
     both_start = jnp.stack(
         [
@@ -1435,8 +1438,6 @@
         ]
     )
     code_grad = jnp.transpose(code_part + both_start[:, None], (0, 2, 1, 3))
-    far_branch = from_neighbour(same, cross)
-    far_branch = (far_branch, swap(far_branch, "section", 1))
 
     own_gain = jnp.concatenate([gain1_g, gain2_g], axis=0)
     total_gain = own_gain + swap(own_gain, "section", 1)
@@ -1453,10 +1454,12 @@
         copies = jnp.broadcast_to(value, (lax.axis_size(axis),) + value.shape)
         return jnp.sum(lax.all_to_all(order.after(copies), axis, 0, 0), axis=0)
 
+    mix_sum = local_mix.gathered(info, world_mix)
+    far_branch = from_neighbour(same, branch_cross)
     gain_total = over(gain_total, "tensor")
-    order.until(gain_total)
-
-    mix_sum = local_mix.gathered(info, global_mix.third())
+    order.until(gain_total, *feed_sum.near)
+    feed_parts = feed_sum.far()
+    far_branch = (far_branch, swap(far_branch, "section", 1))
     output = call(
         output_kernel,
         [shape((utts, code_count, frames, width // 2), low16)],
@@ -1464,10 +1467,9 @@
         [SM] + [VM] * 5,
         us=3.1,
     )[0]
-    feed_parts = feed_sum.far()
+    mix_parts = mix_sum.far()
     gain_total = over(gain_total, "dp")
     order.until(gain_total)
-    mix_parts = mix_sum.far()
     up_grad, down_grad = call(
         feed_final_kernel,
         [shape((width, wide), f32), shape((wide, width), f32)],

time: 448 us -> 438 us (0.978)
  blocking collectives: 91.9 us -> 81.1 us
    all_to_all x1 -> x0, blocking collectives: 9.72 us -> none  [over(): return jnp.sum(lax.all_to_all(order.after(copies), axis, 0, 0), axis=0)]
    ppermute x75, waiting for transfers between devices: 64.9 us -> 59 us  [swap(): return lax.ppermute(value, axis, [(i, i ^ flip) for i in range(count)])]
    all_to_all x1 -> x2, waiting for transfers between devices: 6.93 us -> 9.34 us  [over(): return jnp.sum(lax.all_to_all(order.after(copies), axis, 0, 0), axis=0)]
    unnamed x170 -> x160, local copies, waits for them, and re-layouts: 23.6 us -> 24.4 us
  transfers between devices with their start and end apart: 80 -> 81, of which waited for: 24 -> 22; matrix products, arithmetic and copies ran while one was open for 3% -> 3% of each run, Pallas kernels for 28% -> 28%
where the time goes in v5:
time: 438 us; the launch traced here: 432 us
  Pallas kernels  161 us (37%)
  starting transfers between devices  83.6 us (19%)
  blocking collectives  81.1 us (19%)
  waiting for transfers between devices  68.4 us (16%)
  local copies, waits for them, and re-layouts  32.5 us (7%)
    pallas_call x39, Pallas kernels, call(): pl.pallas_call(body, out_shape=tuple(outs), grid=grid, in_specs=list(spec...  161 us
    all_gather x4, blocking collectives, gather(): gathered = lax.all_gather(rows, 'tensor')  81.1 us
    ppermute x75, starting transfers between devices, swap(): return lax.ppermute(value, axis, [(i, i ^ flip) for i in range(count)])  61.7 us
    ppermute x75, waiting for transfers between devices, swap(): return lax.ppermute(value, axis, [(i, i ^ flip) for i in range(count)])  59 us
    unnamed x160, local copies, waits for them, and re-layouts  24.4 us
    all_to_all x4, starting transfers between devices, scatter(): return lax.all_to_all(partial, 'tensor', 0, 0)  15.4 us
    all_to_all x2, waiting for transfers between devices, over(): return jnp.sum(lax.all_to_all(order.after(copies), axis, 0, 0), axis=0)  9.34 us
  transfers between devices with their start and end apart: 81, of which 22 were waited for; matrix products, arithmetic and copies ran while one was open for 3% of the time, Pallas kernels for 28%

profile of v5, /device:TPU:0, one launch (start us, length us, event | category | flops | bytes accessed | tf_op | source)
XLA Modules:
  0.0 432.1 jit_solution(5899480642221999043)
XLA Ops:
  5.9 19.5 %all-gather = bf16[256,1024]{1,0:T(8,128)(2,1)} all-gather(bf16[64,1024]{1,0:T(8,128)(2,1)} %get-tuple-element.180), channel_id=2, replica_groups=mesh['section'=2,'dp'=4,'tensor'=4] {'tensor'}, dimensions={0}, use_global_device_ids=true | all-gather | bytes 655360 | tf_op jit(solution)/shard_map/all_gather | solution.py:1025
  26.2 3.3 shard_map.136
  30.3 2.5 collective-permute-start.6
  32.9 5.7 %shard_map.137 = (bf16[256,1024]{1,0:T(8,128)(2,1)}, bf16[3,256,256]{2,1,0:T(8,128)(2,1)}, f32[4,256,256]{2,1,0:T(8,128)}, bf16[256,256]{1,0:T(8,128)(2,1)}, bf1...) custom-call(s32[5]{0:T(128)} %pad_add_fusion.info, bf16[4,64,1024]{2,1,0:T(8,128)(2,1)} %bitcast.49, ...), custom_call_target="tpu_custom_call" | custom-call | flops 1140000000 | tf_op jit(solution)/shard_map/pallas_call | solution.py:46
  38.6 5.2 %collective-permute-done.5.rest_1_ = bf16[2,256,256]{2,1,0:T(8,128)(2,1)S(1)} collective-permute-done((bf16[2,256,256]{2,1,0:T(8,128)(2,1)}, bf16[2,256,256]{2,1,0:T(8,128)(2,1)S(1)}, u32[]{:S(2)}, u32[]{:S(2)}) %collective-permute-start.5) | collective-permute-done | bytes 262176 | tf_op jit(solution)/shard_map/ppermute | solution.py:64
  45.2 4.1 all-to-all-start
  57.5 3.9 shard_map.139
  66.3 4.0 collective-permute-done.10.rest_3_
  73.0 25.3 %all-gather.1 = bf16[256,1024]{1,0:T(8,128)(2,1)} all-gather(bf16[64,1024]{1,0:T(8,128)(2,1)} %get-tuple-element.200), channel_id=3, replica_groups=mesh['section'=2,'dp'=4,'tensor'=4] {'tensor'}, dimensions={0}, use_global_device_ids=true | all-gather | bytes 655360 | tf_op jit(solution)/shard_map/all_gather | solution.py:1025
  98.4 6.1 %shard_map.141 = (bf16[256,1024]{1,0:T(8,128)(2,1)}, f32[256,1024]{1,0:T(8,128)}, bf16[256,1024]{1,0:T(8,128)(2,1)}, bf16[256,512]{1,0:T(8,128)(2,1)}, bf16[4,64,1024]{2,1,0:T(8,128)(2,1)}) custom-call(s32[5]{0:T(128)} %pad_add_fusion.info, bf16[4,64,1024]{2,1,0:T(8,128)(2,1)} %bitcast.50, bf16[1024,1024]{1,0:T(8,128)(2,1)} %bitcast.37, ...), custom_call_target="tpu_custom_call" | custom-call | flops 1120000000 | tf_op jit(solution)/shard_map/pallas_call | solution.py:46
  104.5 4.0 all-to-all-start.1
  114.4 7.2 %collective-permute-done.14.rest_2_ = bf16[4,256,256]{2,1,0:T(8,128)(2,1)S(1)} collective-permute-done((bf16[4,256,256]{2,1,0:T(8,128)(2,1)}, bf16[4,256,256]{2,1,0:T(8,128)(2,1)S(1)}, u32[]{:S(2)}, u32[]{:S(2)}) %collective-permute-start.14) | collective-permute-done | bytes 524320 | tf_op jit(solution)/shard_map/ppermute | solution.py:64
  122.6 2.5 collective-permute-done.15.rest_3_
  126.7 2.9 collective-permute-done.18.rest_10_
  133.2 2.8 collective-permute-done.21.rest_5_
  136.6 9.0 %shard_map.143 = (f32[384,1024]{1,0:T(8,128)}, bf16[384,1024]{1,0:T(8,128)(2,1)}, bf16[4,384,256]{2,1,0:T(8,128)(2,1)}, bf16[4,384,128]{2,1,0:T(8,128)(2,1)}, f3...) custom-call(s32[5]{0:T(128)} %pad_add_fusion.info, ...), custom_call_target="tpu_custom_call" | custom-call | flops 1800000000 | tf_op jit(solution)/shard_map/pallas_call | solution.py:46
  149.1 3.7 shard_map.144
  154.6 7.8 %shard_map.145 = (bf16[4,384,256]{2,1,0:T(8,128)(2,1)}, bf16[4,384,256]{2,1,0:T(8,128)(2,1)}, bf16[384,1024]{1,0:T(8,128)(2,1)}) custom-call(bf16[384,1024]{1,0:T(8,128)(2,1)} %get-tuple-element.235.second, bf16[384,1024]{1,0:T(8,128)(2,1)} %get-tuple-element.225.top, bf16[4,4,256,256]{3,2,1,0:T(8,128)(2,1)} %get-tuple-element.194.rest_0_, ...), custom_call_target="tpu_custom_call" | custom-call | flops 1580000000 | tf_op jit(solution)/shard_map/pallas_call | solution.py:46
  166.7 8.0 %shard_map.146 = (bf16[4,384,256]{2,1,0:T(8,128)(2,1)}, bf16[4,384,256]{2,1,0:T(8,128)(2,1)}, bf16[384,1024]{1,0:T(8,128)(2,1)}, bf16[384,1024]{1,0:T(8,128)(2,1...) custom-call(bf16[192,1024]{1,0:T(8,128)(2,1)} %copy-done.67, bf16[192,1024]{1,0:T(8,128)(2,1)} %copy-done.70, ...), custom_call_target="tpu_custom_call" | custom-call | flops 1640000000 | tf_op jit(solution)/shard_map/pallas_call | solution.py:46
  181.2 7.6 %shard_map.148 = (bf16[2,4,256,256]{3,2,1,0:T(8,128)(2,1)}, bf16[2,4,256,256]{3,2,1,0:T(8,128)(2,1)}, bf16[2,4,256,256]{3,2,1,0:T(8,128)(2,1)}, bf16[2,4,256,256]{3,2,1,0:T(8,128)(2,1)}) custom-call(bf16[384,1024]{1,0:T(8,128)(2,1)} %get-tuple-element.235.second, bf16[384,1024]{1,0:T(8,128)(2,1)} %get-tuple-element.236.far_second, ...), custom_call_target="tpu_custom_call" | custom-call | flops 1520000000 | tf_op jit(solution)/shard_map/pallas_call | solution.py:46
  194.0 11.5 %shard_map.149 = (f32[384,1024]{1,0:T(8,128)}, bf16[384,1024]{1,0:T(8,128)(2,1)}, bf16[4,384,256]{2,1,0:T(8,128)(2,1)}, bf16[4,384,128]{2,1,0:T(8,128)(2,1)}, bf...) custom-call(s32[5]{0:T(128)} %pad_add_fusion.info, f32[384,1024]{1,0:T(8,128)} %get-tuple-element.243.hidden, ...), custom_call_target="tpu_custom_call" | custom-call | flops 2280000000 | tf_op jit(solution)/shard_map/pallas_call | solution.py:46
  206.1 6.2 %shard_map.150 = (bf16[2,4,256,256]{3,2,1,0:T(8,128)(2,1)}, bf16[2,4,256,256]{3,2,1,0:T(8,128)(2,1)}, bf16[2,4,256,256]{3,2,1,0:T(8,128)(2,1)}, bf16[2,4,256,256]{3,2,1,0:T(8,128)(2,1)}) custom-call(bf16[384,1024]{1,0:T(8,128)(2,1)} %get-tuple-element.249.first, bf16[4,384,256]{2,1,0:T(8,128)(2,1)} %get-tuple-element.250.grad_query_keys, ...), custom_call_target="tpu_custom_call" | custom-call | flops 1200000000 | tf_op jit(solution)/shard_map/pallas_call | solution.py:46
  214.2 2.8 collective-permute-done.32.from_x.refs_1_
  218.8 4.2 shard_map.151
  223.1 18.3 %all-gather.2 = bf16[256,1024]{1,0:T(8,128)(2,1)} all-gather(bf16[64,1024]{1,0:T(8,128)(2,1)} %get-tuple-element.260.returned), channel_id=4, replica_groups=mesh['section'=2,'dp'=4,'tensor'=4] {'tensor'}, dimensions={0}, use_global_device_ids=true | all-gather | bytes 655360 | tf_op jit(solution)/shard_map/all_gather | solution.py:1025
  241.4 2.6 shard_map.152
  247.9 7.2 %shard_map.153 = (bf16[256,1024]{1,0:T(8,128)(2,1)}, bf16[256,1024]{1,0:T(8,128)(2,1)}, bf16[256,512]{1,0:T(8,128)(2,1)}, bf16[4,64,1024]{2,1,0:T(8,128)(2,1)}) custom-call(s32[5]{0:T(128)} %pad_add_fusion.info, bf16[4,64,1024]{2,1,0:T(8,128)(2,1)} %bitcast.48, f32[256,1024]{1,0:T(8,128)} %get-tuple-element.276.rest_1_, bf16[1024,1024]{1,0:T(8,128)(2,1)} %bitcast.38, ...), custom_call_target="tpu_custom_call" | custom-call | flops 1260000000 | tf_op jit(solution)/shard_map/pallas_call | solution.py:46
  255.1 3.5 all-to-all-start.2
  260.8 3.1 shard_map.154
  263.9 2.6 shard_map.155
  268.6 4.2 shard_map.156
  278.7 18.1 %all-gather.3 = bf16[256,1024]{1,0:T(8,128)(2,1)} all-gather(bf16[64,1024]{1,0:T(8,128)(2,1)} %get-tuple-element.291), channel_id=5, replica_groups=mesh['section'=2,'dp'=4,'tensor'=4] {'tensor'}, dimensions={0}, use_global_device_ids=true | all-gather | bytes 655360 | tf_op jit(solution)/shard_map/all_gather | solution.py:1025
  296.8 7.2 %shard_map.158 = (bf16[256,1024]{1,0:T(8,128)(2,1)}, bf16[3,256,256]{2,1,0:T(8,128)(2,1)}, bf16[3,256,128]{2,1,0:T(8,128)(2,1)}, bf16[4,64,1024]{2,1,0:T(8,128)(2,1)}) custom-call(s32[5]{0:T(128)} %pad_add_fusion.info, bf16[4,64,1024]{2,1,0:T(8,128)(2,1)} %bitcast.51, bf16[3,256,256]{2,1,0:T(8,128)(2,1)} %get-tuple-element.294.rest_1_, ...), custom_call_target="tpu_custom_call" | custom-call | flops 1360000000 | tf_op jit(solution)/shard_map/pallas_call | solution.py:46
  304.1 3.7 all-to-all-start.3
  312.2 3.2 shard_map.160
  321.4 3.7 shard_map.161
  339.1 2.7 collective-permute-done.54.arrived.refs_1_
  348.5 2.5 shard_map.167
  356.4 6.1 %shard_map.168 = (bf16[384,1024]{1,0:T(8,128)(2,1)}, bf16[192,1024]{1,0:T(8,128)(2,1)}, bf16[192,1024]{1,0:T(8,128)(2,1)}) custom-call(bf16[4,384,256]{2,1,0:T(8,128)(2,1)} %get-tuple-element.326.own_active, bf16[4,384,256]{2,1,0:T(8,128)(2,1)} %get-tuple-element.239.far_active, bf16[4,4,256,256]{3,2,1,0:T(8,128)(2,1)} %get-tuple-element.194.rest_0_, ...), custom_call_target="tpu_custom_call" | custom-call | flops 1220000000 | tf_op jit(solution)/shard_map/pallas_call | solution.py:46
  362.6 6.2 %collective-permute-done.58.refs_2_ = bf16[2,256,256]{2,1,0:T(8,128)(2,1)S(1)} collective-permute-done((bf16[2,256,256]{2,1,0:T(8,128)(2,1)S(1)}, bf16[2,256,256]{2,1,0:T(8,128)(2,1)S(1)}, u32[]{:S(2)}, u32[]{:S(2)}) %collective-permute-start.58) | collective-permute-done | bytes 262176 | tf_op jit(solution)/shard_map/ppermute | solution.py:64
  379.5 8.3 %collective-permute-done.65.far_same = bf16[192,1024]{1,0:T(8,128)(2,1)S(1)} collective-permute-done((bf16[192,1024]{1,0:T(8,128)(2,1)}, bf16[192,1024]{1,0:T(8,128)(2,1)S(1)}, u32[]{:S(2)}, u32[]{:S(2)}) %collective-permute-start.65) | collective-permute-done | bytes 393248 | tf_op jit(solution)/shard_map/ppermute | solution.py:64
  394.4 3.3 all-to-all-start.4
  397.7 5.6 %all-to-all-done.4 = f32[4,2,1024]{2,1,0:T(2,128)S(1)} async-done(((f32[4,2,1024]{2,1,0:T(2,128)}), f32[4,2,1024]{2,1,0:T(2,128)S(1)}, u32[]{:S(2)}, u32[]{:S(2)}) %all-to-all-start.4) | async-done | bytes 32800 | tf_op jit(solution)/shard_map/all_to_all | solution.py:1455
  408.9 3.1 shard_map.171
  412.6 3.3 all-to-all-start.5
  416.8 3.7 all-to-all-done.5
  421.2 6.1 %shard_map.172 = (f32[1024,1024]{1,0:T(8,128)}, f32[1024,1024]{1,0:T(8,128)}) custom-call(s32[5]{0:T(128)} %pad_add_fusion.info, bf16[8,256,256]{2,1,0:T(8,128)(2,1)} %constant_dynamic-update-slice_fusion.rest_0_, bf16[8,256,256]{2,1,0:T(8,128)(2,1)} %copy-done.47, bf16[8,256,256]{2,1,0:T(8,128)(2,1)} %collective-permute-done.63.rest_2_, ...), custom_call_target="tpu_custom_call" | custom-call | flops 1360000000 | tf_op jit(solution)/shard_map/pallas_call | solution.py:46
  428.0 3.9 shard_map.173
  (342 shorter events, 138.2 us)
Async XLA Ops:
  2.2 23.3 %collective-permute-start.1 = (bf16[3,1024,256]{2,1,0:T(8,128)(2,1)}, bf16[3,1024,256]{2,1,0:T(8,128)(2,1)}, u32[]{:S(2)}, u32[]{:S(2)}) collective-permute-start(bf16[3,1024,256]{2,1,0:T(8,128)(2,1)} %bitcast.40), channel_id=1, source_target_pairs={{0,16},{16,0},{1,17},{17,1},{2,18},{18,2},{3,19},{19,3},{4,20},{20... | collective-permute-start | bytes 4718600 | tf_op jit(solution)/shard_map/ppermute | solution.py:64
  2.5 22.9 %collective-permute-start.2 = (bf16[256,1024]{1,0:T(8,128)(2,1)}, bf16[256,1024]{1,0:T(8,128)(2,1)S(1)}, u32[]{:S(2)}, u32[]{:S(2)}) collective-permute-start(bf16[256,1024]{1,0:T(8,128)(2,1)} %bitcast.44), channel_id=1, source_target_pairs={{0,16},{16,0},{1,17},{17,1},{2,18},{18,2},{3,19},{19,3},{4,20},{20... | collective-permute-start | bytes 1572872 | tf_op jit(solution)/shard_map/ppermute | solution.py:64
  29.5 27.9 %collective-permute-start.3 = (bf16[1024,1024]{1,0:T(8,128)(2,1)S(1)}, bf16[1024,1024]{1,0:T(8,128)(2,1)}, u32[]{:S(2)}, u32[]{:S(2)}) collective-permute-start(bf16[1024,1024]{1,0:T(8,128)(2,1)S(1)} %bitcast.39), channel_id=1, source_target_pairs={{0,16},{16,0},{1,17},{17,1},{2,18},{18,2},{3,19},{19,3},{4,20},{20... | collective-permute-start | bytes 6291464 | tf_op jit(solution)/shard_map/ppermute | solution.py:64
  29.6 27.9 %collective-permute-start.4 = (bf16[1024,1024]{1,0:T(8,128)(2,1)}, bf16[1024,1024]{1,0:T(8,128)(2,1)}, u32[]{:S(2)}, u32[]{:S(2)}) collective-permute-start(bf16[1024,1024]{1,0:T(8,128)(2,1)} %bitcast.9.own_down.rest_3_.rest_4_), channel_id=1, source_target_pairs={{0,16},{16,0},{1,17},{17,1},{2,18},{18,2},{3,19},{19,3},{4,20},{20... | collective-permute-start | bytes 6291464 | tf_op jit(solution)/shard_map/ppermute | solution.py:64
  30.1 13.7 %collective-permute-start.5 = (bf16[2,256,256]{2,1,0:T(8,128)(2,1)}, bf16[2,256,256]{2,1,0:T(8,128)(2,1)S(1)}, u32[]{:S(2)}, u32[]{:S(2)}) collective-permute-start(bf16[2,256,256]{2,1,0:T(8,128)(2,1)} %get-tuple-element.196), channel_id=1, source_target_pairs={{0,1},{1,0},{2,3},{3,2},{4,5},{5,4},{6,7},{7,6},{8,9},{9,8},{10,11... | collective-permute-start | bytes 786440 | tf_op jit(solution)/shard_map/ppermute | solution.py:64
  30.3 14.8 %collective-permute-start.6 = (bf16[2,256,256]{2,1,0:T(8,128)(2,1)}, bf16[2,256,256]{2,1,0:T(8,128)(2,1)S(1)}, u32[]{:S(2)}, u32[]{:S(2)}) collective-permute-start(bf16[2,256,256]{2,1,0:T(8,128)(2,1)} %get-tuple-element.196), channel_id=1, source_target_pairs={{0,2},{1,3},{2,0},{3,1},{4,6},{5,7},{6,4},{7,5},{8,10},{9,11},{10,... | collective-permute-start | bytes 786440 | tf_op jit(solution)/shard_map/ppermute | solution.py:64
  45.2 19.2 %all-to-all-start = ((bf16[4,64,1024]{2,1,0:T(8,128)(2,1)}), bf16[4,64,1024]{2,1,0:T(8,128)(2,1)}, u32[]{:S(2)}, u32[]{:S(2)}) async-start(bf16[4,64,1024]{2,1,0:T(8,128)(2,1)} %get-tuple-element.197), calls=%async_computation | async-start | bytes 1048576 | tf_op jit(solution)/shard_map/all_to_all | solution.py:1030
  52.5 19.2 %collective-permute-start.8 = (bf16[2,2,256,256]{3,2,1,0:T(8,128)(2,1)}, bf16[2,2,256,256]{3,2,1,0:T(8,128)(2,1)S(1)}, u32[]{:S(2)}, u32[]{:S(2)}) collective-permute-start(bf16[2,2,256,256]{3,2,1,0:T(8,128)(2,1)} %pad_maximum_fusion), channel_id=1, source_target_pairs={{0,4},{4,0},{8,12},{12,8},{1,5},{5,1},{9,13},{13,9},{2,6},{6,2},{1... | collective-permute-start | bytes 1572872 | tf_op jit(solution)/shard_map/ppermute | solution.py:64
  54.0 44.3 %collective-permute-start.9 = (bf16[2,2,256,256]{3,2,1,0:T(8,128)(2,1)}, bf16[2,2,256,256]{3,2,1,0:T(8,128)(2,1)S(1)}, u32[]{:S(2)}, u32[]{:S(2)}) collective-permute-start(bf16[2,2,256,256]{3,2,1,0:T(8,128)(2,1)} %pad_maximum_fusion), channel_id=1, source_target_pairs={{0,8},{4,12},{8,0},{12,4},{1,9},{5,13},{9,1},{13,5},{2,10},{6,14},... | collective-permute-start | bytes 1572872 | tf_op jit(solution)/shard_map/ppermute | solution.py:64
  55.5 14.8 %collective-permute-start.10 = (bf16[2,256,256]{2,1,0:T(8,128)(2,1)}, bf16[2,256,256]{2,1,0:T(8,128)(2,1)}, u32[]{:S(2)}, u32[]{:S(2)}) collective-permute-start(bf16[2,256,256]{2,1,0:T(8,128)(2,1)} %copy-done.13), channel_id=1, source_target_pairs={{0,1},{1,0},{2,3},{3,2},{4,5},{5,4},{6,7},{7,6},{8,9},{9,8},{10,11... | collective-permute-start | bytes 786440 | tf_op jit(solution)/shard_map/ppermute | solution.py:64
  61.4 37.0 %collective-permute-start.7 = (bf16[4,256,256]{2,1,0:T(8,128)(2,1)}, bf16[4,256,256]{2,1,0:T(8,128)(2,1)}, u32[]{:S(2)}, u32[]{:S(2)}) collective-permute-start(bf16[4,256,256]{2,1,0:T(8,128)(2,1)} %get-tuple-element.201), channel_id=1, source_target_pairs={{0,2},{1,3},{2,0},{3,1},{4,6},{5,7},{6,4},{7,5},{8,10},{9,11},{10,... | collective-permute-start | bytes 1572872 | tf_op jit(solution)/shard_map/ppermute | solution.py:64
  63.8 34.5 %collective-permute-start.13 = (bf16[192,1024]{1,0:T(8,128)(2,1)}, bf16[192,1024]{1,0:T(8,128)(2,1)S(1)}, u32[]{:S(2)}, u32[]{:S(2)}) collective-permute-start(bf16[192,1024]{1,0:T(8,128)(2,1)} %get-tuple-element.208), channel_id=1, source_target_pairs={{0,1},{1,0},{2,3},{3,2},{4,5},{5,4},{6,7},{7,6},{8,9},{9,8},{10,11... | collective-permute-start | bytes 1179656 | tf_op jit(solution)/shard_map/ppermute | solution.py:64
  70.3 28.0 %collective-permute-start.11 = (bf16[2,256,256]{2,1,0:T(8,128)(2,1)}, bf16[2,256,256]{2,1,0:T(8,128)(2,1)S(1)}, u32[]{:S(2)}, u32[]{:S(2)}) collective-permute-start(bf16[2,256,256]{2,1,0:T(8,128)(2,1)} %collective-permute-done.10.rest_3_), channel_id=1, source_target_pairs={{0,4},{4,0},{8,12},{12,8},{1,5},{5,1},{9,13},{13,9},{2,6},{6,2},{1... | collective-permute-start | bytes 786440 | tf_op jit(solution)/shard_map/ppermute | solution.py:64
  71.6 26.7 %collective-permute-start.12 = (bf16[2,256,256]{2,1,0:T(8,128)(2,1)}, bf16[2,256,256]{2,1,0:T(8,128)(2,1)S(1)}, u32[]{:S(2)}, u32[]{:S(2)}) collective-permute-start(bf16[2,256,256]{2,1,0:T(8,128)(2,1)} %collective-permute-done.10.rest_3_), channel_id=1, source_target_pairs={{0,8},{4,12},{8,0},{12,4},{1,9},{5,13},{9,1},{13,5},{2,10},{6,14},... | collective-permute-start | bytes 786440 | tf_op jit(solution)/shard_map/ppermute | solution.py:64
  104.5 26.0 %all-to-all-start.1 = ((bf16[4,64,1024]{2,1,0:T(8,128)(2,1)}), bf16[4,64,1024]{2,1,0:T(8,128)(2,1)S(1)}, u32[]{:S(2)}, u32[]{:S(2)}) async-start(bf16[4,64,1024]{2,1,0:T(8,128)(2,1)} %get-tuple-element.210), calls=%async_computation.1 | async-start | bytes 1048576 | tf_op jit(solution)/shard_map/all_to_all | solution.py:1030
  110.1 15.1 %collective-permute-start.15 = (bf16[4,256,256]{2,1,0:T(8,128)(2,1)}, bf16[4,256,256]{2,1,0:T(8,128)(2,1)S(1)}, u32[]{:S(2)}, u32[]{:S(2)}) collective-permute-start(bf16[4,256,256]{2,1,0:T(8,128)(2,1)} %collective-permute-done.7.rest_1_), channel_id=1, source_target_pairs={{0,8},{4,12},{8,0},{12,4},{1,9},{5,13},{9,1},{13,5},{2,10},{6,14},... | collective-permute-start | bytes 1572872 | tf_op jit(solution)/shard_map/ppermute | solution.py:64
  111.6 18.8 %collective-permute-start.16 = (bf16[2,256,256]{2,1,0:T(8,128)(2,1)S(1)}, bf16[2,256,256]{2,1,0:T(8,128)(2,1)S(1)}, u32[]{:S(2)}, u32[]{:S(2)}) collective-permute-start(bf16[2,256,256]{2,1,0:T(8,128)(2,1)S(1)} %slice_bitcast_fusion.1), channel_id=1, source_target_pairs={{0,8},{4,12},{8,0},{12,4},{1,9},{5,13},{9,1},{13,5},{2,10},{6,14},... | collective-permute-start | bytes 786440 | tf_op jit(solution)/shard_map/ppermute | solution.py:64
  112.2 18.2 %collective-permute-start.17 = (bf16[2,256,256]{2,1,0:T(8,128)(2,1)S(1)}, bf16[2,256,256]{2,1,0:T(8,128)(2,1)S(1)}, u32[]{:S(2)}, u32[]{:S(2)}) collective-permute-start(bf16[2,256,256]{2,1,0:T(8,128)(2,1)S(1)} %slice_bitcast_fusion), channel_id=1, source_target_pairs={{0,4},{4,0},{8,12},{12,8},{1,5},{5,1},{9,13},{13,9},{2,6},{6,2},{1... | collective-permute-start | bytes 786440 | tf_op jit(solution)/shard_map/ppermute | solution.py:64
  112.8 16.8 %collective-permute-start.18 = (bf16[1,256,256]{2,1,0:T(8,128)(2,1)S(1)}, bf16[1,256,256]{2,1,0:T(8,128)(2,1)S(1)}, u32[]{:S(2)}, u32[]{:S(2)}) collective-permute-start(bf16[1,256,256]{2,1,0:T(8,128)(2,1)S(1)} %slice.32), channel_id=1, source_target_pairs={{0,8},{4,12},{8,0},{12,4},{1,9},{5,13},{9,1},{13,5},{2,10},{6,14},... | collective-permute-start | bytes 393224 | tf_op jit(solution)/shard_map/ppermute | solution.py:64
  190.8 26.2 %collective-permute-start.32 = (bf16[2,4,256,256]{3,2,1,0:T(8,128)(2,1)}, bf16[2,4,256,256]{3,2,1,0:T(8,128)(2,1)S(1)}, u32[]{:S(2)}, u32[]{:S(2)}) collective-permute-start(bf16[2,4,256,256]{3,2,1,0:T(8,128)(2,1)} %get-tuple-element.262), channel_id=1, source_target_pairs={{0,4},{4,0},{8,12},{12,8},{1,5},{5,1},{9,13},{13,9},{2,6},{6,2},{1... | collective-permute-start | bytes 3145736 | tf_op jit(solution)/shard_map/ppermute | solution.py:64
  191.7 26.2 %collective-permute-start.33 = (bf16[2,4,256,256]{3,2,1,0:T(8,128)(2,1)}, bf16[2,4,256,256]{3,2,1,0:T(8,128)(2,1)S(1)}, u32[]{:S(2)}, u32[]{:S(2)}) collective-permute-start(bf16[2,4,256,256]{3,2,1,0:T(8,128)(2,1)} %get-tuple-element.263), channel_id=1, source_target_pairs={{0,8},{4,12},{8,0},{12,4},{1,9},{5,13},{9,1},{13,5},{2,10},{6,14},... | collective-permute-start | bytes 3145736 | tf_op jit(solution)/shard_map/ppermute | solution.py:64
  192.9 21.0 %collective-permute-start.37 = (bf16[256,128]{1,0:T(8,128)(2,1)S(1)}, bf16[256,128]{1,0:T(8,128)(2,1)S(1)}, u32[]{:S(2)}, u32[]{:S(2)}) collective-permute-start(bf16[256,128]{1,0:T(8,128)(2,1)S(1)} %copy-done.77), channel_id=1, source_target_pairs={{0,16},{16,0},{1,17},{17,1},{2,18},{18,2},{3,19},{19,3},{4,20},{20... | collective-permute-start | bytes 196616 | tf_op jit(solution)/shard_map/ppermute | solution.py:64
  212.2 35.7 %collective-permute-start.34 = (bf16[2,4,256,256]{3,2,1,0:T(8,128)(2,1)}, bf16[2,4,256,256]{3,2,1,0:T(8,128)(2,1)S(1)}, u32[]{:S(2)}, u32[]{:S(2)}) collective-permute-start(bf16[2,4,256,256]{3,2,1,0:T(8,128)(2,1)} %get-tuple-element.265), channel_id=1, source_target_pairs={{0,4},{4,0},{8,12},{12,8},{1,5},{5,1},{9,13},{13,9},{2,6},{6,2},{1... | collective-permute-start | bytes 3145736 | tf_op jit(solution)/shard_map/ppermute | solution.py:64
  213.9 34.0 %collective-permute-start.35 = (bf16[2,4,256,256]{3,2,1,0:T(8,128)(2,1)}, bf16[2,4,256,256]{3,2,1,0:T(8,128)(2,1)S(1)}, u32[]{:S(2)}, u32[]{:S(2)}) collective-permute-start(bf16[2,4,256,256]{3,2,1,0:T(8,128)(2,1)} %get-tuple-element.266), channel_id=1, source_target_pairs={{0,8},{4,12},{8,0},{12,4},{1,9},{5,13},{9,1},{13,5},{2,10},{6,14},... | collective-permute-start | bytes 3145736 | tf_op jit(solution)/shard_map/ppermute | solution.py:64
  217.0 28.3 %collective-permute-start.36 = (bf16[256,1024]{1,0:T(8,128)(2,1)S(1)}, bf16[256,1024]{1,0:T(8,128)(2,1)S(1)}, u32[]{:S(2)}, u32[]{:S(2)}) collective-permute-start(bf16[256,1024]{1,0:T(8,128)(2,1)S(1)} %copy-done.32), channel_id=1, source_target_pairs={{0,16},{16,0},{1,17},{17,1},{2,18},{18,2},{3,19},{19,3},{4,20},{20... | collective-permute-start | bytes 1572872 | tf_op jit(solution)/shard_map/ppermute | solution.py:64
  217.9 30.0 %collective-permute-start.38 = (bf16[256,1024]{1,0:T(8,128)(2,1)S(1)}, bf16[256,1024]{1,0:T(8,128)(2,1)S(1)}, u32[]{:S(2)}, u32[]{:S(2)}) collective-permute-start(bf16[256,1024]{1,0:T(8,128)(2,1)S(1)} %copy-done.33), channel_id=1, source_target_pairs={{0,16},{16,0},{1,17},{17,1},{2,18},{18,2},{3,19},{19,3},{4,20},{20... | collective-permute-start | bytes 1572872 | tf_op jit(solution)/shard_map/ppermute | solution.py:64
  217.9 26.1 %collective-permute-start.39 = (bf16[256,512]{1,0:T(8,128)(2,1)S(1)}, bf16[256,512]{1,0:T(8,128)(2,1)S(1)}, u32[]{:S(2)}, u32[]{:S(2)}) collective-permute-start(bf16[256,512]{1,0:T(8,128)(2,1)S(1)} %copy-done.72), channel_id=1, source_target_pairs={{0,16},{16,0},{1,17},{17,1},{2,18},{18,2},{3,19},{19,3},{4,20},{20... | collective-permute-start | bytes 786440 | tf_op jit(solution)/shard_map/ppermute | solution.py:64
  244.0 15.2 %collective-permute-start.40 = (bf16[4,256,256]{2,1,0:T(8,128)(2,1)}, bf16[4,256,256]{2,1,0:T(8,128)(2,1)S(1)}, u32[]{:S(2)}, u32[]{:S(2)}) collective-permute-start(bf16[4,256,256]{2,1,0:T(8,128)(2,1)} %get-tuple-element.279), channel_id=1, source_target_pairs={{0,8},{4,12},{8,0},{12,4},{1,9},{5,13},{9,1},{13,5},{2,10},{6,14},... | collective-permute-start | bytes 1572872 | tf_op jit(solution)/shard_map/ppermute | solution.py:64
  255.1 20.6 %all-to-all-start.2 = ((bf16[4,64,1024]{2,1,0:T(8,128)(2,1)}), bf16[4,64,1024]{2,1,0:T(8,128)(2,1)S(1)}, u32[]{:S(2)}, u32[]{:S(2)}) async-start(bf16[4,64,1024]{2,1,0:T(8,128)(2,1)} %get-tuple-element.277), calls=%async_computation.2 | async-start | bytes 1048576 | tf_op jit(solution)/shard_map/all_to_all | solution.py:1030
  266.6 30.3 %collective-permute-start.44 = (bf16[4,256,256]{2,1,0:T(8,128)(2,1)}, bf16[4,256,256]{2,1,0:T(8,128)(2,1)S(1)}, u32[]{:S(2)}, u32[]{:S(2)}) collective-permute-start(bf16[4,256,256]{2,1,0:T(8,128)(2,1)} %get-tuple-element.292), channel_id=1, source_target_pairs={{0,8},{4,12},{8,0},{12,4},{1,9},{5,13},{9,1},{13,5},{2,10},{6,14},... | collective-permute-start | bytes 1572872 | tf_op jit(solution)/shard_map/ppermute | solution.py:64
  266.9 30.0 %collective-permute-start.45 = (bf16[4,256,256]{2,1,0:T(8,128)(2,1)}, bf16[4,256,256]{2,1,0:T(8,128)(2,1)S(1)}, u32[]{:S(2)}, u32[]{:S(2)}) collective-permute-start(bf16[4,256,256]{2,1,0:T(8,128)(2,1)} %get-tuple-element.282), channel_id=1, source_target_pairs={{0,4},{4,0},{8,12},{12,8},{1,5},{5,1},{9,13},{13,9},{2,6},{6,2},{1... | collective-permute-start | bytes 1572872 | tf_op jit(solution)/shard_map/ppermute | solution.py:64
  272.9 35.1 %collective-permute-start.46 = (bf16[2,2,256,256]{3,2,1,0:T(8,128)(2,1)}, bf16[2,2,256,256]{3,2,1,0:T(8,128)(2,1)S(1)}, u32[]{:S(2)}, u32[]{:S(2)}) collective-permute-start(bf16[2,2,256,256]{3,2,1,0:T(8,128)(2,1)} %get-tuple-element.298), channel_id=1, source_target_pairs={{0,4},{4,0},{8,12},{12,8},{1,5},{5,1},{9,13},{13,9},{2,6},{6,2},{1... | collective-permute-start | bytes 1572872 | tf_op jit(solution)/shard_map/ppermute | solution.py:64
  274.1 33.9 %collective-permute-start.47 = (bf16[2,2,256,256]{3,2,1,0:T(8,128)(2,1)}, bf16[2,2,256,256]{3,2,1,0:T(8,128)(2,1)S(1)}, u32[]{:S(2)}, u32[]{:S(2)}) collective-permute-start(bf16[2,2,256,256]{3,2,1,0:T(8,128)(2,1)} %get-tuple-element.299), channel_id=1, source_target_pairs={{0,8},{4,12},{8,0},{12,4},{1,9},{5,13},{9,1},{13,5},{2,10},{6,14},... | collective-permute-start | bytes 1572872 | tf_op jit(solution)/shard_map/ppermute | solution.py:64
  304.1 23.9 %all-to-all-start.3 = ((bf16[4,64,1024]{2,1,0:T(8,128)(2,1)}), bf16[4,64,1024]{2,1,0:T(8,128)(2,1)S(1)}, u32[]{:S(2)}, u32[]{:S(2)}) async-start(bf16[4,64,1024]{2,1,0:T(8,128)(2,1)} %get-tuple-element.296), calls=%async_computation.3 | async-start | bytes 1048576 | tf_op jit(solution)/shard_map/all_to_all | solution.py:1030
  311.6 14.7 %collective-permute-start.50 = (bf16[2,256,256]{2,1,0:T(8,128)(2,1)}, bf16[2,256,256]{2,1,0:T(8,128)(2,1)S(1)}, u32[]{:S(2)}, u32[]{:S(2)}) collective-permute-start(bf16[2,256,256]{2,1,0:T(8,128)(2,1)} %get-tuple-element.314), channel_id=1, source_target_pairs={{0,8},{4,12},{8,0},{12,4},{1,9},{5,13},{9,1},{13,5},{2,10},{6,14},... | collective-permute-start | bytes 786440 | tf_op jit(solution)/shard_map/ppermute | solution.py:64
  315.4 26.5 %collective-permute-start.54 = (bf16[2,2,256,256]{3,2,1,0:T(8,128)(2,1)}, bf16[2,2,256,256]{3,2,1,0:T(8,128)(2,1)S(1)}, u32[]{:S(2)}, u32[]{:S(2)}) collective-permute-start(bf16[2,2,256,256]{3,2,1,0:T(8,128)(2,1)} %get-tuple-element.320), channel_id=1, source_target_pairs={{0,1},{1,0},{2,3},{3,2},{4,5},{5,4},{6,7},{7,6},{8,9},{9,8},{10,11... | collective-permute-start | bytes 1572872 | tf_op jit(solution)/shard_map/ppermute | solution.py:64
  317.4 30.4 %collective-permute-start.57 = (bf16[1,4,256,256]{3,2,1,0:T(8,128)(2,1)S(1)}, bf16[1,4,256,256]{3,2,1,0:T(8,128)(2,1)S(1)}, u32[]{:S(2)}, u32[]{:S(2)}) collective-permute-start(bf16[1,4,256,256]{3,2,1,0:T(8,128)(2,1)S(1)} %copy-done.64), channel_id=1, source_target_pairs={{0,2},{1,3},{2,0},{3,1},{4,6},{5,7},{6,4},{7,5},{8,10},{9,11},{10,... | collective-permute-start | bytes 1572872 | tf_op jit(solution)/shard_map/ppermute | solution.py:64
  354.0 33.8 %collective-permute-start.62 = (bf16[8,256,256]{2,1,0:T(8,128)(2,1)}, bf16[8,256,256]{2,1,0:T(8,128)(2,1)S(1)}, u32[]{:S(2)}, u32[]{:S(2)}) collective-permute-start(bf16[8,256,256]{2,1,0:T(8,128)(2,1)} %constant_dynamic-update-slice_fusion.rest_0_), channel_id=1, source_target_pairs={{0,4},{4,0},{8,12},{12,8},{1,5},{5,1},{9,13},{13,9},{2,6},{6,2},{1... | collective-permute-start | bytes 3145736 | tf_op jit(solution)/shard_map/ppermute | solution.py:64
  354.5 14.3 %collective-permute-start.58 = (bf16[2,256,256]{2,1,0:T(8,128)(2,1)S(1)}, bf16[2,256,256]{2,1,0:T(8,128)(2,1)S(1)}, u32[]{:S(2)}, u32[]{:S(2)}) collective-permute-start(bf16[2,256,256]{2,1,0:T(8,128)(2,1)S(1)} %copy-done.74), channel_id=1, source_target_pairs={{0,2},{1,3},{2,0},{3,1},{4,6},{5,7},{6,4},{7,5},{8,10},{9,11},{10,... | collective-permute-start | bytes 786440 | tf_op jit(solution)/shard_map/ppermute | solution.py:64
  355.0 34.3 %collective-permute-start.63 = (bf16[8,256,256]{2,1,0:T(8,128)(2,1)}, bf16[8,256,256]{2,1,0:T(8,128)(2,1)}, u32[]{:S(2)}, u32[]{:S(2)}) collective-permute-start(bf16[8,256,256]{2,1,0:T(8,128)(2,1)} %constant_dynamic-update-slice_fusion.rest_0_), channel_id=1, source_target_pairs={{0,8},{4,12},{8,0},{12,4},{1,9},{5,13},{9,1},{13,5},{2,10},{6,14},... | collective-permute-start | bytes 3145736 | tf_op jit(solution)/shard_map/ppermute | solution.py:64
  376.8 15.4 %collective-permute-start.71 = (bf16[4,256,256]{2,1,0:T(8,128)(2,1)}, bf16[4,256,256]{2,1,0:T(8,128)(2,1)}, u32[]{:S(2)}, u32[]{:S(2)}) collective-permute-start(bf16[4,256,256]{2,1,0:T(8,128)(2,1)} %constant_dynamic-update-slice_fusion.2.rest_0_), channel_id=1, source_target_pairs={{0,4},{4,0},{8,12},{12,8},{1,5},{5,1},{9,13},{13,9},{2,6},{6,2},{1... | collective-permute-start | bytes 1572872 | tf_op jit(solution)/shard_map/ppermute | solution.py:64
  379.3 28.7 %collective-permute-start.64 = (bf16[384,1024]{1,0:T(8,128)(2,1)S(1)}, bf16[384,1024]{1,0:T(8,128)(2,1)S(1)}, u32[]{:S(2)}, u32[]{:S(2)}) collective-permute-start(bf16[384,1024]{1,0:T(8,128)(2,1)S(1)} %copy-done.15), channel_id=1, source_target_pairs={{0,16},{16,0},{1,17},{17,1},{2,18},{18,2},{3,19},{19,3},{4,20},{20... | collective-permute-start | bytes 2359304 | tf_op jit(solution)/shard_map/ppermute | solution.py:64
  387.8 17.1 %collective-permute-start.72 = (bf16[4,256,256]{2,1,0:T(8,128)(2,1)}, bf16[4,256,256]{2,1,0:T(8,128)(2,1)}, u32[]{:S(2)}, u32[]{:S(2)}) collective-permute-start(bf16[4,256,256]{2,1,0:T(8,128)(2,1)} %constant_dynamic-update-slice_fusion.2.rest_0_), channel_id=1, source_target_pairs={{0,8},{4,12},{8,0},{12,4},{1,9},{5,13},{9,1},{13,5},{2,10},{6,14},... | collective-permute-start | bytes 1572872 | tf_op jit(solution)/shard_map/ppermute | solution.py:64
  389.3 19.3 %collective-permute-start.66 = (bf16[192,1024]{1,0:T(8,128)(2,1)S(1)}, bf16[192,1024]{1,0:T(8,128)(2,1)}, u32[]{:S(2)}, u32[]{:S(2)}) collective-permute-start(bf16[192,1024]{1,0:T(8,128)(2,1)S(1)} %collective-permute-done.65.far_same), channel_id=1, source_target_pairs={{0,16},{16,0},{1,17},{17,1},{2,18},{18,2},{3,19},{19,3},{4,20},{20... | collective-permute-start | bytes 1179656 | tf_op jit(solution)/shard_map/ppermute | solution.py:64
  391.5 29.7 %collective-permute-start.68 = (bf16[4,256,256]{2,1,0:T(8,128)(2,1)}, bf16[4,256,256]{2,1,0:T(8,128)(2,1)}, u32[]{:S(2)}, u32[]{:S(2)}) collective-permute-start(bf16[4,256,256]{2,1,0:T(8,128)(2,1)} %slice.42), channel_id=1, source_target_pairs={{0,8},{4,12},{8,0},{12,4},{1,9},{5,13},{9,1},{13,5},{2,10},{6,14},... | collective-permute-start | bytes 1572872 | tf_op jit(solution)/shard_map/ppermute | solution.py:64
  392.2 29.0 %collective-permute-start.69 = (bf16[4,256,256]{2,1,0:T(8,128)(2,1)S(1)}, bf16[4,256,256]{2,1,0:T(8,128)(2,1)}, u32[]{:S(2)}, u32[]{:S(2)}) collective-permute-start(bf16[4,256,256]{2,1,0:T(8,128)(2,1)S(1)} %slice.43), channel_id=1, source_target_pairs={{0,4},{4,0},{8,12},{12,8},{1,5},{5,1},{9,13},{13,9},{2,6},{6,2},{1... | collective-permute-start | bytes 1572872 | tf_op jit(solution)/shard_map/ppermute | solution.py:64
  405.0 22.3 %collective-permute-start.73 = (bf16[2,256,256]{2,1,0:T(8,128)(2,1)}, bf16[2,256,256]{2,1,0:T(8,128)(2,1)}, u32[]{:S(2)}, u32[]{:S(2)}) collective-permute-start(bf16[2,256,256]{2,1,0:T(8,128)(2,1)} %slice.44), channel_id=1, source_target_pairs={{0,8},{4,12},{8,0},{12,4},{1,9},{5,13},{9,1},{13,5},{2,10},{6,14},... | collective-permute-start | bytes 786440 | tf_op jit(solution)/shard_map/ppermute | solution.py:64
  408.0 19.3 %collective-permute-start.74 = (bf16[2,256,256]{2,1,0:T(8,128)(2,1)}, bf16[2,256,256]{2,1,0:T(8,128)(2,1)S(1)}, u32[]{:S(2)}, u32[]{:S(2)}) collective-permute-start(bf16[2,256,256]{2,1,0:T(8,128)(2,1)} %slice.45), channel_id=1, source_target_pairs={{0,4},{4,0},{8,12},{12,8},{1,5},{5,1},{9,13},{13,9},{2,6},{6,2},{1... | collective-permute-start | bytes 786440 | tf_op jit(solution)/shard_map/ppermute | solution.py:64
  (112 other events, 827.0 us)

commit v6 on v5

--- a/solution.py
+++ b/solution.py
@@ -41,7 +41,7 @@
     def until(self, *values):
         self.tokens += values
 
-    def call(self, body, outs, args, specs, scratch=(), limit=56, us=2.0, grid=()):
+    def call(self, body, outs, args, specs, scratch=(), limit=28, us=2.0, grid=()):
         args = (self.after(args[0]),) + tuple(args[1:])
         results = pl.pallas_call(
             body,
@@ -255,7 +255,7 @@
         scores = jnp.where(allowed, scores, negative)
         raised = jnp.exp(scores - jnp.max(scores, axis=-1, keepdims=True))
         exact = raised / jnp.sum(raised, axis=-1, keepdims=True)
-        probs[h] = exact
+        probs[h] = exact.astype(low16)
         heads.append(dot(exact.astype(low16), packed[2, :, lanes]).astype(low16))
     mixed[...] = jnp.concatenate(heads, axis=1)
     given[...] = mixed[:, other_half(info, mixed.shape[1])]
@@ -351,7 +351,7 @@
     columns = [[], [], []]
     for h in range(packed.shape[2] // HEAD_DIM):
         lanes = slice(h * HEAD_DIM, (h + 1) * HEAD_DIM)
-        exact = probs[h]
+        exact = probs[h].astype(f32)
         grad = grad_mixed[:, lanes]
         columns[2].append(dot_tn(exact.astype(low16), grad).astype(low16))
         grad_probs = dot_nt(grad, packed[2, :, lanes])
@@ -492,7 +492,7 @@
                     whole = whole + raised[j]
                 for j in range(i + 1):
                     exact[(i, j)] = raised[j] / whole
-            probs[k, u] = from_pairs(exact)
+            probs[k, u] = from_pairs(exact).astype(low16)
             for i in range(3):
                 total = None
                 for j in range(i + 1):
@@ -627,7 +627,7 @@
             key = query_keys[k, at, half:].astype(f32)
             val = values_in[k, at, :].astype(f32)
             grad = grad_mixed[at]
-            exact = by_pair(probs[k, u], size)
+            exact = by_pair(probs[k, u].astype(f32), size)
             grad_probs = by_pair(head_sums(pair_rows(grad, val, size), table), size)
             scored = {}
             for i in range(3):
@@ -1068,7 +1068,7 @@
         [
             shape((rows_g, width), low16),
             shape((3, rows_g, heads_width), low16),
-            shape((heads_width // HEAD_DIM, rows_g, rows_g), f32),
+            shape((heads_width // HEAD_DIM, rows_g, rows_g), low16),
             shape((rows_g, heads_width), low16),
             shape((rows_g, half), low16),
             shape((4, frames, width), low16),
@@ -1081,6 +1081,7 @@
             sem(8),
         ],
         us=5.7,
+        limit=60,
     )
     partial, mix_z1, mix_z2 = lax.optimization_barrier((partial, mix_z1, mix_z2))
     arrived = scatter(partial)
@@ -1152,6 +1153,7 @@
             sem(8),
         ],
         us=5.6,
+        limit=60,
     )
     arrived = scatter(partial)
     order.until(feed_x, feed_y, mix_w[6], mix_w[7], mix_w[10], mix_w[11])
@@ -1181,7 +1183,7 @@
             shape((rows_l, width), low16),
             shape((4, rows_l, 2 * half), low16),
             shape((4, rows_l, half), low16),
-            shape((4, utts, 2 * rows_l // utts, half), f32),
+            shape((4, utts, 2 * rows_l // utts, half), low16),
             shape((rows_l, 4 * half), low16),
             shape((rows_l, width), low16),
         ],
@@ -1193,6 +1195,7 @@
             sem(32),
         ],
         us=9,
+        limit=60,
     )
     hidden_l, second_l, second_given = call(
         local_norm_kernel,
@@ -1259,8 +1262,23 @@
             us=7.6,
         ),
     )
+    own_branch, branch_same, branch_cross = call(
+        local_drop_kernel,
+        [wide_rows, half_rows, half_rows],
+        (active_l, far_active) + feed_l,
+        [VM] * 2 + [ANY] * FEED_REFS,
+        [
+            pltpu.VMEM((tiles, UNIT, width), low16),
+            pltpu.VMEM((2 * rows_l, width), f32),
+            sem(QUARTERS * tiles),
+        ],
+        us=6.1,
+    )
+    branch_cross = swap(branch_cross, "section", 1)
+    other_branch = swap(own_branch, "section", 1)
     far_same = order.after(far_same)
     far_back = (far_same, swap(far_same, "section", 1))
+    far_branch = from_neighbour(branch_same, branch_cross)
     far_first, far_mixed, far_second_g, far_active_g = (
         swap(order.after(value), "section", 1)
         for value in (first_g, mixed_given, second_g, active_given)
@@ -1334,11 +1352,14 @@
             sem(8),
         ],
         us=6.3,
+        limit=60,
     )
     arrived = scatter(partial)
     far_top_g, far_lifted_g = swap(top_g, "section", 1), swap(lifted_given, "section", 1)
     local_feed.third()
     local_mix.second()
+    far_branch = order.after(far_branch)
+    far_branch = (far_branch, swap(far_branch, "section", 1))
     global_feed = Sum(
         order,
         1,
@@ -1379,6 +1400,7 @@
             sem(8),
         ],
         us=6.8,
+        limit=60,
     )
     arrived = scatter(partial)
     far_mid_g, far_grads_g = swap(mid_g, "section", 1), swap(grads_given, "section", 1)
@@ -1399,67 +1421,6 @@
             us=3,
         ),
     )
-    kept_start, given_start, gain1_g = call(
-        start_back_kernel,
-        [
-            shape((frames, width // 2), f32),
-            shape((frames, width // 2), f32),
-            shape((1, width), f32),
-        ],
-        (info, arrived, start_g, gain_g, grad_hidden_g),
-        [SM] + [VM] * 4,
-        [pltpu.VMEM((frames, width), f32)],
-        us=2.1,
-    )
-    world_feed = global_feed.third()
-    global_mix.second()
-    local_mix.fourth()
-    world_mix = global_mix.third()
-    feed_sum = local_feed.gathered(info, world_feed)
-    own_branch, same, cross = call(
-        local_drop_kernel,
-        [wide_rows, half_rows, half_rows],
-        (active_l, far_active) + feed_l,
-        [VM] * 2 + [ANY] * FEED_REFS,
-        [
-            pltpu.VMEM((tiles, UNIT, width), low16),
-            pltpu.VMEM((2 * rows_l, width), f32),
-            sem(QUARTERS * tiles),
-        ],
-        us=6.1,
-    )
-    other_branch = swap(own_branch, "section", 1)
-    branch_cross = swap(cross, "section", 1)
-    arrived_start = swap(given_start, "section", 1)
-    both_start = jnp.stack(
-        [
-            jnp.where(first_core, kept_start, arrived_start),
-            jnp.where(first_core, arrived_start, kept_start),
-        ]
-    )
-    code_grad = jnp.transpose(code_part + both_start[:, None], (0, 2, 1, 3))
-
-    own_gain = jnp.concatenate([gain1_g, gain2_g], axis=0)
-    total_gain = own_gain + swap(own_gain, "section", 1)
-    local_gain = jnp.concatenate([gain1_l, gain2_l], axis=0)
-    gain_total = jnp.where(first_core, total_gain, local_gain)
-    gain_total = jnp.concatenate(
-        [
-            lax.dynamic_slice_in_dim(gain_total, (low ^ m) * UNIT, UNIT, 1)
-            for m in range(QUARTERS)
-        ],
-        axis=1,
-    )
-    def over(value, axis):
-        copies = jnp.broadcast_to(value, (lax.axis_size(axis),) + value.shape)
-        return jnp.sum(lax.all_to_all(order.after(copies), axis, 0, 0), axis=0)
-
-    mix_sum = local_mix.gathered(info, world_mix)
-    far_branch = from_neighbour(same, branch_cross)
-    gain_total = over(gain_total, "tensor")
-    order.until(gain_total, *feed_sum.near)
-    feed_parts = feed_sum.far()
-    far_branch = (far_branch, swap(far_branch, "section", 1))
     output = call(
         output_kernel,
         [shape((utts, code_count, frames, width // 2), low16)],
@@ -1467,9 +1428,54 @@
         [SM] + [VM] * 5,
         us=3.1,
     )[0]
+    kept_start, given_start, gain1_g = call(
+        start_back_kernel,
+        [
+            shape((frames, width // 2), f32),
+            shape((frames, width // 2), f32),
+            shape((1, width), f32),
+        ],
+        (info, arrived, start_g, gain_g, grad_hidden_g),
+        [SM] + [VM] * 4,
+        [pltpu.VMEM((frames, width), f32)],
+        us=2.1,
+    )
+    world_feed = global_feed.third()
+    global_mix.second()
+    local_mix.fourth()
+    world_mix = global_mix.third()
+    feed_sum = local_feed.gathered(info, world_feed)
+    arrived_start = swap(given_start, "section", 1)
+    both_start = jnp.stack(
+        [
+            jnp.where(first_core, kept_start, arrived_start),
+            jnp.where(first_core, arrived_start, kept_start),
+        ]
+    )
+    code_grad = jnp.transpose(code_part + both_start[:, None], (0, 2, 1, 3))
+
+    own_gain = jnp.concatenate([gain1_g, gain2_g], axis=0)
+    total_gain = own_gain + swap(own_gain, "section", 1)
+    local_gain = jnp.concatenate([gain1_l, gain2_l], axis=0)
+    gain_total = jnp.where(first_core, total_gain, local_gain)
+    gain_total = jnp.concatenate(
+        [
+            lax.dynamic_slice_in_dim(gain_total, (low ^ m) * UNIT, UNIT, 1)
+            for m in range(QUARTERS)
+        ],
+        axis=1,
+    )
+    def over(value, axis):
+        copies = jnp.broadcast_to(value, (lax.axis_size(axis),) + value.shape)
+        return jnp.sum(lax.all_to_all(order.after(copies), axis, 0, 0), axis=0)
+
+    gain_total = over(gain_total, "tensor")
+    order.until(gain_total)
+    mix_sum = local_mix.gathered(info, world_mix)
+    gain_total = over(gain_total, "dp")
+    order.until(gain_total, *feed_sum.near)
+    feed_parts = feed_sum.far()
     mix_parts = mix_sum.far()
-    gain_total = over(gain_total, "dp")
-    order.until(gain_total)
     up_grad, down_grad = call(
         feed_final_kernel,
         [shape((width, wide), f32), shape((wide, width), f32)],

time: 438 us -> 411 us (0.938)
  Pallas kernels: 161 us -> 117 us
  local copies, waits for them, and re-layouts: 32.5 us -> 45.4 us
  blocking collectives: 81.1 us -> 88.7 us
  waiting for transfers between devices: 68.4 us -> 62.3 us
    pallas_call x39, Pallas kernels: 161 us -> 117 us  [call(): pl.pallas_call(body, out_shape=tuple(outs), grid=grid, in_specs=list(spec...]
    unnamed x160 -> x258, local copies, waits for them, and re-layouts: 24.4 us -> 37.3 us
    all_to_all x0 -> x1, blocking collectives: none -> 11.8 us  [over(): return jnp.sum(lax.all_to_all(order.after(copies), axis, 0, 0), axis=0)]
    all_to_all x2 -> x1, waiting for transfers between devices: 9.34 us -> 7.12 us  [over(): return jnp.sum(lax.all_to_all(order.after(copies), axis, 0, 0), axis=0)]
  transfers between devices with their start and end apart: 81 -> 80, of which waited for: 22 -> 24; matrix products, arithmetic and copies ran while one was open for 3% -> 4% of each run, Pallas kernels for 28% -> 22%
where the time goes in v6:
time: 411 us; the launch traced here: 405 us
  Pallas kernels  117 us (28%)
  blocking collectives  88.7 us (22%)
  starting transfers between devices  83.4 us (20%)
  waiting for transfers between devices  62.3 us (15%)
  local copies, waits for them, and re-layouts  45.4 us (11%)
  other arithmetic  5.02 us (1%)
    pallas_call x39, Pallas kernels, call(): pl.pallas_call(body, out_shape=tuple(outs), grid=grid, in_specs=list(spec...  117 us
    all_gather x4, blocking collectives, gather(): gathered = lax.all_gather(rows, 'tensor')  76.9 us
    ppermute x75, starting transfers between devices, swap(): return lax.ppermute(value, axis, [(i, i ^ flip) for i in range(count)])  61.2 us
    ppermute x75, waiting for transfers between devices, swap(): return lax.ppermute(value, axis, [(i, i ^ flip) for i in range(count)])  55.2 us
    unnamed x258, local copies, waits for them, and re-layouts  37.3 us
    all_to_all x4, starting transfers between devices, scatter(): return lax.all_to_all(partial, 'tensor', 0, 0)  19 us
    all_to_all x1, blocking collectives, over(): return jnp.sum(lax.all_to_all(order.after(copies), axis, 0, 0), axis=0)  11.8 us
  transfers between devices with their start and end apart: 80, of which 24 were waited for; matrix products, arithmetic and copies ran while one was open for 4% of the time, Pallas kernels for 22%

profile of v6, /device:TPU:0, one launch (start us, length us, event | category | flops | bytes accessed | tf_op | source)
XLA Modules:
  0.0 404.6 jit_solution(11375329459252294539)
XLA Ops:
  6.1 17.9 %all-gather = bf16[256,1024]{1,0:T(8,128)(2,1)} all-gather(bf16[64,1024]{1,0:T(8,128)(2,1)S(1)} %get-tuple-element.181), channel_id=2, replica_groups=mesh['section'=2,'dp'=4,'tensor'=4] {'tensor'}, dimensions={0}, use_global_device_ids=true | all-gather | bytes 655360 | tf_op jit(solution)/shard_map/all_gather | solution.py:1025
  24.1 2.1 shard_map.136
  27.8 2.2 collective-permute-start.5
  29.9 2.5 collective-permute-start.6
  32.5 5.5 %shard_map.137 = (bf16[256,1024]{1,0:T(8,128)(2,1)}, bf16[3,256,256]{2,1,0:T(8,128)(2,1)}, bf16[4,256,256]{2,1,0:T(8,128)(2,1)}, bf16[256,256]{1,0:T(8,128)(2,1)...) custom-call(s32[5]{0:T(128)} %copy-done.93, bf16[4,64,1024]{2,1,0:T(8,128)(2,1)} %bitcast.56, ...), custom_call_target="tpu_custom_call" | custom-call | flops 1140000000 | tf_op jit(solution)/shard_map/pallas_call | solution.py:46
  38.0 3.7 collective-permute-done.5.rest_1_
  41.7 2.7 collective-permute-done.6.rest_2_
  44.4 4.1 %all-to-all-start = ((bf16[4,64,1024]{2,1,0:T(8,128)(2,1)}), bf16[4,64,1024]{2,1,0:T(8,128)(2,1)}, u32[]{:S(2)}, u32[]{:S(2)}) async-start(bf16[4,64,1024]{2,1,0:T(8,128)(2,1)} %get-tuple-element.198), calls=%async_computation | async-start | bytes 1048576 | tf_op jit(solution)/shard_map/all_to_all | solution.py:1030
  55.0 2.0 collective-permute-start.10
  57.0 3.1 shard_map.139
  61.5 2.4 collective-permute-start.7
  66.6 3.1 collective-permute-done.10.rest_3_
  72.1 25.6 %all-gather.1 = bf16[256,1024]{1,0:T(8,128)(2,1)} all-gather(bf16[64,1024]{1,0:T(8,128)(2,1)S(1)} %get-tuple-element.201), channel_id=3, replica_groups=mesh['section'=2,'dp'=4,'tensor'=4] {'tensor'}, dimensions={0}, use_global_device_ids=true | all-gather | bytes 655360 | tf_op jit(solution)/shard_map/all_gather | solution.py:1025
  97.7 6.1 %shard_map.141 = (bf16[256,1024]{1,0:T(8,128)(2,1)}, f32[256,1024]{1,0:T(8,128)}, bf16[256,1024]{1,0:T(8,128)(2,1)}, bf16[256,512]{1,0:T(8,128)(2,1)}, bf16[4,64,1024]{2,1,0:T(8,128)(2,1)}) custom-call(s32[5]{0:T(128)} %copy-done.93, bf16[4,64,1024]{2,1,0:T(8,128)(2,1)} %bitcast.57, bf16[1024,1024]{1,0:T(8,128)(2,1)} %bitcast.36, ...), custom_call_target="tpu_custom_call" | custom-call | flops 1120000000 | tf_op jit(solution)/shard_map/pallas_call | solution.py:46
  103.8 3.7 all-to-all-start.1
  114.4 6.4 %collective-permute-done.14.rest_2_ = bf16[4,256,256]{2,1,0:T(8,128)(2,1)S(1)} collective-permute-done((bf16[4,256,256]{2,1,0:T(8,128)(2,1)S(1)}, bf16[4,256,256]{2,1,0:T(8,128)(2,1)S(1)}, u32[]{:S(2)}, u32[]{:S(2)}) %collective-permute-start.14) | collective-permute-done | bytes 524320 | tf_op jit(solution)/shard_map/ppermute | solution.py:64
  126.2 2.6 collective-permute-done.18.rest_10_
  131.7 3.6 collective-permute-done.21.rest_5_
  136.0 8.8 %shard_map.143 = (f32[384,1024]{1,0:T(8,128)}, bf16[384,1024]{1,0:T(8,128)(2,1)}, bf16[4,384,256]{2,1,0:T(8,128)(2,1)}, bf16[4,384,128]{2,1,0:T(8,128)(2,1)}, bf...) custom-call(s32[5]{0:T(128)} %copy-done.93, ...), custom_call_target="tpu_custom_call" | custom-call | flops 1800000000 | tf_op jit(solution)/shard_map/pallas_call | solution.py:46
  144.9 2.5 collective-permute-done.23.other_part
  154.4 7.1 %shard_map.145 = (bf16[4,384,256]{2,1,0:T(8,128)(2,1)S(1)}, bf16[4,384,256]{2,1,0:T(8,128)(2,1)S(1)}, bf16[384,1024]{1,0:T(8,128)(2,1)S(1)}) custom-call(bf16[384,1024]{1,0:T(8,128)(2,1)S(1)} %get-tuple-element.236.second, bf16[384,1024]{1,0:T(8,128)(2,1)S(1)} %get-tuple-element.227.top, bf16[4,4,256,256]{3,2,1,0:T(8,128)(2,1)S(1)} %copy-done.24, ...), custom_call_target="tpu_custom_call" | custom-call | flops 1580000000 | tf_op jit(solution)/shard_map/pallas_call | solution.py:46
  163.9 7.2 %shard_map.146 = (bf16[4,384,256]{2,1,0:T(8,128)(2,1)S(1)}, bf16[4,384,256]{2,1,0:T(8,128)(2,1)S(1)}, bf16[384,1024]{1,0:T(8,128)(2,1)S(1)}, bf16[384,1024]{1,0:...) custom-call(bf16[192,1024]{1,0:T(8,128)(2,1)S(1)} %collective-permute-done.24.second_same, ...), custom_call_target="tpu_custom_call" | custom-call | flops 1640000000 | tf_op jit(solution)/shard_map/pallas_call | solution.py:46
  174.8 3.5 shard_map.148
  178.5 4.1 %shard_map.149 = (bf16[384,1024]{1,0:T(8,128)(2,1)}, bf16[192,1024]{1,0:T(8,128)(2,1)S(1)}, bf16[192,1024]{1,0:T(8,128)(2,1)S(1)}) custom-call(bf16[4,384,256]{2,1,0:T(8,128)(2,1)S(1)} %get-tuple-element.243.own_active, bf16[4,384,256]{2,1,0:T(8,128)(2,1)S(1)} %get-tuple-element.240.far_active, bf16[4,4,256,256]{3,2,1,0:T(8,128)(2,1)S(1)} %copy-done.25, ...), custom_call_target="tpu_custom_call" | custom-call | flops 1220000000 | tf_op jit(solution)/shard_map/pallas_call | solution.py:46
  186.8 12.5 %shard_map.151 = (f32[384,1024]{1,0:T(8,128)S(1)}, bf16[384,1024]{1,0:T(8,128)(2,1)S(1)}, bf16[4,384,256]{2,1,0:T(8,128)(2,1)S(1)}, bf16[4,384,128]{2,1,0:T(8,12...) custom-call(s32[5]{0:T(128)S(1)} %copy-done.95, f32[384,1024]{1,0:T(8,128)S(1)} %get-tuple-element.248.hidden, ...), custom_call_target="tpu_custom_call" | custom-call | flops 2280000000 | tf_op jit(solution)/shard_map/pallas_call | solution.py:46
  199.9 2.7 shard_map.152
  206.1 4.1 %collective-permute-done.33.from_x.refs_1_ = bf16[2,4,256,256]{3,2,1,0:T(8,128)(2,1)S(1)} collective-permute-done((bf16[2,4,256,256]{3,2,1,0:T(8,128)(2,1)S(1)}, bf16[2,4,256,256]{3,2,1,0:T(8,128)(2,1)S(1)}, u32[]{:S(2)}, u32[]{:S(2)}) %collective-permute-start.33) | collective-permute-done | bytes 1048608 | tf_op jit(solution)/shard_map/ppermute | solution.py:64
  214.0 16.8 %all-gather.2 = bf16[256,1024]{1,0:T(8,128)(2,1)} all-gather(bf16[64,1024]{1,0:T(8,128)(2,1)S(1)} %get-tuple-element.265.returned), channel_id=4, replica_groups=mesh['section'=2,'dp'=4,'tensor'=4] {'tensor'}, dimensions={0}, use_global_device_ids=true | all-gather | bytes 655360 | tf_op jit(solution)/shard_map/all_gather | solution.py:1025
  238.7 6.3 %shard_map.155 = (bf16[256,1024]{1,0:T(8,128)(2,1)}, bf16[256,1024]{1,0:T(8,128)(2,1)}, bf16[256,512]{1,0:T(8,128)(2,1)}, bf16[4,64,1024]{2,1,0:T(8,128)(2,1)}) custom-call(s32[5]{0:T(128)} %copy-done.93, bf16[4,64,1024]{2,1,0:T(8,128)(2,1)} %bitcast.55, f32[256,1024]{1,0:T(8,128)} %get-tuple-element.281.rest_1_, bf16[1024,1024]{1,0:T(8,128)(2,1)} %bitcast.37, ...), custom_call_target="tpu_custom_call" | custom-call | flops 1260000000 | tf_op jit(solution)/shard_map/pallas_call | solution.py:46
  245.0 5.5 %all-to-all-start.2 = ((bf16[4,64,1024]{2,1,0:T(8,128)(2,1)}), bf16[4,64,1024]{2,1,0:T(8,128)(2,1)}, u32[]{:S(2)}, u32[]{:S(2)}) async-start(bf16[4,64,1024]{2,1,0:T(8,128)(2,1)} %get-tuple-element.282), calls=%async_computation.2 | async-start | bytes 1048576 | tf_op jit(solution)/shard_map/all_to_all | solution.py:1030
  255.6 2.1 shard_map.156
  264.2 2.2 shard_map.158
  275.1 16.6 %all-gather.3 = bf16[256,1024]{1,0:T(8,128)(2,1)} all-gather(bf16[64,1024]{1,0:T(8,128)(2,1)S(1)} %get-tuple-element.296), channel_id=5, replica_groups=mesh['section'=2,'dp'=4,'tensor'=4] {'tensor'}, dimensions={0}, use_global_device_ids=true | all-gather | bytes 655360 | tf_op jit(solution)/shard_map/all_gather | solution.py:1025
  291.7 6.6 %shard_map.160 = (bf16[256,1024]{1,0:T(8,128)(2,1)}, bf16[3,256,256]{2,1,0:T(8,128)(2,1)}, bf16[3,256,128]{2,1,0:T(8,128)(2,1)}, bf16[4,64,1024]{2,1,0:T(8,128)(2,1)}) custom-call(s32[5]{0:T(128)} %copy-done.93, bf16[4,64,1024]{2,1,0:T(8,128)(2,1)} %bitcast.58, bf16[3,256,256]{2,1,0:T(8,128)(2,1)} %get-tuple-element.299.rest_1_, ...), custom_call_target="tpu_custom_call" | custom-call | flops 1360000000 | tf_op jit(solution)/shard_map/pallas_call | solution.py:46
  298.3 5.7 %all-to-all-start.3 = ((bf16[4,64,1024]{2,1,0:T(8,128)(2,1)}), bf16[4,64,1024]{2,1,0:T(8,128)(2,1)}, u32[]{:S(2)}, u32[]{:S(2)}) async-start(bf16[4,64,1024]{2,1,0:T(8,128)(2,1)} %get-tuple-element.301), calls=%async_computation.3 | async-start | bytes 1048576 | tf_op jit(solution)/shard_map/all_to_all | solution.py:1030
  309.9 2.3 shard_map.162
  312.2 2.0 collective-permute-start.60
  314.3 2.4 collective-permute-start.63
  317.1 2.2 shard_map.163
  323.9 2.5 shard_map.164
  333.7 4.5 %collective-permute-done.60.arrived.refs_1_ = bf16[2,2,256,256]{3,2,1,0:T(8,128)(2,1)} collective-permute-done((bf16[2,2,256,256]{3,2,1,0:T(8,128)(2,1)}, bf16[2,2,256,256]{3,2,1,0:T(8,128)(2,1)}, u32[]{:S(2)}, u32[]{:S(2)}) %collective-permute-start.60) | collective-permute-done | bytes 524320 | tf_op jit(solution)/shard_map/ppermute | solution.py:64
  346.7 11.8 %all_to_all.30 = f32[4,2,1024]{2,1,0:T(2,128)S(1)} all-to-all(f32[4,2,1024]{2,1,0:T(2,128)S(1)} %broadcast_in_dim.22), channel_id=1, replica_groups=mesh['section'=2,'dp'=4,'tensor'=4] {'tensor'}, dimensions={0} | all-to-all | bytes 65536 | tf_op jit(solution)/shard_map/all_to_all | solution.py:1470
  363.6 7.7 %collective-permute-done.66.rest_1_ = bf16[8,256,256]{2,1,0:T(8,128)(2,1)S(1)} collective-permute-done((bf16[8,256,256]{2,1,0:T(8,128)(2,1)}, bf16[8,256,256]{2,1,0:T(8,128)(2,1)S(1)}, u32[]{:S(2)}, u32[]{:S(2)}) %collective-permute-start.66) | collective-permute-done | bytes 1048608 | tf_op jit(solution)/shard_map/ppermute | solution.py:64
  376.9 3.3 all-to-all-start.5
  380.2 2.4 collective-permute-done.71.rest_1_
  387.4 7.1 %all-to-all-done.5 = f32[4,2,1024]{2,1,0:T(2,128)S(1)} async-done(((f32[4,2,1024]{2,1,0:T(2,128)}), f32[4,2,1024]{2,1,0:T(2,128)S(1)}, u32[]{:S(2)}, u32[]{:S(2)}) %all-to-all-start.5) | async-done | bytes 32800 | tf_op jit(solution)/shard_map/all_to_all | solution.py:1470
  395.2 5.8 %shard_map.172 = (f32[1024,1024]{1,0:T(8,128)}, f32[1024,1024]{1,0:T(8,128)}) custom-call(s32[5]{0:T(128)S(1)} %copy-done.97, bf16[8,256,256]{2,1,0:T(8,128)(2,1)} %constant_dynamic-update-slice_fusion.rest_0_, bf16[8,256,256]{2,1,0:T(8,128)(2,1)S(1)} %collective-permute-done.66.rest_1_, bf16[8,256,256]{2,1,0:T(8,128)(2,1)} %collective-permute-done.67.rest_2_, ...), custom_call_target="tpu_custom_call" | custom-call | flops 1360000000 | tf_op jit(solution)/shard_map/pallas_call | solution.py:46
  401.0 3.4 shard_map.173
  (439 shorter events, 131.2 us)
Async XLA Ops:
  2.2 21.9 %collective-permute-start.1 = (bf16[3,1024,256]{2,1,0:T(8,128)(2,1)}, bf16[3,1024,256]{2,1,0:T(8,128)(2,1)}, u32[]{:S(2)}, u32[]{:S(2)}) collective-permute-start(bf16[3,1024,256]{2,1,0:T(8,128)(2,1)} %bitcast.40), channel_id=1, source_target_pairs={{0,16},{16,0},{1,17},{17,1},{2,18},{18,2},{3,19},{19,3},{4,20},{20... | collective-permute-start | bytes 4718600 | tf_op jit(solution)/shard_map/ppermute | solution.py:64
  2.5 21.5 %collective-permute-start.2 = (bf16[256,1024]{1,0:T(8,128)(2,1)}, bf16[256,1024]{1,0:T(8,128)(2,1)S(1)}, u32[]{:S(2)}, u32[]{:S(2)}) collective-permute-start(bf16[256,1024]{1,0:T(8,128)(2,1)} %bitcast.44), channel_id=1, source_target_pairs={{0,16},{16,0},{1,17},{17,1},{2,18},{18,2},{3,19},{19,3},{4,20},{20... | collective-permute-start | bytes 1572872 | tf_op jit(solution)/shard_map/ppermute | solution.py:64
  27.3 29.7 %collective-permute-start.3 = (bf16[1024,1024]{1,0:T(8,128)(2,1)S(1)}, bf16[1024,1024]{1,0:T(8,128)(2,1)}, u32[]{:S(2)}, u32[]{:S(2)}) collective-permute-start(bf16[1024,1024]{1,0:T(8,128)(2,1)S(1)} %bitcast.38), channel_id=1, source_target_pairs={{0,16},{16,0},{1,17},{17,1},{2,18},{18,2},{3,19},{19,3},{4,20},{20... | collective-permute-start | bytes 6291464 | tf_op jit(solution)/shard_map/ppermute | solution.py:64
  27.3 29.7 %collective-permute-start.4 = (bf16[1024,1024]{1,0:T(8,128)(2,1)}, bf16[1024,1024]{1,0:T(8,128)(2,1)}, u32[]{:S(2)}, u32[]{:S(2)}) collective-permute-start(bf16[1024,1024]{1,0:T(8,128)(2,1)} %bitcast.9.own_down.rest_3_.rest_4_), channel_id=1, source_target_pairs={{0,16},{16,0},{1,17},{17,1},{2,18},{18,2},{3,19},{19,3},{4,20},{20... | collective-permute-start | bytes 6291464 | tf_op jit(solution)/shard_map/ppermute | solution.py:64
  29.9 14.5 %collective-permute-start.6 = (bf16[2,256,256]{2,1,0:T(8,128)(2,1)S(1)}, bf16[2,256,256]{2,1,0:T(8,128)(2,1)S(1)}, u32[]{:S(2)}, u32[]{:S(2)}) collective-permute-start(bf16[2,256,256]{2,1,0:T(8,128)(2,1)S(1)} %get-tuple-element.197), channel_id=1, source_target_pairs={{0,2},{1,3},{2,0},{3,1},{4,6},{5,7},{6,4},{7,5},{8,10},{9,11},{10,... | collective-permute-start | bytes 786440 | tf_op jit(solution)/shard_map/ppermute | solution.py:64
  44.4 20.0 %all-to-all-start = ((bf16[4,64,1024]{2,1,0:T(8,128)(2,1)}), bf16[4,64,1024]{2,1,0:T(8,128)(2,1)}, u32[]{:S(2)}, u32[]{:S(2)}) async-start(bf16[4,64,1024]{2,1,0:T(8,128)(2,1)} %get-tuple-element.198), calls=%async_computation | async-start | bytes 1048576 | tf_op jit(solution)/shard_map/all_to_all | solution.py:1030
  52.0 19.1 %collective-permute-start.8 = (bf16[2,2,256,256]{3,2,1,0:T(8,128)(2,1)}, bf16[2,2,256,256]{3,2,1,0:T(8,128)(2,1)S(1)}, u32[]{:S(2)}, u32[]{:S(2)}) collective-permute-start(bf16[2,2,256,256]{3,2,1,0:T(8,128)(2,1)} %pad_maximum_fusion), channel_id=1, source_target_pairs={{0,4},{4,0},{8,12},{12,8},{1,5},{5,1},{9,13},{13,9},{2,6},{6,2},{1... | collective-permute-start | bytes 1572872 | tf_op jit(solution)/shard_map/ppermute | solution.py:64
  53.5 44.1 %collective-permute-start.9 = (bf16[2,2,256,256]{3,2,1,0:T(8,128)(2,1)}, bf16[2,2,256,256]{3,2,1,0:T(8,128)(2,1)}, u32[]{:S(2)}, u32[]{:S(2)}) collective-permute-start(bf16[2,2,256,256]{3,2,1,0:T(8,128)(2,1)} %pad_maximum_fusion), channel_id=1, source_target_pairs={{0,8},{4,12},{8,0},{12,4},{1,9},{5,13},{9,1},{13,5},{2,10},{6,14},... | collective-permute-start | bytes 1572872 | tf_op jit(solution)/shard_map/ppermute | solution.py:64
  55.0 14.7 %collective-permute-start.10 = (bf16[2,256,256]{2,1,0:T(8,128)(2,1)}, bf16[2,256,256]{2,1,0:T(8,128)(2,1)}, u32[]{:S(2)}, u32[]{:S(2)}) collective-permute-start(bf16[2,256,256]{2,1,0:T(8,128)(2,1)} %copy-done.39), channel_id=1, source_target_pairs={{0,1},{1,0},{2,3},{3,2},{4,5},{5,4},{6,7},{7,6},{8,9},{9,8},{10,11... | collective-permute-start | bytes 786440 | tf_op jit(solution)/shard_map/ppermute | solution.py:64
  61.5 36.2 %collective-permute-start.7 = (bf16[4,256,256]{2,1,0:T(8,128)(2,1)}, bf16[4,256,256]{2,1,0:T(8,128)(2,1)S(1)}, u32[]{:S(2)}, u32[]{:S(2)}) collective-permute-start(bf16[4,256,256]{2,1,0:T(8,128)(2,1)} %get-tuple-element.202), channel_id=1, source_target_pairs={{0,2},{1,3},{2,0},{3,1},{4,6},{5,7},{6,4},{7,5},{8,10},{9,11},{10,... | collective-permute-start | bytes 1572872 | tf_op jit(solution)/shard_map/ppermute | solution.py:64
  63.8 33.8 %collective-permute-start.13 = (bf16[192,1024]{1,0:T(8,128)(2,1)}, bf16[192,1024]{1,0:T(8,128)(2,1)S(1)}, u32[]{:S(2)}, u32[]{:S(2)}) collective-permute-start(bf16[192,1024]{1,0:T(8,128)(2,1)} %get-tuple-element.209), channel_id=1, source_target_pairs={{0,1},{1,0},{2,3},{3,2},{4,5},{5,4},{6,7},{7,6},{8,9},{9,8},{10,11... | collective-permute-start | bytes 1179656 | tf_op jit(solution)/shard_map/ppermute | solution.py:64
  69.7 27.9 %collective-permute-start.11 = (bf16[2,256,256]{2,1,0:T(8,128)(2,1)}, bf16[2,256,256]{2,1,0:T(8,128)(2,1)S(1)}, u32[]{:S(2)}, u32[]{:S(2)}) collective-permute-start(bf16[2,256,256]{2,1,0:T(8,128)(2,1)} %collective-permute-done.10.rest_3_), channel_id=1, source_target_pairs={{0,4},{4,0},{8,12},{12,8},{1,5},{5,1},{9,13},{13,9},{2,6},{6,2},{1... | collective-permute-start | bytes 786440 | tf_op jit(solution)/shard_map/ppermute | solution.py:64
  71.1 26.6 %collective-permute-start.12 = (bf16[2,256,256]{2,1,0:T(8,128)(2,1)}, bf16[2,256,256]{2,1,0:T(8,128)(2,1)S(1)}, u32[]{:S(2)}, u32[]{:S(2)}) collective-permute-start(bf16[2,256,256]{2,1,0:T(8,128)(2,1)} %collective-permute-done.10.rest_3_), channel_id=1, source_target_pairs={{0,8},{4,12},{8,0},{12,4},{1,9},{5,13},{9,1},{13,5},{2,10},{6,14},... | collective-permute-start | bytes 786440 | tf_op jit(solution)/shard_map/ppermute | solution.py:64
  103.8 27.2 %all-to-all-start.1 = ((bf16[4,64,1024]{2,1,0:T(8,128)(2,1)}), bf16[4,64,1024]{2,1,0:T(8,128)(2,1)S(1)}, u32[]{:S(2)}, u32[]{:S(2)}) async-start(bf16[4,64,1024]{2,1,0:T(8,128)(2,1)} %get-tuple-element.211), calls=%async_computation.1 | async-start | bytes 1048576 | tf_op jit(solution)/shard_map/all_to_all | solution.py:1030
  109.1 14.9 %collective-permute-start.15 = (bf16[4,256,256]{2,1,0:T(8,128)(2,1)S(1)}, bf16[4,256,256]{2,1,0:T(8,128)(2,1)S(1)}, u32[]{:S(2)}, u32[]{:S(2)}) collective-permute-start(bf16[4,256,256]{2,1,0:T(8,128)(2,1)S(1)} %collective-permute-done.7.rest_1_), channel_id=1, source_target_pairs={{0,8},{4,12},{8,0},{12,4},{1,9},{5,13},{9,1},{13,5},{2,10},{6,14},... | collective-permute-start | bytes 1572872 | tf_op jit(solution)/shard_map/ppermute | solution.py:64
  110.6 19.0 %collective-permute-start.16 = (bf16[2,256,256]{2,1,0:T(8,128)(2,1)S(1)}, bf16[2,256,256]{2,1,0:T(8,128)(2,1)S(1)}, u32[]{:S(2)}, u32[]{:S(2)}) collective-permute-start(bf16[2,256,256]{2,1,0:T(8,128)(2,1)S(1)} %slice_bitcast_fusion.1), channel_id=1, source_target_pairs={{0,8},{4,12},{8,0},{12,4},{1,9},{5,13},{9,1},{13,5},{2,10},{6,14},... | collective-permute-start | bytes 786440 | tf_op jit(solution)/shard_map/ppermute | solution.py:64
  112.2 17.4 %collective-permute-start.17 = (bf16[2,256,256]{2,1,0:T(8,128)(2,1)S(1)}, bf16[2,256,256]{2,1,0:T(8,128)(2,1)S(1)}, u32[]{:S(2)}, u32[]{:S(2)}) collective-permute-start(bf16[2,256,256]{2,1,0:T(8,128)(2,1)S(1)} %slice_bitcast_fusion), channel_id=1, source_target_pairs={{0,4},{4,0},{8,12},{12,8},{1,5},{5,1},{9,13},{13,9},{2,6},{6,2},{1... | collective-permute-start | bytes 786440 | tf_op jit(solution)/shard_map/ppermute | solution.py:64
  112.8 16.1 %collective-permute-start.18 = (bf16[1,256,256]{2,1,0:T(8,128)(2,1)S(1)}, bf16[1,256,256]{2,1,0:T(8,128)(2,1)S(1)}, u32[]{:S(2)}, u32[]{:S(2)}) collective-permute-start(bf16[1,256,256]{2,1,0:T(8,128)(2,1)S(1)} %slice.32), channel_id=1, source_target_pairs={{0,8},{4,12},{8,0},{12,4},{1,9},{5,13},{9,1},{13,5},{2,10},{6,14},... | collective-permute-start | bytes 393224 | tf_op jit(solution)/shard_map/ppermute | solution.py:64
  184.3 26.0 %collective-permute-start.33 = (bf16[2,4,256,256]{3,2,1,0:T(8,128)(2,1)S(1)}, bf16[2,4,256,256]{3,2,1,0:T(8,128)(2,1)S(1)}, u32[]{:S(2)}, u32[]{:S(2)}) collective-permute-start(bf16[2,4,256,256]{3,2,1,0:T(8,128)(2,1)S(1)} %get-tuple-element.267), channel_id=1, source_target_pairs={{0,4},{4,0},{8,12},{12,8},{1,5},{5,1},{9,13},{13,9},{2,6},{6,2},{1... | collective-permute-start | bytes 3145736 | tf_op jit(solution)/shard_map/ppermute | solution.py:64
  184.9 26.0 %collective-permute-start.34 = (bf16[2,4,256,256]{3,2,1,0:T(8,128)(2,1)S(1)}, bf16[2,4,256,256]{3,2,1,0:T(8,128)(2,1)S(1)}, u32[]{:S(2)}, u32[]{:S(2)}) collective-permute-start(bf16[2,4,256,256]{3,2,1,0:T(8,128)(2,1)S(1)} %get-tuple-element.268), channel_id=1, source_target_pairs={{0,8},{4,12},{8,0},{12,4},{1,9},{5,13},{9,1},{13,5},{2,10},{6,14},... | collective-permute-start | bytes 3145736 | tf_op jit(solution)/shard_map/ppermute | solution.py:64
  203.6 33.2 %collective-permute-start.35 = (bf16[2,4,256,256]{3,2,1,0:T(8,128)(2,1)S(1)}, bf16[2,4,256,256]{3,2,1,0:T(8,128)(2,1)S(1)}, u32[]{:S(2)}, u32[]{:S(2)}) collective-permute-start(bf16[2,4,256,256]{3,2,1,0:T(8,128)(2,1)S(1)} %get-tuple-element.270), channel_id=1, source_target_pairs={{0,4},{4,0},{8,12},{12,8},{1,5},{5,1},{9,13},{13,9},{2,6},{6,2},{1... | collective-permute-start | bytes 3145736 | tf_op jit(solution)/shard_map/ppermute | solution.py:64
  205.3 32.5 %collective-permute-start.36 = (bf16[2,4,256,256]{3,2,1,0:T(8,128)(2,1)S(1)}, bf16[2,4,256,256]{3,2,1,0:T(8,128)(2,1)S(1)}, u32[]{:S(2)}, u32[]{:S(2)}) collective-permute-start(bf16[2,4,256,256]{3,2,1,0:T(8,128)(2,1)S(1)} %get-tuple-element.271), channel_id=1, source_target_pairs={{0,8},{4,12},{8,0},{12,4},{1,9},{5,13},{9,1},{13,5},{2,10},{6,14},... | collective-permute-start | bytes 3145736 | tf_op jit(solution)/shard_map/ppermute | solution.py:64
  210.2 23.4 %collective-permute-start.39 = (bf16[256,1024]{1,0:T(8,128)(2,1)S(1)}, bf16[256,1024]{1,0:T(8,128)(2,1)S(1)}, u32[]{:S(2)}, u32[]{:S(2)}) collective-permute-start(bf16[256,1024]{1,0:T(8,128)(2,1)S(1)} %copy-done.56), channel_id=1, source_target_pairs={{0,16},{16,0},{1,17},{17,1},{2,18},{18,2},{3,19},{19,3},{4,20},{20... | collective-permute-start | bytes 1572872 | tf_op jit(solution)/shard_map/ppermute | solution.py:64
  210.9 25.0 %collective-permute-start.37 = (bf16[256,1024]{1,0:T(8,128)(2,1)S(1)}, bf16[256,1024]{1,0:T(8,128)(2,1)S(1)}, u32[]{:S(2)}, u32[]{:S(2)}) collective-permute-start(bf16[256,1024]{1,0:T(8,128)(2,1)S(1)} %copy-done.54), channel_id=1, source_target_pairs={{0,16},{16,0},{1,17},{17,1},{2,18},{18,2},{3,19},{19,3},{4,20},{20... | collective-permute-start | bytes 1572872 | tf_op jit(solution)/shard_map/ppermute | solution.py:64
  211.0 20.9 %collective-permute-start.40 = (bf16[256,512]{1,0:T(8,128)(2,1)S(1)}, bf16[256,512]{1,0:T(8,128)(2,1)S(1)}, u32[]{:S(2)}, u32[]{:S(2)}) collective-permute-start(bf16[256,512]{1,0:T(8,128)(2,1)S(1)} %copy-done.124), channel_id=1, source_target_pairs={{0,16},{16,0},{1,17},{17,1},{2,18},{18,2},{3,19},{19,3},{4,20},{20... | collective-permute-start | bytes 786440 | tf_op jit(solution)/shard_map/ppermute | solution.py:64
  232.6 17.9 %collective-permute-start.41 = (bf16[4,256,256]{2,1,0:T(8,128)(2,1)}, bf16[4,256,256]{2,1,0:T(8,128)(2,1)S(1)}, u32[]{:S(2)}, u32[]{:S(2)}) collective-permute-start(bf16[4,256,256]{2,1,0:T(8,128)(2,1)} %get-tuple-element.284), channel_id=1, source_target_pairs={{0,8},{4,12},{8,0},{12,4},{1,9},{5,13},{9,1},{13,5},{2,10},{6,14},... | collective-permute-start | bytes 1572872 | tf_op jit(solution)/shard_map/ppermute | solution.py:64
  234.4 16.1 %collective-permute-start.42 = (bf16[4,256,256]{2,1,0:T(8,128)(2,1)}, bf16[4,256,256]{2,1,0:T(8,128)(2,1)}, u32[]{:S(2)}, u32[]{:S(2)}) collective-permute-start(bf16[4,256,256]{2,1,0:T(8,128)(2,1)} %get-tuple-element.269), channel_id=1, source_target_pairs={{0,4},{4,0},{8,12},{12,8},{1,5},{5,1},{9,13},{13,9},{2,6},{6,2},{1... | collective-permute-start | bytes 1572872 | tf_op jit(solution)/shard_map/ppermute | solution.py:64
  245.0 23.7 %all-to-all-start.2 = ((bf16[4,64,1024]{2,1,0:T(8,128)(2,1)}), bf16[4,64,1024]{2,1,0:T(8,128)(2,1)}, u32[]{:S(2)}, u32[]{:S(2)}) async-start(bf16[4,64,1024]{2,1,0:T(8,128)(2,1)} %get-tuple-element.282), calls=%async_computation.2 | async-start | bytes 1048576 | tf_op jit(solution)/shard_map/all_to_all | solution.py:1030
  260.7 31.0 %collective-permute-start.46 = (bf16[4,256,256]{2,1,0:T(8,128)(2,1)}, bf16[4,256,256]{2,1,0:T(8,128)(2,1)}, u32[]{:S(2)}, u32[]{:S(2)}) collective-permute-start(bf16[4,256,256]{2,1,0:T(8,128)(2,1)} %get-tuple-element.287), channel_id=1, source_target_pairs={{0,4},{4,0},{8,12},{12,8},{1,5},{5,1},{9,13},{13,9},{2,6},{6,2},{1... | collective-permute-start | bytes 1572872 | tf_op jit(solution)/shard_map/ppermute | solution.py:64
  261.3 50.9 %collective-permute-start.51 = (bf16[384,1024]{1,0:T(8,128)(2,1)}, bf16[384,1024]{1,0:T(8,128)(2,1)}, u32[]{:S(2)}, u32[]{:S(2)}) collective-permute-start(bf16[384,1024]{1,0:T(8,128)(2,1)} %get-tuple-element.315.own_part), channel_id=1, source_target_pairs={{0,16},{16,0},{1,17},{17,1},{2,18},{18,2},{3,19},{19,3},{4,20},{20... | collective-permute-start | bytes 2359304 | tf_op jit(solution)/shard_map/ppermute | solution.py:64
  262.2 41.9 %collective-permute-start.52 = (bf16[192,1024]{1,0:T(8,128)(2,1)}, bf16[192,1024]{1,0:T(8,128)(2,1)S(1)}, u32[]{:S(2)}, u32[]{:S(2)}) collective-permute-start(bf16[192,1024]{1,0:T(8,128)(2,1)} %shard_map.150), channel_id=1, source_target_pairs={{0,1},{1,0},{2,3},{3,2},{4,5},{5,4},{6,7},{7,6},{8,9},{9,8},{10,11... | collective-permute-start | bytes 1179656 | tf_op jit(solution)/shard_map/ppermute | solution.py:64
  267.9 36.6 %collective-permute-start.47 = (bf16[2,2,256,256]{3,2,1,0:T(8,128)(2,1)}, bf16[2,2,256,256]{3,2,1,0:T(8,128)(2,1)}, u32[]{:S(2)}, u32[]{:S(2)}) collective-permute-start(bf16[2,2,256,256]{3,2,1,0:T(8,128)(2,1)} %get-tuple-element.303), channel_id=1, source_target_pairs={{0,4},{4,0},{8,12},{12,8},{1,5},{5,1},{9,13},{13,9},{2,6},{6,2},{1... | collective-permute-start | bytes 1572872 | tf_op jit(solution)/shard_map/ppermute | solution.py:64
  274.3 30.3 %collective-permute-start.48 = (bf16[2,2,256,256]{3,2,1,0:T(8,128)(2,1)}, bf16[2,2,256,256]{3,2,1,0:T(8,128)(2,1)}, u32[]{:S(2)}, u32[]{:S(2)}) collective-permute-start(bf16[2,2,256,256]{3,2,1,0:T(8,128)(2,1)} %copy-done.104), channel_id=1, source_target_pairs={{0,8},{4,12},{8,0},{12,4},{1,9},{5,13},{9,1},{13,5},{2,10},{6,14},... | collective-permute-start | bytes 1572872 | tf_op jit(solution)/shard_map/ppermute | solution.py:64
  298.3 28.1 %all-to-all-start.3 = ((bf16[4,64,1024]{2,1,0:T(8,128)(2,1)}), bf16[4,64,1024]{2,1,0:T(8,128)(2,1)}, u32[]{:S(2)}, u32[]{:S(2)}) async-start(bf16[4,64,1024]{2,1,0:T(8,128)(2,1)} %get-tuple-element.301), calls=%async_computation.3 | async-start | bytes 1048576 | tf_op jit(solution)/shard_map/all_to_all | solution.py:1030
  304.1 16.6 %collective-permute-start.53 = (bf16[192,1024]{1,0:T(8,128)(2,1)S(1)}, bf16[192,1024]{1,0:T(8,128)(2,1)S(1)}, u32[]{:S(2)}, u32[]{:S(2)}) collective-permute-start(bf16[192,1024]{1,0:T(8,128)(2,1)S(1)} %collective-permute-done.52.far_same), channel_id=1, source_target_pairs={{0,16},{16,0},{1,17},{17,1},{2,18},{18,2},{3,19},{19,3},{4,20},{20... | collective-permute-start | bytes 1179656 | tf_op jit(solution)/shard_map/ppermute | solution.py:64
  307.4 14.9 %collective-permute-start.56 = (bf16[2,256,256]{2,1,0:T(8,128)(2,1)S(1)}, bf16[2,256,256]{2,1,0:T(8,128)(2,1)S(1)}, u32[]{:S(2)}, u32[]{:S(2)}) collective-permute-start(bf16[2,256,256]{2,1,0:T(8,128)(2,1)S(1)} %get-tuple-element.327), channel_id=1, source_target_pairs={{0,8},{4,12},{8,0},{12,4},{1,9},{5,13},{9,1},{13,5},{2,10},{6,14},... | collective-permute-start | bytes 786440 | tf_op jit(solution)/shard_map/ppermute | solution.py:64
  312.2 25.9 %collective-permute-start.60 = (bf16[2,2,256,256]{3,2,1,0:T(8,128)(2,1)}, bf16[2,2,256,256]{3,2,1,0:T(8,128)(2,1)}, u32[]{:S(2)}, u32[]{:S(2)}) collective-permute-start(bf16[2,2,256,256]{3,2,1,0:T(8,128)(2,1)} %get-tuple-element.333), channel_id=1, source_target_pairs={{0,1},{1,0},{2,3},{3,2},{4,5},{5,4},{6,7},{7,6},{8,9},{9,8},{10,11... | collective-permute-start | bytes 1572872 | tf_op jit(solution)/shard_map/ppermute | solution.py:64
  314.3 26.7 %collective-permute-start.63 = (bf16[1,4,256,256]{3,2,1,0:T(8,128)(2,1)}, bf16[1,4,256,256]{3,2,1,0:T(8,128)(2,1)}, u32[]{:S(2)}, u32[]{:S(2)}) collective-permute-start(bf16[1,4,256,256]{3,2,1,0:T(8,128)(2,1)} %get-tuple-element.337), channel_id=1, source_target_pairs={{0,2},{1,3},{2,0},{3,1},{4,6},{5,7},{6,4},{7,5},{8,10},{9,11},{10,... | collective-permute-start | bytes 1572872 | tf_op jit(solution)/shard_map/ppermute | solution.py:64
  342.4 16.2 %collective-permute-start.64 = (bf16[2,256,256]{2,1,0:T(8,128)(2,1)}, bf16[2,256,256]{2,1,0:T(8,128)(2,1)S(1)}, u32[]{:S(2)}, u32[]{:S(2)}) collective-permute-start(bf16[2,256,256]{2,1,0:T(8,128)(2,1)} %shard_map.168), channel_id=1, source_target_pairs={{0,2},{1,3},{2,0},{3,1},{4,6},{5,7},{6,4},{7,5},{8,10},{9,11},{10,... | collective-permute-start | bytes 786440 | tf_op jit(solution)/shard_map/ppermute | solution.py:64
  345.1 26.2 %collective-permute-start.66 = (bf16[8,256,256]{2,1,0:T(8,128)(2,1)}, bf16[8,256,256]{2,1,0:T(8,128)(2,1)S(1)}, u32[]{:S(2)}, u32[]{:S(2)}) collective-permute-start(bf16[8,256,256]{2,1,0:T(8,128)(2,1)} %constant_dynamic-update-slice_fusion.rest_0_), channel_id=1, source_target_pairs={{0,4},{4,0},{8,12},{12,8},{1,5},{5,1},{9,13},{13,9},{2,6},{6,2},{1... | collective-permute-start | bytes 3145736 | tf_op jit(solution)/shard_map/ppermute | solution.py:64
  345.5 27.5 %collective-permute-start.67 = (bf16[8,256,256]{2,1,0:T(8,128)(2,1)}, bf16[8,256,256]{2,1,0:T(8,128)(2,1)}, u32[]{:S(2)}, u32[]{:S(2)}) collective-permute-start(bf16[8,256,256]{2,1,0:T(8,128)(2,1)} %constant_dynamic-update-slice_fusion.rest_0_), channel_id=1, source_target_pairs={{0,8},{4,12},{8,0},{12,4},{1,9},{5,13},{9,1},{13,5},{2,10},{6,14},... | collective-permute-start | bytes 3145736 | tf_op jit(solution)/shard_map/ppermute | solution.py:64
  362.1 20.5 %collective-permute-start.71 = (bf16[4,256,256]{2,1,0:T(8,128)(2,1)}, bf16[4,256,256]{2,1,0:T(8,128)(2,1)S(1)}, u32[]{:S(2)}, u32[]{:S(2)}) collective-permute-start(bf16[4,256,256]{2,1,0:T(8,128)(2,1)} %constant_dynamic-update-slice_fusion.2.rest_0_), channel_id=1, source_target_pairs={{0,4},{4,0},{8,12},{12,8},{1,5},{5,1},{9,13},{13,9},{2,6},{6,2},{1... | collective-permute-start | bytes 1572872 | tf_op jit(solution)/shard_map/ppermute | solution.py:64
  362.4 21.7 %collective-permute-start.72 = (bf16[4,256,256]{2,1,0:T(8,128)(2,1)}, bf16[4,256,256]{2,1,0:T(8,128)(2,1)S(1)}, u32[]{:S(2)}, u32[]{:S(2)}) collective-permute-start(bf16[4,256,256]{2,1,0:T(8,128)(2,1)} %constant_dynamic-update-slice_fusion.2.rest_0_), channel_id=1, source_target_pairs={{0,8},{4,12},{8,0},{12,4},{1,9},{5,13},{9,1},{13,5},{2,10},{6,14},... | collective-permute-start | bytes 1572872 | tf_op jit(solution)/shard_map/ppermute | solution.py:64
  372.1 23.1 %collective-permute-start.68 = (bf16[4,256,256]{2,1,0:T(8,128)(2,1)}, bf16[4,256,256]{2,1,0:T(8,128)(2,1)}, u32[]{:S(2)}, u32[]{:S(2)}) collective-permute-start(bf16[4,256,256]{2,1,0:T(8,128)(2,1)} %slice.42), channel_id=1, source_target_pairs={{0,8},{4,12},{8,0},{12,4},{1,9},{5,13},{9,1},{13,5},{2,10},{6,14},... | collective-permute-start | bytes 1572872 | tf_op jit(solution)/shard_map/ppermute | solution.py:64
  374.9 20.3 %collective-permute-start.69 = (bf16[4,256,256]{2,1,0:T(8,128)(2,1)}, bf16[4,256,256]{2,1,0:T(8,128)(2,1)}, u32[]{:S(2)}, u32[]{:S(2)}) collective-permute-start(bf16[4,256,256]{2,1,0:T(8,128)(2,1)} %slice.43), channel_id=1, source_target_pairs={{0,4},{4,0},{8,12},{12,8},{1,5},{5,1},{9,13},{13,9},{2,6},{6,2},{1... | collective-permute-start | bytes 1572872 | tf_op jit(solution)/shard_map/ppermute | solution.py:64
  376.9 17.7 %all-to-all-start.5 = ((f32[4,2,1024]{2,1,0:T(2,128)}), f32[4,2,1024]{2,1,0:T(2,128)S(1)}, u32[]{:S(2)}, u32[]{:S(2)}) async-start(f32[4,2,1024]{2,1,0:T(2,128)} %broadcast_in_dim.23), calls=%async_computation.5 | async-start | bytes 65536 | tf_op jit(solution)/shard_map/all_to_all | solution.py:1470
  383.3 17.7 %collective-permute-start.73 = (bf16[2,256,256]{2,1,0:T(8,128)(2,1)}, bf16[2,256,256]{2,1,0:T(8,128)(2,1)S(1)}, u32[]{:S(2)}, u32[]{:S(2)}) collective-permute-start(bf16[2,256,256]{2,1,0:T(8,128)(2,1)} %slice.44), channel_id=1, source_target_pairs={{0,8},{4,12},{8,0},{12,4},{1,9},{5,13},{9,1},{13,5},{2,10},{6,14},... | collective-permute-start | bytes 786440 | tf_op jit(solution)/shard_map/ppermute | solution.py:64
  384.9 16.1 %collective-permute-start.74 = (bf16[2,256,256]{2,1,0:T(8,128)(2,1)}, bf16[2,256,256]{2,1,0:T(8,128)(2,1)S(1)}, u32[]{:S(2)}, u32[]{:S(2)}) collective-permute-start(bf16[2,256,256]{2,1,0:T(8,128)(2,1)} %slice.45), channel_id=1, source_target_pairs={{0,4},{4,0},{8,12},{12,8},{1,5},{5,1},{9,13},{13,9},{2,6},{6,2},{1... | collective-permute-start | bytes 786440 | tf_op jit(solution)/shard_map/ppermute | solution.py:64
  (160 other events, 1392.1 us)

commit v7 on v6

--- a/solution.py
+++ b/solution.py
@@ -41,14 +41,15 @@
     def until(self, *values):
         self.tokens += values
 
-    def call(self, body, outs, args, specs, scratch=(), limit=28, us=2.0, grid=()):
+    def call(self, body, outs, args, specs, scratch=(), limit=28, us=2.0, grid=(), place=VM, aliases=()):
         args = (self.after(args[0]),) + tuple(args[1:])
         results = pl.pallas_call(
             body,
             out_shape=tuple(outs),
             grid=grid,
             in_specs=list(specs),
-            out_specs=tuple(VM for _ in outs),
+            out_specs=place if isinstance(place, tuple) else (place,) * len(outs),
+            input_output_aliases=dict(aliases),
             scratch_shapes=list(scratch),
             compiler_params=pltpu.CompilerParams(vmem_limit_bytes=limit * MIB),
             cost_estimate=pl.CostEstimate(
@@ -379,16 +380,14 @@
 
 
 def mix_unit(refs, k, m, u):
-    whole, near = refs[0], refs[1:4]
-    both = refs[4:8]
-    last = refs[8:12]
+    whole, near, x_part, y_part, far = refs[0], refs[1:4], refs[4], refs[5], refs[6:8]
     if k == 0:
         return whole.at[m, u]
     if m == 0:
         return near[k - 1].at[u]
-    if k == 3:
-        return last[m - 1].at[u] if m < 3 else last[2 + u].at[0]
-    return both[m - 1].at[k - 1, u] if m < 3 else both[2 + u].at[k - 1]
+    if m == 3:
+        return far[u].at[k - 1]
+    return (x_part if m == 1 else y_part).at[u, k - 1]
 
 
 def feed_unit(refs, k, m, u):
@@ -399,7 +398,7 @@
     return refs[4].at[u] if u < 2 else refs[5].at[u - 2]
 
 
-MIX_REFS, FEED_REFS = 12, 6
+MIX_REFS, FEED_REFS = 8, 6
 
 
 def pair_rows(a, b, size):
@@ -877,38 +876,105 @@
     return (far_kept[index] if index < count else far_arrived[index - count]).astype(f32)
 
 
-def feed_final_kernel(info, *rest):
-    refs, (up, down) = rest[:5], rest[5:]
+def write_feed(info, quarters, unit, count, up, down, rows, columns, sems):
     low, sec = info[LOW], info[SEC]
     wide = up.shape[1] // 2
-    count = refs[0].shape[0] // 2
-    for m in range(QUARTERS):
+    made = Copies(sems)
+    for place, m in enumerate(quarters):
         at = pl.ds(block_at(low, m), UNIT)
         for source, half in ((0, sec), (count, 1 - sec)):
             for part in range(2):
                 hidden = pl.ds(pl.multiple_of(half * wide + part * UNIT, UNIT), UNIT)
-                up[at, hidden] = quarter_unit(refs, m, source + 2 * part)
-                down[hidden, at] = quarter_unit(refs, m, source + 2 * part + 1)
-
-
-def mix_final_kernel(info, *rest):
-    refs, (qkv, out) = rest[:5], rest[5:]
+                rows[place, :, hidden] = unit(m, source + 2 * part)
+                columns[place, hidden, :] = unit(m, source + 2 * part + 1)
+        made.start(rows.at[place], up.at[at, :])
+        made.start(columns.at[place], down.at[:, at])
+    made.wait()
+
+
+def feed_near_kernel(info, own, x_part, y_part, up, down, rows, columns, sems):
+    parts = (own, x_part, y_part)
+    write_feed(
+        info, (0, 1, 2), lambda m, n: parts[m][n].astype(f32), own.shape[0] // 2,
+        up, down, rows, columns, sems,
+    )
+
+
+def feed_far_kernel(info, far_kept, far_arrived, up_before, down_before,
+                    up, down, rows, columns, sems):
+    count = far_kept.shape[0]
+
+    def unit(m, n):
+        return (far_kept[n] if n < count else far_arrived[n - count]).astype(f32)
+
+    write_feed(info, (3,), unit, count, up, down, rows, columns, sems)
+
+
+def write_mix(info, quarters, unit, count, qkv, out, rows, columns, sems):
     low, sec = info[LOW], info[SEC]
     width = out.shape[0] // 2
-    count = refs[0].shape[0] // 2
-    for m in range(QUARTERS):
+    made = Copies(sems)
+    for place, m in enumerate(quarters):
         at = pl.ds(block_at(low, m), UNIT)
-        at_left = pl.ds(block_at(low, m), width)
-        at_right = pl.ds(pl.multiple_of(block_at(low, m) + width, width), width)
         for source, half in ((0, sec), (count, 1 - sec)):
             lanes = pl.ds(pl.multiple_of(half * width, width), width)
-            query_keys = quarter_unit(refs, m, source)
-            qkv[0, at, lanes] = query_keys[:, :width]
-            qkv[1, at, lanes] = query_keys[:, width:]
-            rest_unit = quarter_unit(refs, m, source + 1)
-            qkv[2, at, lanes] = rest_unit[:, :width]
-            out[lanes, at_left] = rest_unit[:width, width:]
-            out[lanes, at_right] = rest_unit[width:, width:]
+            query_keys = unit(m, source)
+            rows[place, 0, :, lanes] = query_keys[:, :width]
+            rows[place, 1, :, lanes] = query_keys[:, width:]
+            rest_unit = unit(m, source + 1)
+            rows[place, 2, :, lanes] = rest_unit[:, :width]
+            columns[place, lanes, :width] = rest_unit[:width, width:]
+            columns[place, lanes, width:] = rest_unit[width:, width:]
+        made.start(rows.at[place], qkv.at[:, at, :])
+        made.start(columns.at[place], out.at[:, at])
+    made.wait()
+
+
+GAIN_ROWS = 32
+
+
+def gain_pack_kernel(gain, packed):
+    rows = []
+    for g in range(gain.shape[0]):
+        rest = gain[g : g + 1, :]
+        for _ in range(3):
+            part = rest.astype(low16).astype(f32)
+            rest = rest - part
+            rows += [part[:, span(m)] for m in range(QUARTERS)]
+    rows.append(jnp.zeros((GAIN_ROWS - len(rows), UNIT), f32))
+    packed[...] = jnp.concatenate(rows, axis=0).astype(low16)
+
+
+def unit_rows(ref, n):
+    return ref[n * UNIT : (n + 1) * UNIT, :].astype(f32)
+
+
+def mix_near_kernel(info, own, x_part, y_part, qkv, out, rows, columns, sems):
+    parts = (own, x_part, y_part)
+    count = (own.shape[0] - GAIN_ROWS) // (2 * UNIT)
+    write_mix(
+        info, (0, 1, 2), lambda m, n: unit_rows(parts[m], n), count, qkv, out, rows, columns, sems
+    )
+
+
+def mix_far_kernel(info, own, x_part, y_part, far_kept, far_arrived, qkv_before, out_before,
+                   qkv, out, gain, rows, columns, sems):
+    count = far_kept.shape[0] // UNIT
+
+    def unit(m, n):
+        return unit_rows(far_kept, n) if n < count else unit_rows(far_arrived, n - count)
+
+    total = None
+    for ref in (own, x_part, y_part, far_arrived):
+        part = ref[ref.shape[0] - GAIN_ROWS :, :].astype(f32)
+        total = part if total is None else total + part
+    for g in range(gain.shape[0]):
+        for m in range(QUARTERS):
+            at = [3 * QUARTERS * g + QUARTERS * t + m for t in range(3)]
+            gain[g : g + 1, span(m)] = (
+                total[at[0] : at[0] + 1] + total[at[1] : at[1] + 1] + total[at[2] : at[2] + 1]
+            )
+    write_mix(info, (3,), unit, count, qkv, out, rows, columns, sems)
 
 
 def sum_rest(value):
@@ -971,7 +1037,7 @@
         )[0]
         self.terms = (self.keep, self.once, swap(far, "tensor", 2))
 
-    def gathered(self, info, world):
+    def gathered(self, info, world, extra=None):
         near = half_at(0, self.count)
         given, kept = self.order.call(
             pick_kernel,
@@ -980,22 +1046,22 @@
             [SM] + [near if term.ndim == 4 else VM for term in self.terms] + [VM],
             grid=(1,),
         )
-        units = jnp.concatenate([kept, swap(given, "section", 1)])
-        return Gather(units)
+        arrived = swap(given, "section", 1)
+        if extra is None:
+            return Gather(jnp.concatenate([kept, arrived]), self.count)
+        rows = [kept.reshape(-1, UNIT), arrived.reshape(-1, UNIT), extra]
+        return Gather(jnp.concatenate(rows), self.count * UNIT)
 
 
 class Gather:
-    def __init__(self, units):
-        self.units = units
-        self.count = units.shape[0] // 2
+    def __init__(self, units, count):
+        self.units, self.count = units, count
         self.near = (swap(units, "dp", 1), swap(units, "dp", 2))
 
     def far(self):
         x_part, y_part = self.near
-        self.rest = (
-            swap(x_part[: self.count], "dp", 2), swap(y_part[self.count :], "dp", 1)
-        )
-        return (self.units,) + self.near + self.rest
+        rest = (swap(x_part[: self.count], "dp", 2), swap(y_part[self.count :], "dp", 1))
+        return (self.units,) + self.near + rest
 
 
 def on_device(codes, lengths, gains, w_qkv, w_out, w_up, w_down, cotangent):
@@ -1049,8 +1115,32 @@
         [SM, VM, VM, VM],
         us=2,
     )
+    first_rows, *attention_w = lax.optimization_barrier((first_rows,) + attention_w)
+    attention_w = tuple(attention_w)
     first_blocks = gather(first_rows)
-
+    feed_w = with_other(order.after(own_w[2:]))
+
+    first_g, packed_g, probs_g, mixed_g, mixed_given, partial = call(
+        global_attention_kernel,
+        [
+            shape((rows_g, width), low16),
+            shape((3, rows_g, heads_width), low16),
+            shape((heads_width // HEAD_DIM, rows_g, rows_g), low16),
+            shape((rows_g, heads_width), low16),
+            shape((rows_g, half), low16),
+            shape((4, frames, width), low16),
+        ],
+        (info, first_blocks) + attention_w,
+        [SM, VM] + [ANY] * 4,
+        [
+            pltpu.VMEM((3, width, heads_width), low16),
+            pltpu.VMEM((heads_width, width), low16),
+            sem(8),
+        ],
+        us=5.7,
+        limit=60,
+    )
+    arrived = scatter(partial)
     mix_piece, mix_whole = call(
         mix_piece_kernel,
         [shape((2, UNIT, UNIT), low16), shape((QUARTERS, 2, UNIT, UNIT), low16)],
@@ -1061,41 +1151,6 @@
     )
     mix_z1 = swap(mix_piece, "tensor", 1)
     mix_z2 = swap(mix_piece, "tensor", 2)
-    feed_w = with_other(order.after(own_w[2:]))
-
-    first_g, packed_g, probs_g, mixed_g, mixed_given, partial = call(
-        global_attention_kernel,
-        [
-            shape((rows_g, width), low16),
-            shape((3, rows_g, heads_width), low16),
-            shape((heads_width // HEAD_DIM, rows_g, rows_g), low16),
-            shape((rows_g, heads_width), low16),
-            shape((rows_g, half), low16),
-            shape((4, frames, width), low16),
-        ],
-        (info, first_blocks) + attention_w,
-        [SM, VM] + [ANY] * 4,
-        [
-            pltpu.VMEM((3, width, heads_width), low16),
-            pltpu.VMEM((heads_width, width), low16),
-            sem(8),
-        ],
-        us=5.7,
-        limit=60,
-    )
-    partial, mix_z1, mix_z2 = lax.optimization_barrier((partial, mix_z1, mix_z2))
-    arrived = scatter(partial)
-    mix_z3 = swap(order.after(mix_z2), "tensor", 1)
-    top_l, top_given = call(
-        local_top_kernel,
-        [shape((rows_l, width), low16), shape((rows_l // utts, width), low16)],
-        (info, cot_rows),
-        [SM, VM],
-        us=2.3,
-    )
-    mix_near = jnp.stack(order.after([mix_z1, mix_z2]))
-    mix_x = swap(mix_near, "dp", 1)
-    mix_y = swap(mix_near, "dp", 2)
     feed_piece, feed_whole = call(
         feed_piece_kernel,
         [shape((4, UNIT, UNIT), low16), shape((QUARTERS, 4, UNIT, UNIT), low16)],
@@ -1104,8 +1159,13 @@
         [sem(4 * QUARTERS)],
         us=4,
     )
-    feed_z2 = swap(feed_piece, "tensor", 2)
-    top_same = swap(order.after(top_given), "tensor", 1)
+    top_l, top_given = call(
+        local_top_kernel,
+        [shape((rows_l, width), low16), shape((rows_l // utts, width), low16)],
+        (info, cot_rows),
+        [SM, VM],
+        us=2.3,
+    )
     hidden_g, second_rows = call(
         middle_kernel,
         [shape((frames, width), f32), shape((frames, width), low16)],
@@ -1113,28 +1173,13 @@
         [VM] * 3,
         us=2,
     )
-    mix_z3 = order.after(mix_z3)
-    mix_x3 = swap(mix_z3, "dp", 1)
-    mix_y3 = swap(mix_z3, "dp", 2)
+    second_rows, mix_z1, mix_z2, feed_piece = lax.optimization_barrier(
+        (second_rows, mix_z1, mix_z2, feed_piece)
+    )
+    mix_z3 = swap(mix_z2, "tensor", 1)
     second_blocks = gather(second_rows)
-    order.until(feed_z2, mix_x, mix_y, mix_x3, mix_y3, top_same)
-    feed_z2, mix_x, mix_y, mix_x3, mix_y3 = order.after((feed_z2, mix_x, mix_y, mix_x3, mix_y3))
-    mix_w = (
-        mix_whole,
-        mix_z1,
-        mix_z2,
-        mix_z3,
-        mix_x,
-        mix_y,
-        swap(mix_x[:, 0], "dp", 2),
-        swap(mix_y[:, 1], "dp", 1),
-        mix_x3,
-        mix_y3,
-        swap(mix_x3[:1], "dp", 2),
-        swap(mix_y3[1:], "dp", 1),
-    )
-    feed_x = swap(feed_z2, "dp", 1)
-    feed_y = swap(feed_z2, "dp", 2)
+    feed_z2 = swap(order.after(feed_piece), "tensor", 2)
+    order.until(mix_z3)
     second_g, lifted_g, active_g, active_given, partial = call(
         global_feed_kernel,
         [
@@ -1156,7 +1201,11 @@
         limit=60,
     )
     arrived = scatter(partial)
-    order.until(feed_x, feed_y, mix_w[6], mix_w[7], mix_w[10], mix_w[11])
+    mix_near = jnp.stack(order.after([mix_z1, mix_z2, mix_z3]), axis=1)
+    mix_x = swap(mix_near, "dp", 1)
+    mix_y = swap(mix_near, "dp", 2)
+    mix_far = (swap(mix_x[0], "dp", 2), swap(mix_y[1], "dp", 1))
+    order.until(*mix_far, feed_z2)
     sent = call(
         sent_kernel,
         [shape((frames, width), low16)],
@@ -1165,6 +1214,36 @@
         us=1.9,
     )[0]
     other_sent = swap(sent, "section", 1)
+    mix_w = (mix_whole, mix_z1, mix_z2, mix_z3, mix_x, mix_y) + mix_far
+    feed_z2 = order.after(feed_z2)
+    feed_x = swap(feed_z2, "dp", 1)
+    feed_y = swap(feed_z2, "dp", 2)
+    top_same = swap(order.after(top_given), "tensor", 1)
+
+    start_l, first_l, query_keys, values_l, probs_l, mixed_l, partial = call(
+        local_attention_kernel,
+        [
+            shape((rows_l, width), f32),
+            shape((rows_l, width), low16),
+            shape((4, rows_l, 2 * half), low16),
+            shape((4, rows_l, half), low16),
+            shape((4, utts, 2 * rows_l // utts, half), low16),
+            shape((rows_l, 4 * half), low16),
+            shape((rows_l, width), low16),
+        ],
+        (info, code_rows, sent, other_sent, gain_l) + mix_w,
+        [SM] + [VM] * 4 + [ANY] * MIX_REFS,
+        [
+            pltpu.VMEM((4, 2, width, UNIT), low16),
+            pltpu.VMEM((4 * half, width), low16),
+            sem(32),
+        ],
+        us=9,
+        limit=60,
+    )
+    partial, feed_x, feed_y, top_same = lax.optimization_barrier(
+        (partial, feed_x, feed_y, top_same)
+    )
     feed_l = (
         feed_whole,
         feed_z2,
@@ -1173,30 +1252,6 @@
         swap(feed_x[:2], "dp", 2),
         swap(feed_y[2:], "dp", 1),
     )
-
-    order.until(*feed_l)
-
-    start_l, first_l, query_keys, values_l, probs_l, mixed_l, partial = call(
-        local_attention_kernel,
-        [
-            shape((rows_l, width), f32),
-            shape((rows_l, width), low16),
-            shape((4, rows_l, 2 * half), low16),
-            shape((4, rows_l, half), low16),
-            shape((4, utts, 2 * rows_l // utts, half), low16),
-            shape((rows_l, 4 * half), low16),
-            shape((rows_l, width), low16),
-        ],
-        (info, code_rows, sent, other_sent, gain_l) + mix_w,
-        [SM] + [VM] * 4 + [ANY] * MIX_REFS,
-        [
-            pltpu.VMEM((4, 2, width, UNIT), low16),
-            pltpu.VMEM((4 * half, width), low16),
-            sem(32),
-        ],
-        us=9,
-        limit=60,
-    )
     hidden_l, second_l, second_given = call(
         local_norm_kernel,
         [
@@ -1209,7 +1264,7 @@
         us=3.7,
     )
     second_same = swap(second_given, "tensor", 1)
-    top_cross = swap(order.after(top_same), "section", 1)
+    top_cross = swap(top_same, "section", 1)
     feed_scratch = [
         pltpu.VMEM((tiles, width, UNIT), low16),
         pltpu.VMEM((tiles, UNIT, width), low16),
@@ -1319,6 +1374,7 @@
             us=6,
         ),
     )
+    local_feed.second()
     returned, code_part, gain1_l = call(
         local_end_kernel,
         [
@@ -1333,7 +1389,6 @@
     )
 
     top_blocks = gather(returned)
-    local_feed.second()
     order.until(*local_mix.once, far_first, far_mixed, far_second_g, far_active_g)
     top_g, grad_lifted_g, lifted_given, partial = call(
         global_feed_back_kernel,
@@ -1471,25 +1526,65 @@
 
     gain_total = over(gain_total, "tensor")
     order.until(gain_total)
-    mix_sum = local_mix.gathered(info, world_mix)
-    gain_total = over(gain_total, "dp")
-    order.until(gain_total, *feed_sum.near)
+    packed_gain = call(
+        gain_pack_kernel, [shape((GAIN_ROWS, UNIT), low16)], (gain_total,), [VM], us=0.7
+    )[0]
+    mix_sum = local_mix.gathered(info, world_mix, packed_gain)
+    order.until(*feed_sum.near)
     feed_parts = feed_sum.far()
+    def finals(count, rows, columns):
+        return [
+            pltpu.VMEM((count,) + rows, f32), pltpu.VMEM((count,) + columns, f32), sem(2 * count)
+        ]
+
+    feed_shapes = [shape((width, wide), f32), shape((wide, width), f32)]
+    mix_shapes = [shape((3, width, heads_width), f32), shape((heads_width, width), f32)]
+    feed_part = ((UNIT, wide), (wide, UNIT))
+    mix_part = ((3, UNIT, heads_width), (heads_width, UNIT))
+    feed_grads = call(
+        feed_near_kernel,
+        feed_shapes,
+        (info,) + feed_parts[:3],
+        [SM] + [VM] * 3,
+        finals(3, *feed_part),
+        us=5,
+        place=ANY,
+    )
+    mix_sum.near = order.after(mix_sum.near)
     mix_parts = mix_sum.far()
+    mix_grads = call(
+        mix_near_kernel,
+        mix_shapes,
+        (info,) + mix_parts[:3],
+        [SM] + [VM] * 3,
+        finals(3, *mix_part),
+        us=3,
+        place=ANY,
+    )
     up_grad, down_grad = call(
-        feed_final_kernel,
-        [shape((width, wide), f32), shape((wide, width), f32)],
-        (info,) + feed_parts,
-        [SM] + [VM] * 5,
-        us=6.8,
-    )
-    qkv_grad, out_grad = call(
-        mix_final_kernel,
-        [shape((3, width, heads_width), f32), shape((heads_width, width), f32)],
-        (info,) + mix_parts,
-        [SM] + [VM] * 5,
-        us=4.5,
-    )
+        feed_far_kernel,
+        feed_shapes,
+        (info,) + feed_parts[3:] + tuple(feed_grads),
+        [SM] + [VM] * 2 + [ANY] * 2,
+        finals(1, *feed_part),
+        us=2,
+        place=ANY,
+        aliases=((3, 0), (4, 1)),
+    )
+    qkv_grad, out_grad, gain_total = call(
+        mix_far_kernel,
+        mix_shapes + [shape((2, width), f32)],
+        (info,) + mix_parts + tuple(mix_grads),
+        [SM] + [VM] * 5 + [ANY] * 2,
+        finals(1, *mix_part),
+        us=1.5,
+        place=(ANY, ANY, VM),
+        aliases=((6, 0), (7, 1)),
+    )
+    step = QUARTERS
+    while step < lax.axis_size("dp"):
+        gain_total = gain_total + swap(gain_total, "dp", step)
+        step *= 2
     return (
         jnp.transpose(output, (0, 2, 1, 3)),
         code_grad,

time: 411 us -> 404 us (0.983)
  waiting for transfers between devices: 62.3 us -> 81.3 us
  starting transfers between devices: 83.4 us -> 70.5 us
  blocking collectives: 88.7 us -> 81.4 us
    ppermute x75 -> x71, waiting for transfers between devices: 55.2 us -> 75.5 us  [swap(): return lax.ppermute(value, axis, [(i, i ^ flip) for i in range(count)])]
    ppermute x75 -> x71, starting transfers between devices: 61.2 us -> 51.1 us  [swap(): return lax.ppermute(value, axis, [(i, i ^ flip) for i in range(count)])]
    all_to_all x1 -> x0, waiting for transfers between devices: 7.12 us -> none  [over(): return jnp.sum(lax.all_to_all(order.after(copies), axis, 0, 0), axis=0)]
    all_gather x4, blocking collectives: 76.9 us -> 70.7 us  [gather(): gathered = lax.all_gather(rows, 'tensor')]
    all_to_all x4, waiting for transfers between devices: 0.01 us -> 5.79 us  [scatter(): return lax.all_to_all(partial, 'tensor', 0, 0)]
    unnamed x258 -> x241, local copies, waits for them, and re-layouts: 37.3 us -> 40.2 us
    pallas_call x39 -> x42, Pallas kernels: 117 us -> 118 us  [call(): pl.pallas_call(body, out_shape=tuple(outs), grid=grid, in_specs=list(spec...]
  transfers between devices with their start and end apart: 80 -> 75, of which waited for: 24 -> 30; matrix products, arithmetic and copies ran while one was open for 4% -> 1% of each run, Pallas kernels for 22% -> 25%
where the time goes in v7:
time: 404 us; the launch traced here: 397 us
  Pallas kernels  118 us (29%)
  blocking collectives  81.4 us (20%)
  waiting for transfers between devices  81.3 us (20%)
  starting transfers between devices  70.5 us (17%)
  local copies, waits for them, and re-layouts  41.3 us (10%)
    pallas_call x42, Pallas kernels, call(): pl.pallas_call(body, out_shape=tuple(outs), grid=grid, in_specs=list(spec...  118 us
    ppermute x71, waiting for transfers between devices, swap(): return lax.ppermute(value, axis, [(i, i ^ flip) for i in range(count)])  75.5 us
    all_gather x4, blocking collectives, gather(): gathered = lax.all_gather(rows, 'tensor')  70.7 us
    ppermute x71, starting transfers between devices, swap(): return lax.ppermute(value, axis, [(i, i ^ flip) for i in range(count)])  51.1 us
    unnamed x241, local copies, waits for them, and re-layouts  40.2 us
    all_to_all x4, starting transfers between devices, scatter(): return lax.all_to_all(partial, 'tensor', 0, 0)  19.4 us
    all_to_all x1, blocking collectives, over(): return jnp.sum(lax.all_to_all(order.after(copies), axis, 0, 0), axis=0)  10.7 us
  transfers between devices with their start and end apart: 75, of which 30 were waited for; matrix products, arithmetic and copies ran while one was open for 1% of the time, Pallas kernels for 25%

profile of v7, /device:TPU:0, one launch (start us, length us, event | category | flops | bytes accessed | tf_op | source)
XLA Modules:
  0.0 397.5 jit_solution(6071053972727255274)
XLA Ops:
  6.7 17.9 %all-gather = bf16[256,1024]{1,0:T(8,128)(2,1)} all-gather(bf16[64,1024]{1,0:T(8,128)(2,1)S(1)} %get-tuple-element.198), channel_id=2, replica_groups=mesh['section'=2,'dp'=4,'tensor'=4] {'tensor'}, dimensions={0}, use_global_device_ids=true | all-gather | bytes 655360 | tf_op jit(solution)/shard_map/all_gather | solution.py:1091
  25.3 5.5 %shard_map.136 = (bf16[256,1024]{1,0:T(8,128)(2,1)}, bf16[3,256,256]{2,1,0:T(8,128)(2,1)}, bf16[4,256,256]{2,1,0:T(8,128)(2,1)}, bf16[256,256]{1,0:T(8,128)(2,1)...) custom-call(s32[5]{0:T(128)} %copy-done.81, bf16[4,64,1024]{2,1,0:T(8,128)(2,1)} %bitcast.70, ...), custom_call_target="tpu_custom_call" | custom-call | flops 1140000000 | tf_op jit(solution)/shard_map/pallas_call | solution.py:46
  30.8 5.4 %all-to-all-start = ((bf16[4,64,1024]{2,1,0:T(8,128)(2,1)}), bf16[4,64,1024]{2,1,0:T(8,128)(2,1)}, u32[]{:S(2)}, u32[]{:S(2)}) async-start(bf16[4,64,1024]{2,1,0:T(8,128)(2,1)} %get-tuple-element.204), calls=%async_computation | async-start | bytes 1048576 | tf_op jit(solution)/shard_map/all_to_all | solution.py:1096
  39.3 2.0 shard_map.137
  41.3 2.1 collective-permute-start.5
  43.4 2.4 collective-permute-start.6
  45.8 2.3 shard_map.138
  54.3 2.3 collective-permute-done.5.rest_1_
  56.7 5.6 %collective-permute-done.6.rest_2_ = bf16[2,256,256]{2,1,0:T(8,128)(2,1)S(1)} collective-permute-done((bf16[2,256,256]{2,1,0:T(8,128)(2,1)S(1)}, bf16[2,256,256]{2,1,0:T(8,128)(2,1)S(1)}, u32[]{:S(2)}, u32[]{:S(2)}) %collective-permute-start.6) | collective-permute-done | bytes 262176 | tf_op jit(solution)/shard_map/ppermute | solution.py:65
  62.2 20.2 %all-gather.1 = bf16[256,1024]{1,0:T(8,128)(2,1)} all-gather(bf16[64,1024]{1,0:T(8,128)(2,1)S(1)} %get-tuple-element.221), channel_id=3, replica_groups=mesh['section'=2,'dp'=4,'tensor'=4] {'tensor'}, dimensions={0}, use_global_device_ids=true | all-gather | bytes 655360 | tf_op jit(solution)/shard_map/all_gather | solution.py:1091
  82.5 5.8 %shard_map.141 = (bf16[256,1024]{1,0:T(8,128)(2,1)}, f32[256,1024]{1,0:T(8,128)}, bf16[256,1024]{1,0:T(8,128)(2,1)}, bf16[256,512]{1,0:T(8,128)(2,1)}, bf16[4,64,1024]{2,1,0:T(8,128)(2,1)}) custom-call(s32[5]{0:T(128)} %copy-done.81, bf16[4,64,1024]{2,1,0:T(8,128)(2,1)} %bitcast.72, bf16[1024,1024]{1,0:T(8,128)(2,1)} %bitcast.41, ...), custom_call_target="tpu_custom_call" | custom-call | flops 1120000000 | tf_op jit(solution)/shard_map/pallas_call | solution.py:46
  93.0 3.6 all-to-all-start.1
  96.7 9.1 %collective-permute-done.10.rest_5_ = bf16[2,3,256,256]{3,2,1,0:T(8,128)(2,1)S(1)} collective-permute-done((bf16[2,3,256,256]{3,2,1,0:T(8,128)(2,1)}, bf16[2,3,256,256]{3,2,1,0:T(8,128)(2,1)S(1)}, u32[]{:S(2)}, u32[]{:S(2)}) %collective-permute-start.10) | collective-permute-done | bytes 786464 | tf_op jit(solution)/shard_map/ppermute | solution.py:65
  109.9 8.4 %collective-permute-done.12.rest_1_ = bf16[4,256,256]{2,1,0:T(8,128)(2,1)S(1)} collective-permute-done((bf16[4,256,256]{2,1,0:T(8,128)(2,1)}, bf16[4,256,256]{2,1,0:T(8,128)(2,1)S(1)}, u32[]{:S(2)}, u32[]{:S(2)}) %collective-permute-start.12) | collective-permute-done | bytes 524320 | tf_op jit(solution)/shard_map/ppermute | solution.py:65
  119.8 3.9 all-to-all-done.1.arrived
  127.9 8.7 %shard_map.143 = (f32[384,1024]{1,0:T(8,128)}, bf16[384,1024]{1,0:T(8,128)(2,1)}, bf16[4,384,256]{2,1,0:T(8,128)(2,1)}, bf16[4,384,128]{2,1,0:T(8,128)(2,1)}, bf...) custom-call(s32[5]{0:T(128)} %copy-done.81, ...), custom_call_target="tpu_custom_call" | custom-call | flops 1800000000 | tf_op jit(solution)/shard_map/pallas_call | solution.py:46
  136.6 2.0 collective-permute-done.14.rest_2_
  145.7 1.9 collective-permute-done.18.rest_4_
  149.6 7.1 %shard_map.145 = (bf16[4,384,256]{2,1,0:T(8,128)(2,1)S(1)}, bf16[4,384,256]{2,1,0:T(8,128)(2,1)S(1)}, bf16[384,1024]{1,0:T(8,128)(2,1)S(1)}) custom-call(bf16[384,1024]{1,0:T(8,128)(2,1)S(1)} %get-tuple-element.255.second, bf16[384,1024]{1,0:T(8,128)(2,1)S(1)} %get-tuple-element.244.top, bf16[4,4,256,256]{3,2,1,0:T(8,128)(2,1)S(1)} %copy-done.26, ...), custom_call_target="tpu_custom_call" | custom-call | flops 1580000000 | tf_op jit(solution)/shard_map/pallas_call | solution.py:46
  158.5 8.2 %shard_map.146 = (bf16[4,384,256]{2,1,0:T(8,128)(2,1)S(1)}, bf16[4,384,256]{2,1,0:T(8,128)(2,1)S(1)}, bf16[384,1024]{1,0:T(8,128)(2,1)S(1)}, bf16[384,1024]{1,0:...) custom-call(bf16[192,1024]{1,0:T(8,128)(2,1)S(1)} %collective-permute-done.20.second_same, ...), custom_call_target="tpu_custom_call" | custom-call | flops 1640000000 | tf_op jit(solution)/shard_map/pallas_call | solution.py:46
  169.6 3.5 shard_map.148
  173.2 4.1 %shard_map.149 = (bf16[384,1024]{1,0:T(8,128)(2,1)}, bf16[192,1024]{1,0:T(8,128)(2,1)S(1)}, bf16[192,1024]{1,0:T(8,128)(2,1)S(1)}) custom-call(bf16[4,384,256]{2,1,0:T(8,128)(2,1)S(1)} %get-tuple-element.262.own_active, bf16[4,384,256]{2,1,0:T(8,128)(2,1)S(1)} %get-tuple-element.259.far_active, bf16[4,4,256,256]{3,2,1,0:T(8,128)(2,1)S(1)} %copy-done.27, ...), custom_call_target="tpu_custom_call" | custom-call | flops 1220000000 | tf_op jit(solution)/shard_map/pallas_call | solution.py:46
  183.9 13.0 %shard_map.151 = (f32[384,1024]{1,0:T(8,128)S(1)}, bf16[384,1024]{1,0:T(8,128)(2,1)S(1)}, bf16[4,384,256]{2,1,0:T(8,128)(2,1)S(1)}, bf16[4,384,128]{2,1,0:T(8,12...) custom-call(s32[5]{0:T(128)S(1)} %copy-done.84, f32[384,1024]{1,0:T(8,128)S(1)} %get-tuple-element.267.hidden, ...), custom_call_target="tpu_custom_call" | custom-call | flops 2280000000 | tf_op jit(solution)/shard_map/pallas_call | solution.py:46
  197.5 2.7 shard_map.152
  202.2 3.6 collective-permute-done.28.from_x.refs_1_
  214.9 15.9 %all-gather.2 = bf16[256,1024]{1,0:T(8,128)(2,1)} all-gather(bf16[64,1024]{1,0:T(8,128)(2,1)S(1)} %get-tuple-element.288.returned), channel_id=4, replica_groups=mesh['section'=2,'dp'=4,'tensor'=4] {'tensor'}, dimensions={0}, use_global_device_ids=true | all-gather | bytes 655360 | tf_op jit(solution)/shard_map/all_gather | solution.py:1091
  234.2 6.2 %shard_map.155 = (bf16[256,1024]{1,0:T(8,128)(2,1)}, bf16[256,1024]{1,0:T(8,128)(2,1)}, bf16[256,512]{1,0:T(8,128)(2,1)}, bf16[4,64,1024]{2,1,0:T(8,128)(2,1)}) custom-call(s32[5]{0:T(128)} %copy-done.81, bf16[4,64,1024]{2,1,0:T(8,128)(2,1)} %bitcast.69, f32[256,1024]{1,0:T(8,128)} %get-tuple-element.300.rest_1_, bf16[1024,1024]{1,0:T(8,128)(2,1)} %bitcast.42, ...), custom_call_target="tpu_custom_call" | custom-call | flops 1260000000 | tf_op jit(solution)/shard_map/pallas_call | solution.py:46
  240.5 4.7 %all-to-all-start.2 = ((bf16[4,64,1024]{2,1,0:T(8,128)(2,1)}), bf16[4,64,1024]{2,1,0:T(8,128)(2,1)}, u32[]{:S(2)}, u32[]{:S(2)}) async-start(bf16[4,64,1024]{2,1,0:T(8,128)(2,1)} %get-tuple-element.301), calls=%async_computation.2 | async-start | bytes 1048576 | tf_op jit(solution)/shard_map/all_to_all | solution.py:1096
  250.3 2.0 shard_map.156
  255.7 2.0 collective-permute-start.48
  257.7 2.2 shard_map.158
  268.4 16.6 %all-gather.3 = bf16[256,1024]{1,0:T(8,128)(2,1)} all-gather(bf16[64,1024]{1,0:T(8,128)(2,1)S(1)} %get-tuple-element.315), channel_id=5, replica_groups=mesh['section'=2,'dp'=4,'tensor'=4] {'tensor'}, dimensions={0}, use_global_device_ids=true | all-gather | bytes 655360 | tf_op jit(solution)/shard_map/all_gather | solution.py:1091
  285.0 6.6 %shard_map.160 = (bf16[256,1024]{1,0:T(8,128)(2,1)}, bf16[3,256,256]{2,1,0:T(8,128)(2,1)}, bf16[3,256,128]{2,1,0:T(8,128)(2,1)}, bf16[4,64,1024]{2,1,0:T(8,128)(2,1)}) custom-call(s32[5]{0:T(128)} %copy-done.81, bf16[4,64,1024]{2,1,0:T(8,128)(2,1)} %bitcast.71, bf16[3,256,256]{2,1,0:T(8,128)(2,1)} %get-tuple-element.318.rest_1_, ...), custom_call_target="tpu_custom_call" | custom-call | flops 1360000000 | tf_op jit(solution)/shard_map/pallas_call | solution.py:46
  291.6 5.7 %all-to-all-start.3 = ((bf16[4,64,1024]{2,1,0:T(8,128)(2,1)}), bf16[4,64,1024]{2,1,0:T(8,128)(2,1)}, u32[]{:S(2)}, u32[]{:S(2)}) async-start(bf16[4,64,1024]{2,1,0:T(8,128)(2,1)} %get-tuple-element.320), calls=%async_computation.3 | async-start | bytes 1048576 | tf_op jit(solution)/shard_map/all_to_all | solution.py:1096
  303.7 2.3 shard_map.162
  306.1 2.0 collective-permute-start.56
  308.1 2.4 collective-permute-start.59
  312.0 2.2 shard_map.163
  317.2 2.4 shard_map.164
  342.0 10.7 %all_to_all.25 = f32[4,2,1024]{2,1,0:T(2,128)S(1)} all-to-all(f32[4,2,1024]{2,1,0:T(2,128)S(1)} %broadcast_in_dim.19), channel_id=1, replica_groups=mesh['section'=2,'dp'=4,'tensor'=4] {'tensor'}, dimensions={0} | all-to-all | bytes 65536 | tf_op jit(solution)/shard_map/all_to_all | solution.py:1525
  357.5 8.7 %collective-permute-done.62.x_part = bf16[8,256,256]{2,1,0:T(8,128)(2,1)S(1)} collective-permute-done((bf16[8,256,256]{2,1,0:T(8,128)(2,1)}, bf16[8,256,256]{2,1,0:T(8,128)(2,1)S(1)}, u32[]{:S(2)}, u32[]{:S(2)}) %collective-permute-start.62) | collective-permute-done | bytes 1048608 | tf_op jit(solution)/shard_map/ppermute | solution.py:65
  368.4 4.1 %shard_map.173 = (f32[1024,1024]{1,0:T(8,128)}, f32[1024,1024]{1,0:T(8,128)}) custom-call(s32[5]{0:T(128)S(1)} %copy-done.86, bf16[8,256,256]{2,1,0:T(8,128)(2,1)} %constant_dynamic-update-slice_fusion.own, bf16[8,256,256]{2,1,0:T(8,128)(2,1)S(1)} %collective-permute-done.62.x_part, bf16[8,256,256]{2,1,0:T(8,128)(2,1)S(1)} %collective-permute-done.63.y_part), custom_call_target="tpu_custom_call" | custom-call | flops 1000000000 | tf_op jit(solution)/shard_map/pallas_call | solution.py:46
  372.6 5.2 %collective-permute-done.65.x_part = bf16[1056,256]{1,0:T(8,128)(2,1)S(1)} collective-permute-done((bf16[1056,256]{1,0:T(8,128)(2,1)S(1)}, bf16[1056,256]{1,0:T(8,128)(2,1)S(1)}, u32[]{:S(2)}, u32[]{:S(2)}) %collective-permute-start.65) | collective-permute-done | bytes 540704 | tf_op jit(solution)/shard_map/ppermute | solution.py:65
  381.5 2.3 shard_map.174
  383.8 6.8 %collective-permute-done.67.far_kept = bf16[4,256,256]{2,1,0:T(8,128)(2,1)S(1)} collective-permute-done((bf16[4,256,256]{2,1,0:T(8,128)(2,1)S(1)}, bf16[4,256,256]{2,1,0:T(8,128)(2,1)S(1)}, u32[]{:S(2)}, u32[]{:S(2)}) %collective-permute-start.67) | collective-permute-done | bytes 524320 | tf_op jit(solution)/shard_map/ppermute | solution.py:65
  390.6 2.0 shard_map.175
  392.6 2.5 collective-permute-done.69.far_kept
  395.1 2.2 shard_map.176
  (411 shorter events, 126.1 us)
Async XLA Ops:
  24.7 21.1 %collective-permute-start.3 = (bf16[1024,1024]{1,0:T(8,128)(2,1)S(1)}, bf16[1024,1024]{1,0:T(8,128)(2,1)}, u32[]{:S(2)}, u32[]{:S(2)}) collective-permute-start(bf16[1024,1024]{1,0:T(8,128)(2,1)S(1)} %bitcast.43), channel_id=1, source_target_pairs={{0,16},{16,0},{1,17},{17,1},{2,18},{18,2},{3,19},{19,3},{4,20},{20... | collective-permute-start | bytes 6291464 | tf_op jit(solution)/shard_map/ppermute | solution.py:65
  24.8 21.0 %collective-permute-start.4 = (bf16[1024,1024]{1,0:T(8,128)(2,1)}, bf16[1024,1024]{1,0:T(8,128)(2,1)}, u32[]{:S(2)}, u32[]{:S(2)}) collective-permute-start(bf16[1024,1024]{1,0:T(8,128)(2,1)} %bitcast.45), channel_id=1, source_target_pairs={{0,16},{16,0},{1,17},{17,1},{2,18},{18,2},{3,19},{19,3},{4,20},{20... | collective-permute-start | bytes 6291464 | tf_op jit(solution)/shard_map/ppermute | solution.py:65
  30.8 21.4 %all-to-all-start = ((bf16[4,64,1024]{2,1,0:T(8,128)(2,1)}), bf16[4,64,1024]{2,1,0:T(8,128)(2,1)}, u32[]{:S(2)}, u32[]{:S(2)}) async-start(bf16[4,64,1024]{2,1,0:T(8,128)(2,1)} %get-tuple-element.204), calls=%async_computation | async-start | bytes 1048576 | tf_op jit(solution)/shard_map/all_to_all | solution.py:1096
  41.3 15.3 %collective-permute-start.5 = (bf16[2,256,256]{2,1,0:T(8,128)(2,1)S(1)}, bf16[2,256,256]{2,1,0:T(8,128)(2,1)S(1)}, u32[]{:S(2)}, u32[]{:S(2)}) collective-permute-start(bf16[2,256,256]{2,1,0:T(8,128)(2,1)S(1)} %get-tuple-element.219), channel_id=1, source_target_pairs={{0,1},{1,0},{2,3},{3,2},{4,5},{5,4},{6,7},{7,6},{8,9},{9,8},{10,11... | collective-permute-start | bytes 786440 | tf_op jit(solution)/shard_map/ppermute | solution.py:65
  43.4 18.8 %collective-permute-start.6 = (bf16[2,256,256]{2,1,0:T(8,128)(2,1)S(1)}, bf16[2,256,256]{2,1,0:T(8,128)(2,1)S(1)}, u32[]{:S(2)}, u32[]{:S(2)}) collective-permute-start(bf16[2,256,256]{2,1,0:T(8,128)(2,1)S(1)} %get-tuple-element.219), channel_id=1, source_target_pairs={{0,2},{1,3},{2,0},{3,1},{4,6},{5,7},{6,4},{7,5},{8,10},{9,11},{10,... | collective-permute-start | bytes 786440 | tf_op jit(solution)/shard_map/ppermute | solution.py:65
  62.2 20.2 %collective-permute-start.7 = (bf16[2,256,256]{2,1,0:T(8,128)(2,1)S(1)}, bf16[2,256,256]{2,1,0:T(8,128)(2,1)S(1)}, u32[]{:S(2)}, u32[]{:S(2)}) collective-permute-start(bf16[2,256,256]{2,1,0:T(8,128)(2,1)S(1)} %collective-permute-done.6.rest_2_), channel_id=1, source_target_pairs={{0,1},{1,0},{2,3},{3,2},{4,5},{5,4},{6,7},{7,6},{8,9},{9,8},{10,11... | collective-permute-start | bytes 786440 | tf_op jit(solution)/shard_map/ppermute | solution.py:65
  89.3 16.5 %collective-permute-start.10 = (bf16[2,3,256,256]{3,2,1,0:T(8,128)(2,1)}, bf16[2,3,256,256]{3,2,1,0:T(8,128)(2,1)S(1)}, u32[]{:S(2)}, u32[]{:S(2)}) collective-permute-start(bf16[2,3,256,256]{3,2,1,0:T(8,128)(2,1)} %pad_maximum_fusion), channel_id=1, source_target_pairs={{0,8},{4,12},{8,0},{12,4},{1,9},{5,13},{9,1},{13,5},{2,10},{6,14},... | collective-permute-start | bytes 2359304 | tf_op jit(solution)/shard_map/ppermute | solution.py:65
  90.8 18.8 %collective-permute-start.8 = (bf16[2,3,256,256]{3,2,1,0:T(8,128)(2,1)}, bf16[2,3,256,256]{3,2,1,0:T(8,128)(2,1)S(1)}, u32[]{:S(2)}, u32[]{:S(2)}) collective-permute-start(bf16[2,3,256,256]{3,2,1,0:T(8,128)(2,1)} %pad_maximum_fusion), channel_id=1, source_target_pairs={{0,4},{4,0},{8,12},{12,8},{1,5},{5,1},{9,13},{13,9},{2,6},{6,2},{1... | collective-permute-start | bytes 2359304 | tf_op jit(solution)/shard_map/ppermute | solution.py:65
  92.3 26.0 %collective-permute-start.12 = (bf16[4,256,256]{2,1,0:T(8,128)(2,1)}, bf16[4,256,256]{2,1,0:T(8,128)(2,1)S(1)}, u32[]{:S(2)}, u32[]{:S(2)}) collective-permute-start(bf16[4,256,256]{2,1,0:T(8,128)(2,1)} %copy-done.96), channel_id=1, source_target_pairs={{0,2},{1,3},{2,0},{3,1},{4,6},{5,7},{6,4},{7,5},{8,10},{9,11},{10,... | collective-permute-start | bytes 1572872 | tf_op jit(solution)/shard_map/ppermute | solution.py:65
  93.0 30.7 %all-to-all-start.1 = ((bf16[4,64,1024]{2,1,0:T(8,128)(2,1)}), bf16[4,64,1024]{2,1,0:T(8,128)(2,1)S(1)}, u32[]{:S(2)}, u32[]{:S(2)}) async-start(bf16[4,64,1024]{2,1,0:T(8,128)(2,1)} %get-tuple-element.224), calls=%async_computation.1 | async-start | bytes 1048576 | tf_op jit(solution)/shard_map/all_to_all | solution.py:1096
  105.8 12.5 %collective-permute-start.11 = (bf16[3,256,256]{2,1,0:T(8,128)(2,1)S(1)}, bf16[3,256,256]{2,1,0:T(8,128)(2,1)S(1)}, u32[]{:S(2)}, u32[]{:S(2)}) collective-permute-start(bf16[3,256,256]{2,1,0:T(8,128)(2,1)S(1)} %slice_bitcast_fusion), channel_id=1, source_target_pairs={{0,4},{4,0},{8,12},{12,8},{1,5},{5,1},{9,13},{13,9},{2,6},{6,2},{1... | collective-permute-start | bytes 1179656 | tf_op jit(solution)/shard_map/ppermute | solution.py:65
  124.8 13.8 %collective-permute-start.14 = (bf16[4,256,256]{2,1,0:T(8,128)(2,1)S(1)}, bf16[4,256,256]{2,1,0:T(8,128)(2,1)S(1)}, u32[]{:S(2)}, u32[]{:S(2)}) collective-permute-start(bf16[4,256,256]{2,1,0:T(8,128)(2,1)S(1)} %collective-permute-done.12.rest_1_), channel_id=1, source_target_pairs={{0,4},{4,0},{8,12},{12,8},{1,5},{5,1},{9,13},{13,9},{2,6},{6,2},{1... | collective-permute-start | bytes 1572872 | tf_op jit(solution)/shard_map/ppermute | solution.py:65
  125.4 13.5 %collective-permute-start.15 = (bf16[4,256,256]{2,1,0:T(8,128)(2,1)S(1)}, bf16[4,256,256]{2,1,0:T(8,128)(2,1)S(1)}, u32[]{:S(2)}, u32[]{:S(2)}) collective-permute-start(bf16[4,256,256]{2,1,0:T(8,128)(2,1)S(1)} %collective-permute-done.12.rest_1_), channel_id=1, source_target_pairs={{0,8},{4,12},{8,0},{12,4},{1,9},{5,13},{9,1},{13,5},{2,10},{6,14},... | collective-permute-start | bytes 1572872 | tf_op jit(solution)/shard_map/ppermute | solution.py:65
  144.9 11.7 %collective-permute-start.20 = (bf16[192,1024]{1,0:T(8,128)(2,1)S(1)}, bf16[192,1024]{1,0:T(8,128)(2,1)S(1)}, u32[]{:S(2)}, u32[]{:S(2)}) collective-permute-start(bf16[192,1024]{1,0:T(8,128)(2,1)S(1)} %get-tuple-element.242), channel_id=1, source_target_pairs={{0,1},{1,0},{2,3},{3,2},{4,5},{5,4},{6,7},{7,6},{8,9},{9,8},{10,11... | collective-permute-start | bytes 1179656 | tf_op jit(solution)/shard_map/ppermute | solution.py:65
  145.7 11.0 %collective-permute-start.22 = (bf16[192,1024]{1,0:T(8,128)(2,1)}, bf16[192,1024]{1,0:T(8,128)(2,1)S(1)}, u32[]{:S(2)}, u32[]{:S(2)}) collective-permute-start(bf16[192,1024]{1,0:T(8,128)(2,1)} %collective-permute-done.16.top_same), channel_id=1, source_target_pairs={{0,16},{16,0},{1,17},{17,1},{2,18},{18,2},{3,19},{19,3},{4,20},{20... | collective-permute-start | bytes 1179656 | tf_op jit(solution)/shard_map/ppermute | solution.py:65
  168.6 11.2 %collective-permute-start.26 = (bf16[192,1024]{1,0:T(8,128)(2,1)S(1)}, bf16[192,1024]{1,0:T(8,128)(2,1)S(1)}, u32[]{:S(2)}, u32[]{:S(2)}) collective-permute-start(bf16[192,1024]{1,0:T(8,128)(2,1)S(1)} %shard_map.147), channel_id=1, source_target_pairs={{0,1},{1,0},{2,3},{3,2},{4,5},{5,4},{6,7},{7,6},{8,9},{9,8},{10,11... | collective-permute-start | bytes 1179656 | tf_op jit(solution)/shard_map/ppermute | solution.py:65
  169.6 14.2 %collective-permute-start.25 = (bf16[384,1024]{1,0:T(8,128)(2,1)S(1)}, bf16[384,1024]{1,0:T(8,128)(2,1)S(1)}, u32[]{:S(2)}, u32[]{:S(2)}) collective-permute-start(bf16[384,1024]{1,0:T(8,128)(2,1)S(1)} %get-tuple-element.248.own_back), channel_id=1, source_target_pairs={{0,16},{16,0},{1,17},{17,1},{2,18},{18,2},{3,19},{19,3},{4,20},{20... | collective-permute-start | bytes 2359304 | tf_op jit(solution)/shard_map/ppermute | solution.py:65
  179.8 26.0 %collective-permute-start.28 = (bf16[2,4,256,256]{3,2,1,0:T(8,128)(2,1)S(1)}, bf16[2,4,256,256]{3,2,1,0:T(8,128)(2,1)S(1)}, u32[]{:S(2)}, u32[]{:S(2)}) collective-permute-start(bf16[2,4,256,256]{3,2,1,0:T(8,128)(2,1)S(1)} %get-tuple-element.282), channel_id=1, source_target_pairs={{0,4},{4,0},{8,12},{12,8},{1,5},{5,1},{9,13},{13,9},{2,6},{6,2},{1... | collective-permute-start | bytes 3145736 | tf_op jit(solution)/shard_map/ppermute | solution.py:65
  181.4 26.0 %collective-permute-start.29 = (bf16[2,4,256,256]{3,2,1,0:T(8,128)(2,1)S(1)}, bf16[2,4,256,256]{3,2,1,0:T(8,128)(2,1)S(1)}, u32[]{:S(2)}, u32[]{:S(2)}) collective-permute-start(bf16[2,4,256,256]{3,2,1,0:T(8,128)(2,1)S(1)} %get-tuple-element.283), channel_id=1, source_target_pairs={{0,8},{4,12},{8,0},{12,4},{1,9},{5,13},{9,1},{13,5},{2,10},{6,14},... | collective-permute-start | bytes 3145736 | tf_op jit(solution)/shard_map/ppermute | solution.py:65
  201.1 31.1 %collective-permute-start.31 = (bf16[2,4,256,256]{3,2,1,0:T(8,128)(2,1)S(1)}, bf16[2,4,256,256]{3,2,1,0:T(8,128)(2,1)S(1)}, u32[]{:S(2)}, u32[]{:S(2)}) collective-permute-start(bf16[2,4,256,256]{3,2,1,0:T(8,128)(2,1)S(1)} %get-tuple-element.289), channel_id=1, source_target_pairs={{0,4},{4,0},{8,12},{12,8},{1,5},{5,1},{9,13},{13,9},{2,6},{6,2},{1... | collective-permute-start | bytes 3145736 | tf_op jit(solution)/shard_map/ppermute | solution.py:65
  201.7 31.6 %collective-permute-start.32 = (bf16[2,4,256,256]{3,2,1,0:T(8,128)(2,1)S(1)}, bf16[2,4,256,256]{3,2,1,0:T(8,128)(2,1)S(1)}, u32[]{:S(2)}, u32[]{:S(2)}) collective-permute-start(bf16[2,4,256,256]{3,2,1,0:T(8,128)(2,1)S(1)} %get-tuple-element.290), channel_id=1, source_target_pairs={{0,8},{4,12},{8,0},{12,4},{1,9},{5,13},{9,1},{13,5},{2,10},{6,14},... | collective-permute-start | bytes 3145736 | tf_op jit(solution)/shard_map/ppermute | solution.py:65
  207.4 24.1 %collective-permute-start.33 = (bf16[256,1024]{1,0:T(8,128)(2,1)S(1)}, bf16[256,1024]{1,0:T(8,128)(2,1)S(1)}, u32[]{:S(2)}, u32[]{:S(2)}) collective-permute-start(bf16[256,1024]{1,0:T(8,128)(2,1)S(1)} %copy-done.55), channel_id=1, source_target_pairs={{0,16},{16,0},{1,17},{17,1},{2,18},{18,2},{3,19},{19,3},{4,20},{20... | collective-permute-start | bytes 1572872 | tf_op jit(solution)/shard_map/ppermute | solution.py:65
  212.8 32.5 %collective-permute-start.38 = (bf16[4,256,256]{2,1,0:T(8,128)(2,1)}, bf16[4,256,256]{2,1,0:T(8,128)(2,1)S(1)}, u32[]{:S(2)}, u32[]{:S(2)}) collective-permute-start(bf16[4,256,256]{2,1,0:T(8,128)(2,1)} %get-tuple-element.284), channel_id=1, source_target_pairs={{0,4},{4,0},{8,12},{12,8},{1,5},{5,1},{9,13},{13,9},{2,6},{6,2},{1... | collective-permute-start | bytes 1572872 | tf_op jit(solution)/shard_map/ppermute | solution.py:65
  213.3 31.9 %collective-permute-start.37 = (bf16[4,256,256]{2,1,0:T(8,128)(2,1)}, bf16[4,256,256]{2,1,0:T(8,128)(2,1)}, u32[]{:S(2)}, u32[]{:S(2)}) collective-permute-start(bf16[4,256,256]{2,1,0:T(8,128)(2,1)} %get-tuple-element.303), channel_id=1, source_target_pairs={{0,8},{4,12},{8,0},{12,4},{1,9},{5,13},{9,1},{13,5},{2,10},{6,14},... | collective-permute-start | bytes 1572872 | tf_op jit(solution)/shard_map/ppermute | solution.py:65
  240.5 22.3 %all-to-all-start.2 = ((bf16[4,64,1024]{2,1,0:T(8,128)(2,1)}), bf16[4,64,1024]{2,1,0:T(8,128)(2,1)}, u32[]{:S(2)}, u32[]{:S(2)}) async-start(bf16[4,64,1024]{2,1,0:T(8,128)(2,1)} %get-tuple-element.301), calls=%async_computation.2 | async-start | bytes 1048576 | tf_op jit(solution)/shard_map/all_to_all | solution.py:1096
  245.2 12.5 %collective-permute-start.40 = (bf16[256,1024]{1,0:T(8,128)(2,1)}, bf16[256,1024]{1,0:T(8,128)(2,1)S(1)}, u32[]{:S(2)}, u32[]{:S(2)}) collective-permute-start(bf16[256,1024]{1,0:T(8,128)(2,1)} %get-tuple-element.311.top), channel_id=1, source_target_pairs={{0,16},{16,0},{1,17},{17,1},{2,18},{18,2},{3,19},{19,3},{4,20},{20... | collective-permute-start | bytes 1572872 | tf_op jit(solution)/shard_map/ppermute | solution.py:65
  253.6 14.5 %collective-permute-start.41 = (bf16[4,256,256]{2,1,0:T(8,128)(2,1)}, bf16[4,256,256]{2,1,0:T(8,128)(2,1)}, u32[]{:S(2)}, u32[]{:S(2)}) collective-permute-start(bf16[4,256,256]{2,1,0:T(8,128)(2,1)} %get-tuple-element.316), channel_id=1, source_target_pairs={{0,8},{4,12},{8,0},{12,4},{1,9},{5,13},{9,1},{13,5},{2,10},{6,14},... | collective-permute-start | bytes 1572872 | tf_op jit(solution)/shard_map/ppermute | solution.py:65
  254.0 31.0 %collective-permute-start.42 = (bf16[4,256,256]{2,1,0:T(8,128)(2,1)}, bf16[4,256,256]{2,1,0:T(8,128)(2,1)}, u32[]{:S(2)}, u32[]{:S(2)}) collective-permute-start(bf16[4,256,256]{2,1,0:T(8,128)(2,1)} %get-tuple-element.306), channel_id=1, source_target_pairs={{0,4},{4,0},{8,12},{12,8},{1,5},{5,1},{9,13},{13,9},{2,6},{6,2},{1... | collective-permute-start | bytes 1572872 | tf_op jit(solution)/shard_map/ppermute | solution.py:65
  255.5 50.6 %collective-permute-start.47 = (bf16[384,1024]{1,0:T(8,128)(2,1)}, bf16[384,1024]{1,0:T(8,128)(2,1)}, u32[]{:S(2)}, u32[]{:S(2)}) collective-permute-start(bf16[384,1024]{1,0:T(8,128)(2,1)} %get-tuple-element.334.own_part), channel_id=1, source_target_pairs={{0,16},{16,0},{1,17},{17,1},{2,18},{18,2},{3,19},{19,3},{4,20},{20... | collective-permute-start | bytes 2359304 | tf_op jit(solution)/shard_map/ppermute | solution.py:65
  255.7 41.7 %collective-permute-start.48 = (bf16[192,1024]{1,0:T(8,128)(2,1)}, bf16[192,1024]{1,0:T(8,128)(2,1)S(1)}, u32[]{:S(2)}, u32[]{:S(2)}) collective-permute-start(bf16[192,1024]{1,0:T(8,128)(2,1)} %shard_map.150), channel_id=1, source_target_pairs={{0,1},{1,0},{2,3},{3,2},{4,5},{5,4},{6,7},{7,6},{8,9},{9,8},{10,11... | collective-permute-start | bytes 1179656 | tf_op jit(solution)/shard_map/ppermute | solution.py:65
  261.5 36.5 %collective-permute-start.43 = (bf16[2,2,256,256]{3,2,1,0:T(8,128)(2,1)}, bf16[2,2,256,256]{3,2,1,0:T(8,128)(2,1)}, u32[]{:S(2)}, u32[]{:S(2)}) collective-permute-start(bf16[2,2,256,256]{3,2,1,0:T(8,128)(2,1)} %get-tuple-element.322), channel_id=1, source_target_pairs={{0,4},{4,0},{8,12},{12,8},{1,5},{5,1},{9,13},{13,9},{2,6},{6,2},{1... | collective-permute-start | bytes 1572872 | tf_op jit(solution)/shard_map/ppermute | solution.py:65
  268.1 29.9 %collective-permute-start.44 = (bf16[2,2,256,256]{3,2,1,0:T(8,128)(2,1)}, bf16[2,2,256,256]{3,2,1,0:T(8,128)(2,1)}, u32[]{:S(2)}, u32[]{:S(2)}) collective-permute-start(bf16[2,2,256,256]{3,2,1,0:T(8,128)(2,1)} %copy-done.97), channel_id=1, source_target_pairs={{0,8},{4,12},{8,0},{12,4},{1,9},{5,13},{9,1},{13,5},{2,10},{6,14},... | collective-permute-start | bytes 1572872 | tf_op jit(solution)/shard_map/ppermute | solution.py:65
  291.6 28.1 %all-to-all-start.3 = ((bf16[4,64,1024]{2,1,0:T(8,128)(2,1)}), bf16[4,64,1024]{2,1,0:T(8,128)(2,1)}, u32[]{:S(2)}, u32[]{:S(2)}) async-start(bf16[4,64,1024]{2,1,0:T(8,128)(2,1)} %get-tuple-element.320), calls=%async_computation.3 | async-start | bytes 1048576 | tf_op jit(solution)/shard_map/all_to_all | solution.py:1096
  297.3 13.1 %collective-permute-start.46 = (bf16[256,1024]{1,0:T(8,128)(2,1)}, bf16[256,1024]{1,0:T(8,128)(2,1)S(1)}, u32[]{:S(2)}, u32[]{:S(2)}) collective-permute-start(bf16[256,1024]{1,0:T(8,128)(2,1)} %get-tuple-element.331.mid), channel_id=1, source_target_pairs={{0,16},{16,0},{1,17},{17,1},{2,18},{18,2},{3,19},{19,3},{4,20},{20... | collective-permute-start | bytes 1572872 | tf_op jit(solution)/shard_map/ppermute | solution.py:65
  297.4 18.2 %collective-permute-start.49 = (bf16[192,1024]{1,0:T(8,128)(2,1)S(1)}, bf16[192,1024]{1,0:T(8,128)(2,1)S(1)}, u32[]{:S(2)}, u32[]{:S(2)}) collective-permute-start(bf16[192,1024]{1,0:T(8,128)(2,1)S(1)} %collective-permute-done.48.far_same), channel_id=1, source_target_pairs={{0,16},{16,0},{1,17},{17,1},{2,18},{18,2},{3,19},{19,3},{4,20},{20... | collective-permute-start | bytes 1179656 | tf_op jit(solution)/shard_map/ppermute | solution.py:65
  300.8 15.4 %collective-permute-start.52 = (bf16[2,256,256]{2,1,0:T(8,128)(2,1)S(1)}, bf16[2,256,256]{2,1,0:T(8,128)(2,1)S(1)}, u32[]{:S(2)}, u32[]{:S(2)}) collective-permute-start(bf16[2,256,256]{2,1,0:T(8,128)(2,1)S(1)} %get-tuple-element.346), channel_id=1, source_target_pairs={{0,8},{4,12},{8,0},{12,4},{1,9},{5,13},{9,1},{13,5},{2,10},{6,14},... | collective-permute-start | bytes 786440 | tf_op jit(solution)/shard_map/ppermute | solution.py:65
  306.1 25.9 %collective-permute-start.56 = (bf16[2,2,256,256]{3,2,1,0:T(8,128)(2,1)}, bf16[2,2,256,256]{3,2,1,0:T(8,128)(2,1)}, u32[]{:S(2)}, u32[]{:S(2)}) collective-permute-start(bf16[2,2,256,256]{3,2,1,0:T(8,128)(2,1)} %get-tuple-element.352), channel_id=1, source_target_pairs={{0,1},{1,0},{2,3},{3,2},{4,5},{5,4},{6,7},{7,6},{8,9},{9,8},{10,11... | collective-permute-start | bytes 1572872 | tf_op jit(solution)/shard_map/ppermute | solution.py:65
  308.1 26.8 %collective-permute-start.59 = (bf16[1,4,256,256]{3,2,1,0:T(8,128)(2,1)}, bf16[1,4,256,256]{3,2,1,0:T(8,128)(2,1)}, u32[]{:S(2)}, u32[]{:S(2)}) collective-permute-start(bf16[1,4,256,256]{3,2,1,0:T(8,128)(2,1)} %get-tuple-element.356), channel_id=1, source_target_pairs={{0,2},{1,3},{2,0},{3,1},{4,6},{5,7},{6,4},{7,5},{8,10},{9,11},{10,... | collective-permute-start | bytes 1572872 | tf_op jit(solution)/shard_map/ppermute | solution.py:65
  310.5 13.2 %collective-permute-start.53 = (bf16[2,256,256]{2,1,0:T(8,128)(2,1)}, bf16[2,256,256]{2,1,0:T(8,128)(2,1)}, u32[]{:S(2)}, u32[]{:S(2)}) collective-permute-start(bf16[2,256,256]{2,1,0:T(8,128)(2,1)} %get-tuple-element.324), channel_id=1, source_target_pairs={{0,4},{4,0},{8,12},{12,8},{1,5},{5,1},{9,13},{13,9},{2,6},{6,2},{1... | collective-permute-start | bytes 786440 | tf_op jit(solution)/shard_map/ppermute | solution.py:65
  336.9 15.9 %collective-permute-start.60 = (bf16[2,256,256]{2,1,0:T(8,128)(2,1)}, bf16[2,256,256]{2,1,0:T(8,128)(2,1)S(1)}, u32[]{:S(2)}, u32[]{:S(2)}) collective-permute-start(bf16[2,256,256]{2,1,0:T(8,128)(2,1)} %shard_map.168), channel_id=1, source_target_pairs={{0,2},{1,3},{2,0},{3,1},{4,6},{5,7},{6,4},{7,5},{8,10},{9,11},{10,... | collective-permute-start | bytes 786440 | tf_op jit(solution)/shard_map/ppermute | solution.py:65
  340.0 26.2 %collective-permute-start.62 = (bf16[8,256,256]{2,1,0:T(8,128)(2,1)}, bf16[8,256,256]{2,1,0:T(8,128)(2,1)S(1)}, u32[]{:S(2)}, u32[]{:S(2)}) collective-permute-start(bf16[8,256,256]{2,1,0:T(8,128)(2,1)} %constant_dynamic-update-slice_fusion.own), channel_id=1, source_target_pairs={{0,4},{4,0},{8,12},{12,8},{1,5},{5,1},{9,13},{13,9},{2,6},{6,2},{1... | collective-permute-start | bytes 3145736 | tf_op jit(solution)/shard_map/ppermute | solution.py:65
  341.5 26.3 %collective-permute-start.63 = (bf16[8,256,256]{2,1,0:T(8,128)(2,1)}, bf16[8,256,256]{2,1,0:T(8,128)(2,1)S(1)}, u32[]{:S(2)}, u32[]{:S(2)}) collective-permute-start(bf16[8,256,256]{2,1,0:T(8,128)(2,1)} %constant_dynamic-update-slice_fusion.own), channel_id=1, source_target_pairs={{0,8},{4,12},{8,0},{12,4},{1,9},{5,13},{9,1},{13,5},{2,10},{6,14},... | collective-permute-start | bytes 3145736 | tf_op jit(solution)/shard_map/ppermute | solution.py:65
  355.6 22.2 %collective-permute-start.65 = (bf16[1056,256]{1,0:T(8,128)(2,1)S(1)}, bf16[1056,256]{1,0:T(8,128)(2,1)S(1)}, u32[]{:S(2)}, u32[]{:S(2)}) collective-permute-start(bf16[1056,256]{1,0:T(8,128)(2,1)S(1)} %pad_maximum_fusion.1.own), channel_id=1, source_target_pairs={{0,4},{4,0},{8,12},{12,8},{1,5},{5,1},{9,13},{13,9},{2,6},{6,2},{1... | collective-permute-start | bytes 1622024 | tf_op jit(solution)/shard_map/ppermute | solution.py:65
  357.2 22.2 %collective-permute-start.66 = (bf16[1056,256]{1,0:T(8,128)(2,1)S(1)}, bf16[1056,256]{1,0:T(8,128)(2,1)S(1)}, u32[]{:S(2)}, u32[]{:S(2)}) collective-permute-start(bf16[1056,256]{1,0:T(8,128)(2,1)S(1)} %pad_maximum_fusion.1.own), channel_id=1, source_target_pairs={{0,8},{4,12},{8,0},{12,4},{1,9},{5,13},{9,1},{13,5},{2,10},{6,14},... | collective-permute-start | bytes 1622024 | tf_op jit(solution)/shard_map/ppermute | solution.py:65
  366.2 24.3 %collective-permute-start.67 = (bf16[4,256,256]{2,1,0:T(8,128)(2,1)S(1)}, bf16[4,256,256]{2,1,0:T(8,128)(2,1)S(1)}, u32[]{:S(2)}, u32[]{:S(2)}) collective-permute-start(bf16[4,256,256]{2,1,0:T(8,128)(2,1)S(1)} %slice.34), channel_id=1, source_target_pairs={{0,8},{4,12},{8,0},{12,4},{1,9},{5,13},{9,1},{13,5},{2,10},{6,14},... | collective-permute-start | bytes 1572872 | tf_op jit(solution)/shard_map/ppermute | solution.py:65
  367.8 22.8 %collective-permute-start.68 = (bf16[4,256,256]{2,1,0:T(8,128)(2,1)S(1)}, bf16[4,256,256]{2,1,0:T(8,128)(2,1)S(1)}, u32[]{:S(2)}, u32[]{:S(2)}) collective-permute-start(bf16[4,256,256]{2,1,0:T(8,128)(2,1)S(1)} %slice.35), channel_id=1, source_target_pairs={{0,4},{4,0},{8,12},{12,8},{1,5},{5,1},{9,13},{13,9},{2,6},{6,2},{1... | collective-permute-start | bytes 1572872 | tf_op jit(solution)/shard_map/ppermute | solution.py:65
  379.4 15.7 %collective-permute-start.70 = (bf16[544,256]{1,0:T(8,128)(2,1)S(1)}, bf16[544,256]{1,0:T(8,128)(2,1)S(1)}, u32[]{:S(2)}, u32[]{:S(2)}) collective-permute-start(bf16[544,256]{1,0:T(8,128)(2,1)S(1)} %slice.31), channel_id=1, source_target_pairs={{0,4},{4,0},{8,12},{12,8},{1,5},{5,1},{9,13},{13,9},{2,6},{6,2},{1... | collective-permute-start | bytes 835592 | tf_op jit(solution)/shard_map/ppermute | solution.py:65
  380.0 15.1 %collective-permute-start.69 = (bf16[512,256]{1,0:T(8,128)(2,1)S(1)}, bf16[512,256]{1,0:T(8,128)(2,1)S(1)}, u32[]{:S(2)}, u32[]{:S(2)}) collective-permute-start(bf16[512,256]{1,0:T(8,128)(2,1)S(1)} %slice.30), channel_id=1, source_target_pairs={{0,8},{4,12},{8,0},{12,4},{1,9},{5,13},{9,1},{13,5},{2,10},{6,14},... | collective-permute-start | bytes 786440 | tf_op jit(solution)/shard_map/ppermute | solution.py:65
  (147 other events, 1081.2 us)

commit v8 on v7

--- a/solution.py
+++ b/solution.py
@@ -20,7 +20,7 @@
 SM = pl.BlockSpec(memory_space=pltpu.SMEM)
 ANY = pl.BlockSpec(memory_space=pltpu.HBM)
 MIB = 1 << 20
-PACE = 2 * 10**8
+PACE = 0
 
 LOW, SEC, SHARD, LENGTHS = 0, 1, 2, 3
 
@@ -1362,6 +1362,7 @@
         us=11.4,
     )
     other_back = swap(back, "section", 1)
+    order.until(far_branch)
     local_mix = Sum(
         order,
         4,
@@ -1374,7 +1375,6 @@
             us=6,
         ),
     )
-    local_feed.second()
     returned, code_part, gain1_l = call(
         local_end_kernel,
         [
@@ -1389,6 +1389,7 @@
     )
 
     top_blocks = gather(returned)
+    local_feed.second()
     order.until(*local_mix.once, far_first, far_mixed, far_second_g, far_active_g)
     top_g, grad_lifted_g, lifted_given, partial = call(
         global_feed_back_kernel,
@@ -1407,7 +1408,7 @@
             sem(8),
         ],
         us=6.3,
-        limit=60,
+        limit=28,
     )
     arrived = scatter(partial)
     far_top_g, far_lifted_g = swap(top_g, "section", 1), swap(lifted_given, "section", 1)
@@ -1476,6 +1477,53 @@
             us=3,
         ),
     )
+    kept_start, given_start, gain1_g = call(
+        start_back_kernel,
+        [
+            shape((frames, width // 2), f32),
+            shape((frames, width // 2), f32),
+            shape((1, width), f32),
+        ],
+        (info, arrived, start_g, gain_g, grad_hidden_g),
+        [SM] + [VM] * 4,
+        [pltpu.VMEM((frames, width), f32)],
+        us=2.1,
+    )
+    world_feed = global_feed.third()
+    global_mix.second()
+    local_mix.fourth()
+    world_mix = global_mix.third()
+    feed_sum = local_feed.gathered(info, world_feed)
+    arrived_start = swap(given_start, "section", 1)
+    both_start = jnp.stack(
+        [
+            jnp.where(first_core, kept_start, arrived_start),
+            jnp.where(first_core, arrived_start, kept_start),
+        ]
+    )
+    code_grad = jnp.transpose(code_part + both_start[:, None], (0, 2, 1, 3))
+
+    own_gain = jnp.concatenate([gain1_g, gain2_g], axis=0)
+    total_gain = own_gain + swap(own_gain, "section", 1)
+    local_gain = jnp.concatenate([gain1_l, gain2_l], axis=0)
+    gain_total = jnp.where(first_core, total_gain, local_gain)
+    gain_total = jnp.concatenate(
+        [
+            lax.dynamic_slice_in_dim(gain_total, (low ^ m) * UNIT, UNIT, 1)
+            for m in range(QUARTERS)
+        ],
+        axis=1,
+    )
+    def over(value, axis):
+        copies = jnp.broadcast_to(value, (lax.axis_size(axis),) + value.shape)
+        return jnp.sum(lax.all_to_all(order.after(copies), axis, 0, 0), axis=0)
+
+    gain_total = over(gain_total, "tensor")
+    order.until(gain_total)
+    packed_gain = call(
+        gain_pack_kernel, [shape((GAIN_ROWS, UNIT), low16)], (gain_total,), [VM], us=0.7
+    )[0]
+    mix_sum = local_mix.gathered(info, world_mix, packed_gain)
     output = call(
         output_kernel,
         [shape((utts, code_count, frames, width // 2), low16)],
@@ -1483,53 +1531,6 @@
         [SM] + [VM] * 5,
         us=3.1,
     )[0]
-    kept_start, given_start, gain1_g = call(
-        start_back_kernel,
-        [
-            shape((frames, width // 2), f32),
-            shape((frames, width // 2), f32),
-            shape((1, width), f32),
-        ],
-        (info, arrived, start_g, gain_g, grad_hidden_g),
-        [SM] + [VM] * 4,
-        [pltpu.VMEM((frames, width), f32)],
-        us=2.1,
-    )
-    world_feed = global_feed.third()
-    global_mix.second()
-    local_mix.fourth()
-    world_mix = global_mix.third()
-    feed_sum = local_feed.gathered(info, world_feed)
-    arrived_start = swap(given_start, "section", 1)
-    both_start = jnp.stack(
-        [
-            jnp.where(first_core, kept_start, arrived_start),
-            jnp.where(first_core, arrived_start, kept_start),
-        ]
-    )
-    code_grad = jnp.transpose(code_part + both_start[:, None], (0, 2, 1, 3))
-
-    own_gain = jnp.concatenate([gain1_g, gain2_g], axis=0)
-    total_gain = own_gain + swap(own_gain, "section", 1)
-    local_gain = jnp.concatenate([gain1_l, gain2_l], axis=0)
-    gain_total = jnp.where(first_core, total_gain, local_gain)
-    gain_total = jnp.concatenate(
-        [
-            lax.dynamic_slice_in_dim(gain_total, (low ^ m) * UNIT, UNIT, 1)
-            for m in range(QUARTERS)
-        ],
-        axis=1,
-    )
-    def over(value, axis):
-        copies = jnp.broadcast_to(value, (lax.axis_size(axis),) + value.shape)
-        return jnp.sum(lax.all_to_all(order.after(copies), axis, 0, 0), axis=0)
-
-    gain_total = over(gain_total, "tensor")
-    order.until(gain_total)
-    packed_gain = call(
-        gain_pack_kernel, [shape((GAIN_ROWS, UNIT), low16)], (gain_total,), [VM], us=0.7
-    )[0]
-    mix_sum = local_mix.gathered(info, world_mix, packed_gain)
     order.until(*feed_sum.near)
     feed_parts = feed_sum.far()
     def finals(count, rows, columns):

time: 404 us -> 399 us (0.988)
  local copies, waits for them, and re-layouts: 41.3 us -> 47.7 us
  Pallas kernels: 118 us -> 112 us
  waiting for transfers between devices: 81.3 us -> 76.1 us
    pallas_call x42, Pallas kernels: 118 us -> 112 us  [call(): pl.pallas_call(body, out_shape=tuple(outs), grid=grid, in_specs=list(spec...]
    unnamed x241 -> x263, local copies, waits for them, and re-layouts: 40.2 us -> 45.6 us
  transfers between devices with their start and end apart: 75 -> 75, of which waited for: 30 -> 27; matrix products, arithmetic and copies ran while one was open for 1% -> 2% of each run, Pallas kernels for 25% -> 24%
where the time goes in v8:
time: 399 us; the launch traced here: 393 us
  Pallas kernels  112 us (28%)
  blocking collectives  79.6 us (20%)
  waiting for transfers between devices  76.1 us (19%)
  starting transfers between devices  71.1 us (18%)
  local copies, waits for them, and re-layouts  47.7 us (12%)
  other arithmetic  4.24 us (1%)
    pallas_call x42, Pallas kernels, call(): pl.pallas_call(body, out_shape=tuple(outs), grid=grid, in_specs=list(spec...  112 us
    ppermute x71, waiting for transfers between devices, swap(): return lax.ppermute(value, axis, [(i, i ^ flip) for i in range(count)])  72.2 us
    all_gather x4, blocking collectives, gather(): gathered = lax.all_gather(rows, 'tensor')  70.2 us
    ppermute x71, starting transfers between devices, swap(): return lax.ppermute(value, axis, [(i, i ^ flip) for i in range(count)])  51.4 us
    unnamed x263, local copies, waits for them, and re-layouts  45.6 us
    all_to_all x4, starting transfers between devices, scatter(): return lax.all_to_all(partial, 'tensor', 0, 0)  19.7 us
    all_to_all x1, blocking collectives, over(): return jnp.sum(lax.all_to_all(order.after(copies), axis, 0, 0), axis=0)  9.37 us
  transfers between devices with their start and end apart: 75, of which 27 were waited for; matrix products, arithmetic and copies ran while one was open for 2% of the time, Pallas kernels for 24%

profile of v8, /device:TPU:0, one launch (start us, length us, event | category | flops | bytes accessed | tf_op | source)
XLA Modules:
  0.0 392.7 jit_solution(16067685369063303163)
XLA Ops:
  6.6 17.9 %all-gather = bf16[256,1024]{1,0:T(8,128)(2,1)} all-gather(bf16[64,1024]{1,0:T(8,128)(2,1)S(1)} %get-tuple-element.198), channel_id=2, replica_groups=mesh['section'=2,'dp'=4,'tensor'=4] {'tensor'}, dimensions={0}, use_global_device_ids=true | all-gather | bytes 655360 | tf_op jit(solution)/shard_map/all_gather | solution.py:1091
  25.0 5.5 %shard_map.136 = (bf16[256,1024]{1,0:T(8,128)(2,1)}, bf16[3,256,256]{2,1,0:T(8,128)(2,1)}, bf16[4,256,256]{2,1,0:T(8,128)(2,1)}, bf16[256,256]{1,0:T(8,128)(2,1)...) custom-call(s32[5]{0:T(128)} %copy-done.99, bf16[4,64,1024]{2,1,0:T(8,128)(2,1)} %bitcast.71, ...), custom_call_target="tpu_custom_call" | custom-call | tf_op jit(solution)/shard_map/pallas_call | solution.py:46
  30.6 5.4 %all-to-all-start = ((bf16[4,64,1024]{2,1,0:T(8,128)(2,1)}), bf16[4,64,1024]{2,1,0:T(8,128)(2,1)}, u32[]{:S(2)}, u32[]{:S(2)}) async-start(bf16[4,64,1024]{2,1,0:T(8,128)(2,1)} %get-tuple-element.204), calls=%async_computation | async-start | bytes 1048576 | tf_op jit(solution)/shard_map/all_to_all | solution.py:1096
  43.3 2.0 collective-permute-start.5
  45.3 2.4 collective-permute-start.6
  47.7 2.3 shard_map.138
  54.2 3.3 collective-permute-done.5.rest_1_
  57.5 4.5 %collective-permute-done.6.rest_2_ = bf16[2,256,256]{2,1,0:T(8,128)(2,1)S(1)} collective-permute-done((bf16[2,256,256]{2,1,0:T(8,128)(2,1)}, bf16[2,256,256]{2,1,0:T(8,128)(2,1)S(1)}, u32[]{:S(2)}, u32[]{:S(2)}) %collective-permute-start.6) | collective-permute-done | bytes 262176 | tf_op jit(solution)/shard_map/ppermute | solution.py:65
  62.0 20.2 %all-gather.1 = bf16[256,1024]{1,0:T(8,128)(2,1)} all-gather(bf16[64,1024]{1,0:T(8,128)(2,1)S(1)} %get-tuple-element.221), channel_id=3, replica_groups=mesh['section'=2,'dp'=4,'tensor'=4] {'tensor'}, dimensions={0}, use_global_device_ids=true | all-gather | bytes 655360 | tf_op jit(solution)/shard_map/all_gather | solution.py:1091
  82.2 5.8 %shard_map.141 = (bf16[256,1024]{1,0:T(8,128)(2,1)}, f32[256,1024]{1,0:T(8,128)}, bf16[256,1024]{1,0:T(8,128)(2,1)}, bf16[256,512]{1,0:T(8,128)(2,1)}, bf16[4,64,1024]{2,1,0:T(8,128)(2,1)}) custom-call(s32[5]{0:T(128)} %copy-done.99, bf16[4,64,1024]{2,1,0:T(8,128)(2,1)} %bitcast.72, bf16[1024,1024]{1,0:T(8,128)(2,1)} %bitcast.42, ...), custom_call_target="tpu_custom_call" | custom-call | tf_op jit(solution)/shard_map/pallas_call | solution.py:46
  92.8 3.6 all-to-all-start.1
  96.4 9.1 %collective-permute-done.10.rest_5_ = bf16[2,3,256,256]{3,2,1,0:T(8,128)(2,1)S(1)} collective-permute-done((bf16[2,3,256,256]{3,2,1,0:T(8,128)(2,1)}, bf16[2,3,256,256]{3,2,1,0:T(8,128)(2,1)S(1)}, u32[]{:S(2)}, u32[]{:S(2)}) %collective-permute-start.10) | collective-permute-done | bytes 786464 | tf_op jit(solution)/shard_map/ppermute | solution.py:65
  105.6 1.9 collective-permute-start.11
  109.7 8.4 %collective-permute-done.12.rest_1_ = bf16[4,256,256]{2,1,0:T(8,128)(2,1)S(1)} collective-permute-done((bf16[4,256,256]{2,1,0:T(8,128)(2,1)}, bf16[4,256,256]{2,1,0:T(8,128)(2,1)S(1)}, u32[]{:S(2)}, u32[]{:S(2)}) %collective-permute-start.12) | collective-permute-done | bytes 524320 | tf_op jit(solution)/shard_map/ppermute | solution.py:65
  119.6 3.9 %all-to-all-done.1.arrived = bf16[4,64,1024]{2,1,0:T(8,128)(2,1)S(1)} async-done(((bf16[4,64,1024]{2,1,0:T(8,128)(2,1)}), bf16[4,64,1024]{2,1,0:T(8,128)(2,1)S(1)}, u32[]{:S(2)}, u32[]{:S(2)}) %all-to-all-start.1) | async-done | bytes 524320 | tf_op jit(solution)/shard_map/all_to_all | solution.py:1096
  127.7 8.6 %shard_map.143 = (f32[384,1024]{1,0:T(8,128)}, bf16[384,1024]{1,0:T(8,128)(2,1)}, bf16[4,384,256]{2,1,0:T(8,128)(2,1)}, bf16[4,384,128]{2,1,0:T(8,128)(2,1)}, bf...) custom-call(s32[5]{0:T(128)} %copy-done.99, ...), custom_call_target="tpu_custom_call" | custom-call | tf_op jit(solution)/shard_map/pallas_call | solution.py:46
  136.4 2.0 collective-permute-done.14.rest_2_
  138.6 2.5 collective-permute-done.17.other_part
  147.8 5.4 %collective-permute-done.18.rest_4_ = bf16[2,256,256]{2,1,0:T(8,128)(2,1)S(1)} collective-permute-done((bf16[2,256,256]{2,1,0:T(8,128)(2,1)S(1)}, bf16[2,256,256]{2,1,0:T(8,128)(2,1)S(1)}, u32[]{:S(2)}, u32[]{:S(2)}) %collective-permute-start.18) | collective-permute-done | bytes 262176 | tf_op jit(solution)/shard_map/ppermute | solution.py:65
  154.1 7.1 %shard_map.145 = (bf16[4,384,256]{2,1,0:T(8,128)(2,1)S(1)}, bf16[4,384,256]{2,1,0:T(8,128)(2,1)S(1)}, bf16[384,1024]{1,0:T(8,128)(2,1)S(1)}) custom-call(bf16[384,1024]{1,0:T(8,128)(2,1)S(1)} %get-tuple-element.255.second, bf16[384,1024]{1,0:T(8,128)(2,1)S(1)} %get-tuple-element.244.top, bf16[4,4,256,256]{3,2,1,0:T(8,128)(2,1)S(1)} %copy-done.5, ...), custom_call_target="tpu_custom_call" | custom-call | tf_op jit(solution)/shard_map/pallas_call | solution.py:46
  163.0 8.2 %shard_map.146 = (bf16[4,384,256]{2,1,0:T(8,128)(2,1)S(1)}, bf16[4,384,256]{2,1,0:T(8,128)(2,1)S(1)}, bf16[384,1024]{1,0:T(8,128)(2,1)S(1)}, bf16[384,1024]{1,0:...) custom-call(bf16[192,1024]{1,0:T(8,128)(2,1)S(1)} %collective-permute-done.20.second_same, ...), custom_call_target="tpu_custom_call" | custom-call | tf_op jit(solution)/shard_map/pallas_call | solution.py:46
  174.4 3.5 shard_map.148
  178.0 3.3 shard_map.149
  186.8 13.1 %shard_map.151 = (f32[384,1024]{1,0:T(8,128)S(1)}, bf16[384,1024]{1,0:T(8,128)(2,1)S(1)}, bf16[4,384,256]{2,1,0:T(8,128)(2,1)S(1)}, bf16[4,384,128]{2,1,0:T(8,12...) custom-call(s32[5]{0:T(128)S(1)} %copy-done.101, f32[384,1024]{1,0:T(8,128)S(1)} %get-tuple-element.267.hidden, ...), custom_call_target="tpu_custom_call" | custom-call | tf_op jit(solution)/shard_map/pallas_call | solution.py:46
  201.3 2.7 shard_map.152
  211.3 15.7 %all-gather.2 = bf16[256,1024]{1,0:T(8,128)(2,1)S(1)} all-gather(bf16[64,1024]{1,0:T(8,128)(2,1)S(1)} %get-tuple-element.284.returned), channel_id=4, replica_groups=mesh['section'=2,'dp'=4,'tensor'=4] {'tensor'}, dimensions={0}, use_global_device_ids=true | all-gather | bytes 655360 | tf_op jit(solution)/shard_map/all_gather | solution.py:1091
  234.6 3.4 shard_map.155
  240.4 5.0 %all-to-all-start.2 = ((bf16[4,64,1024]{2,1,0:T(8,128)(2,1)}), bf16[4,64,1024]{2,1,0:T(8,128)(2,1)S(1)}, u32[]{:S(2)}, u32[]{:S(2)}) async-start(bf16[4,64,1024]{2,1,0:T(8,128)(2,1)} %copy-done.78), calls=%async_computation.2 | async-start | bytes 1048576 | tf_op jit(solution)/shard_map/all_to_all | solution.py:1096
  250.5 2.2 shard_map.156
  256.7 2.4 shard_map.158
  263.9 16.3 %all-gather.3 = bf16[256,1024]{1,0:T(8,128)(2,1)} all-gather(bf16[64,1024]{1,0:T(8,128)(2,1)S(1)} %get-tuple-element.315), channel_id=5, replica_groups=mesh['section'=2,'dp'=4,'tensor'=4] {'tensor'}, dimensions={0}, use_global_device_ids=true | all-gather | bytes 655360 | tf_op jit(solution)/shard_map/all_gather | solution.py:1091
  280.2 6.7 %shard_map.160 = (bf16[256,1024]{1,0:T(8,128)(2,1)}, bf16[3,256,256]{2,1,0:T(8,128)(2,1)}, bf16[3,256,128]{2,1,0:T(8,128)(2,1)}, bf16[4,64,1024]{2,1,0:T(8,128)(2,1)}) custom-call(s32[5]{0:T(128)} %copy-done.99, bf16[4,64,1024]{2,1,0:T(8,128)(2,1)} %bitcast.70, bf16[3,256,256]{2,1,0:T(8,128)(2,1)} %get-tuple-element.318.rest_1_, ...), custom_call_target="tpu_custom_call" | custom-call | tf_op jit(solution)/shard_map/pallas_call | solution.py:46
  286.9 5.6 %all-to-all-start.3 = ((bf16[4,64,1024]{2,1,0:T(8,128)(2,1)}), bf16[4,64,1024]{2,1,0:T(8,128)(2,1)}, u32[]{:S(2)}, u32[]{:S(2)}) async-start(bf16[4,64,1024]{2,1,0:T(8,128)(2,1)} %get-tuple-element.320), calls=%async_computation.3 | async-start | bytes 1048576 | tf_op jit(solution)/shard_map/all_to_all | solution.py:1096
  297.3 2.3 shard_map.162
  299.7 2.0 collective-permute-start.53
  301.7 2.4 collective-permute-start.56
  305.1 2.2 shard_map.163
  321.7 4.9 %collective-permute-done.53.arrived.refs_1_ = bf16[2,2,256,256]{3,2,1,0:T(8,128)(2,1)S(1)} collective-permute-done((bf16[2,2,256,256]{3,2,1,0:T(8,128)(2,1)}, bf16[2,2,256,256]{3,2,1,0:T(8,128)(2,1)S(1)}, u32[]{:S(2)}, u32[]{:S(2)}) %collective-permute-start.53) | collective-permute-done | bytes 524320 | tf_op jit(solution)/shard_map/ppermute | solution.py:65
  329.5 2.0 shard_map.169
  332.9 1.9 constant_dynamic-update-slice_fusion.1
  338.3 9.4 %all_to_all.25 = f32[4,2,1024]{2,1,0:T(2,128)} all-to-all(f32[4,2,1024]{2,1,0:T(2,128)S(1)} %broadcast_in_dim.19), channel_id=1, replica_groups=mesh['section'=2,'dp'=4,'tensor'=4] {'tensor'}, dimensions={0} | all-to-all | bytes 65536 | tf_op jit(solution)/shard_map/all_to_all | solution.py:1519
  354.9 7.0 %collective-permute-done.62.x_part = bf16[8,256,256]{2,1,0:T(8,128)(2,1)S(1)} collective-permute-done((bf16[8,256,256]{2,1,0:T(8,128)(2,1)}, bf16[8,256,256]{2,1,0:T(8,128)(2,1)S(1)}, u32[]{:S(2)}, u32[]{:S(2)}) %collective-permute-start.62) | collective-permute-done | bytes 1048608 | tf_op jit(solution)/shard_map/ppermute | solution.py:65
  367.7 4.5 %shard_map.173 = (f32[1024,1024]{1,0:T(8,128)}, f32[1024,1024]{1,0:T(8,128)}) custom-call(s32[5]{0:T(128)S(1)} %copy-done.102, bf16[8,256,256]{2,1,0:T(8,128)(2,1)} %constant_dynamic-update-slice_fusion.own, bf16[8,256,256]{2,1,0:T(8,128)(2,1)S(1)} %collective-permute-done.62.x_part, bf16[8,256,256]{2,1,0:T(8,128)(2,1)} %collective-permute-done.63.y_part), custom_call_target="tpu_custom_call" | custom-call | tf_op jit(solution)/shard_map/pallas_call | solution.py:46
  377.6 2.3 shard_map.174
  379.9 5.8 %collective-permute-done.67.far_kept = bf16[4,256,256]{2,1,0:T(8,128)(2,1)S(1)} collective-permute-done((bf16[4,256,256]{2,1,0:T(8,128)(2,1)S(1)}, bf16[4,256,256]{2,1,0:T(8,128)(2,1)S(1)}, u32[]{:S(2)}, u32[]{:S(2)}) %collective-permute-start.67) | collective-permute-done | bytes 524320 | tf_op jit(solution)/shard_map/ppermute | solution.py:65
  385.7 2.0 shard_map.175
  387.7 2.6 collective-permute-done.69.far_kept
  390.3 2.2 shard_map.176
  (433 shorter events, 126.8 us)
Async XLA Ops:
  24.5 23.1 %collective-permute-start.3 = (bf16[1024,1024]{1,0:T(8,128)(2,1)}, bf16[1024,1024]{1,0:T(8,128)(2,1)}, u32[]{:S(2)}, u32[]{:S(2)}) collective-permute-start(bf16[1024,1024]{1,0:T(8,128)(2,1)} %bitcast.41), channel_id=1, source_target_pairs={{0,16},{16,0},{1,17},{17,1},{2,18},{18,2},{3,19},{19,3},{4,20},{20... | collective-permute-start | bytes 6291464 | tf_op jit(solution)/shard_map/ppermute | solution.py:65
  24.5 23.1 %collective-permute-start.4 = (bf16[1024,1024]{1,0:T(8,128)(2,1)}, bf16[1024,1024]{1,0:T(8,128)(2,1)}, u32[]{:S(2)}, u32[]{:S(2)}) collective-permute-start(bf16[1024,1024]{1,0:T(8,128)(2,1)} %bitcast.45), channel_id=1, source_target_pairs={{0,16},{16,0},{1,17},{17,1},{2,18},{18,2},{3,19},{19,3},{4,20},{20... | collective-permute-start | bytes 6291464 | tf_op jit(solution)/shard_map/ppermute | solution.py:65
  30.6 21.5 %all-to-all-start = ((bf16[4,64,1024]{2,1,0:T(8,128)(2,1)}), bf16[4,64,1024]{2,1,0:T(8,128)(2,1)}, u32[]{:S(2)}, u32[]{:S(2)}) async-start(bf16[4,64,1024]{2,1,0:T(8,128)(2,1)} %get-tuple-element.204), calls=%async_computation | async-start | bytes 1048576 | tf_op jit(solution)/shard_map/all_to_all | solution.py:1096
  43.3 14.2 %collective-permute-start.5 = (bf16[2,256,256]{2,1,0:T(8,128)(2,1)}, bf16[2,256,256]{2,1,0:T(8,128)(2,1)S(1)}, u32[]{:S(2)}, u32[]{:S(2)}) collective-permute-start(bf16[2,256,256]{2,1,0:T(8,128)(2,1)} %get-tuple-element.219), channel_id=1, source_target_pairs={{0,1},{1,0},{2,3},{3,2},{4,5},{5,4},{6,7},{7,6},{8,9},{9,8},{10,11... | collective-permute-start | bytes 786440 | tf_op jit(solution)/shard_map/ppermute | solution.py:65
  45.3 16.7 %collective-permute-start.6 = (bf16[2,256,256]{2,1,0:T(8,128)(2,1)}, bf16[2,256,256]{2,1,0:T(8,128)(2,1)S(1)}, u32[]{:S(2)}, u32[]{:S(2)}) collective-permute-start(bf16[2,256,256]{2,1,0:T(8,128)(2,1)} %get-tuple-element.219), channel_id=1, source_target_pairs={{0,2},{1,3},{2,0},{3,1},{4,6},{5,7},{6,4},{7,5},{8,10},{9,11},{10,... | collective-permute-start | bytes 786440 | tf_op jit(solution)/shard_map/ppermute | solution.py:65
  62.0 20.2 %collective-permute-start.7 = (bf16[2,256,256]{2,1,0:T(8,128)(2,1)S(1)}, bf16[2,256,256]{2,1,0:T(8,128)(2,1)S(1)}, u32[]{:S(2)}, u32[]{:S(2)}) collective-permute-start(bf16[2,256,256]{2,1,0:T(8,128)(2,1)S(1)} %collective-permute-done.6.rest_2_), channel_id=1, source_target_pairs={{0,1},{1,0},{2,3},{3,2},{4,5},{5,4},{6,7},{7,6},{8,9},{9,8},{10,11... | collective-permute-start | bytes 786440 | tf_op jit(solution)/shard_map/ppermute | solution.py:65
  89.0 16.5 %collective-permute-start.10 = (bf16[2,3,256,256]{3,2,1,0:T(8,128)(2,1)}, bf16[2,3,256,256]{3,2,1,0:T(8,128)(2,1)S(1)}, u32[]{:S(2)}, u32[]{:S(2)}) collective-permute-start(bf16[2,3,256,256]{3,2,1,0:T(8,128)(2,1)} %pad_maximum_fusion), channel_id=1, source_target_pairs={{0,8},{4,12},{8,0},{12,4},{1,9},{5,13},{9,1},{13,5},{2,10},{6,14},... | collective-permute-start | bytes 2359304 | tf_op jit(solution)/shard_map/ppermute | solution.py:65
  90.6 18.8 %collective-permute-start.8 = (bf16[2,3,256,256]{3,2,1,0:T(8,128)(2,1)}, bf16[2,3,256,256]{3,2,1,0:T(8,128)(2,1)S(1)}, u32[]{:S(2)}, u32[]{:S(2)}) collective-permute-start(bf16[2,3,256,256]{3,2,1,0:T(8,128)(2,1)} %pad_maximum_fusion), channel_id=1, source_target_pairs={{0,4},{4,0},{8,12},{12,8},{1,5},{5,1},{9,13},{13,9},{2,6},{6,2},{1... | collective-permute-start | bytes 2359304 | tf_op jit(solution)/shard_map/ppermute | solution.py:65
  92.0 26.0 %collective-permute-start.12 = (bf16[4,256,256]{2,1,0:T(8,128)(2,1)}, bf16[4,256,256]{2,1,0:T(8,128)(2,1)S(1)}, u32[]{:S(2)}, u32[]{:S(2)}) collective-permute-start(bf16[4,256,256]{2,1,0:T(8,128)(2,1)} %copy-done.121), channel_id=1, source_target_pairs={{0,2},{1,3},{2,0},{3,1},{4,6},{5,7},{6,4},{7,5},{8,10},{9,11},{10,... | collective-permute-start | bytes 1572872 | tf_op jit(solution)/shard_map/ppermute | solution.py:65
  92.8 30.7 %all-to-all-start.1 = ((bf16[4,64,1024]{2,1,0:T(8,128)(2,1)}), bf16[4,64,1024]{2,1,0:T(8,128)(2,1)S(1)}, u32[]{:S(2)}, u32[]{:S(2)}) async-start(bf16[4,64,1024]{2,1,0:T(8,128)(2,1)} %get-tuple-element.224), calls=%async_computation.1 | async-start | bytes 1048576 | tf_op jit(solution)/shard_map/all_to_all | solution.py:1096
  105.6 12.5 %collective-permute-start.11 = (bf16[3,256,256]{2,1,0:T(8,128)(2,1)S(1)}, bf16[3,256,256]{2,1,0:T(8,128)(2,1)S(1)}, u32[]{:S(2)}, u32[]{:S(2)}) collective-permute-start(bf16[3,256,256]{2,1,0:T(8,128)(2,1)S(1)} %slice_bitcast_fusion), channel_id=1, source_target_pairs={{0,4},{4,0},{8,12},{12,8},{1,5},{5,1},{9,13},{13,9},{2,6},{6,2},{1... | collective-permute-start | bytes 1179656 | tf_op jit(solution)/shard_map/ppermute | solution.py:65
  124.6 13.8 %collective-permute-start.14 = (bf16[4,256,256]{2,1,0:T(8,128)(2,1)S(1)}, bf16[4,256,256]{2,1,0:T(8,128)(2,1)S(1)}, u32[]{:S(2)}, u32[]{:S(2)}) collective-permute-start(bf16[4,256,256]{2,1,0:T(8,128)(2,1)S(1)} %collective-permute-done.12.rest_1_), channel_id=1, source_target_pairs={{0,4},{4,0},{8,12},{12,8},{1,5},{5,1},{9,13},{13,9},{2,6},{6,2},{1... | collective-permute-start | bytes 1572872 | tf_op jit(solution)/shard_map/ppermute | solution.py:65
  125.2 13.5 %collective-permute-start.15 = (bf16[4,256,256]{2,1,0:T(8,128)(2,1)S(1)}, bf16[4,256,256]{2,1,0:T(8,128)(2,1)S(1)}, u32[]{:S(2)}, u32[]{:S(2)}) collective-permute-start(bf16[4,256,256]{2,1,0:T(8,128)(2,1)S(1)} %collective-permute-done.12.rest_1_), channel_id=1, source_target_pairs={{0,8},{4,12},{8,0},{12,4},{1,9},{5,13},{9,1},{13,5},{2,10},{6,14},... | collective-permute-start | bytes 1572872 | tf_op jit(solution)/shard_map/ppermute | solution.py:65
  144.7 16.5 %collective-permute-start.20 = (bf16[192,1024]{1,0:T(8,128)(2,1)S(1)}, bf16[192,1024]{1,0:T(8,128)(2,1)S(1)}, u32[]{:S(2)}, u32[]{:S(2)}) collective-permute-start(bf16[192,1024]{1,0:T(8,128)(2,1)S(1)} %get-tuple-element.242), channel_id=1, source_target_pairs={{0,1},{1,0},{2,3},{3,2},{4,5},{5,4},{6,7},{7,6},{8,9},{9,8},{10,11... | collective-permute-start | bytes 1179656 | tf_op jit(solution)/shard_map/ppermute | solution.py:65
  147.8 13.5 %collective-permute-start.22 = (bf16[192,1024]{1,0:T(8,128)(2,1)}, bf16[192,1024]{1,0:T(8,128)(2,1)S(1)}, u32[]{:S(2)}, u32[]{:S(2)}) collective-permute-start(bf16[192,1024]{1,0:T(8,128)(2,1)} %collective-permute-done.16.top_same), channel_id=1, source_target_pairs={{0,16},{16,0},{1,17},{17,1},{2,18},{18,2},{3,19},{19,3},{4,20},{20... | collective-permute-start | bytes 1179656 | tf_op jit(solution)/shard_map/ppermute | solution.py:65
  173.1 11.8 %collective-permute-start.26 = (bf16[192,1024]{1,0:T(8,128)(2,1)S(1)}, bf16[192,1024]{1,0:T(8,128)(2,1)S(1)}, u32[]{:S(2)}, u32[]{:S(2)}) collective-permute-start(bf16[192,1024]{1,0:T(8,128)(2,1)S(1)} %shard_map.147), channel_id=1, source_target_pairs={{0,1},{1,0},{2,3},{3,2},{4,5},{5,4},{6,7},{7,6},{8,9},{9,8},{10,11... | collective-permute-start | bytes 1179656 | tf_op jit(solution)/shard_map/ppermute | solution.py:65
  174.4 11.3 %collective-permute-start.25 = (bf16[384,1024]{1,0:T(8,128)(2,1)S(1)}, bf16[384,1024]{1,0:T(8,128)(2,1)S(1)}, u32[]{:S(2)}, u32[]{:S(2)}) collective-permute-start(bf16[384,1024]{1,0:T(8,128)(2,1)S(1)} %get-tuple-element.248.own_back), channel_id=1, source_target_pairs={{0,16},{16,0},{1,17},{17,1},{2,18},{18,2},{3,19},{19,3},{4,20},{20... | collective-permute-start | bytes 2359304 | tf_op jit(solution)/shard_map/ppermute | solution.py:65
  181.9 25.8 %collective-permute-start.30 = (bf16[2,4,256,256]{3,2,1,0:T(8,128)(2,1)S(1)}, bf16[2,4,256,256]{3,2,1,0:T(8,128)(2,1)S(1)}, u32[]{:S(2)}, u32[]{:S(2)}) collective-permute-start(bf16[2,4,256,256]{3,2,1,0:T(8,128)(2,1)S(1)} %get-tuple-element.286), channel_id=1, source_target_pairs={{0,4},{4,0},{8,12},{12,8},{1,5},{5,1},{9,13},{13,9},{2,6},{6,2},{1... | collective-permute-start | bytes 3145736 | tf_op jit(solution)/shard_map/ppermute | solution.py:65
  183.4 24.9 %collective-permute-start.31 = (bf16[2,4,256,256]{3,2,1,0:T(8,128)(2,1)S(1)}, bf16[2,4,256,256]{3,2,1,0:T(8,128)(2,1)S(1)}, u32[]{:S(2)}, u32[]{:S(2)}) collective-permute-start(bf16[2,4,256,256]{3,2,1,0:T(8,128)(2,1)S(1)} %get-tuple-element.287), channel_id=1, source_target_pairs={{0,8},{4,12},{8,0},{12,4},{1,9},{5,13},{9,1},{13,5},{2,10},{6,14},... | collective-permute-start | bytes 3145736 | tf_op jit(solution)/shard_map/ppermute | solution.py:65
  185.1 15.5 %collective-permute-start.28 = (bf16[192,1024]{1,0:T(8,128)(2,1)S(1)}, bf16[192,1024]{1,0:T(8,128)(2,1)S(1)}, u32[]{:S(2)}, u32[]{:S(2)}) collective-permute-start(bf16[192,1024]{1,0:T(8,128)(2,1)S(1)} %shard_map.150), channel_id=1, source_target_pairs={{0,1},{1,0},{2,3},{3,2},{4,5},{5,4},{6,7},{7,6},{8,9},{9,8},{10,11... | collective-permute-start | bytes 1179656 | tf_op jit(solution)/shard_map/ppermute | solution.py:65
  205.0 27.6 %collective-permute-start.32 = (bf16[2,4,256,256]{3,2,1,0:T(8,128)(2,1)S(1)}, bf16[2,4,256,256]{3,2,1,0:T(8,128)(2,1)S(1)}, u32[]{:S(2)}, u32[]{:S(2)}) collective-permute-start(bf16[2,4,256,256]{3,2,1,0:T(8,128)(2,1)S(1)} %get-tuple-element.289), channel_id=1, source_target_pairs={{0,4},{4,0},{8,12},{12,8},{1,5},{5,1},{9,13},{13,9},{2,6},{6,2},{1... | collective-permute-start | bytes 3145736 | tf_op jit(solution)/shard_map/ppermute | solution.py:65
  206.5 27.1 %collective-permute-start.33 = (bf16[2,4,256,256]{3,2,1,0:T(8,128)(2,1)S(1)}, bf16[2,4,256,256]{3,2,1,0:T(8,128)(2,1)S(1)}, u32[]{:S(2)}, u32[]{:S(2)}) collective-permute-start(bf16[2,4,256,256]{3,2,1,0:T(8,128)(2,1)S(1)} %get-tuple-element.290), channel_id=1, source_target_pairs={{0,8},{4,12},{8,0},{12,4},{1,9},{5,13},{9,1},{13,5},{2,10},{6,14},... | collective-permute-start | bytes 3145736 | tf_op jit(solution)/shard_map/ppermute | solution.py:65
  207.7 22.3 %collective-permute-start.36 = (bf16[256,1024]{1,0:T(8,128)(2,1)S(1)}, bf16[256,1024]{1,0:T(8,128)(2,1)S(1)}, u32[]{:S(2)}, u32[]{:S(2)}) collective-permute-start(bf16[256,1024]{1,0:T(8,128)(2,1)S(1)} %copy-done.82), channel_id=1, source_target_pairs={{0,16},{16,0},{1,17},{17,1},{2,18},{18,2},{3,19},{19,3},{4,20},{20... | collective-permute-start | bytes 1572872 | tf_op jit(solution)/shard_map/ppermute | solution.py:65
  208.3 23.6 %collective-permute-start.34 = (bf16[256,1024]{1,0:T(8,128)(2,1)S(1)}, bf16[256,1024]{1,0:T(8,128)(2,1)S(1)}, u32[]{:S(2)}, u32[]{:S(2)}) collective-permute-start(bf16[256,1024]{1,0:T(8,128)(2,1)S(1)} %copy-done.80), channel_id=1, source_target_pairs={{0,16},{16,0},{1,17},{17,1},{2,18},{18,2},{3,19},{19,3},{4,20},{20... | collective-permute-start | bytes 1572872 | tf_op jit(solution)/shard_map/ppermute | solution.py:65
  208.4 19.9 %collective-permute-start.37 = (bf16[256,512]{1,0:T(8,128)(2,1)S(1)}, bf16[256,512]{1,0:T(8,128)(2,1)S(1)}, u32[]{:S(2)}, u32[]{:S(2)}) collective-permute-start(bf16[256,512]{1,0:T(8,128)(2,1)S(1)} %copy-done.128), channel_id=1, source_target_pairs={{0,16},{16,0},{1,17},{17,1},{2,18},{18,2},{3,19},{19,3},{4,20},{20... | collective-permute-start | bytes 786440 | tf_op jit(solution)/shard_map/ppermute | solution.py:65
  229.0 16.5 %collective-permute-start.38 = (bf16[4,256,256]{2,1,0:T(8,128)(2,1)}, bf16[4,256,256]{2,1,0:T(8,128)(2,1)}, u32[]{:S(2)}, u32[]{:S(2)}) collective-permute-start(bf16[4,256,256]{2,1,0:T(8,128)(2,1)} %get-tuple-element.303), channel_id=1, source_target_pairs={{0,8},{4,12},{8,0},{12,4},{1,9},{5,13},{9,1},{13,5},{2,10},{6,14},... | collective-permute-start | bytes 1572872 | tf_op jit(solution)/shard_map/ppermute | solution.py:65
  230.8 14.6 %collective-permute-start.39 = (bf16[4,256,256]{2,1,0:T(8,128)(2,1)}, bf16[4,256,256]{2,1,0:T(8,128)(2,1)}, u32[]{:S(2)}, u32[]{:S(2)}) collective-permute-start(bf16[4,256,256]{2,1,0:T(8,128)(2,1)} %get-tuple-element.288), channel_id=1, source_target_pairs={{0,4},{4,0},{8,12},{12,8},{1,5},{5,1},{9,13},{13,9},{2,6},{6,2},{1... | collective-permute-start | bytes 1572872 | tf_op jit(solution)/shard_map/ppermute | solution.py:65
  240.4 23.3 %all-to-all-start.2 = ((bf16[4,64,1024]{2,1,0:T(8,128)(2,1)}), bf16[4,64,1024]{2,1,0:T(8,128)(2,1)S(1)}, u32[]{:S(2)}, u32[]{:S(2)}) async-start(bf16[4,64,1024]{2,1,0:T(8,128)(2,1)} %copy-done.78), calls=%async_computation.2 | async-start | bytes 1048576 | tf_op jit(solution)/shard_map/all_to_all | solution.py:1096
  245.3 11.3 %collective-permute-start.41 = (bf16[256,1024]{1,0:T(8,128)(2,1)}, bf16[256,1024]{1,0:T(8,128)(2,1)S(1)}, u32[]{:S(2)}, u32[]{:S(2)}) collective-permute-start(bf16[256,1024]{1,0:T(8,128)(2,1)} %copy-done.90), channel_id=1, source_target_pairs={{0,16},{16,0},{1,17},{17,1},{2,18},{18,2},{3,19},{19,3},{4,20},{20... | collective-permute-start | bytes 1572872 | tf_op jit(solution)/shard_map/ppermute | solution.py:65
  254.0 26.2 %collective-permute-start.42 = (bf16[4,256,256]{2,1,0:T(8,128)(2,1)}, bf16[4,256,256]{2,1,0:T(8,128)(2,1)}, u32[]{:S(2)}, u32[]{:S(2)}) collective-permute-start(bf16[4,256,256]{2,1,0:T(8,128)(2,1)} %get-tuple-element.316), channel_id=1, source_target_pairs={{0,8},{4,12},{8,0},{12,4},{1,9},{5,13},{9,1},{13,5},{2,10},{6,14},... | collective-permute-start | bytes 1572872 | tf_op jit(solution)/shard_map/ppermute | solution.py:65
  254.5 25.7 %collective-permute-start.43 = (bf16[4,256,256]{2,1,0:T(8,128)(2,1)}, bf16[4,256,256]{2,1,0:T(8,128)(2,1)}, u32[]{:S(2)}, u32[]{:S(2)}) collective-permute-start(bf16[4,256,256]{2,1,0:T(8,128)(2,1)} %get-tuple-element.306), channel_id=1, source_target_pairs={{0,4},{4,0},{8,12},{12,8},{1,5},{5,1},{9,13},{13,9},{2,6},{6,2},{1... | collective-permute-start | bytes 1572872 | tf_op jit(solution)/shard_map/ppermute | solution.py:65
  260.7 31.8 %collective-permute-start.44 = (bf16[2,2,256,256]{3,2,1,0:T(8,128)(2,1)}, bf16[2,2,256,256]{3,2,1,0:T(8,128)(2,1)}, u32[]{:S(2)}, u32[]{:S(2)}) collective-permute-start(bf16[2,2,256,256]{3,2,1,0:T(8,128)(2,1)} %get-tuple-element.322), channel_id=1, source_target_pairs={{0,4},{4,0},{8,12},{12,8},{1,5},{5,1},{9,13},{13,9},{2,6},{6,2},{1... | collective-permute-start | bytes 1572872 | tf_op jit(solution)/shard_map/ppermute | solution.py:65
  262.1 30.4 %collective-permute-start.45 = (bf16[2,2,256,256]{3,2,1,0:T(8,128)(2,1)}, bf16[2,2,256,256]{3,2,1,0:T(8,128)(2,1)}, u32[]{:S(2)}, u32[]{:S(2)}) collective-permute-start(bf16[2,2,256,256]{3,2,1,0:T(8,128)(2,1)} %get-tuple-element.323), channel_id=1, source_target_pairs={{0,8},{4,12},{8,0},{12,4},{1,9},{5,13},{9,1},{13,5},{2,10},{6,14},... | collective-permute-start | bytes 1572872 | tf_op jit(solution)/shard_map/ppermute | solution.py:65
  286.9 23.8 %all-to-all-start.3 = ((bf16[4,64,1024]{2,1,0:T(8,128)(2,1)}), bf16[4,64,1024]{2,1,0:T(8,128)(2,1)}, u32[]{:S(2)}, u32[]{:S(2)}) async-start(bf16[4,64,1024]{2,1,0:T(8,128)(2,1)} %get-tuple-element.320), calls=%async_computation.3 | async-start | bytes 1048576 | tf_op jit(solution)/shard_map/all_to_all | solution.py:1096
  292.5 12.5 %collective-permute-start.47 = (bf16[256,1024]{1,0:T(8,128)(2,1)}, bf16[256,1024]{1,0:T(8,128)(2,1)S(1)}, u32[]{:S(2)}, u32[]{:S(2)}) collective-permute-start(bf16[256,1024]{1,0:T(8,128)(2,1)} %get-tuple-element.331.mid), channel_id=1, source_target_pairs={{0,16},{16,0},{1,17},{17,1},{2,18},{18,2},{3,19},{19,3},{4,20},{20... | collective-permute-start | bytes 1572872 | tf_op jit(solution)/shard_map/ppermute | solution.py:65
  295.5 12.9 %collective-permute-start.49 = (bf16[2,256,256]{2,1,0:T(8,128)(2,1)S(1)}, bf16[2,256,256]{2,1,0:T(8,128)(2,1)S(1)}, u32[]{:S(2)}, u32[]{:S(2)}) collective-permute-start(bf16[2,256,256]{2,1,0:T(8,128)(2,1)S(1)} %get-tuple-element.340), channel_id=1, source_target_pairs={{0,8},{4,12},{8,0},{12,4},{1,9},{5,13},{9,1},{13,5},{2,10},{6,14},... | collective-permute-start | bytes 786440 | tf_op jit(solution)/shard_map/ppermute | solution.py:65
  299.7 26.9 %collective-permute-start.53 = (bf16[2,2,256,256]{3,2,1,0:T(8,128)(2,1)}, bf16[2,2,256,256]{3,2,1,0:T(8,128)(2,1)S(1)}, u32[]{:S(2)}, u32[]{:S(2)}) collective-permute-start(bf16[2,2,256,256]{3,2,1,0:T(8,128)(2,1)} %get-tuple-element.346), channel_id=1, source_target_pairs={{0,1},{1,0},{2,3},{3,2},{4,5},{5,4},{6,7},{7,6},{8,9},{9,8},{10,11... | collective-permute-start | bytes 1572872 | tf_op jit(solution)/shard_map/ppermute | solution.py:65
  301.7 27.8 %collective-permute-start.56 = (bf16[1,4,256,256]{3,2,1,0:T(8,128)(2,1)}, bf16[1,4,256,256]{3,2,1,0:T(8,128)(2,1)}, u32[]{:S(2)}, u32[]{:S(2)}) collective-permute-start(bf16[1,4,256,256]{3,2,1,0:T(8,128)(2,1)} %get-tuple-element.350), channel_id=1, source_target_pairs={{0,2},{1,3},{2,0},{3,1},{4,6},{5,7},{6,4},{7,5},{8,10},{9,11},{10,... | collective-permute-start | bytes 1572872 | tf_op jit(solution)/shard_map/ppermute | solution.py:65
  332.5 16.0 %collective-permute-start.57 = (bf16[2,256,256]{2,1,0:T(8,128)(2,1)}, bf16[2,256,256]{2,1,0:T(8,128)(2,1)}, u32[]{:S(2)}, u32[]{:S(2)}) collective-permute-start(bf16[2,256,256]{2,1,0:T(8,128)(2,1)} %copy-done.103), channel_id=1, source_target_pairs={{0,2},{1,3},{2,0},{3,1},{4,6},{5,7},{6,4},{7,5},{8,10},{9,11},{10,... | collective-permute-start | bytes 786440 | tf_op jit(solution)/shard_map/ppermute | solution.py:65
  335.6 26.2 %collective-permute-start.62 = (bf16[8,256,256]{2,1,0:T(8,128)(2,1)}, bf16[8,256,256]{2,1,0:T(8,128)(2,1)S(1)}, u32[]{:S(2)}, u32[]{:S(2)}) collective-permute-start(bf16[8,256,256]{2,1,0:T(8,128)(2,1)} %constant_dynamic-update-slice_fusion.own), channel_id=1, source_target_pairs={{0,4},{4,0},{8,12},{12,8},{1,5},{5,1},{9,13},{13,9},{2,6},{6,2},{1... | collective-permute-start | bytes 3145736 | tf_op jit(solution)/shard_map/ppermute | solution.py:65
  336.6 26.4 %collective-permute-start.63 = (bf16[8,256,256]{2,1,0:T(8,128)(2,1)}, bf16[8,256,256]{2,1,0:T(8,128)(2,1)}, u32[]{:S(2)}, u32[]{:S(2)}) collective-permute-start(bf16[8,256,256]{2,1,0:T(8,128)(2,1)} %constant_dynamic-update-slice_fusion.own), channel_id=1, source_target_pairs={{0,8},{4,12},{8,0},{12,4},{1,9},{5,13},{9,1},{13,5},{2,10},{6,14},... | collective-permute-start | bytes 3145736 | tf_op jit(solution)/shard_map/ppermute | solution.py:65
  350.9 13.3 %collective-permute-start.58 = (bf16[384,1024]{1,0:T(8,128)(2,1)}, bf16[384,1024]{1,0:T(8,128)(2,1)S(1)}, u32[]{:S(2)}, u32[]{:S(2)}) collective-permute-start(bf16[384,1024]{1,0:T(8,128)(2,1)} %copy-done.66), channel_id=1, source_target_pairs={{0,16},{16,0},{1,17},{17,1},{2,18},{18,2},{3,19},{19,3},{4,20},{20... | collective-permute-start | bytes 2359304 | tf_op jit(solution)/shard_map/ppermute | solution.py:65
  352.4 21.0 %collective-permute-start.65 = (bf16[1056,256]{1,0:T(8,128)(2,1)S(1)}, bf16[1056,256]{1,0:T(8,128)(2,1)S(1)}, u32[]{:S(2)}, u32[]{:S(2)}) collective-permute-start(bf16[1056,256]{1,0:T(8,128)(2,1)S(1)} %pad_maximum_fusion.1.own), channel_id=1, source_target_pairs={{0,4},{4,0},{8,12},{12,8},{1,5},{5,1},{9,13},{13,9},{2,6},{6,2},{1... | collective-permute-start | bytes 1622024 | tf_op jit(solution)/shard_map/ppermute | solution.py:65
  353.5 21.0 %collective-permute-start.66 = (bf16[1056,256]{1,0:T(8,128)(2,1)S(1)}, bf16[1056,256]{1,0:T(8,128)(2,1)S(1)}, u32[]{:S(2)}, u32[]{:S(2)}) collective-permute-start(bf16[1056,256]{1,0:T(8,128)(2,1)S(1)} %pad_maximum_fusion.1.own), channel_id=1, source_target_pairs={{0,8},{4,12},{8,0},{12,4},{1,9},{5,13},{9,1},{13,5},{2,10},{6,14},... | collective-permute-start | bytes 1622024 | tf_op jit(solution)/shard_map/ppermute | solution.py:65
  364.1 21.6 %collective-permute-start.67 = (bf16[4,256,256]{2,1,0:T(8,128)(2,1)S(1)}, bf16[4,256,256]{2,1,0:T(8,128)(2,1)S(1)}, u32[]{:S(2)}, u32[]{:S(2)}) collective-permute-start(bf16[4,256,256]{2,1,0:T(8,128)(2,1)S(1)} %slice.34), channel_id=1, source_target_pairs={{0,8},{4,12},{8,0},{12,4},{1,9},{5,13},{9,1},{13,5},{2,10},{6,14},... | collective-permute-start | bytes 1572872 | tf_op jit(solution)/shard_map/ppermute | solution.py:65
  365.1 20.6 %collective-permute-start.68 = (bf16[4,256,256]{2,1,0:T(8,128)(2,1)S(1)}, bf16[4,256,256]{2,1,0:T(8,128)(2,1)S(1)}, u32[]{:S(2)}, u32[]{:S(2)}) collective-permute-start(bf16[4,256,256]{2,1,0:T(8,128)(2,1)S(1)} %slice.35), channel_id=1, source_target_pairs={{0,4},{4,0},{8,12},{12,8},{1,5},{5,1},{9,13},{13,9},{2,6},{6,2},{1... | collective-permute-start | bytes 1572872 | tf_op jit(solution)/shard_map/ppermute | solution.py:65
  374.5 15.8 %collective-permute-start.70 = (bf16[544,256]{1,0:T(8,128)(2,1)S(1)}, bf16[544,256]{1,0:T(8,128)(2,1)S(1)}, u32[]{:S(2)}, u32[]{:S(2)}) collective-permute-start(bf16[544,256]{1,0:T(8,128)(2,1)S(1)} %slice.31), channel_id=1, source_target_pairs={{0,4},{4,0},{8,12},{12,8},{1,5},{5,1},{9,13},{13,9},{2,6},{6,2},{1... | collective-permute-start | bytes 835592 | tf_op jit(solution)/shard_map/ppermute | solution.py:65
  375.6 14.6 %collective-permute-start.69 = (bf16[512,256]{1,0:T(8,128)(2,1)S(1)}, bf16[512,256]{1,0:T(8,128)(2,1)S(1)}, u32[]{:S(2)}, u32[]{:S(2)}) collective-permute-start(bf16[512,256]{1,0:T(8,128)(2,1)S(1)} %slice.30), channel_id=1, source_target_pairs={{0,8},{4,12},{8,0},{12,4},{1,9},{5,13},{9,1},{13,5},{2,10},{6,14},... | collective-permute-start | bytes 786440 | tf_op jit(solution)/shard_map/ppermute | solution.py:65
  (158 other events, 1202.5 us)

commit v9 on v8

--- a/solution.py
+++ b/solution.py
@@ -41,7 +41,7 @@
     def until(self, *values):
         self.tokens += values
 
-    def call(self, body, outs, args, specs, scratch=(), limit=28, us=2.0, grid=(), place=VM, aliases=()):
+    def call(self, body, outs, args, specs, scratch=(), limit=36, us=2.0, grid=(), place=VM, aliases=()):
         args = (self.after(args[0]),) + tuple(args[1:])
         results = pl.pallas_call(
             body,
@@ -1360,6 +1360,7 @@
             sem(32),
         ],
         us=11.4,
+        limit=60,
     )
     other_back = swap(back, "section", 1)
     order.until(far_branch)

time: 399 us -> 394 us (0.987)
  local copies, waits for them, and re-layouts: 47.7 us -> 41.2 us
  Pallas kernels: 112 us -> 106 us
  waiting for transfers between devices: 76.1 us -> 80.5 us
    unnamed x263 -> x227, local copies, waits for them, and re-layouts: 45.6 us -> 39 us
    pallas_call x42, Pallas kernels: 112 us -> 106 us  [call(): pl.pallas_call(body, out_shape=tuple(outs), grid=grid, in_specs=list(spec...]
  transfers between devices with their start and end apart: 75 -> 75, of which waited for: 27 -> 30; matrix products, arithmetic and copies ran while one was open for 2% -> 1% of each run, Pallas kernels for 24% -> 23%
where the time goes in v9:
time: 394 us; the launch traced here: 387 us
  Pallas kernels  106 us (27%)
  waiting for transfers between devices  80.5 us (20%)
  blocking collectives  80.2 us (20%)
  starting transfers between devices  72.7 us (18%)
  local copies, waits for them, and re-layouts  41.2 us (10%)
  other arithmetic  4.24 us (1%)
    pallas_call x42, Pallas kernels, call(): pl.pallas_call(body, out_shape=tuple(outs), grid=grid, in_specs=list(spec...  106 us
    ppermute x71, waiting for transfers between devices, swap(): return lax.ppermute(value, axis, [(i, i ^ flip) for i in range(count)])  74.3 us
    all_gather x4, blocking collectives, gather(): gathered = lax.all_gather(rows, 'tensor')  69.7 us
    ppermute x71, starting transfers between devices, swap(): return lax.ppermute(value, axis, [(i, i ^ flip) for i in range(count)])  53.4 us
    unnamed x227, local copies, waits for them, and re-layouts  39 us
    all_to_all x4, starting transfers between devices, scatter(): return lax.all_to_all(partial, 'tensor', 0, 0)  19.2 us
    all_to_all x1, blocking collectives, over(): return jnp.sum(lax.all_to_all(order.after(copies), axis, 0, 0), axis=0)  10.5 us
  transfers between devices with their start and end apart: 75, of which 30 were waited for; matrix products, arithmetic and copies ran while one was open for 1% of the time, Pallas kernels for 23%

profile of v9, /device:TPU:0, one launch (start us, length us, event | category | flops | bytes accessed | tf_op | source)
XLA Modules:
  0.0 387.3 jit_solution(4562390668455365769)
XLA Ops:
  6.7 17.9 %all-gather = bf16[256,1024]{1,0:T(8,128)(2,1)} all-gather(bf16[64,1024]{1,0:T(8,128)(2,1)S(1)} %get-tuple-element.198), channel_id=2, replica_groups=mesh['section'=2,'dp'=4,'tensor'=4] {'tensor'}, dimensions={0}, use_global_device_ids=true | all-gather | bytes 655360 | tf_op jit(solution)/shard_map/all_gather | solution.py:1091
  25.2 5.5 %shard_map.136 = (bf16[256,1024]{1,0:T(8,128)(2,1)}, bf16[3,256,256]{2,1,0:T(8,128)(2,1)}, bf16[4,256,256]{2,1,0:T(8,128)(2,1)}, bf16[256,256]{1,0:T(8,128)(2,1)...) custom-call(s32[5]{0:T(128)} %copy-done.77, bf16[4,64,1024]{2,1,0:T(8,128)(2,1)} %bitcast.71, ...), custom_call_target="tpu_custom_call" | custom-call | tf_op jit(solution)/shard_map/pallas_call | solution.py:46
  30.7 5.4 %all-to-all-start = ((bf16[4,64,1024]{2,1,0:T(8,128)(2,1)}), bf16[4,64,1024]{2,1,0:T(8,128)(2,1)S(1)}, u32[]{:S(2)}, u32[]{:S(2)}) async-start(bf16[4,64,1024]{2,1,0:T(8,128)(2,1)} %get-tuple-element.204), calls=%async_computation | async-start | bytes 1048576 | tf_op jit(solution)/shard_map/all_to_all | solution.py:1096
  41.6 2.1 collective-permute-start.5
  43.7 2.4 collective-permute-start.6
  46.1 2.3 shard_map.138
  52.2 4.4 %collective-permute-done.5.rest_1_ = bf16[2,256,256]{2,1,0:T(8,128)(2,1)S(1)} collective-permute-done((bf16[2,256,256]{2,1,0:T(8,128)(2,1)S(1)}, bf16[2,256,256]{2,1,0:T(8,128)(2,1)S(1)}, u32[]{:S(2)}, u32[]{:S(2)}) %collective-permute-start.5) | collective-permute-done | bytes 262176 | tf_op jit(solution)/shard_map/ppermute | solution.py:65
  56.6 5.6 %collective-permute-done.6.rest_2_ = bf16[2,256,256]{2,1,0:T(8,128)(2,1)S(1)} collective-permute-done((bf16[2,256,256]{2,1,0:T(8,128)(2,1)S(1)}, bf16[2,256,256]{2,1,0:T(8,128)(2,1)S(1)}, u32[]{:S(2)}, u32[]{:S(2)}) %collective-permute-start.6) | collective-permute-done | bytes 262176 | tf_op jit(solution)/shard_map/ppermute | solution.py:65
  62.1 20.2 %all-gather.1 = bf16[256,1024]{1,0:T(8,128)(2,1)} all-gather(bf16[64,1024]{1,0:T(8,128)(2,1)S(1)} %get-tuple-element.221), channel_id=3, replica_groups=mesh['section'=2,'dp'=4,'tensor'=4] {'tensor'}, dimensions={0}, use_global_device_ids=true | all-gather | bytes 655360 | tf_op jit(solution)/shard_map/all_gather | solution.py:1091
  82.4 5.8 %shard_map.141 = (bf16[256,1024]{1,0:T(8,128)(2,1)}, f32[256,1024]{1,0:T(8,128)}, bf16[256,1024]{1,0:T(8,128)(2,1)}, bf16[256,512]{1,0:T(8,128)(2,1)}, bf16[4,64,1024]{2,1,0:T(8,128)(2,1)}) custom-call(s32[5]{0:T(128)} %copy-done.77, bf16[4,64,1024]{2,1,0:T(8,128)(2,1)} %bitcast.72, bf16[1024,1024]{1,0:T(8,128)(2,1)} %bitcast.42, ...), custom_call_target="tpu_custom_call" | custom-call | tf_op jit(solution)/shard_map/pallas_call | solution.py:46
  92.9 3.6 all-to-all-start.1
  96.6 7.9 %collective-permute-done.10.rest_5_ = bf16[2,3,256,256]{3,2,1,0:T(8,128)(2,1)} collective-permute-done((bf16[2,3,256,256]{3,2,1,0:T(8,128)(2,1)}, bf16[2,3,256,256]{3,2,1,0:T(8,128)(2,1)}, u32[]{:S(2)}, u32[]{:S(2)}) %collective-permute-start.10) | collective-permute-done | bytes 786464 | tf_op jit(solution)/shard_map/ppermute | solution.py:65
  109.8 8.2 %collective-permute-done.12.rest_1_ = bf16[4,256,256]{2,1,0:T(8,128)(2,1)S(1)} collective-permute-done((bf16[4,256,256]{2,1,0:T(8,128)(2,1)S(1)}, bf16[4,256,256]{2,1,0:T(8,128)(2,1)S(1)}, u32[]{:S(2)}, u32[]{:S(2)}) %collective-permute-start.12) | collective-permute-done | bytes 524320 | tf_op jit(solution)/shard_map/ppermute | solution.py:65
  118.7 4.7 %all-to-all-done.1.arrived = bf16[4,64,1024]{2,1,0:T(8,128)(2,1)S(1)} async-done(((bf16[4,64,1024]{2,1,0:T(8,128)(2,1)}), bf16[4,64,1024]{2,1,0:T(8,128)(2,1)S(1)}, u32[]{:S(2)}, u32[]{:S(2)}) %all-to-all-start.1) | async-done | bytes 524320 | tf_op jit(solution)/shard_map/all_to_all | solution.py:1096
  126.6 8.6 %shard_map.143 = (f32[384,1024]{1,0:T(8,128)}, bf16[384,1024]{1,0:T(8,128)(2,1)}, bf16[4,384,256]{2,1,0:T(8,128)(2,1)}, bf16[4,384,128]{2,1,0:T(8,128)(2,1)}, bf...) custom-call(s32[5]{0:T(128)} %copy-done.77, ...), custom_call_target="tpu_custom_call" | custom-call | tf_op jit(solution)/shard_map/pallas_call | solution.py:46
  135.3 2.1 collective-permute-done.14.rest_2_
  137.6 2.5 collective-permute-done.17.other_part
  147.9 5.4 %collective-permute-done.18.rest_4_ = bf16[2,256,256]{2,1,0:T(8,128)(2,1)S(1)} collective-permute-done((bf16[2,256,256]{2,1,0:T(8,128)(2,1)S(1)}, bf16[2,256,256]{2,1,0:T(8,128)(2,1)S(1)}, u32[]{:S(2)}, u32[]{:S(2)}) %collective-permute-start.18) | collective-permute-done | bytes 262176 | tf_op jit(solution)/shard_map/ppermute | solution.py:65
  154.2 7.1 %shard_map.145 = (bf16[4,384,256]{2,1,0:T(8,128)(2,1)S(1)}, bf16[4,384,256]{2,1,0:T(8,128)(2,1)S(1)}, bf16[384,1024]{1,0:T(8,128)(2,1)S(1)}) custom-call(bf16[384,1024]{1,0:T(8,128)(2,1)S(1)} %get-tuple-element.255.second, bf16[384,1024]{1,0:T(8,128)(2,1)S(1)} %get-tuple-element.244.top, bf16[4,4,256,256]{3,2,1,0:T(8,128)(2,1)S(1)} %copy-done.5, ...), custom_call_target="tpu_custom_call" | custom-call | tf_op jit(solution)/shard_map/pallas_call | solution.py:46
  163.1 7.2 %shard_map.146 = (bf16[4,384,256]{2,1,0:T(8,128)(2,1)S(1)}, bf16[4,384,256]{2,1,0:T(8,128)(2,1)S(1)}, bf16[384,1024]{1,0:T(8,128)(2,1)S(1)}, bf16[384,1024]{1,0:...) custom-call(bf16[192,1024]{1,0:T(8,128)(2,1)S(1)} %collective-permute-done.20.second_same, ...), custom_call_target="tpu_custom_call" | custom-call | tf_op jit(solution)/shard_map/pallas_call | solution.py:46
  173.5 4.1 %shard_map.148 = (bf16[2,4,256,256]{3,2,1,0:T(8,128)(2,1)}, bf16[2,4,256,256]{3,2,1,0:T(8,128)(2,1)}, bf16[2,4,256,256]{3,2,1,0:T(8,128)(2,1)S(1)}, bf16[2,4,256,256]{3,2,1,0:T(8,128)(2,1)S(1)}) custom-call(bf16[384,1024]{1,0:T(8,128)(2,1)S(1)} %get-tuple-element.255.second, bf16[384,1024]{1,0:T(8,128)(2,1)S(1)} %get-tuple-element.256.far_second, ...), custom_call_target="tpu_custom_call" | custom-call | tf_op jit(solution)/shard_map/pallas_call | solution.py:46
  177.6 3.3 shard_map.149
  187.9 11.2 %shard_map.151 = (f32[384,1024]{1,0:T(8,128)}, bf16[384,1024]{1,0:T(8,128)(2,1)}, bf16[4,384,256]{2,1,0:T(8,128)(2,1)}, bf16[4,384,128]{2,1,0:T(8,128)(2,1)}, bf...) custom-call(s32[5]{0:T(128)} %copy-done.77, f32[384,1024]{1,0:T(8,128)} %copy-done.10, bf16[384,1024]{1,0:T(8,128)(2,1)} %copy-done.48, ...), custom_call_target="tpu_custom_call" | custom-call | tf_op jit(solution)/shard_map/pallas_call | solution.py:46
  203.7 2.7 shard_map.152
  213.1 15.2 %all-gather.2 = bf16[256,1024]{1,0:T(8,128)(2,1)S(1)} all-gather(bf16[64,1024]{1,0:T(8,128)(2,1)S(1)} %get-tuple-element.284.returned), channel_id=4, replica_groups=mesh['section'=2,'dp'=4,'tensor'=4] {'tensor'}, dimensions={0}, use_global_device_ids=true | all-gather | bytes 655360 | tf_op jit(solution)/shard_map/all_gather | solution.py:1091
  228.3 2.5 shard_map.154
  233.5 3.4 shard_map.155
  240.0 4.7 %all-to-all-start.2 = ((bf16[4,64,1024]{2,1,0:T(8,128)(2,1)}), bf16[4,64,1024]{2,1,0:T(8,128)(2,1)}, u32[]{:S(2)}, u32[]{:S(2)}) async-start(bf16[4,64,1024]{2,1,0:T(8,128)(2,1)} %copy-done.58), calls=%async_computation.2 | async-start | bytes 1048576 | tf_op jit(solution)/shard_map/all_to_all | solution.py:1096
  247.3 2.5 shard_map.156
  254.5 2.4 shard_map.158
  262.7 16.4 %all-gather.3 = bf16[256,1024]{1,0:T(8,128)(2,1)} all-gather(bf16[64,1024]{1,0:T(8,128)(2,1)S(1)} %get-tuple-element.315), channel_id=5, replica_groups=mesh['section'=2,'dp'=4,'tensor'=4] {'tensor'}, dimensions={0}, use_global_device_ids=true | all-gather | bytes 655360 | tf_op jit(solution)/shard_map/all_gather | solution.py:1091
  279.1 6.6 %shard_map.160 = (bf16[256,1024]{1,0:T(8,128)(2,1)}, bf16[3,256,256]{2,1,0:T(8,128)(2,1)}, bf16[3,256,128]{2,1,0:T(8,128)(2,1)}, bf16[4,64,1024]{2,1,0:T(8,128)(2,1)}) custom-call(s32[5]{0:T(128)} %copy-done.77, bf16[4,64,1024]{2,1,0:T(8,128)(2,1)} %bitcast.70, bf16[3,256,256]{2,1,0:T(8,128)(2,1)} %get-tuple-element.318.rest_1_, ...), custom_call_target="tpu_custom_call" | custom-call | tf_op jit(solution)/shard_map/pallas_call | solution.py:46
  285.7 5.5 %all-to-all-start.3 = ((bf16[4,64,1024]{2,1,0:T(8,128)(2,1)}), bf16[4,64,1024]{2,1,0:T(8,128)(2,1)}, u32[]{:S(2)}, u32[]{:S(2)}) async-start(bf16[4,64,1024]{2,1,0:T(8,128)(2,1)} %get-tuple-element.320), calls=%async_computation.3 | async-start | bytes 1048576 | tf_op jit(solution)/shard_map/all_to_all | solution.py:1096
  293.4 1.8 shard_map.161
  295.9 2.3 shard_map.162
  299.0 2.0 collective-permute-start.53
  301.1 2.4 collective-permute-start.56
  304.8 2.2 shard_map.163
  320.2 5.1 %collective-permute-done.53.arrived.refs_1_ = bf16[2,2,256,256]{3,2,1,0:T(8,128)(2,1)S(1)} collective-permute-done((bf16[2,2,256,256]{3,2,1,0:T(8,128)(2,1)}, bf16[2,2,256,256]{3,2,1,0:T(8,128)(2,1)S(1)}, u32[]{:S(2)}, u32[]{:S(2)}) %collective-permute-start.53) | collective-permute-done | bytes 524320 | tf_op jit(solution)/shard_map/ppermute | solution.py:65
  333.8 10.5 %all_to_all.25 = f32[4,2,1024]{2,1,0:T(2,128)} all-to-all(f32[4,2,1024]{2,1,0:T(2,128)S(1)} %broadcast_in_dim.19), channel_id=1, replica_groups=mesh['section'=2,'dp'=4,'tensor'=4] {'tensor'}, dimensions={0} | all-to-all | bytes 65536 | tf_op jit(solution)/shard_map/all_to_all | solution.py:1520
  352.9 3.3 collective-permute-done.62.x_part
  361.6 3.4 shard_map.173
  365.0 2.8 collective-permute-done.65.x_part
  372.6 2.3 shard_map.174
  374.9 5.5 %collective-permute-done.67.far_kept = bf16[4,256,256]{2,1,0:T(8,128)(2,1)S(1)} collective-permute-done((bf16[4,256,256]{2,1,0:T(8,128)(2,1)S(1)}, bf16[4,256,256]{2,1,0:T(8,128)(2,1)S(1)}, u32[]{:S(2)}, u32[]{:S(2)}) %collective-permute-start.67) | collective-permute-done | bytes 524320 | tf_op jit(solution)/shard_map/ppermute | solution.py:65
  380.4 2.0 shard_map.175
  382.4 2.5 collective-permute-done.69.far_kept
  384.9 2.2 shard_map.176
  (397 shorter events, 125.6 us)
Async XLA Ops:
  24.7 21.4 %collective-permute-start.3 = (bf16[1024,1024]{1,0:T(8,128)(2,1)}, bf16[1024,1024]{1,0:T(8,128)(2,1)}, u32[]{:S(2)}, u32[]{:S(2)}) collective-permute-start(bf16[1024,1024]{1,0:T(8,128)(2,1)} %bitcast.41), channel_id=1, source_target_pairs={{0,16},{16,0},{1,17},{17,1},{2,18},{18,2},{3,19},{19,3},{4,20},{20... | collective-permute-start | bytes 6291464 | tf_op jit(solution)/shard_map/ppermute | solution.py:65
  24.7 21.4 %collective-permute-start.4 = (bf16[1024,1024]{1,0:T(8,128)(2,1)}, bf16[1024,1024]{1,0:T(8,128)(2,1)}, u32[]{:S(2)}, u32[]{:S(2)}) collective-permute-start(bf16[1024,1024]{1,0:T(8,128)(2,1)} %bitcast.45), channel_id=1, source_target_pairs={{0,16},{16,0},{1,17},{17,1},{2,18},{18,2},{3,19},{19,3},{4,20},{20... | collective-permute-start | bytes 6291464 | tf_op jit(solution)/shard_map/ppermute | solution.py:65
  30.7 21.3 %all-to-all-start = ((bf16[4,64,1024]{2,1,0:T(8,128)(2,1)}), bf16[4,64,1024]{2,1,0:T(8,128)(2,1)S(1)}, u32[]{:S(2)}, u32[]{:S(2)}) async-start(bf16[4,64,1024]{2,1,0:T(8,128)(2,1)} %get-tuple-element.204), calls=%async_computation | async-start | bytes 1048576 | tf_op jit(solution)/shard_map/all_to_all | solution.py:1096
  41.6 15.0 %collective-permute-start.5 = (bf16[2,256,256]{2,1,0:T(8,128)(2,1)S(1)}, bf16[2,256,256]{2,1,0:T(8,128)(2,1)S(1)}, u32[]{:S(2)}, u32[]{:S(2)}) collective-permute-start(bf16[2,256,256]{2,1,0:T(8,128)(2,1)S(1)} %get-tuple-element.219), channel_id=1, source_target_pairs={{0,1},{1,0},{2,3},{3,2},{4,5},{5,4},{6,7},{7,6},{8,9},{9,8},{10,11... | collective-permute-start | bytes 786440 | tf_op jit(solution)/shard_map/ppermute | solution.py:65
  43.7 18.4 %collective-permute-start.6 = (bf16[2,256,256]{2,1,0:T(8,128)(2,1)S(1)}, bf16[2,256,256]{2,1,0:T(8,128)(2,1)S(1)}, u32[]{:S(2)}, u32[]{:S(2)}) collective-permute-start(bf16[2,256,256]{2,1,0:T(8,128)(2,1)S(1)} %get-tuple-element.219), channel_id=1, source_target_pairs={{0,2},{1,3},{2,0},{3,1},{4,6},{5,7},{6,4},{7,5},{8,10},{9,11},{10,... | collective-permute-start | bytes 786440 | tf_op jit(solution)/shard_map/ppermute | solution.py:65
  62.1 20.2 %collective-permute-start.7 = (bf16[2,256,256]{2,1,0:T(8,128)(2,1)S(1)}, bf16[2,256,256]{2,1,0:T(8,128)(2,1)S(1)}, u32[]{:S(2)}, u32[]{:S(2)}) collective-permute-start(bf16[2,256,256]{2,1,0:T(8,128)(2,1)S(1)} %collective-permute-done.6.rest_2_), channel_id=1, source_target_pairs={{0,1},{1,0},{2,3},{3,2},{4,5},{5,4},{6,7},{7,6},{8,9},{9,8},{10,11... | collective-permute-start | bytes 786440 | tf_op jit(solution)/shard_map/ppermute | solution.py:65
  89.1 15.3 %collective-permute-start.10 = (bf16[2,3,256,256]{3,2,1,0:T(8,128)(2,1)}, bf16[2,3,256,256]{3,2,1,0:T(8,128)(2,1)}, u32[]{:S(2)}, u32[]{:S(2)}) collective-permute-start(bf16[2,3,256,256]{3,2,1,0:T(8,128)(2,1)} %pad_maximum_fusion), channel_id=1, source_target_pairs={{0,8},{4,12},{8,0},{12,4},{1,9},{5,13},{9,1},{13,5},{2,10},{6,14},... | collective-permute-start | bytes 2359304 | tf_op jit(solution)/shard_map/ppermute | solution.py:65
  90.7 17.8 %collective-permute-start.8 = (bf16[2,3,256,256]{3,2,1,0:T(8,128)(2,1)}, bf16[2,3,256,256]{3,2,1,0:T(8,128)(2,1)}, u32[]{:S(2)}, u32[]{:S(2)}) collective-permute-start(bf16[2,3,256,256]{3,2,1,0:T(8,128)(2,1)} %pad_maximum_fusion), channel_id=1, source_target_pairs={{0,4},{4,0},{8,12},{12,8},{1,5},{5,1},{9,13},{13,9},{2,6},{6,2},{1... | collective-permute-start | bytes 2359304 | tf_op jit(solution)/shard_map/ppermute | solution.py:65
  92.2 25.8 %collective-permute-start.12 = (bf16[4,256,256]{2,1,0:T(8,128)(2,1)S(1)}, bf16[4,256,256]{2,1,0:T(8,128)(2,1)S(1)}, u32[]{:S(2)}, u32[]{:S(2)}) collective-permute-start(bf16[4,256,256]{2,1,0:T(8,128)(2,1)S(1)} %get-tuple-element.230), channel_id=1, source_target_pairs={{0,2},{1,3},{2,0},{3,1},{4,6},{5,7},{6,4},{7,5},{8,10},{9,11},{10,... | collective-permute-start | bytes 1572872 | tf_op jit(solution)/shard_map/ppermute | solution.py:65
  92.9 30.5 %all-to-all-start.1 = ((bf16[4,64,1024]{2,1,0:T(8,128)(2,1)}), bf16[4,64,1024]{2,1,0:T(8,128)(2,1)S(1)}, u32[]{:S(2)}, u32[]{:S(2)}) async-start(bf16[4,64,1024]{2,1,0:T(8,128)(2,1)} %get-tuple-element.224), calls=%async_computation.1 | async-start | bytes 1048576 | tf_op jit(solution)/shard_map/all_to_all | solution.py:1096
  105.4 12.5 %collective-permute-start.11 = (bf16[3,256,256]{2,1,0:T(8,128)(2,1)S(1)}, bf16[3,256,256]{2,1,0:T(8,128)(2,1)S(1)}, u32[]{:S(2)}, u32[]{:S(2)}) collective-permute-start(bf16[3,256,256]{2,1,0:T(8,128)(2,1)S(1)} %slice_bitcast_fusion), channel_id=1, source_target_pairs={{0,4},{4,0},{8,12},{12,8},{1,5},{5,1},{9,13},{13,9},{2,6},{6,2},{1... | collective-permute-start | bytes 1179656 | tf_op jit(solution)/shard_map/ppermute | solution.py:65
  123.5 13.8 %collective-permute-start.14 = (bf16[4,256,256]{2,1,0:T(8,128)(2,1)S(1)}, bf16[4,256,256]{2,1,0:T(8,128)(2,1)S(1)}, u32[]{:S(2)}, u32[]{:S(2)}) collective-permute-start(bf16[4,256,256]{2,1,0:T(8,128)(2,1)S(1)} %collective-permute-done.12.rest_1_), channel_id=1, source_target_pairs={{0,4},{4,0},{8,12},{12,8},{1,5},{5,1},{9,13},{13,9},{2,6},{6,2},{1... | collective-permute-start | bytes 1572872 | tf_op jit(solution)/shard_map/ppermute | solution.py:65
  124.1 13.5 %collective-permute-start.15 = (bf16[4,256,256]{2,1,0:T(8,128)(2,1)S(1)}, bf16[4,256,256]{2,1,0:T(8,128)(2,1)S(1)}, u32[]{:S(2)}, u32[]{:S(2)}) collective-permute-start(bf16[4,256,256]{2,1,0:T(8,128)(2,1)S(1)} %collective-permute-done.12.rest_1_), channel_id=1, source_target_pairs={{0,8},{4,12},{8,0},{12,4},{1,9},{5,13},{9,1},{13,5},{2,10},{6,14},... | collective-permute-start | bytes 1572872 | tf_op jit(solution)/shard_map/ppermute | solution.py:65
  124.6 10.7 %collective-permute-start.16 = (bf16[192,1024]{1,0:T(8,128)(2,1)S(1)}, bf16[192,1024]{1,0:T(8,128)(2,1)S(1)}, u32[]{:S(2)}, u32[]{:S(2)}) collective-permute-start(bf16[192,1024]{1,0:T(8,128)(2,1)S(1)} %get-tuple-element.239), channel_id=1, source_target_pairs={{0,1},{1,0},{2,3},{3,2},{4,5},{5,4},{6,7},{7,6},{8,9},{9,8},{10,11... | collective-permute-start | bytes 1179656 | tf_op jit(solution)/shard_map/ppermute | solution.py:65
  144.9 16.5 %collective-permute-start.20 = (bf16[192,1024]{1,0:T(8,128)(2,1)S(1)}, bf16[192,1024]{1,0:T(8,128)(2,1)S(1)}, u32[]{:S(2)}, u32[]{:S(2)}) collective-permute-start(bf16[192,1024]{1,0:T(8,128)(2,1)S(1)} %get-tuple-element.242), channel_id=1, source_target_pairs={{0,1},{1,0},{2,3},{3,2},{4,5},{5,4},{6,7},{7,6},{8,9},{9,8},{10,11... | collective-permute-start | bytes 1179656 | tf_op jit(solution)/shard_map/ppermute | solution.py:65
  147.9 13.5 %collective-permute-start.22 = (bf16[192,1024]{1,0:T(8,128)(2,1)S(1)}, bf16[192,1024]{1,0:T(8,128)(2,1)S(1)}, u32[]{:S(2)}, u32[]{:S(2)}) collective-permute-start(bf16[192,1024]{1,0:T(8,128)(2,1)S(1)} %collective-permute-done.16.top_same), channel_id=1, source_target_pairs={{0,16},{16,0},{1,17},{17,1},{2,18},{18,2},{3,19},{19,3},{4,20},{20... | collective-permute-start | bytes 1179656 | tf_op jit(solution)/shard_map/ppermute | solution.py:65
  172.3 13.1 %collective-permute-start.26 = (bf16[192,1024]{1,0:T(8,128)(2,1)S(1)}, bf16[192,1024]{1,0:T(8,128)(2,1)S(1)}, u32[]{:S(2)}, u32[]{:S(2)}) collective-permute-start(bf16[192,1024]{1,0:T(8,128)(2,1)S(1)} %shard_map.147), channel_id=1, source_target_pairs={{0,1},{1,0},{2,3},{3,2},{4,5},{5,4},{6,7},{7,6},{8,9},{9,8},{10,11... | collective-permute-start | bytes 1179656 | tf_op jit(solution)/shard_map/ppermute | solution.py:65
  173.5 12.3 %collective-permute-start.25 = (bf16[384,1024]{1,0:T(8,128)(2,1)S(1)}, bf16[384,1024]{1,0:T(8,128)(2,1)S(1)}, u32[]{:S(2)}, u32[]{:S(2)}) collective-permute-start(bf16[384,1024]{1,0:T(8,128)(2,1)S(1)} %get-tuple-element.248.own_back), channel_id=1, source_target_pairs={{0,16},{16,0},{1,17},{17,1},{2,18},{18,2},{3,19},{19,3},{4,20},{20... | collective-permute-start | bytes 2359304 | tf_op jit(solution)/shard_map/ppermute | solution.py:65
  182.4 25.8 %collective-permute-start.30 = (bf16[2,4,256,256]{3,2,1,0:T(8,128)(2,1)}, bf16[2,4,256,256]{3,2,1,0:T(8,128)(2,1)}, u32[]{:S(2)}, u32[]{:S(2)}) collective-permute-start(bf16[2,4,256,256]{3,2,1,0:T(8,128)(2,1)} %get-tuple-element.286), channel_id=1, source_target_pairs={{0,4},{4,0},{8,12},{12,8},{1,5},{5,1},{9,13},{13,9},{2,6},{6,2},{1... | collective-permute-start | bytes 3145736 | tf_op jit(solution)/shard_map/ppermute | solution.py:65
  183.9 25.1 %collective-permute-start.31 = (bf16[2,4,256,256]{3,2,1,0:T(8,128)(2,1)}, bf16[2,4,256,256]{3,2,1,0:T(8,128)(2,1)}, u32[]{:S(2)}, u32[]{:S(2)}) collective-permute-start(bf16[2,4,256,256]{3,2,1,0:T(8,128)(2,1)} %get-tuple-element.287), channel_id=1, source_target_pairs={{0,8},{4,12},{8,0},{12,4},{1,9},{5,13},{9,1},{13,5},{2,10},{6,14},... | collective-permute-start | bytes 3145736 | tf_op jit(solution)/shard_map/ppermute | solution.py:65
  185.5 14.2 %collective-permute-start.28 = (bf16[192,1024]{1,0:T(8,128)(2,1)S(1)}, bf16[192,1024]{1,0:T(8,128)(2,1)S(1)}, u32[]{:S(2)}, u32[]{:S(2)}) collective-permute-start(bf16[192,1024]{1,0:T(8,128)(2,1)S(1)} %shard_map.150), channel_id=1, source_target_pairs={{0,1},{1,0},{2,3},{3,2},{4,5},{5,4},{6,7},{7,6},{8,9},{9,8},{10,11... | collective-permute-start | bytes 1179656 | tf_op jit(solution)/shard_map/ppermute | solution.py:65
  206.4 27.1 %collective-permute-start.32 = (bf16[2,4,256,256]{3,2,1,0:T(8,128)(2,1)S(1)}, bf16[2,4,256,256]{3,2,1,0:T(8,128)(2,1)S(1)}, u32[]{:S(2)}, u32[]{:S(2)}) collective-permute-start(bf16[2,4,256,256]{3,2,1,0:T(8,128)(2,1)S(1)} %get-tuple-element.289), channel_id=1, source_target_pairs={{0,4},{4,0},{8,12},{12,8},{1,5},{5,1},{9,13},{13,9},{2,6},{6,2},{1... | collective-permute-start | bytes 3145736 | tf_op jit(solution)/shard_map/ppermute | solution.py:65
  207.6 25.9 %collective-permute-start.33 = (bf16[2,4,256,256]{3,2,1,0:T(8,128)(2,1)S(1)}, bf16[2,4,256,256]{3,2,1,0:T(8,128)(2,1)S(1)}, u32[]{:S(2)}, u32[]{:S(2)}) collective-permute-start(bf16[2,4,256,256]{3,2,1,0:T(8,128)(2,1)S(1)} %get-tuple-element.290), channel_id=1, source_target_pairs={{0,8},{4,12},{8,0},{12,4},{1,9},{5,13},{9,1},{13,5},{2,10},{6,14},... | collective-permute-start | bytes 3145736 | tf_op jit(solution)/shard_map/ppermute | solution.py:65
  208.2 24.3 %collective-permute-start.36 = (bf16[256,1024]{1,0:T(8,128)(2,1)}, bf16[256,1024]{1,0:T(8,128)(2,1)S(1)}, u32[]{:S(2)}, u32[]{:S(2)}) collective-permute-start(bf16[256,1024]{1,0:T(8,128)(2,1)} %get-tuple-element.296.second), channel_id=1, source_target_pairs={{0,16},{16,0},{1,17},{17,1},{2,18},{18,2},{3,19},{19,3},{4,20},{20... | collective-permute-start | bytes 1572872 | tf_op jit(solution)/shard_map/ppermute | solution.py:65
  209.0 24.4 %collective-permute-start.34 = (bf16[256,1024]{1,0:T(8,128)(2,1)S(1)}, bf16[256,1024]{1,0:T(8,128)(2,1)S(1)}, u32[]{:S(2)}, u32[]{:S(2)}) collective-permute-start(bf16[256,1024]{1,0:T(8,128)(2,1)S(1)} %copy-done.59), channel_id=1, source_target_pairs={{0,16},{16,0},{1,17},{17,1},{2,18},{18,2},{3,19},{19,3},{4,20},{20... | collective-permute-start | bytes 1572872 | tf_op jit(solution)/shard_map/ppermute | solution.py:65
  209.0 21.8 %collective-permute-start.37 = (bf16[256,512]{1,0:T(8,128)(2,1)}, bf16[256,512]{1,0:T(8,128)(2,1)S(1)}, u32[]{:S(2)}, u32[]{:S(2)}) collective-permute-start(bf16[256,512]{1,0:T(8,128)(2,1)} %get-tuple-element.298), channel_id=1, source_target_pairs={{0,16},{16,0},{1,17},{17,1},{2,18},{18,2},{3,19},{19,3},{4,20},{20... | collective-permute-start | bytes 786440 | tf_op jit(solution)/shard_map/ppermute | solution.py:65
  230.8 14.0 %collective-permute-start.38 = (bf16[4,256,256]{2,1,0:T(8,128)(2,1)}, bf16[4,256,256]{2,1,0:T(8,128)(2,1)}, u32[]{:S(2)}, u32[]{:S(2)}) collective-permute-start(bf16[4,256,256]{2,1,0:T(8,128)(2,1)} %get-tuple-element.303), channel_id=1, source_target_pairs={{0,8},{4,12},{8,0},{12,4},{1,9},{5,13},{9,1},{13,5},{2,10},{6,14},... | collective-permute-start | bytes 1572872 | tf_op jit(solution)/shard_map/ppermute | solution.py:65
  232.4 12.3 %collective-permute-start.39 = (bf16[4,256,256]{2,1,0:T(8,128)(2,1)}, bf16[4,256,256]{2,1,0:T(8,128)(2,1)}, u32[]{:S(2)}, u32[]{:S(2)}) collective-permute-start(bf16[4,256,256]{2,1,0:T(8,128)(2,1)} %get-tuple-element.288), channel_id=1, source_target_pairs={{0,4},{4,0},{8,12},{12,8},{1,5},{5,1},{9,13},{13,9},{2,6},{6,2},{1... | collective-permute-start | bytes 1572872 | tf_op jit(solution)/shard_map/ppermute | solution.py:65
  240.0 20.7 %all-to-all-start.2 = ((bf16[4,64,1024]{2,1,0:T(8,128)(2,1)}), bf16[4,64,1024]{2,1,0:T(8,128)(2,1)}, u32[]{:S(2)}, u32[]{:S(2)}) async-start(bf16[4,64,1024]{2,1,0:T(8,128)(2,1)} %copy-done.58), calls=%async_computation.2 | async-start | bytes 1048576 | tf_op jit(solution)/shard_map/all_to_all | solution.py:1096
  251.0 28.0 %collective-permute-start.42 = (bf16[4,256,256]{2,1,0:T(8,128)(2,1)}, bf16[4,256,256]{2,1,0:T(8,128)(2,1)}, u32[]{:S(2)}, u32[]{:S(2)}) collective-permute-start(bf16[4,256,256]{2,1,0:T(8,128)(2,1)} %get-tuple-element.316), channel_id=1, source_target_pairs={{0,8},{4,12},{8,0},{12,4},{1,9},{5,13},{9,1},{13,5},{2,10},{6,14},... | collective-permute-start | bytes 1572872 | tf_op jit(solution)/shard_map/ppermute | solution.py:65
  251.5 27.5 %collective-permute-start.43 = (bf16[4,256,256]{2,1,0:T(8,128)(2,1)}, bf16[4,256,256]{2,1,0:T(8,128)(2,1)}, u32[]{:S(2)}, u32[]{:S(2)}) collective-permute-start(bf16[4,256,256]{2,1,0:T(8,128)(2,1)} %get-tuple-element.306), channel_id=1, source_target_pairs={{0,4},{4,0},{8,12},{12,8},{1,5},{5,1},{9,13},{13,9},{2,6},{6,2},{1... | collective-permute-start | bytes 1572872 | tf_op jit(solution)/shard_map/ppermute | solution.py:65
  258.5 32.7 %collective-permute-start.44 = (bf16[2,2,256,256]{3,2,1,0:T(8,128)(2,1)}, bf16[2,2,256,256]{3,2,1,0:T(8,128)(2,1)}, u32[]{:S(2)}, u32[]{:S(2)}) collective-permute-start(bf16[2,2,256,256]{3,2,1,0:T(8,128)(2,1)} %get-tuple-element.322), channel_id=1, source_target_pairs={{0,4},{4,0},{8,12},{12,8},{1,5},{5,1},{9,13},{13,9},{2,6},{6,2},{1... | collective-permute-start | bytes 1572872 | tf_op jit(solution)/shard_map/ppermute | solution.py:65
  259.2 32.0 %collective-permute-start.45 = (bf16[2,2,256,256]{3,2,1,0:T(8,128)(2,1)}, bf16[2,2,256,256]{3,2,1,0:T(8,128)(2,1)}, u32[]{:S(2)}, u32[]{:S(2)}) collective-permute-start(bf16[2,2,256,256]{3,2,1,0:T(8,128)(2,1)} %get-tuple-element.323), channel_id=1, source_target_pairs={{0,8},{4,12},{8,0},{12,4},{1,9},{5,13},{9,1},{13,5},{2,10},{6,14},... | collective-permute-start | bytes 1572872 | tf_op jit(solution)/shard_map/ppermute | solution.py:65
  285.7 24.3 %all-to-all-start.3 = ((bf16[4,64,1024]{2,1,0:T(8,128)(2,1)}), bf16[4,64,1024]{2,1,0:T(8,128)(2,1)}, u32[]{:S(2)}, u32[]{:S(2)}) async-start(bf16[4,64,1024]{2,1,0:T(8,128)(2,1)} %get-tuple-element.320), calls=%async_computation.3 | async-start | bytes 1048576 | tf_op jit(solution)/shard_map/all_to_all | solution.py:1096
  291.2 13.5 %collective-permute-start.47 = (bf16[256,1024]{1,0:T(8,128)(2,1)}, bf16[256,1024]{1,0:T(8,128)(2,1)S(1)}, u32[]{:S(2)}, u32[]{:S(2)}) collective-permute-start(bf16[256,1024]{1,0:T(8,128)(2,1)} %get-tuple-element.331.mid), channel_id=1, source_target_pairs={{0,16},{16,0},{1,17},{17,1},{2,18},{18,2},{3,19},{19,3},{4,20},{20... | collective-permute-start | bytes 1572872 | tf_op jit(solution)/shard_map/ppermute | solution.py:65
  295.2 12.5 %collective-permute-start.49 = (bf16[2,256,256]{2,1,0:T(8,128)(2,1)S(1)}, bf16[2,256,256]{2,1,0:T(8,128)(2,1)S(1)}, u32[]{:S(2)}, u32[]{:S(2)}) collective-permute-start(bf16[2,256,256]{2,1,0:T(8,128)(2,1)S(1)} %get-tuple-element.340), channel_id=1, source_target_pairs={{0,8},{4,12},{8,0},{12,4},{1,9},{5,13},{9,1},{13,5},{2,10},{6,14},... | collective-permute-start | bytes 786440 | tf_op jit(solution)/shard_map/ppermute | solution.py:65
  299.0 26.3 %collective-permute-start.53 = (bf16[2,2,256,256]{3,2,1,0:T(8,128)(2,1)}, bf16[2,2,256,256]{3,2,1,0:T(8,128)(2,1)S(1)}, u32[]{:S(2)}, u32[]{:S(2)}) collective-permute-start(bf16[2,2,256,256]{3,2,1,0:T(8,128)(2,1)} %get-tuple-element.346), channel_id=1, source_target_pairs={{0,1},{1,0},{2,3},{3,2},{4,5},{5,4},{6,7},{7,6},{8,9},{9,8},{10,11... | collective-permute-start | bytes 1572872 | tf_op jit(solution)/shard_map/ppermute | solution.py:65
  301.1 26.3 %collective-permute-start.56 = (bf16[1,4,256,256]{3,2,1,0:T(8,128)(2,1)}, bf16[1,4,256,256]{3,2,1,0:T(8,128)(2,1)S(1)}, u32[]{:S(2)}, u32[]{:S(2)}) collective-permute-start(bf16[1,4,256,256]{3,2,1,0:T(8,128)(2,1)} %get-tuple-element.350), channel_id=1, source_target_pairs={{0,2},{1,3},{2,0},{3,1},{4,6},{5,7},{6,4},{7,5},{8,10},{9,11},{10,... | collective-permute-start | bytes 1572872 | tf_op jit(solution)/shard_map/ppermute | solution.py:65
  307.0 10.3 %collective-permute-start.51 = (bf16[2,1,256,256]{3,2,1,0:T(8,128)(2,1)}, bf16[2,1,256,256]{3,2,1,0:T(8,128)(2,1)S(1)}, u32[]{:S(2)}, u32[]{:S(2)}) collective-permute-start(bf16[2,1,256,256]{3,2,1,0:T(8,128)(2,1)} %get-tuple-element.342), channel_id=1, source_target_pairs={{0,4},{4,0},{8,12},{12,8},{1,5},{5,1},{9,13},{13,9},{2,6},{6,2},{1... | collective-permute-start | bytes 786440 | tf_op jit(solution)/shard_map/ppermute | solution.py:65
  328.3 16.9 %collective-permute-start.57 = (bf16[2,256,256]{2,1,0:T(8,128)(2,1)}, bf16[2,256,256]{2,1,0:T(8,128)(2,1)}, u32[]{:S(2)}, u32[]{:S(2)}) collective-permute-start(bf16[2,256,256]{2,1,0:T(8,128)(2,1)} %shard_map.167), channel_id=1, source_target_pairs={{0,2},{1,3},{2,0},{3,1},{4,6},{5,7},{6,4},{7,5},{8,10},{9,11},{10,... | collective-permute-start | bytes 786440 | tf_op jit(solution)/shard_map/ppermute | solution.py:65
  330.2 26.1 %collective-permute-start.62 = (bf16[8,256,256]{2,1,0:T(8,128)(2,1)S(1)}, bf16[8,256,256]{2,1,0:T(8,128)(2,1)S(1)}, u32[]{:S(2)}, u32[]{:S(2)}) collective-permute-start(bf16[8,256,256]{2,1,0:T(8,128)(2,1)S(1)} %constant_dynamic-update-slice_fusion.own), channel_id=1, source_target_pairs={{0,4},{4,0},{8,12},{12,8},{1,5},{5,1},{9,13},{13,9},{2,6},{6,2},{1... | collective-permute-start | bytes 3145736 | tf_op jit(solution)/shard_map/ppermute | solution.py:65
  331.5 26.0 %collective-permute-start.63 = (bf16[8,256,256]{2,1,0:T(8,128)(2,1)S(1)}, bf16[8,256,256]{2,1,0:T(8,128)(2,1)S(1)}, u32[]{:S(2)}, u32[]{:S(2)}) collective-permute-start(bf16[8,256,256]{2,1,0:T(8,128)(2,1)S(1)} %constant_dynamic-update-slice_fusion.own), channel_id=1, source_target_pairs={{0,8},{4,12},{8,0},{12,4},{1,9},{5,13},{9,1},{13,5},{2,10},{6,14},... | collective-permute-start | bytes 3145736 | tf_op jit(solution)/shard_map/ppermute | solution.py:65
  350.1 17.7 %collective-permute-start.65 = (bf16[1056,256]{1,0:T(8,128)(2,1)S(1)}, bf16[1056,256]{1,0:T(8,128)(2,1)S(1)}, u32[]{:S(2)}, u32[]{:S(2)}) collective-permute-start(bf16[1056,256]{1,0:T(8,128)(2,1)S(1)} %pad_maximum_fusion.1.own), channel_id=1, source_target_pairs={{0,4},{4,0},{8,12},{12,8},{1,5},{5,1},{9,13},{13,9},{2,6},{6,2},{1... | collective-permute-start | bytes 1622024 | tf_op jit(solution)/shard_map/ppermute | solution.py:65
  351.4 17.7 %collective-permute-start.66 = (bf16[1056,256]{1,0:T(8,128)(2,1)S(1)}, bf16[1056,256]{1,0:T(8,128)(2,1)S(1)}, u32[]{:S(2)}, u32[]{:S(2)}) collective-permute-start(bf16[1056,256]{1,0:T(8,128)(2,1)S(1)} %pad_maximum_fusion.1.own), channel_id=1, source_target_pairs={{0,8},{4,12},{8,0},{12,4},{1,9},{5,13},{9,1},{13,5},{2,10},{6,14},... | collective-permute-start | bytes 1622024 | tf_op jit(solution)/shard_map/ppermute | solution.py:65
  357.7 22.7 %collective-permute-start.67 = (bf16[4,256,256]{2,1,0:T(8,128)(2,1)S(1)}, bf16[4,256,256]{2,1,0:T(8,128)(2,1)S(1)}, u32[]{:S(2)}, u32[]{:S(2)}) collective-permute-start(bf16[4,256,256]{2,1,0:T(8,128)(2,1)S(1)} %slice.34), channel_id=1, source_target_pairs={{0,8},{4,12},{8,0},{12,4},{1,9},{5,13},{9,1},{13,5},{2,10},{6,14},... | collective-permute-start | bytes 1572872 | tf_op jit(solution)/shard_map/ppermute | solution.py:65
  359.2 21.1 %collective-permute-start.68 = (bf16[4,256,256]{2,1,0:T(8,128)(2,1)S(1)}, bf16[4,256,256]{2,1,0:T(8,128)(2,1)S(1)}, u32[]{:S(2)}, u32[]{:S(2)}) collective-permute-start(bf16[4,256,256]{2,1,0:T(8,128)(2,1)S(1)} %slice.35), channel_id=1, source_target_pairs={{0,4},{4,0},{8,12},{12,8},{1,5},{5,1},{9,13},{13,9},{2,6},{6,2},{1... | collective-permute-start | bytes 1572872 | tf_op jit(solution)/shard_map/ppermute | solution.py:65
  369.2 15.7 %collective-permute-start.70 = (bf16[544,256]{1,0:T(8,128)(2,1)S(1)}, bf16[544,256]{1,0:T(8,128)(2,1)S(1)}, u32[]{:S(2)}, u32[]{:S(2)}) collective-permute-start(bf16[544,256]{1,0:T(8,128)(2,1)S(1)} %slice.31), channel_id=1, source_target_pairs={{0,4},{4,0},{8,12},{12,8},{1,5},{5,1},{9,13},{13,9},{2,6},{6,2},{1... | collective-permute-start | bytes 835592 | tf_op jit(solution)/shard_map/ppermute | solution.py:65
  370.0 14.9 %collective-permute-start.69 = (bf16[512,256]{1,0:T(8,128)(2,1)S(1)}, bf16[512,256]{1,0:T(8,128)(2,1)S(1)}, u32[]{:S(2)}, u32[]{:S(2)}) collective-permute-start(bf16[512,256]{1,0:T(8,128)(2,1)S(1)} %slice.30), channel_id=1, source_target_pairs={{0,8},{4,12},{8,0},{12,4},{1,9},{5,13},{9,1},{13,5},{2,10},{6,14},... | collective-permute-start | bytes 786440 | tf_op jit(solution)/shard_map/ppermute | solution.py:65
  (140 other events, 1011.5 us)

commit v10 on v9

--- a/solution.py
+++ b/solution.py
@@ -41,7 +41,7 @@
     def until(self, *values):
         self.tokens += values
 
-    def call(self, body, outs, args, specs, scratch=(), limit=36, us=2.0, grid=(), place=VM, aliases=()):
+    def call(self, body, outs, args, specs, scratch=(), limit=40, us=2.0, grid=(), place=VM, aliases=()):
         args = (self.after(args[0]),) + tuple(args[1:])
         results = pl.pallas_call(
             body,

time: 394 us -> 394 us (level)
  no operation moved by 1% of the time
where the time goes in v10:
time: 394 us; the launch traced here: 388 us
  Pallas kernels  106 us (27%)
  waiting for transfers between devices  80.5 us (20%)
  blocking collectives  80.2 us (20%)
  starting transfers between devices  72.6 us (18%)
  local copies, waits for them, and re-layouts  42 us (11%)
  other arithmetic  4.24 us (1%)
    pallas_call x42, Pallas kernels, call(): pl.pallas_call(body, out_shape=tuple(outs), grid=grid, in_specs=list(spec...  106 us
    ppermute x71, waiting for transfers between devices, swap(): return lax.ppermute(value, axis, [(i, i ^ flip) for i in range(count)])  74.3 us
    all_gather x4, blocking collectives, gather(): gathered = lax.all_gather(rows, 'tensor')  69.7 us
    ppermute x71, starting transfers between devices, swap(): return lax.ppermute(value, axis, [(i, i ^ flip) for i in range(count)])  53.4 us
    unnamed x227, local copies, waits for them, and re-layouts  39.7 us
    all_to_all x4, starting transfers between devices, scatter(): return lax.all_to_all(partial, 'tensor', 0, 0)  19.2 us
    all_to_all x1, blocking collectives, over(): return jnp.sum(lax.all_to_all(order.after(copies), axis, 0, 0), axis=0)  10.5 us
  transfers between devices with their start and end apart: 75, of which 30 were waited for; matrix products, arithmetic and copies ran while one was open for 1% of the time, Pallas kernels for 23%

profile of v10, /device:TPU:0, one launch (start us, length us, event | category | flops | bytes accessed | tf_op | source)
XLA Modules:
  0.0 387.9 jit_solution(1187530116427441126)
XLA Ops:
  6.7 17.9 %all-gather = bf16[256,1024]{1,0:T(8,128)(2,1)} all-gather(bf16[64,1024]{1,0:T(8,128)(2,1)S(1)} %get-tuple-element.198), channel_id=2, replica_groups=mesh['section'=2,'dp'=4,'tensor'=4] {'tensor'}, dimensions={0}, use_global_device_ids=true | all-gather | bytes 655360 | tf_op jit(solution)/shard_map/all_gather | solution.py:1091
  25.2 5.5 %shard_map.136 = (bf16[256,1024]{1,0:T(8,128)(2,1)}, bf16[3,256,256]{2,1,0:T(8,128)(2,1)}, bf16[4,256,256]{2,1,0:T(8,128)(2,1)}, bf16[256,256]{1,0:T(8,128)(2,1)...) custom-call(s32[5]{0:T(128)} %copy-done.77, bf16[4,64,1024]{2,1,0:T(8,128)(2,1)} %bitcast.71, ...), custom_call_target="tpu_custom_call" | custom-call | tf_op jit(solution)/shard_map/pallas_call | solution.py:46
  30.7 5.4 %all-to-all-start = ((bf16[4,64,1024]{2,1,0:T(8,128)(2,1)}), bf16[4,64,1024]{2,1,0:T(8,128)(2,1)S(1)}, u32[]{:S(2)}, u32[]{:S(2)}) async-start(bf16[4,64,1024]{2,1,0:T(8,128)(2,1)} %get-tuple-element.204), calls=%async_computation | async-start | bytes 1048576 | tf_op jit(solution)/shard_map/all_to_all | solution.py:1096
  41.6 2.1 collective-permute-start.5
  43.7 2.4 collective-permute-start.6
  46.1 2.3 shard_map.138
  52.2 4.4 %collective-permute-done.5.rest_1_ = bf16[2,256,256]{2,1,0:T(8,128)(2,1)S(1)} collective-permute-done((bf16[2,256,256]{2,1,0:T(8,128)(2,1)S(1)}, bf16[2,256,256]{2,1,0:T(8,128)(2,1)S(1)}, u32[]{:S(2)}, u32[]{:S(2)}) %collective-permute-start.5) | collective-permute-done | bytes 262176 | tf_op jit(solution)/shard_map/ppermute | solution.py:65
  56.6 5.6 %collective-permute-done.6.rest_2_ = bf16[2,256,256]{2,1,0:T(8,128)(2,1)S(1)} collective-permute-done((bf16[2,256,256]{2,1,0:T(8,128)(2,1)S(1)}, bf16[2,256,256]{2,1,0:T(8,128)(2,1)S(1)}, u32[]{:S(2)}, u32[]{:S(2)}) %collective-permute-start.6) | collective-permute-done | bytes 262176 | tf_op jit(solution)/shard_map/ppermute | solution.py:65
  62.1 20.2 %all-gather.1 = bf16[256,1024]{1,0:T(8,128)(2,1)} all-gather(bf16[64,1024]{1,0:T(8,128)(2,1)S(1)} %get-tuple-element.221), channel_id=3, replica_groups=mesh['section'=2,'dp'=4,'tensor'=4] {'tensor'}, dimensions={0}, use_global_device_ids=true | all-gather | bytes 655360 | tf_op jit(solution)/shard_map/all_gather | solution.py:1091
  82.4 5.8 %shard_map.141 = (bf16[256,1024]{1,0:T(8,128)(2,1)}, f32[256,1024]{1,0:T(8,128)}, bf16[256,1024]{1,0:T(8,128)(2,1)}, bf16[256,512]{1,0:T(8,128)(2,1)}, bf16[4,64,1024]{2,1,0:T(8,128)(2,1)}) custom-call(s32[5]{0:T(128)} %copy-done.77, bf16[4,64,1024]{2,1,0:T(8,128)(2,1)} %bitcast.72, bf16[1024,1024]{1,0:T(8,128)(2,1)} %bitcast.42, ...), custom_call_target="tpu_custom_call" | custom-call | tf_op jit(solution)/shard_map/pallas_call | solution.py:46
  92.9 3.6 all-to-all-start.1
  96.6 7.9 %collective-permute-done.10.rest_5_ = bf16[2,3,256,256]{3,2,1,0:T(8,128)(2,1)} collective-permute-done((bf16[2,3,256,256]{3,2,1,0:T(8,128)(2,1)}, bf16[2,3,256,256]{3,2,1,0:T(8,128)(2,1)}, u32[]{:S(2)}, u32[]{:S(2)}) %collective-permute-start.10) | collective-permute-done | bytes 786464 | tf_op jit(solution)/shard_map/ppermute | solution.py:65
  109.8 8.2 %collective-permute-done.12.rest_1_ = bf16[4,256,256]{2,1,0:T(8,128)(2,1)S(1)} collective-permute-done((bf16[4,256,256]{2,1,0:T(8,128)(2,1)S(1)}, bf16[4,256,256]{2,1,0:T(8,128)(2,1)S(1)}, u32[]{:S(2)}, u32[]{:S(2)}) %collective-permute-start.12) | collective-permute-done | bytes 524320 | tf_op jit(solution)/shard_map/ppermute | solution.py:65
  118.7 4.7 %all-to-all-done.1.arrived = bf16[4,64,1024]{2,1,0:T(8,128)(2,1)S(1)} async-done(((bf16[4,64,1024]{2,1,0:T(8,128)(2,1)}), bf16[4,64,1024]{2,1,0:T(8,128)(2,1)S(1)}, u32[]{:S(2)}, u32[]{:S(2)}) %all-to-all-start.1) | async-done | bytes 524320 | tf_op jit(solution)/shard_map/all_to_all | solution.py:1096
  126.6 8.6 %shard_map.143 = (f32[384,1024]{1,0:T(8,128)}, bf16[384,1024]{1,0:T(8,128)(2,1)}, bf16[4,384,256]{2,1,0:T(8,128)(2,1)}, bf16[4,384,128]{2,1,0:T(8,128)(2,1)}, bf...) custom-call(s32[5]{0:T(128)} %copy-done.77, ...), custom_call_target="tpu_custom_call" | custom-call | tf_op jit(solution)/shard_map/pallas_call | solution.py:46
  135.3 2.1 collective-permute-done.14.rest_2_
  137.6 2.5 collective-permute-done.17.other_part
  147.9 5.4 %collective-permute-done.18.rest_4_ = bf16[2,256,256]{2,1,0:T(8,128)(2,1)S(1)} collective-permute-done((bf16[2,256,256]{2,1,0:T(8,128)(2,1)S(1)}, bf16[2,256,256]{2,1,0:T(8,128)(2,1)S(1)}, u32[]{:S(2)}, u32[]{:S(2)}) %collective-permute-start.18) | collective-permute-done | bytes 262176 | tf_op jit(solution)/shard_map/ppermute | solution.py:65
  154.2 7.1 %shard_map.145 = (bf16[4,384,256]{2,1,0:T(8,128)(2,1)S(1)}, bf16[4,384,256]{2,1,0:T(8,128)(2,1)S(1)}, bf16[384,1024]{1,0:T(8,128)(2,1)S(1)}) custom-call(bf16[384,1024]{1,0:T(8,128)(2,1)S(1)} %get-tuple-element.255.second, bf16[384,1024]{1,0:T(8,128)(2,1)S(1)} %get-tuple-element.244.top, bf16[4,4,256,256]{3,2,1,0:T(8,128)(2,1)S(1)} %copy-done.5, ...), custom_call_target="tpu_custom_call" | custom-call | tf_op jit(solution)/shard_map/pallas_call | solution.py:46
  163.1 7.2 %shard_map.146 = (bf16[4,384,256]{2,1,0:T(8,128)(2,1)S(1)}, bf16[4,384,256]{2,1,0:T(8,128)(2,1)S(1)}, bf16[384,1024]{1,0:T(8,128)(2,1)S(1)}, bf16[384,1024]{1,0:...) custom-call(bf16[192,1024]{1,0:T(8,128)(2,1)S(1)} %collective-permute-done.20.second_same, ...), custom_call_target="tpu_custom_call" | custom-call | tf_op jit(solution)/shard_map/pallas_call | solution.py:46
  173.5 4.1 %shard_map.148 = (bf16[2,4,256,256]{3,2,1,0:T(8,128)(2,1)}, bf16[2,4,256,256]{3,2,1,0:T(8,128)(2,1)}, bf16[2,4,256,256]{3,2,1,0:T(8,128)(2,1)S(1)}, bf16[2,4,256,256]{3,2,1,0:T(8,128)(2,1)S(1)}) custom-call(bf16[384,1024]{1,0:T(8,128)(2,1)S(1)} %get-tuple-element.255.second, bf16[384,1024]{1,0:T(8,128)(2,1)S(1)} %get-tuple-element.256.far_second, ...), custom_call_target="tpu_custom_call" | custom-call | tf_op jit(solution)/shard_map/pallas_call | solution.py:46
  177.6 3.3 shard_map.149
  187.9 11.2 %shard_map.151 = (f32[384,1024]{1,0:T(8,128)}, bf16[384,1024]{1,0:T(8,128)(2,1)}, bf16[4,384,256]{2,1,0:T(8,128)(2,1)}, bf16[4,384,128]{2,1,0:T(8,128)(2,1)}, bf...) custom-call(s32[5]{0:T(128)} %copy-done.77, f32[384,1024]{1,0:T(8,128)} %copy-done.10, bf16[384,1024]{1,0:T(8,128)(2,1)} %copy-done.48, ...), custom_call_target="tpu_custom_call" | custom-call | tf_op jit(solution)/shard_map/pallas_call | solution.py:46
  203.7 2.7 shard_map.152
  213.1 15.2 %all-gather.2 = bf16[256,1024]{1,0:T(8,128)(2,1)S(1)} all-gather(bf16[64,1024]{1,0:T(8,128)(2,1)S(1)} %get-tuple-element.284.returned), channel_id=4, replica_groups=mesh['section'=2,'dp'=4,'tensor'=4] {'tensor'}, dimensions={0}, use_global_device_ids=true | all-gather | bytes 655360 | tf_op jit(solution)/shard_map/all_gather | solution.py:1091
  228.3 2.5 shard_map.154
  234.1 3.4 shard_map.155
  240.7 4.7 %all-to-all-start.2 = ((bf16[4,64,1024]{2,1,0:T(8,128)(2,1)}), bf16[4,64,1024]{2,1,0:T(8,128)(2,1)}, u32[]{:S(2)}, u32[]{:S(2)}) async-start(bf16[4,64,1024]{2,1,0:T(8,128)(2,1)} %copy-done.58), calls=%async_computation.2 | async-start | bytes 1048576 | tf_op jit(solution)/shard_map/all_to_all | solution.py:1096
  248.0 2.5 shard_map.156
  255.1 2.4 shard_map.158
  263.3 16.4 %all-gather.3 = bf16[256,1024]{1,0:T(8,128)(2,1)} all-gather(bf16[64,1024]{1,0:T(8,128)(2,1)S(1)} %get-tuple-element.315), channel_id=5, replica_groups=mesh['section'=2,'dp'=4,'tensor'=4] {'tensor'}, dimensions={0}, use_global_device_ids=true | all-gather | bytes 655360 | tf_op jit(solution)/shard_map/all_gather | solution.py:1091
  279.7 6.6 %shard_map.160 = (bf16[256,1024]{1,0:T(8,128)(2,1)}, bf16[3,256,256]{2,1,0:T(8,128)(2,1)}, bf16[3,256,128]{2,1,0:T(8,128)(2,1)}, bf16[4,64,1024]{2,1,0:T(8,128)(2,1)}) custom-call(s32[5]{0:T(128)} %copy-done.77, bf16[4,64,1024]{2,1,0:T(8,128)(2,1)} %bitcast.70, bf16[3,256,256]{2,1,0:T(8,128)(2,1)} %get-tuple-element.318.rest_1_, ...), custom_call_target="tpu_custom_call" | custom-call | tf_op jit(solution)/shard_map/pallas_call | solution.py:46
  286.3 5.5 %all-to-all-start.3 = ((bf16[4,64,1024]{2,1,0:T(8,128)(2,1)}), bf16[4,64,1024]{2,1,0:T(8,128)(2,1)}, u32[]{:S(2)}, u32[]{:S(2)}) async-start(bf16[4,64,1024]{2,1,0:T(8,128)(2,1)} %get-tuple-element.320), calls=%async_computation.3 | async-start | bytes 1048576 | tf_op jit(solution)/shard_map/all_to_all | solution.py:1096
  294.0 1.8 shard_map.161
  296.6 2.3 shard_map.162
  299.7 2.0 collective-permute-start.53
  301.7 2.4 collective-permute-start.56
  305.4 2.2 shard_map.163
  320.9 5.1 %collective-permute-done.53.arrived.refs_1_ = bf16[2,2,256,256]{3,2,1,0:T(8,128)(2,1)S(1)} collective-permute-done((bf16[2,2,256,256]{3,2,1,0:T(8,128)(2,1)}, bf16[2,2,256,256]{3,2,1,0:T(8,128)(2,1)S(1)}, u32[]{:S(2)}, u32[]{:S(2)}) %collective-permute-start.53) | collective-permute-done | bytes 524320 | tf_op jit(solution)/shard_map/ppermute | solution.py:65
  334.5 10.5 %all_to_all.25 = f32[4,2,1024]{2,1,0:T(2,128)} all-to-all(f32[4,2,1024]{2,1,0:T(2,128)S(1)} %broadcast_in_dim.19), channel_id=1, replica_groups=mesh['section'=2,'dp'=4,'tensor'=4] {'tensor'}, dimensions={0} | all-to-all | bytes 65536 | tf_op jit(solution)/shard_map/all_to_all | solution.py:1520
  353.6 3.3 collective-permute-done.62.x_part
  362.3 3.4 shard_map.173
  365.6 2.8 collective-permute-done.65.x_part
  373.2 2.3 shard_map.174
  375.5 5.5 %collective-permute-done.67.far_kept = bf16[4,256,256]{2,1,0:T(8,128)(2,1)S(1)} collective-permute-done((bf16[4,256,256]{2,1,0:T(8,128)(2,1)S(1)}, bf16[4,256,256]{2,1,0:T(8,128)(2,1)S(1)}, u32[]{:S(2)}, u32[]{:S(2)}) %collective-permute-start.67) | collective-permute-done | bytes 524320 | tf_op jit(solution)/shard_map/ppermute | solution.py:65
  381.0 2.0 shard_map.175
  383.0 2.5 collective-permute-done.69.far_kept
  385.5 2.2 shard_map.176
  (397 shorter events, 126.3 us)
Async XLA Ops:
  24.7 21.4 %collective-permute-start.3 = (bf16[1024,1024]{1,0:T(8,128)(2,1)}, bf16[1024,1024]{1,0:T(8,128)(2,1)}, u32[]{:S(2)}, u32[]{:S(2)}) collective-permute-start(bf16[1024,1024]{1,0:T(8,128)(2,1)} %bitcast.41), channel_id=1, source_target_pairs={{0,16},{16,0},{1,17},{17,1},{2,18},{18,2},{3,19},{19,3},{4,20},{20... | collective-permute-start | bytes 6291464 | tf_op jit(solution)/shard_map/ppermute | solution.py:65
  24.7 21.4 %collective-permute-start.4 = (bf16[1024,1024]{1,0:T(8,128)(2,1)}, bf16[1024,1024]{1,0:T(8,128)(2,1)}, u32[]{:S(2)}, u32[]{:S(2)}) collective-permute-start(bf16[1024,1024]{1,0:T(8,128)(2,1)} %bitcast.45), channel_id=1, source_target_pairs={{0,16},{16,0},{1,17},{17,1},{2,18},{18,2},{3,19},{19,3},{4,20},{20... | collective-permute-start | bytes 6291464 | tf_op jit(solution)/shard_map/ppermute | solution.py:65
  30.7 21.3 %all-to-all-start = ((bf16[4,64,1024]{2,1,0:T(8,128)(2,1)}), bf16[4,64,1024]{2,1,0:T(8,128)(2,1)S(1)}, u32[]{:S(2)}, u32[]{:S(2)}) async-start(bf16[4,64,1024]{2,1,0:T(8,128)(2,1)} %get-tuple-element.204), calls=%async_computation | async-start | bytes 1048576 | tf_op jit(solution)/shard_map/all_to_all | solution.py:1096
  41.6 15.0 %collective-permute-start.5 = (bf16[2,256,256]{2,1,0:T(8,128)(2,1)S(1)}, bf16[2,256,256]{2,1,0:T(8,128)(2,1)S(1)}, u32[]{:S(2)}, u32[]{:S(2)}) collective-permute-start(bf16[2,256,256]{2,1,0:T(8,128)(2,1)S(1)} %get-tuple-element.219), channel_id=1, source_target_pairs={{0,1},{1,0},{2,3},{3,2},{4,5},{5,4},{6,7},{7,6},{8,9},{9,8},{10,11... | collective-permute-start | bytes 786440 | tf_op jit(solution)/shard_map/ppermute | solution.py:65
  43.7 18.4 %collective-permute-start.6 = (bf16[2,256,256]{2,1,0:T(8,128)(2,1)S(1)}, bf16[2,256,256]{2,1,0:T(8,128)(2,1)S(1)}, u32[]{:S(2)}, u32[]{:S(2)}) collective-permute-start(bf16[2,256,256]{2,1,0:T(8,128)(2,1)S(1)} %get-tuple-element.219), channel_id=1, source_target_pairs={{0,2},{1,3},{2,0},{3,1},{4,6},{5,7},{6,4},{7,5},{8,10},{9,11},{10,... | collective-permute-start | bytes 786440 | tf_op jit(solution)/shard_map/ppermute | solution.py:65
  62.1 20.2 %collective-permute-start.7 = (bf16[2,256,256]{2,1,0:T(8,128)(2,1)S(1)}, bf16[2,256,256]{2,1,0:T(8,128)(2,1)S(1)}, u32[]{:S(2)}, u32[]{:S(2)}) collective-permute-start(bf16[2,256,256]{2,1,0:T(8,128)(2,1)S(1)} %collective-permute-done.6.rest_2_), channel_id=1, source_target_pairs={{0,1},{1,0},{2,3},{3,2},{4,5},{5,4},{6,7},{7,6},{8,9},{9,8},{10,11... | collective-permute-start | bytes 786440 | tf_op jit(solution)/shard_map/ppermute | solution.py:65
  89.1 15.3 %collective-permute-start.10 = (bf16[2,3,256,256]{3,2,1,0:T(8,128)(2,1)}, bf16[2,3,256,256]{3,2,1,0:T(8,128)(2,1)}, u32[]{:S(2)}, u32[]{:S(2)}) collective-permute-start(bf16[2,3,256,256]{3,2,1,0:T(8,128)(2,1)} %pad_maximum_fusion), channel_id=1, source_target_pairs={{0,8},{4,12},{8,0},{12,4},{1,9},{5,13},{9,1},{13,5},{2,10},{6,14},... | collective-permute-start | bytes 2359304 | tf_op jit(solution)/shard_map/ppermute | solution.py:65
  90.7 17.8 %collective-permute-start.8 = (bf16[2,3,256,256]{3,2,1,0:T(8,128)(2,1)}, bf16[2,3,256,256]{3,2,1,0:T(8,128)(2,1)}, u32[]{:S(2)}, u32[]{:S(2)}) collective-permute-start(bf16[2,3,256,256]{3,2,1,0:T(8,128)(2,1)} %pad_maximum_fusion), channel_id=1, source_target_pairs={{0,4},{4,0},{8,12},{12,8},{1,5},{5,1},{9,13},{13,9},{2,6},{6,2},{1... | collective-permute-start | bytes 2359304 | tf_op jit(solution)/shard_map/ppermute | solution.py:65
  92.2 25.8 %collective-permute-start.12 = (bf16[4,256,256]{2,1,0:T(8,128)(2,1)S(1)}, bf16[4,256,256]{2,1,0:T(8,128)(2,1)S(1)}, u32[]{:S(2)}, u32[]{:S(2)}) collective-permute-start(bf16[4,256,256]{2,1,0:T(8,128)(2,1)S(1)} %get-tuple-element.230), channel_id=1, source_target_pairs={{0,2},{1,3},{2,0},{3,1},{4,6},{5,7},{6,4},{7,5},{8,10},{9,11},{10,... | collective-permute-start | bytes 1572872 | tf_op jit(solution)/shard_map/ppermute | solution.py:65
  92.9 30.5 %all-to-all-start.1 = ((bf16[4,64,1024]{2,1,0:T(8,128)(2,1)}), bf16[4,64,1024]{2,1,0:T(8,128)(2,1)S(1)}, u32[]{:S(2)}, u32[]{:S(2)}) async-start(bf16[4,64,1024]{2,1,0:T(8,128)(2,1)} %get-tuple-element.224), calls=%async_computation.1 | async-start | bytes 1048576 | tf_op jit(solution)/shard_map/all_to_all | solution.py:1096
  105.4 12.5 %collective-permute-start.11 = (bf16[3,256,256]{2,1,0:T(8,128)(2,1)S(1)}, bf16[3,256,256]{2,1,0:T(8,128)(2,1)S(1)}, u32[]{:S(2)}, u32[]{:S(2)}) collective-permute-start(bf16[3,256,256]{2,1,0:T(8,128)(2,1)S(1)} %slice_bitcast_fusion), channel_id=1, source_target_pairs={{0,4},{4,0},{8,12},{12,8},{1,5},{5,1},{9,13},{13,9},{2,6},{6,2},{1... | collective-permute-start | bytes 1179656 | tf_op jit(solution)/shard_map/ppermute | solution.py:65
  123.5 13.8 %collective-permute-start.14 = (bf16[4,256,256]{2,1,0:T(8,128)(2,1)S(1)}, bf16[4,256,256]{2,1,0:T(8,128)(2,1)S(1)}, u32[]{:S(2)}, u32[]{:S(2)}) collective-permute-start(bf16[4,256,256]{2,1,0:T(8,128)(2,1)S(1)} %collective-permute-done.12.rest_1_), channel_id=1, source_target_pairs={{0,4},{4,0},{8,12},{12,8},{1,5},{5,1},{9,13},{13,9},{2,6},{6,2},{1... | collective-permute-start | bytes 1572872 | tf_op jit(solution)/shard_map/ppermute | solution.py:65
  124.1 13.5 %collective-permute-start.15 = (bf16[4,256,256]{2,1,0:T(8,128)(2,1)S(1)}, bf16[4,256,256]{2,1,0:T(8,128)(2,1)S(1)}, u32[]{:S(2)}, u32[]{:S(2)}) collective-permute-start(bf16[4,256,256]{2,1,0:T(8,128)(2,1)S(1)} %collective-permute-done.12.rest_1_), channel_id=1, source_target_pairs={{0,8},{4,12},{8,0},{12,4},{1,9},{5,13},{9,1},{13,5},{2,10},{6,14},... | collective-permute-start | bytes 1572872 | tf_op jit(solution)/shard_map/ppermute | solution.py:65
  124.6 10.7 %collective-permute-start.16 = (bf16[192,1024]{1,0:T(8,128)(2,1)S(1)}, bf16[192,1024]{1,0:T(8,128)(2,1)S(1)}, u32[]{:S(2)}, u32[]{:S(2)}) collective-permute-start(bf16[192,1024]{1,0:T(8,128)(2,1)S(1)} %get-tuple-element.239), channel_id=1, source_target_pairs={{0,1},{1,0},{2,3},{3,2},{4,5},{5,4},{6,7},{7,6},{8,9},{9,8},{10,11... | collective-permute-start | bytes 1179656 | tf_op jit(solution)/shard_map/ppermute | solution.py:65
  144.9 16.5 %collective-permute-start.20 = (bf16[192,1024]{1,0:T(8,128)(2,1)S(1)}, bf16[192,1024]{1,0:T(8,128)(2,1)S(1)}, u32[]{:S(2)}, u32[]{:S(2)}) collective-permute-start(bf16[192,1024]{1,0:T(8,128)(2,1)S(1)} %get-tuple-element.242), channel_id=1, source_target_pairs={{0,1},{1,0},{2,3},{3,2},{4,5},{5,4},{6,7},{7,6},{8,9},{9,8},{10,11... | collective-permute-start | bytes 1179656 | tf_op jit(solution)/shard_map/ppermute | solution.py:65
  147.9 13.5 %collective-permute-start.22 = (bf16[192,1024]{1,0:T(8,128)(2,1)S(1)}, bf16[192,1024]{1,0:T(8,128)(2,1)S(1)}, u32[]{:S(2)}, u32[]{:S(2)}) collective-permute-start(bf16[192,1024]{1,0:T(8,128)(2,1)S(1)} %collective-permute-done.16.top_same), channel_id=1, source_target_pairs={{0,16},{16,0},{1,17},{17,1},{2,18},{18,2},{3,19},{19,3},{4,20},{20... | collective-permute-start | bytes 1179656 | tf_op jit(solution)/shard_map/ppermute | solution.py:65
  172.3 13.1 %collective-permute-start.26 = (bf16[192,1024]{1,0:T(8,128)(2,1)S(1)}, bf16[192,1024]{1,0:T(8,128)(2,1)S(1)}, u32[]{:S(2)}, u32[]{:S(2)}) collective-permute-start(bf16[192,1024]{1,0:T(8,128)(2,1)S(1)} %shard_map.147), channel_id=1, source_target_pairs={{0,1},{1,0},{2,3},{3,2},{4,5},{5,4},{6,7},{7,6},{8,9},{9,8},{10,11... | collective-permute-start | bytes 1179656 | tf_op jit(solution)/shard_map/ppermute | solution.py:65
  173.5 12.3 %collective-permute-start.25 = (bf16[384,1024]{1,0:T(8,128)(2,1)S(1)}, bf16[384,1024]{1,0:T(8,128)(2,1)S(1)}, u32[]{:S(2)}, u32[]{:S(2)}) collective-permute-start(bf16[384,1024]{1,0:T(8,128)(2,1)S(1)} %get-tuple-element.248.own_back), channel_id=1, source_target_pairs={{0,16},{16,0},{1,17},{17,1},{2,18},{18,2},{3,19},{19,3},{4,20},{20... | collective-permute-start | bytes 2359304 | tf_op jit(solution)/shard_map/ppermute | solution.py:65
  182.4 25.8 %collective-permute-start.30 = (bf16[2,4,256,256]{3,2,1,0:T(8,128)(2,1)}, bf16[2,4,256,256]{3,2,1,0:T(8,128)(2,1)}, u32[]{:S(2)}, u32[]{:S(2)}) collective-permute-start(bf16[2,4,256,256]{3,2,1,0:T(8,128)(2,1)} %get-tuple-element.286), channel_id=1, source_target_pairs={{0,4},{4,0},{8,12},{12,8},{1,5},{5,1},{9,13},{13,9},{2,6},{6,2},{1... | collective-permute-start | bytes 3145736 | tf_op jit(solution)/shard_map/ppermute | solution.py:65
  183.9 25.1 %collective-permute-start.31 = (bf16[2,4,256,256]{3,2,1,0:T(8,128)(2,1)}, bf16[2,4,256,256]{3,2,1,0:T(8,128)(2,1)}, u32[]{:S(2)}, u32[]{:S(2)}) collective-permute-start(bf16[2,4,256,256]{3,2,1,0:T(8,128)(2,1)} %get-tuple-element.287), channel_id=1, source_target_pairs={{0,8},{4,12},{8,0},{12,4},{1,9},{5,13},{9,1},{13,5},{2,10},{6,14},... | collective-permute-start | bytes 3145736 | tf_op jit(solution)/shard_map/ppermute | solution.py:65
  185.5 14.2 %collective-permute-start.28 = (bf16[192,1024]{1,0:T(8,128)(2,1)S(1)}, bf16[192,1024]{1,0:T(8,128)(2,1)S(1)}, u32[]{:S(2)}, u32[]{:S(2)}) collective-permute-start(bf16[192,1024]{1,0:T(8,128)(2,1)S(1)} %shard_map.150), channel_id=1, source_target_pairs={{0,1},{1,0},{2,3},{3,2},{4,5},{5,4},{6,7},{7,6},{8,9},{9,8},{10,11... | collective-permute-start | bytes 1179656 | tf_op jit(solution)/shard_map/ppermute | solution.py:65
  206.4 27.7 %collective-permute-start.32 = (bf16[2,4,256,256]{3,2,1,0:T(8,128)(2,1)S(1)}, bf16[2,4,256,256]{3,2,1,0:T(8,128)(2,1)S(1)}, u32[]{:S(2)}, u32[]{:S(2)}) collective-permute-start(bf16[2,4,256,256]{3,2,1,0:T(8,128)(2,1)S(1)} %get-tuple-element.289), channel_id=1, source_target_pairs={{0,4},{4,0},{8,12},{12,8},{1,5},{5,1},{9,13},{13,9},{2,6},{6,2},{1... | collective-permute-start | bytes 3145736 | tf_op jit(solution)/shard_map/ppermute | solution.py:65
  207.6 26.5 %collective-permute-start.33 = (bf16[2,4,256,256]{3,2,1,0:T(8,128)(2,1)S(1)}, bf16[2,4,256,256]{3,2,1,0:T(8,128)(2,1)S(1)}, u32[]{:S(2)}, u32[]{:S(2)}) collective-permute-start(bf16[2,4,256,256]{3,2,1,0:T(8,128)(2,1)S(1)} %get-tuple-element.290), channel_id=1, source_target_pairs={{0,8},{4,12},{8,0},{12,4},{1,9},{5,13},{9,1},{13,5},{2,10},{6,14},... | collective-permute-start | bytes 3145736 | tf_op jit(solution)/shard_map/ppermute | solution.py:65
  208.2 24.9 %collective-permute-start.36 = (bf16[256,1024]{1,0:T(8,128)(2,1)}, bf16[256,1024]{1,0:T(8,128)(2,1)S(1)}, u32[]{:S(2)}, u32[]{:S(2)}) collective-permute-start(bf16[256,1024]{1,0:T(8,128)(2,1)} %get-tuple-element.296.second), channel_id=1, source_target_pairs={{0,16},{16,0},{1,17},{17,1},{2,18},{18,2},{3,19},{19,3},{4,20},{20... | collective-permute-start | bytes 1572872 | tf_op jit(solution)/shard_map/ppermute | solution.py:65
  209.0 25.1 %collective-permute-start.34 = (bf16[256,1024]{1,0:T(8,128)(2,1)S(1)}, bf16[256,1024]{1,0:T(8,128)(2,1)S(1)}, u32[]{:S(2)}, u32[]{:S(2)}) collective-permute-start(bf16[256,1024]{1,0:T(8,128)(2,1)S(1)} %copy-done.59), channel_id=1, source_target_pairs={{0,16},{16,0},{1,17},{17,1},{2,18},{18,2},{3,19},{19,3},{4,20},{20... | collective-permute-start | bytes 1572872 | tf_op jit(solution)/shard_map/ppermute | solution.py:65
  209.0 21.8 %collective-permute-start.37 = (bf16[256,512]{1,0:T(8,128)(2,1)}, bf16[256,512]{1,0:T(8,128)(2,1)S(1)}, u32[]{:S(2)}, u32[]{:S(2)}) collective-permute-start(bf16[256,512]{1,0:T(8,128)(2,1)} %get-tuple-element.298), channel_id=1, source_target_pairs={{0,16},{16,0},{1,17},{17,1},{2,18},{18,2},{3,19},{19,3},{4,20},{20... | collective-permute-start | bytes 786440 | tf_op jit(solution)/shard_map/ppermute | solution.py:65
  231.5 13.9 %collective-permute-start.38 = (bf16[4,256,256]{2,1,0:T(8,128)(2,1)}, bf16[4,256,256]{2,1,0:T(8,128)(2,1)}, u32[]{:S(2)}, u32[]{:S(2)}) collective-permute-start(bf16[4,256,256]{2,1,0:T(8,128)(2,1)} %get-tuple-element.303), channel_id=1, source_target_pairs={{0,8},{4,12},{8,0},{12,4},{1,9},{5,13},{9,1},{13,5},{2,10},{6,14},... | collective-permute-start | bytes 1572872 | tf_op jit(solution)/shard_map/ppermute | solution.py:65
  233.1 12.3 %collective-permute-start.39 = (bf16[4,256,256]{2,1,0:T(8,128)(2,1)}, bf16[4,256,256]{2,1,0:T(8,128)(2,1)}, u32[]{:S(2)}, u32[]{:S(2)}) collective-permute-start(bf16[4,256,256]{2,1,0:T(8,128)(2,1)} %get-tuple-element.288), channel_id=1, source_target_pairs={{0,4},{4,0},{8,12},{12,8},{1,5},{5,1},{9,13},{13,9},{2,6},{6,2},{1... | collective-permute-start | bytes 1572872 | tf_op jit(solution)/shard_map/ppermute | solution.py:65
  240.7 20.7 %all-to-all-start.2 = ((bf16[4,64,1024]{2,1,0:T(8,128)(2,1)}), bf16[4,64,1024]{2,1,0:T(8,128)(2,1)}, u32[]{:S(2)}, u32[]{:S(2)}) async-start(bf16[4,64,1024]{2,1,0:T(8,128)(2,1)} %copy-done.58), calls=%async_computation.2 | async-start | bytes 1048576 | tf_op jit(solution)/shard_map/all_to_all | solution.py:1096
  251.7 28.0 %collective-permute-start.42 = (bf16[4,256,256]{2,1,0:T(8,128)(2,1)}, bf16[4,256,256]{2,1,0:T(8,128)(2,1)}, u32[]{:S(2)}, u32[]{:S(2)}) collective-permute-start(bf16[4,256,256]{2,1,0:T(8,128)(2,1)} %get-tuple-element.316), channel_id=1, source_target_pairs={{0,8},{4,12},{8,0},{12,4},{1,9},{5,13},{9,1},{13,5},{2,10},{6,14},... | collective-permute-start | bytes 1572872 | tf_op jit(solution)/shard_map/ppermute | solution.py:65
  252.2 27.5 %collective-permute-start.43 = (bf16[4,256,256]{2,1,0:T(8,128)(2,1)}, bf16[4,256,256]{2,1,0:T(8,128)(2,1)}, u32[]{:S(2)}, u32[]{:S(2)}) collective-permute-start(bf16[4,256,256]{2,1,0:T(8,128)(2,1)} %get-tuple-element.306), channel_id=1, source_target_pairs={{0,4},{4,0},{8,12},{12,8},{1,5},{5,1},{9,13},{13,9},{2,6},{6,2},{1... | collective-permute-start | bytes 1572872 | tf_op jit(solution)/shard_map/ppermute | solution.py:65
  259.2 32.7 %collective-permute-start.44 = (bf16[2,2,256,256]{3,2,1,0:T(8,128)(2,1)}, bf16[2,2,256,256]{3,2,1,0:T(8,128)(2,1)}, u32[]{:S(2)}, u32[]{:S(2)}) collective-permute-start(bf16[2,2,256,256]{3,2,1,0:T(8,128)(2,1)} %get-tuple-element.322), channel_id=1, source_target_pairs={{0,4},{4,0},{8,12},{12,8},{1,5},{5,1},{9,13},{13,9},{2,6},{6,2},{1... | collective-permute-start | bytes 1572872 | tf_op jit(solution)/shard_map/ppermute | solution.py:65
  259.8 32.0 %collective-permute-start.45 = (bf16[2,2,256,256]{3,2,1,0:T(8,128)(2,1)}, bf16[2,2,256,256]{3,2,1,0:T(8,128)(2,1)}, u32[]{:S(2)}, u32[]{:S(2)}) collective-permute-start(bf16[2,2,256,256]{3,2,1,0:T(8,128)(2,1)} %get-tuple-element.323), channel_id=1, source_target_pairs={{0,8},{4,12},{8,0},{12,4},{1,9},{5,13},{9,1},{13,5},{2,10},{6,14},... | collective-permute-start | bytes 1572872 | tf_op jit(solution)/shard_map/ppermute | solution.py:65
  286.3 24.3 %all-to-all-start.3 = ((bf16[4,64,1024]{2,1,0:T(8,128)(2,1)}), bf16[4,64,1024]{2,1,0:T(8,128)(2,1)}, u32[]{:S(2)}, u32[]{:S(2)}) async-start(bf16[4,64,1024]{2,1,0:T(8,128)(2,1)} %get-tuple-element.320), calls=%async_computation.3 | async-start | bytes 1048576 | tf_op jit(solution)/shard_map/all_to_all | solution.py:1096
  291.8 13.5 %collective-permute-start.47 = (bf16[256,1024]{1,0:T(8,128)(2,1)}, bf16[256,1024]{1,0:T(8,128)(2,1)S(1)}, u32[]{:S(2)}, u32[]{:S(2)}) collective-permute-start(bf16[256,1024]{1,0:T(8,128)(2,1)} %get-tuple-element.331.mid), channel_id=1, source_target_pairs={{0,16},{16,0},{1,17},{17,1},{2,18},{18,2},{3,19},{19,3},{4,20},{20... | collective-permute-start | bytes 1572872 | tf_op jit(solution)/shard_map/ppermute | solution.py:65
  295.8 12.5 %collective-permute-start.49 = (bf16[2,256,256]{2,1,0:T(8,128)(2,1)S(1)}, bf16[2,256,256]{2,1,0:T(8,128)(2,1)S(1)}, u32[]{:S(2)}, u32[]{:S(2)}) collective-permute-start(bf16[2,256,256]{2,1,0:T(8,128)(2,1)S(1)} %get-tuple-element.340), channel_id=1, source_target_pairs={{0,8},{4,12},{8,0},{12,4},{1,9},{5,13},{9,1},{13,5},{2,10},{6,14},... | collective-permute-start | bytes 786440 | tf_op jit(solution)/shard_map/ppermute | solution.py:65
  299.7 26.3 %collective-permute-start.53 = (bf16[2,2,256,256]{3,2,1,0:T(8,128)(2,1)}, bf16[2,2,256,256]{3,2,1,0:T(8,128)(2,1)S(1)}, u32[]{:S(2)}, u32[]{:S(2)}) collective-permute-start(bf16[2,2,256,256]{3,2,1,0:T(8,128)(2,1)} %get-tuple-element.346), channel_id=1, source_target_pairs={{0,1},{1,0},{2,3},{3,2},{4,5},{5,4},{6,7},{7,6},{8,9},{9,8},{10,11... | collective-permute-start | bytes 1572872 | tf_op jit(solution)/shard_map/ppermute | solution.py:65
  301.7 26.3 %collective-permute-start.56 = (bf16[1,4,256,256]{3,2,1,0:T(8,128)(2,1)}, bf16[1,4,256,256]{3,2,1,0:T(8,128)(2,1)S(1)}, u32[]{:S(2)}, u32[]{:S(2)}) collective-permute-start(bf16[1,4,256,256]{3,2,1,0:T(8,128)(2,1)} %get-tuple-element.350), channel_id=1, source_target_pairs={{0,2},{1,3},{2,0},{3,1},{4,6},{5,7},{6,4},{7,5},{8,10},{9,11},{10,... | collective-permute-start | bytes 1572872 | tf_op jit(solution)/shard_map/ppermute | solution.py:65
  307.7 10.3 %collective-permute-start.51 = (bf16[2,1,256,256]{3,2,1,0:T(8,128)(2,1)}, bf16[2,1,256,256]{3,2,1,0:T(8,128)(2,1)S(1)}, u32[]{:S(2)}, u32[]{:S(2)}) collective-permute-start(bf16[2,1,256,256]{3,2,1,0:T(8,128)(2,1)} %get-tuple-element.342), channel_id=1, source_target_pairs={{0,4},{4,0},{8,12},{12,8},{1,5},{5,1},{9,13},{13,9},{2,6},{6,2},{1... | collective-permute-start | bytes 786440 | tf_op jit(solution)/shard_map/ppermute | solution.py:65
  328.9 16.9 %collective-permute-start.57 = (bf16[2,256,256]{2,1,0:T(8,128)(2,1)}, bf16[2,256,256]{2,1,0:T(8,128)(2,1)}, u32[]{:S(2)}, u32[]{:S(2)}) collective-permute-start(bf16[2,256,256]{2,1,0:T(8,128)(2,1)} %shard_map.167), channel_id=1, source_target_pairs={{0,2},{1,3},{2,0},{3,1},{4,6},{5,7},{6,4},{7,5},{8,10},{9,11},{10,... | collective-permute-start | bytes 786440 | tf_op jit(solution)/shard_map/ppermute | solution.py:65
  330.8 26.1 %collective-permute-start.62 = (bf16[8,256,256]{2,1,0:T(8,128)(2,1)S(1)}, bf16[8,256,256]{2,1,0:T(8,128)(2,1)S(1)}, u32[]{:S(2)}, u32[]{:S(2)}) collective-permute-start(bf16[8,256,256]{2,1,0:T(8,128)(2,1)S(1)} %constant_dynamic-update-slice_fusion.own), channel_id=1, source_target_pairs={{0,4},{4,0},{8,12},{12,8},{1,5},{5,1},{9,13},{13,9},{2,6},{6,2},{1... | collective-permute-start | bytes 3145736 | tf_op jit(solution)/shard_map/ppermute | solution.py:65
  332.2 26.0 %collective-permute-start.63 = (bf16[8,256,256]{2,1,0:T(8,128)(2,1)S(1)}, bf16[8,256,256]{2,1,0:T(8,128)(2,1)S(1)}, u32[]{:S(2)}, u32[]{:S(2)}) collective-permute-start(bf16[8,256,256]{2,1,0:T(8,128)(2,1)S(1)} %constant_dynamic-update-slice_fusion.own), channel_id=1, source_target_pairs={{0,8},{4,12},{8,0},{12,4},{1,9},{5,13},{9,1},{13,5},{2,10},{6,14},... | collective-permute-start | bytes 3145736 | tf_op jit(solution)/shard_map/ppermute | solution.py:65
  350.7 17.7 %collective-permute-start.65 = (bf16[1056,256]{1,0:T(8,128)(2,1)S(1)}, bf16[1056,256]{1,0:T(8,128)(2,1)S(1)}, u32[]{:S(2)}, u32[]{:S(2)}) collective-permute-start(bf16[1056,256]{1,0:T(8,128)(2,1)S(1)} %pad_maximum_fusion.1.own), channel_id=1, source_target_pairs={{0,4},{4,0},{8,12},{12,8},{1,5},{5,1},{9,13},{13,9},{2,6},{6,2},{1... | collective-permute-start | bytes 1622024 | tf_op jit(solution)/shard_map/ppermute | solution.py:65
  352.1 17.7 %collective-permute-start.66 = (bf16[1056,256]{1,0:T(8,128)(2,1)S(1)}, bf16[1056,256]{1,0:T(8,128)(2,1)S(1)}, u32[]{:S(2)}, u32[]{:S(2)}) collective-permute-start(bf16[1056,256]{1,0:T(8,128)(2,1)S(1)} %pad_maximum_fusion.1.own), channel_id=1, source_target_pairs={{0,8},{4,12},{8,0},{12,4},{1,9},{5,13},{9,1},{13,5},{2,10},{6,14},... | collective-permute-start | bytes 1622024 | tf_op jit(solution)/shard_map/ppermute | solution.py:65
  358.3 22.7 %collective-permute-start.67 = (bf16[4,256,256]{2,1,0:T(8,128)(2,1)S(1)}, bf16[4,256,256]{2,1,0:T(8,128)(2,1)S(1)}, u32[]{:S(2)}, u32[]{:S(2)}) collective-permute-start(bf16[4,256,256]{2,1,0:T(8,128)(2,1)S(1)} %slice.34), channel_id=1, source_target_pairs={{0,8},{4,12},{8,0},{12,4},{1,9},{5,13},{9,1},{13,5},{2,10},{6,14},... | collective-permute-start | bytes 1572872 | tf_op jit(solution)/shard_map/ppermute | solution.py:65
  359.9 21.1 %collective-permute-start.68 = (bf16[4,256,256]{2,1,0:T(8,128)(2,1)S(1)}, bf16[4,256,256]{2,1,0:T(8,128)(2,1)S(1)}, u32[]{:S(2)}, u32[]{:S(2)}) collective-permute-start(bf16[4,256,256]{2,1,0:T(8,128)(2,1)S(1)} %slice.35), channel_id=1, source_target_pairs={{0,4},{4,0},{8,12},{12,8},{1,5},{5,1},{9,13},{13,9},{2,6},{6,2},{1... | collective-permute-start | bytes 1572872 | tf_op jit(solution)/shard_map/ppermute | solution.py:65
  369.8 15.7 %collective-permute-start.70 = (bf16[544,256]{1,0:T(8,128)(2,1)S(1)}, bf16[544,256]{1,0:T(8,128)(2,1)S(1)}, u32[]{:S(2)}, u32[]{:S(2)}) collective-permute-start(bf16[544,256]{1,0:T(8,128)(2,1)S(1)} %slice.31), channel_id=1, source_target_pairs={{0,4},{4,0},{8,12},{12,8},{1,5},{5,1},{9,13},{13,9},{2,6},{6,2},{1... | collective-permute-start | bytes 835592 | tf_op jit(solution)/shard_map/ppermute | solution.py:65
  370.7 14.9 %collective-permute-start.69 = (bf16[512,256]{1,0:T(8,128)(2,1)S(1)}, bf16[512,256]{1,0:T(8,128)(2,1)S(1)}, u32[]{:S(2)}, u32[]{:S(2)}) collective-permute-start(bf16[512,256]{1,0:T(8,128)(2,1)S(1)} %slice.30), channel_id=1, source_target_pairs={{0,8},{4,12},{8,0},{12,4},{1,9},{5,13},{9,1},{13,5},{2,10},{6,14},... | collective-permute-start | bytes 786440 | tf_op jit(solution)/shard_map/ppermute | solution.py:65
  (140 other events, 1008.3 us)
